TPU v7x, 128 devices: a whole 4x4x4 slice. The times are simulated.
128 devices in a mesh: gx: 8 (over z, core), gy: 16 (over y, x).
Axes of the slice: x: 4, y: 4, z: 4, core: 2. Of those that a mesh axis runs over, the one named last changes fastest.
Arguments:
- air_surface_exchanges: bfloat16 [8, 128, 1024], P(None, 'gy', 'gx'), may hold values from -6 to 6
- outbound_patch_tables: int32 [16, 8, 2, 2, 2, 64], P('gy', 'gx'), may hold values from -1 to 63, as said below
- outbound_coefficient_panels: bfloat16 [16, 8, 2, 2, 64, 16, 128], P('gy', 'gx'), may hold values from -1 to 1
- submerged_strata_tally: int32 [256, 4096], P('gy', 'gx'), may hold values from 0 to 10
- thermal_anomaly: float32 [10, 256, 4096], P(None, 'gy', 'gx'), may hold values from -6 to 6
- saltiness_anomaly: float32 [10, 256, 4096], P(None, 'gy', 'gx'), may hold values from -6 to 6
- inbound_patch_tables: int32 [16, 8, 2, 2, 2, 64], P('gy', 'gx'), may hold values from -1 to 63, as said below
- inbound_coefficient_panels: bfloat16 [16, 8, 2, 2, 64, 16, 128], P('gy', 'gx'), may hold values from -0.375 to 0.375
Outputs:
- new_temp: float32 [10, 256, 4096], P(None, 'gy', 'gx')
- new_salt: float32 [10, 256, 4096], P(None, 'gy', 'gx')
- atm_surface: float32 [4, 128, 1024], P(None, 'gy', 'gx')
Inputs may be any that keep to these rules, and one draw needn't show every extreme that they name: outbound_patch_tables: row 0 lies below 64, row 1 below 64, both -1 together in unused slots, which stand at the end of each list. Entries with the same target block stand next to each other in rising order of that block; each list names each target block at most 2 times. No entry targets a latitude tile beyond the grid. inbound_patch_tables: row 0 lies below 64, row 1 below 64, both -1 together in unused slots, which stand at the end of each list. Entries with the same target block stand next to each other in rising order of that block. No entry targets a latitude tile beyond the grid.
All inputs are finite; a program needn't handle non-finite values.
Results may differ from a plain program's by a relative error of at most 0.0017.
Values sent between devices are 32-bit elements; how exact they have to be, the bound alone decides.
No kernel may reach another device: no remote copies, remote signals or barrier semaphores. Data moves between devices by JAX's collectives and lax.ppermute only.
A program may use at most 64 MiB of HBM per device.

v0:
```python
import jax
import jax.numpy as jnp
from jax import lax
from jax.sharding import PartitionSpec as P

HEAT_RATE = 0.1
SHORTWAVE_RATE = 0.1
FRESH_RATE = 0.05
SIDE_RATE = 0.18
MIX_BASE = 0.03
MIX_WIND = 0.09
MIX_DECAY = 0.8


def from_behind(block, axis, distance):
    devices = range(lax.axis_size(axis))
    route = [(i - distance, i) for i in devices if i - distance in devices]
    return lax.ppermute(block, axis, route)


def shifted(shard, axis, by):
    length = lax.axis_size(axis)
    return lax.ppermute(shard, axis, [(i, (i + by) % length) for i in range(length)])


def padded_2(shard, sides, width):
    for axis, dim in sides:
        size, length = (lax.axis_size(axis), shard.shape[dim])
        up = [(i, (i + 1) % size) for i in range(size)]
        down = [(j, i) for i, j in up]
        last = lax.slice_in_dim(shard, length - width, length, axis=dim)
        initial = lax.slice_in_dim(shard, 0, width, axis=dim)
        before = lax.ppermute(last, axis, up)
        after = lax.ppermute(initial, axis, down)
        shard = jnp.concatenate([before, shard, after], axis=dim)
    return shard


def surface_terms(forcing):
    heat_flux = forcing[0] + forcing[1] + forcing[2]
    shortwave = forcing[3]
    fresh_flux = forcing[4] - forcing[5] + forcing[6]
    gust_term = forcing[7] * forcing[7] / (1.0 + forcing[7] * forcing[7])
    return jnp.stack([heat_flux, shortwave, fresh_flux, gust_term])


def advance(padded, wet_pad, planes):
    strata_total = padded.shape[1]
    height = padded.shape[2] - 2
    col_count = padded.shape[3] - 2
    centre = padded[:, :, 1:-1, 1:-1]
    wet_mid = wet_pad[:, 1:-1, 1:-1]
    side_sum = jnp.zeros_like(centre)
    for row_shift, col_shift in ((0, 1), (2, 1), (1, 0), (1, 2)):
        beside = padded[:, :, row_shift : row_shift + height, col_shift : col_shift + col_count]
        wet_beside = wet_pad[:, row_shift : row_shift + height, col_shift : col_shift + col_count]
        side_sum = side_sum + wet_beside * (beside - centre)
    depth_index = jnp.arange(strata_total - 1, dtype=jnp.float32)
    mixing = (MIX_BASE + MIX_WIND * planes[3])[None] * (MIX_DECAY**depth_index)[:, None, None]
    across = mixing * wet_mid[:-1] * wet_mid[1:] * (centre[:, 1:] - centre[:, :-1])
    zero_face = jnp.zeros_like(across[:, :1])
    vertical = jnp.concatenate([across, zero_face], 1) - jnp.concatenate([zero_face, across], 1)
    profile = jnp.exp(-0.5 * jnp.arange(strata_total, dtype=jnp.float32))
    top_level = (jnp.arange(strata_total) == 0).astype(jnp.float32)[:, None, None]
    heat_source = (
        SHORTWAVE_RATE * planes[1][None] * profile[:, None, None]
        + HEAT_RATE * top_level * planes[0][None]
    )
    salt_source = -FRESH_RATE * top_level * planes[2][None] * centre[1, 0][None]
    source = jnp.stack([heat_source, salt_source])
    return centre + wet_mid * (SIDE_RATE * side_sum + vertical + source)


def to_blocks(fields, block_len):
    channels, height, col_count = fields.shape
    arranged = fields.reshape(channels, height, col_count // block_len, block_len).transpose(
        1, 2, 0, 3
    )
    return arranged.reshape(height * (col_count // block_len), channels, block_len)


def from_blocks(blocks, height, col_count):
    block_count, channels, block_len = blocks.shape
    arranged = blocks.reshape(height, col_count // block_len, channels, block_len).transpose(
        2, 0, 1, 3
    )
    return arranged.reshape(channels, height, col_count)


def by_block(pieces, targets):
    return (pieces, jnp.maximum(targets, 0))


def route_forward(pieces, targets):
    moved, moved_ids = from_behind((pieces[0], targets[0]), "gy", -1)
    sectioned = jnp.stack([moved, pieces[1]])
    sectioned_ids = jnp.stack([moved_ids, targets[1]])
    across, across_ids = shifted((sectioned[:, 0], sectioned_ids[:, 0]), "gx", -1)
    arrived = jnp.stack([across, sectioned[:, 1]], 1)
    arrived_ids = jnp.stack([across_ids, sectioned_ids[:, 1]], 1)
    return (arrived, arrived_ids)


def route_back(pieces, targets):
    moved, moved_ids = from_behind((pieces[1], targets[1]), "gy", 1)
    sectioned = jnp.stack([pieces[0], moved])
    sectioned_ids = jnp.stack([targets[0], moved_ids])
    across, across_ids = shifted((sectioned[:, 1], sectioned_ids[:, 1]), "gx", 1)
    landed = jnp.stack([sectioned[:, 0], across], 1)
    landed_ids = jnp.stack([sectioned_ids[:, 0], across_ids], 1)
    return (landed, landed_ids)


def per_device(
    air_surface_exchanges,
    outbound_patch_tables,
    outbound_coefficient_panels,
    submerged_strata_tally,
    thermal_anomaly,
    saltiness_anomaly,
    inbound_patch_tables,
    inbound_coefficient_panels,
):
    channels, atm_rows, atm_cols = air_surface_exchanges.shape
    strata_total, sea_northing_total, sea_easting_total = thermal_anomaly.shape
    block_src = outbound_coefficient_panels.shape[-2]
    block_dst = outbound_coefficient_panels.shape[-1]
    dst_count = sea_northing_total * sea_easting_total // block_dst
    src_count = atm_rows * atm_cols // block_src
    source_blocks = to_blocks(air_surface_exchanges, block_src)
    entry_lists = outbound_patch_tables[0, 0]
    picked = source_blocks[jnp.maximum(entry_lists[:, :, 0], 0)]
    live_mask = (entry_lists[:, :, 0] >= 0).astype(jnp.float32)
    pieces = jnp.einsum(
        "abkcs,abksw->abkcw",
        picked,
        outbound_coefficient_panels[0, 0],
        preferred_element_type=jnp.float32,
    )
    pieces = pieces * live_mask[..., None, None]
    pieces, targets = by_block(pieces, entry_lists[:, :, 1])
    arrived, arrived_ids = route_forward(pieces, targets)
    forcing_blocks = jax.ops.segment_sum(
        arrived.reshape(-1, channels, block_dst), arrived_ids.reshape(-1), num_segments=dst_count
    )
    forcing = from_blocks(forcing_blocks, sea_northing_total, sea_easting_total)
    planes = surface_terms(forcing)
    first_row = lax.axis_index("gy") == 0
    last_row = lax.axis_index("gy") == lax.axis_size("gy") - 1
    strata_real_valued = submerged_strata_tally.astype(jnp.float32)
    piled_quantities = jnp.concatenate(
        [thermal_anomaly, saltiness_anomaly, strata_real_valued[None]], 0
    )
    padded = padded_2(piled_quantities, (("gx", 2), ("gy", 1)), 1)
    transported_quantities = padded[: 2 * strata_total].reshape(
        2, strata_total, sea_northing_total + 2, sea_easting_total + 2
    )
    plane = padded[2 * strata_total]
    rows_here = jnp.arange(plane.shape[0])
    cut_rows = (rows_here < 1) & first_row | (rows_here >= plane.shape[0] - 1) & last_row
    wet_plane = jnp.where(cut_rows[:, None], 0.0, plane)
    wet_pad = (jnp.arange(strata_total, dtype=jnp.float32)[:, None, None] < wet_plane[None]).astype(
        jnp.float32
    )
    stepped = advance(transported_quantities, wet_pad, planes)
    again = padded_2(
        stepped.reshape(2 * strata_total, sea_northing_total, sea_easting_total),
        (("gx", 2), ("gy", 1)),
        1,
    )
    final = advance(
        again.reshape(2, strata_total, sea_northing_total + 2, sea_easting_total + 2),
        wet_pad,
        planes,
    )
    new_temp = final[0]
    new_salt = final[1]
    wet_top = (submerged_strata_tally > 0).astype(jnp.float32)
    surface = jnp.stack(
        [
            new_temp[0] * wet_top,
            new_salt[0] * wet_top,
            (new_temp[0] + new_temp[1] + new_temp[2]) / 3.0 * wet_top,
            wet_top,
        ]
    ).astype(jnp.bfloat16)
    ocean_blocks = to_blocks(surface, block_dst)
    back_entries = inbound_patch_tables[0, 0]
    chosen = ocean_blocks[jnp.maximum(back_entries[:, :, 0], 0)]
    back_live = (back_entries[:, :, 0] >= 0).astype(jnp.float32)
    returns = jnp.einsum(
        "abkcw,abksw->abkcs",
        chosen,
        inbound_coefficient_panels[0, 0],
        preferred_element_type=jnp.float32,
    )
    returns = returns * back_live[..., None, None]
    returns, return_ids = by_block(returns, back_entries[:, :, 1])
    landed, landed_ids = route_back(returns, return_ids)
    atm_blocks = jax.ops.segment_sum(
        landed.reshape(-1, surface.shape[0], block_src),
        landed_ids.reshape(-1),
        num_segments=src_count,
    )
    atm_surface = from_blocks(atm_blocks, atm_rows, atm_cols)
    return (new_temp, new_salt, atm_surface)


def solution(mesh):
    in_specs = (
        P(None, "gy", "gx"),
        P("gy", "gx", None, None, None, None),
        P("gy", "gx", None, None, None, None, None),
        P("gy", "gx"),
        P(None, "gy", "gx"),
        P(None, "gy", "gx"),
        P("gy", "gx", None, None, None, None),
        P("gy", "gx", None, None, None, None, None),
    )
    out_specs = (P(None, "gy", "gx"), P(None, "gy", "gx"), P(None, "gy", "gx"))
    return jax.shard_map(
        per_device, mesh=mesh, in_specs=in_specs, out_specs=out_specs, check_vma=False
    )
```

profile of v0, /device:TPU:8, one launch (start us, length us, event | category | flops | bytes accessed | tf_op | source)
XLA Modules:
  0.0 110.9 jit_solution(9485400437795977612)
XLA Ops:
  0.6 0.8 compare_convert_fusion.1
  1.4 0.8 maximum_reduce_fusion
  2.3 0.8 reshape.243
  3.3 0.8 gather_fusion
  4.1 0.5 convolution_multiply_fusion
  4.6 0.9 fusion.52
  5.5 4.5 %collective-permute-start.6 = (f32[2,64,8,128]{3,2,1,0:T(8,128)}, f32[2,64,8,128]{3,2,1,0:T(8,128)}, u32[]{:S(2)}, u32[]{:S(2)}) collective-permute-start(f32[2,64,8,128]{3,2,1,0:T(8,128)} %get-tuple-element.10), channel_id=1, source_target_pairs={{1,0},{2,1},{3,2},{4,3},{5,4},{6,5},{7,6},{8,7},{9,8},{10,9},{11,1... | collective-permute-start | bytes 1572872 | tf_op jit(solution)/shard_map/ppermute | solution.py:18
  10.0 2.7 %collective-permute-start.4 = (s32[2,64]{1,0:T(2,128)S(1)}, s32[2,64]{1,0:T(2,128)S(1)}, u32[]{:S(2)}, u32[]{:S(2)}) collective-permute-start(s32[2,64]{1,0:T(2,128)S(1)} %bitcast.157), channel_id=1, source_target_pairs={{1,0},{2,1},{3,2},{4,3},{5,4},{6,5},{7,6},{8,7},{9,8},{10,9},{11,1... | collective-permute-start | bytes 1544 | tf_op jit(solution)/shard_map/ppermute | solution.py:18
  12.9 2.9 %collective-permute-start.1 = (f32[21,16,1]{2,1,0:T(8,128)S(1)}, f32[21,16,1]{2,1,0:T(8,128)S(1)}, u32[]{:S(2)}, u32[]{:S(2)}) collective-permute-start(f32[21,16,1]{2,1,0:T(8,128)S(1)} %get-tuple-element.16), channel_id=1, source_target_pairs={{16,0},{32,16},{48,32},{64,48},{80,64},{96,80},{112,96},{0,112},{1... | collective-permute-start | bytes 4040 | tf_op jit(solution)/shard_map/ppermute | solution.py:34
  15.9 0.6 fusion.56
  16.5 3.1 %collective-permute-start.12 = (s32[2,64]{1,0:T(2,128)}, s32[2,64]{1,0:T(2,128)}, u32[]{:S(2)}, u32[]{:S(2)}) collective-permute-start(s32[2,64]{1,0:T(2,128)} %bitcast.31), channel_id=1, source_target_pairs={{0,1},{1,2},{2,3},{3,4},{4,5},{5,6},{6,7},{7,8},{8,9},{9,10},{10,1... | collective-permute-start | bytes 1544 | tf_op jit(solution)/shard_map/ppermute | solution.py:18
  19.6 0.5 iota_power_fusion
  20.1 0.6 compare_select_fusion.1
  20.7 0.5 compare_select_fusion
  21.2 0.6 compare_convert_fusion
  21.8 0.6 and_or_fusion
  22.5 1.6 %collective-permute-start.5 = (s32[2,64]{1,0:T(2,128)S(1)}, s32[2,64]{1,0:T(2,128)S(1)}, u32[]{:S(2)}, u32[]{:S(2)}) collective-permute-start(s32[2,64]{1,0:T(2,128)S(1)} %bitcast.158), channel_id=1, source_target_pairs={{0,112},{16,0},{32,16},{48,32},{64,48},{80,64},{96,80},{112,96},{1... | collective-permute-start | bytes 1544 | tf_op jit(solution)/shard_map/ppermute | solution.py:23
  24.5 1.4 %collective-permute-start.2 = (f32[21,1,514]{2,1,0:T(1,128)S(1)}, f32[21,1,514]{2,1,0:T(1,128)S(1)}, u32[]{:S(2)}, u32[]{:S(2)}) collective-permute-start(f32[21,1,514]{2,1,0:T(1,128)S(1)} %get-tuple-element.11), channel_id=1, source_target_pairs={{0,1},{1,2},{2,3},{3,4},{4,5},{5,6},{6,7},{7,8},{8,9},{9,10},{10,1... | collective-permute-start | bytes 129536 | tf_op jit(solution)/shard_map/ppermute | solution.py:33
  25.9 3.3 %collective-permute-start.3 = (f32[21,1,514]{2,1,0:T(1,128)S(1)}, f32[21,1,514]{2,1,0:T(1,128)S(1)}, u32[]{:S(2)}, u32[]{:S(2)}) collective-permute-start(f32[21,1,514]{2,1,0:T(1,128)S(1)} %get-tuple-element.12), channel_id=1, source_target_pairs={{1,0},{2,1},{3,2},{4,3},{5,4},{6,5},{7,6},{8,7},{9,8},{10,9},{11,1... | collective-permute-start | bytes 129536 | tf_op jit(solution)/shard_map/ppermute | solution.py:34
  29.3 1.9 %collective-permute-done.2 = f32[21,1,514]{2,1,0:T(1,128)S(1)} collective-permute-done((f32[21,1,514]{2,1,0:T(1,128)S(1)}, f32[21,1,514]{2,1,0:T(1,128)S(1)}, u32[]{:S(2)}, u32[]{:S(2)}) %collective-permute-start.2) | collective-permute-done | bytes 43208 | tf_op jit(solution)/shard_map/ppermute | solution.py:33
  31.3 0.6 copy-done.12
  31.9 0.5 pad_maximum_fusion
  32.5 0.7 slice_bitcast_fusion.9
  33.2 1.0 fusion.32
  34.2 1.4 %collective-permute-start.7 = (f32[2,64,8,128]{3,2,1,0:T(8,128)S(1)}, f32[2,64,8,128]{3,2,1,0:T(8,128)S(1)}, u32[]{:S(2)}, u32[]{:S(2)}) collective-permute-start(f32[2,64,8,128]{3,2,1,0:T(8,128)S(1)} %fusion.32), channel_id=1, source_target_pairs={{0,112},{16,0},{32,16},{48,32},{64,48},{80,64},{96,80},{112,96},{1... | collective-permute-start | bytes 1572872 | tf_op jit(solution)/shard_map/ppermute | solution.py:23
  35.7 1.6 %fusion.54 = (f32[10,16,512]{2,1,0:T(8,128)}, f32[10,16,512]{2,1,0:T(8,128)}, f32[10,16,512]{2,1,0:T(8,128)}, f32[10,16,512]{2,1,0:T(8,128)}, f32[10,16,512]{2,1,0:T(8,128)}) fusion(f32[10,18,514]{2,1,0:T(8,128)S(1)} %fusion.28), kind=kLoop, calls=%fused_computation.147 | loop fusion | bytes 3276800 | tf_op jit(solution)/shard_map/slice | solution.py:52
  37.3 5.0 %collective-permute-done.7 = f32[2,64,8,128]{3,2,1,0:T(8,128)S(1)} collective-permute-done((f32[2,64,8,128]{3,2,1,0:T(8,128)S(1)}, f32[2,64,8,128]{3,2,1,0:T(8,128)S(1)}, u32[]{:S(2)}, u32[]{:S(2)}) %collective-permute-start.7) | collective-permute-done | bytes 524320 | tf_op jit(solution)/shard_map/ppermute | solution.py:23
  42.2 2.1 %fusion.1 = f32[2,2,64,8,128]{4,3,2,1,0:T(8,128)} fusion(f32[1,2,64,8,128]{4,3,2,1,0:T(8,128)} %bitcast.16, f32[1,2,64,8,128]{4,3,2,1,0:T(8,128)S(1)} %get-tuple-element.9, f32[2,1,64,8,128]{4,3,2,1,0:T(8,128)S(1)} %bitcast.134), kind=kLoop, calls=%fused_computation.13 | loop fusion | flops 1310720 | bytes 2621440 | tf_op jit(solution)/shard_map/stack | solution.py:99
  44.4 18.9 %scatter_fusion = f32[64,8,128]{2,1,0:T(8,128)S(1)} fusion(f32[64,8,128]{2,1,0:T(8,128)S(1)} %broadcast_in_dim.21, s32[256]{0:T(256)S(1)} %reshape.275, f32[256,8,128]{2,1,0:T(8,128)} %bitcast.129), kind=kCustom, calls=%fused_computation.2 | custom fusion | flops 262144 | bytes 3146752 | tf_op jit(solution)/shard_map/scatter-add | solution.py:143
  63.3 0.5 fusion.49
  64.1 0.4 fusion.30
  65.5 0.8 fusion.6
  66.4 3.1 %collective-permute-start.9 = (f32[20,16,1]{2,1,0:T(8,128)S(1)}, f32[20,16,1]{2,1,0:T(8,128)S(1)}, u32[]{:S(2)}, u32[]{:S(2)}) collective-permute-start(f32[20,16,1]{2,1,0:T(8,128)S(1)} %get-tuple-element.20), channel_id=1, source_target_pairs={{16,0},{32,16},{48,32},{64,48},{80,64},{96,80},{112,96},{0,112},{1... | collective-permute-start | bytes 3848 | tf_op jit(solution)/shard_map/ppermute | solution.py:34
  69.6 3.0 %collective-permute-done.8 = f32[20,16,1]{2,1,0:T(8,128)S(1)} collective-permute-done((f32[20,16,1]{2,1,0:T(8,128)S(1)}, f32[20,16,1]{2,1,0:T(8,128)S(1)}, u32[]{:S(2)}, u32[]{:S(2)}) %collective-permute-start.8) | collective-permute-done | bytes 1312 | tf_op jit(solution)/shard_map/ppermute | solution.py:33
  72.9 1.1 collective-permute-start.10
  74.0 3.1 %collective-permute-start.11 = (f32[20,1,514]{2,1,0:T(1,128)S(1)}, f32[20,1,514]{2,1,0:T(1,128)S(1)}, u32[]{:S(2)}, u32[]{:S(2)}) collective-permute-start(f32[20,1,514]{2,1,0:T(1,128)S(1)} %get-tuple-element.14), channel_id=1, source_target_pairs={{1,0},{2,1},{3,2},{4,3},{5,4},{6,5},{7,6},{8,7},{9,8},{10,9},{11,1... | collective-permute-start | bytes 123368 | tf_op jit(solution)/shard_map/ppermute | solution.py:34
  77.1 0.8 fusion.50
  77.9 1.3 %collective-permute-done.10 = f32[20,1,514]{2,1,0:T(1,128)S(1)} collective-permute-done((f32[20,1,514]{2,1,0:T(1,128)S(1)}, f32[20,1,514]{2,1,0:T(1,128)S(1)}, u32[]{:S(2)}, u32[]{:S(2)}) %collective-permute-start.10) | collective-permute-done | bytes 41152 | tf_op jit(solution)/shard_map/ppermute | solution.py:33
  79.2 0.5 pad_maximum_fusion.1
  80.3 0.8 fusion.9
  81.4 1.0 gather_fusion.1
  82.4 0.7 convolution_multiply_fusion.1
  83.1 3.0 %collective-permute-start.14 = (f32[2,64,4,16]{3,2,1,0:T(4,128)S(1)}, f32[2,64,4,16]{3,2,1,0:T(4,128)S(1)}, u32[]{:S(2)}, u32[]{:S(2)}) collective-permute-start(f32[2,64,4,16]{3,2,1,0:T(4,128)S(1)} %get-tuple-element.29), channel_id=1, source_target_pairs={{0,1},{1,2},{2,3},{3,4},{4,5},{5,6},{6,7},{7,8},{8,9},{9,10},{10,1... | collective-permute-start | bytes 98312 | tf_op jit(solution)/shard_map/ppermute | solution.py:18
  86.2 7.3 %collective-permute-done.14 = f32[2,64,4,16]{3,2,1,0:T(4,128)S(1)} collective-permute-done((f32[2,64,4,16]{3,2,1,0:T(4,128)S(1)}, f32[2,64,4,16]{3,2,1,0:T(4,128)S(1)}, u32[]{:S(2)}, u32[]{:S(2)}) %collective-permute-start.14) | collective-permute-done | bytes 32800 | tf_op jit(solution)/shard_map/ppermute | solution.py:18
  93.6 0.9 slice_bitcast_fusion.1
  94.5 6.7 %collective-permute-done.15 = f32[2,64,4,16]{3,2,1,0:T(4,128)S(1)} collective-permute-done((f32[2,64,4,16]{3,2,1,0:T(4,128)S(1)}, f32[2,64,4,16]{3,2,1,0:T(4,128)S(1)}, u32[]{:S(2)}, u32[]{:S(2)}) %collective-permute-start.15) | collective-permute-done | bytes 32800 | tf_op jit(solution)/shard_map/ppermute | solution.py:23
  101.4 8.8 %scatter_fusion.1 = f32[64,4,16]{2,1,0:T(4,128)S(1)} fusion(f32[64,4,16]{2,1,0:T(4,128)S(1)} %broadcast_in_dim.22, s32[256]{0:T(256)S(1)} %reshape.283, f32[256,4,16]{2,1,0:T(4,128)S(1)} %bitcast.131), kind=kCustom, calls=%fused_computation.3 | custom fusion | flops 16384 | bytes 197632 | tf_op jit(solution)/shard_map/scatter-add | solution.py:200
  110.2 0.7 reshape.252
  (110 shorter events, 4.1 us)
Async XLA Ops:
  0.6 3.5 %copy-start = (bf16[1,1,2,2,64,16,128]{6,5,4,3,2,1,0:T(8,128)(2,1)S(1)}, bf16[1,1,2,2,64,16,128]{6,5,4,3,2,1,0:T(8,128)(2,1)}, u32[]{:S(2)}) copy-start(bf16[1,1,2,2,64,16,128]{6,5,4,3,2,1,0:T(8,128)(2,1)} %param.10) | copy-start | bytes 3145732
  4.6 8.2 %copy-start.15 = (s32[16,512]{1,0:T(8,128)S(1)}, s32[16,512]{1,0:T(8,128)}, u32[]{:S(2)}) copy-start(s32[16,512]{1,0:T(8,128)} %param.11) | copy-start | bytes 98308
  4.6 8.2 %copy-start.1 = (f32[10,16,512]{2,1,0:T(8,128)S(1)}, f32[10,16,512]{2,1,0:T(8,128)}, u32[]{:S(2)}) copy-start(f32[10,16,512]{2,1,0:T(8,128)} %param.13) | copy-start | bytes 983044
  4.6 8.2 %copy-start.2 = (f32[10,16,512]{2,1,0:T(8,128)S(1)}, f32[10,16,512]{2,1,0:T(8,128)}, u32[]{:S(2)}) copy-start(f32[10,16,512]{2,1,0:T(8,128)} %param.12) | copy-start | bytes 983044
  4.6 16.6 %copy-start.17 = (s32[1,1,2,2,2,64]{5,4,3,2,1,0:T(2,128)S(1)}, s32[1,1,2,2,2,64]{5,4,3,2,1,0:T(2,128)}, u32[]{:S(2)}) copy-start(s32[1,1,2,2,2,64]{5,4,3,2,1,0:T(2,128)} %param.14) | copy-start | bytes 6148
  5.5 27.7 %collective-permute-start.6 = (f32[2,64,8,128]{3,2,1,0:T(8,128)}, f32[2,64,8,128]{3,2,1,0:T(8,128)}, u32[]{:S(2)}, u32[]{:S(2)}) collective-permute-start(f32[2,64,8,128]{3,2,1,0:T(8,128)} %get-tuple-element.10), channel_id=1, source_target_pairs={{1,0},{2,1},{3,2},{4,3},{5,4},{6,5},{7,6},{8,7},{9,8},{10,9},{11,1... | collective-permute-start | bytes 1572872 | tf_op jit(solution)/shard_map/ppermute | solution.py:18
  10.0 12.5 %collective-permute-start.4 = (s32[2,64]{1,0:T(2,128)S(1)}, s32[2,64]{1,0:T(2,128)S(1)}, u32[]{:S(2)}, u32[]{:S(2)}) collective-permute-start(s32[2,64]{1,0:T(2,128)S(1)} %bitcast.157), channel_id=1, source_target_pairs={{1,0},{2,1},{3,2},{4,3},{5,4},{6,5},{7,6},{8,7},{9,8},{10,9},{11,1... | collective-permute-start | bytes 1544 | tf_op jit(solution)/shard_map/ppermute | solution.py:18
  12.9 11.2 %collective-permute-start = (f32[21,16,1]{2,1,0:T(8,128)S(1)}, f32[21,16,1]{2,1,0:T(8,128)S(1)}, u32[]{:S(2)}, u32[]{:S(2)}) collective-permute-start(f32[21,16,1]{2,1,0:T(8,128)S(1)} %get-tuple-element.15), channel_id=1, source_target_pairs={{0,16},{16,32},{32,48},{48,64},{64,80},{80,96},{96,112},{112,0},{1... | collective-permute-start | bytes 4040 | tf_op jit(solution)/shard_map/ppermute | solution.py:33
  12.9 11.2 %collective-permute-start.1 = (f32[21,16,1]{2,1,0:T(8,128)S(1)}, f32[21,16,1]{2,1,0:T(8,128)S(1)}, u32[]{:S(2)}, u32[]{:S(2)}) collective-permute-start(f32[21,16,1]{2,1,0:T(8,128)S(1)} %get-tuple-element.16), channel_id=1, source_target_pairs={{16,0},{32,16},{48,32},{64,48},{80,64},{96,80},{112,96},{0,112},{1... | collective-permute-start | bytes 4040 | tf_op jit(solution)/shard_map/ppermute | solution.py:34
  16.5 60.6 %collective-permute-start.12 = (s32[2,64]{1,0:T(2,128)}, s32[2,64]{1,0:T(2,128)}, u32[]{:S(2)}, u32[]{:S(2)}) collective-permute-start(s32[2,64]{1,0:T(2,128)} %bitcast.31), channel_id=1, source_target_pairs={{0,1},{1,2},{2,3},{3,4},{4,5},{5,6},{6,7},{7,8},{8,9},{9,10},{10,1... | collective-permute-start | bytes 1544 | tf_op jit(solution)/shard_map/ppermute | solution.py:18
  22.5 6.7 %collective-permute-start.5 = (s32[2,64]{1,0:T(2,128)S(1)}, s32[2,64]{1,0:T(2,128)S(1)}, u32[]{:S(2)}, u32[]{:S(2)}) collective-permute-start(s32[2,64]{1,0:T(2,128)S(1)} %bitcast.158), channel_id=1, source_target_pairs={{0,112},{16,0},{32,16},{48,32},{64,48},{80,64},{96,80},{112,96},{1... | collective-permute-start | bytes 1544 | tf_op jit(solution)/shard_map/ppermute | solution.py:23
  24.1 7.2 %copy-start.8 = (f32[21,16,1]{2,1,0:T(8,128)}, f32[21,16,1]{2,1,0:T(8,128)S(1)}, u32[]{:S(2)}) copy-start(f32[21,16,1]{2,1,0:T(8,128)S(1)} %collective-permute-done) | copy-start | bytes 4036
  24.1 7.2 %copy-start.10 = (f32[21,16,1]{2,1,0:T(8,128)}, f32[21,16,1]{2,1,0:T(8,128)S(1)}, u32[]{:S(2)}) copy-start(f32[21,16,1]{2,1,0:T(8,128)S(1)} %collective-permute-done.1) | copy-start | bytes 4036
  24.5 6.8 %collective-permute-start.2 = (f32[21,1,514]{2,1,0:T(1,128)S(1)}, f32[21,1,514]{2,1,0:T(1,128)S(1)}, u32[]{:S(2)}, u32[]{:S(2)}) collective-permute-start(f32[21,1,514]{2,1,0:T(1,128)S(1)} %get-tuple-element.11), channel_id=1, source_target_pairs={{0,1},{1,2},{2,3},{3,4},{4,5},{5,6},{6,7},{7,8},{8,9},{9,10},{10,1... | collective-permute-start | bytes 129536 | tf_op jit(solution)/shard_map/ppermute | solution.py:33
  25.9 5.4 %collective-permute-start.3 = (f32[21,1,514]{2,1,0:T(1,128)S(1)}, f32[21,1,514]{2,1,0:T(1,128)S(1)}, u32[]{:S(2)}, u32[]{:S(2)}) collective-permute-start(f32[21,1,514]{2,1,0:T(1,128)S(1)} %get-tuple-element.12), channel_id=1, source_target_pairs={{1,0},{2,1},{3,2},{4,3},{5,4},{6,5},{7,6},{8,7},{9,8},{10,9},{11,1... | collective-permute-start | bytes 129536 | tf_op jit(solution)/shard_map/ppermute | solution.py:34
  31.3 0.6 copy-start.12
  32.5 3.1 %copy-start.9 = (f32[21,16,1]{2,1,0:T(8,128)S(1)}, f32[21,16,1]{2,1,0:T(8,128)}, u32[]{:S(2)}) copy-start(f32[21,16,1]{2,1,0:T(8,128)} %copy-done.8) | copy-start | bytes 4036
  32.5 3.1 %copy-start.11 = (f32[21,16,1]{2,1,0:T(8,128)S(1)}, f32[21,16,1]{2,1,0:T(8,128)}, u32[]{:S(2)}) copy-start(f32[21,16,1]{2,1,0:T(8,128)} %copy-done.10) | copy-start | bytes 4036
  32.5 3.1 %copy-start.13 = (f32[21,1,514]{2,1,0:T(1,128)S(1)}, f32[21,1,514]{2,1,0:T(1,128)}, u32[]{:S(2)}) copy-start(f32[21,1,514]{2,1,0:T(1,128)} %copy-done.12) | copy-start | bytes 129532
  32.5 3.0 %copy-start.21 = (pred[18]{0:T(512)(128)(4,1)S(1)}, pred[18]{0:T(512)(128)(4,1)}, u32[]{:S(2)}) copy-start(pred[18]{0:T(512)(128)(4,1)} %and_or_fusion) | copy-start | bytes 58
  34.2 8.1 %collective-permute-start.7 = (f32[2,64,8,128]{3,2,1,0:T(8,128)S(1)}, f32[2,64,8,128]{3,2,1,0:T(8,128)S(1)}, u32[]{:S(2)}, u32[]{:S(2)}) collective-permute-start(f32[2,64,8,128]{3,2,1,0:T(8,128)S(1)} %fusion.32), channel_id=1, source_target_pairs={{0,112},{16,0},{32,16},{48,32},{64,48},{80,64},{96,80},{112,96},{1... | collective-permute-start | bytes 1572872 | tf_op jit(solution)/shard_map/ppermute | solution.py:23
  44.4 19.4 %copy-start.24 = (f32[9]{0:T(128)S(1)}, f32[9]{0:T(128)}, u32[]{:S(2)}) copy-start(f32[9]{0:T(128)} %iota_power_fusion) | copy-start | bytes 112
  64.0 0.8 copy-start.14
  64.1 0.8 copy-start.19
  64.1 0.8 copy-start.22
  64.1 0.8 copy-start.23
  64.1 1.0 copy-start.3
  64.1 1.1 copy-start.4
  64.1 1.2 %copy-start.5 = (f32[10,16,512]{2,1,0:T(8,128)S(1)}, f32[10,16,512]{2,1,0:T(8,128)}, u32[]{:S(2)}) copy-start(f32[10,16,512]{2,1,0:T(8,128)} %get-tuple-element.23) | copy-start | bytes 983044
  64.1 1.2 %copy-start.6 = (f32[10,16,512]{2,1,0:T(8,128)S(1)}, f32[10,16,512]{2,1,0:T(8,128)}, u32[]{:S(2)}) copy-start(f32[10,16,512]{2,1,0:T(8,128)} %get-tuple-element.24) | copy-start | bytes 983044
  64.1 1.3 %copy-start.7 = (f32[10,16,512]{2,1,0:T(8,128)S(1)}, f32[10,16,512]{2,1,0:T(8,128)}, u32[]{:S(2)}) copy-start(f32[10,16,512]{2,1,0:T(8,128)} %get-tuple-element.25) | copy-start | bytes 983044
  66.3 10.8 %copy-start.18 = (s32[1,2,1,64]{3,2,1,0:T(1,128)S(1)}, s32[1,2,1,64]{3,2,1,0:T(1,128)}, u32[]{:S(2)}) copy-start(s32[1,2,1,64]{3,2,1,0:T(1,128)} %get-tuple-element.36) | copy-start | bytes 1540
  66.4 6.1 %collective-permute-start.8 = (f32[20,16,1]{2,1,0:T(8,128)S(1)}, f32[20,16,1]{2,1,0:T(8,128)S(1)}, u32[]{:S(2)}, u32[]{:S(2)}) collective-permute-start(f32[20,16,1]{2,1,0:T(8,128)S(1)} %get-tuple-element.19), channel_id=1, source_target_pairs={{0,16},{16,32},{32,48},{48,64},{64,80},{80,96},{96,112},{112,0},{1... | collective-permute-start | bytes 3848 | tf_op jit(solution)/shard_map/ppermute | solution.py:33
  66.4 6.1 %collective-permute-start.9 = (f32[20,16,1]{2,1,0:T(8,128)S(1)}, f32[20,16,1]{2,1,0:T(8,128)S(1)}, u32[]{:S(2)}, u32[]{:S(2)}) collective-permute-start(f32[20,16,1]{2,1,0:T(8,128)S(1)} %get-tuple-element.20), channel_id=1, source_target_pairs={{16,0},{32,16},{48,32},{64,48},{80,64},{96,80},{112,96},{0,112},{1... | collective-permute-start | bytes 3848 | tf_op jit(solution)/shard_map/ppermute | solution.py:34
  72.9 6.3 %collective-permute-start.10 = (f32[20,1,514]{2,1,0:T(1,128)S(1)}, f32[20,1,514]{2,1,0:T(1,128)S(1)}, u32[]{:S(2)}, u32[]{:S(2)}) collective-permute-start(f32[20,1,514]{2,1,0:T(1,128)S(1)} %get-tuple-element.13), channel_id=1, source_target_pairs={{0,1},{1,2},{2,3},{3,4},{4,5},{5,6},{6,7},{7,8},{8,9},{9,10},{10,1... | collective-permute-start | bytes 123368 | tf_op jit(solution)/shard_map/ppermute | solution.py:33
  74.0 5.2 %collective-permute-start.11 = (f32[20,1,514]{2,1,0:T(1,128)S(1)}, f32[20,1,514]{2,1,0:T(1,128)S(1)}, u32[]{:S(2)}, u32[]{:S(2)}) collective-permute-start(f32[20,1,514]{2,1,0:T(1,128)S(1)} %get-tuple-element.14), channel_id=1, source_target_pairs={{1,0},{2,1},{3,2},{4,3},{5,4},{6,5},{7,6},{8,7},{9,8},{10,9},{11,1... | collective-permute-start | bytes 123368 | tf_op jit(solution)/shard_map/ppermute | solution.py:34
  77.8 8.3 %collective-permute-start.13 = (s32[2,64]{1,0:T(2,128)S(1)}, s32[2,64]{1,0:T(2,128)S(1)}, u32[]{:S(2)}, u32[]{:S(2)}) collective-permute-start(s32[2,64]{1,0:T(2,128)S(1)} %bitcast.154), channel_id=1, source_target_pairs={{0,16},{16,32},{32,48},{48,64},{64,80},{80,96},{96,112},{112,0},{1... | collective-permute-start | bytes 1544 | tf_op jit(solution)/shard_map/ppermute | solution.py:23
  80.2 0.8 copy-start.16
  80.2 2.1 %copy-start.20 = (f32[2,2,1,64]{3,2,1,0:T(1,128)S(1)}, f32[2,2,1,64]{3,2,1,0:T(1,128)}, u32[]{:S(2)}) copy-start(f32[2,2,1,64]{3,2,1,0:T(1,128)} %compare_convert_fusion) | copy-start | bytes 3076
  80.2 2.1 %copy-start.25 = (bf16[1,1,2,2,64,16,128]{6,5,4,3,2,1,0:T(8,128)(2,1)S(1)}, bf16[1,1,2,2,64,16,128]{6,5,4,3,2,1,0:T(8,128)(2,1)}, u32[]{:S(2)}) copy-start(bf16[1,1,2,2,64,16,128]{6,5,4,3,2,1,0:T(8,128)(2,1)} %param.15) | copy-start | bytes 3145732
  83.1 10.4 %collective-permute-start.14 = (f32[2,64,4,16]{3,2,1,0:T(4,128)S(1)}, f32[2,64,4,16]{3,2,1,0:T(4,128)S(1)}, u32[]{:S(2)}, u32[]{:S(2)}) collective-permute-start(f32[2,64,4,16]{3,2,1,0:T(4,128)S(1)} %get-tuple-element.29), channel_id=1, source_target_pairs={{0,1},{1,2},{2,3},{3,4},{4,5},{5,6},{6,7},{7,8},{8,9},{9,10},{10,1... | collective-permute-start | bytes 98312 | tf_op jit(solution)/shard_map/ppermute | solution.py:18
  93.6 7.6 %collective-permute-start.15 = (f32[2,64,4,16]{3,2,1,0:T(4,128)S(1)}, f32[2,64,4,16]{3,2,1,0:T(4,128)S(1)}, u32[]{:S(2)}, u32[]{:S(2)}) collective-permute-start(f32[2,64,4,16]{3,2,1,0:T(4,128)S(1)} %get-tuple-element.27), channel_id=1, source_target_pairs={{0,16},{16,32},{32,48},{48,64},{64,80},{80,96},{96,112},{112,0},{1... | collective-permute-start | bytes 98312 | tf_op jit(solution)/shard_map/ppermute | solution.py:23
where the time goes:
time: 112 us; the launch traced here: 111 us
  other arithmetic  41.2 us (37%)
  starting transfers between devices  31.4 us (28%)
  waiting for transfers between devices  25.2 us (22%)
  local copies, waits for them, and re-layouts  10.7 us (10%)
  between operations  1.34 us (1%)
    scatter-add x1, other arithmetic, per_device(): jax.ops.segment_sum(arrived.reshape(-1, channels, block_dst), arrived_ids...  18.9 us
    ppermute x4, starting transfers between devices, from_behind(): return lax.ppermute(block, axis, route)  13.4 us
    ppermute x4, starting transfers between devices, padded_2(): after = lax.ppermute(initial, axis, down)  12.5 us
    ppermute x4, waiting for transfers between devices, shifted(): lax.ppermute(shard, axis, [(i, (i + by) % length) for i in range(length)])  11.7 us
    scatter-add x1, other arithmetic, per_device(): jax.ops.segment_sum(landed.reshape(-1, surface.shape[0], block_src), land...  8.79 us
    ppermute x4, waiting for transfers between devices, from_behind(): return lax.ppermute(block, axis, route)  7.26 us
    ppermute x4, waiting for transfers between devices, padded_2(): before = lax.ppermute(last, axis, up)  6.23 us
    ppermute x4, starting transfers between devices, shifted(): lax.ppermute(shard, axis, [(i, (i + by) % length) for i in range(length)])  2.99 us
  transfers between devices with their start and end apart: 16, of which 6 were waited for; matrix products, arithmetic and copies ran while one was open for 33% of the time, Pallas kernels for 0%

commit v1 on v0

v1 whole, which is shorter than its diff:
```python
import jax
import jax.numpy as jnp
from jax import lax
from jax.experimental import pallas as pl
from jax.experimental.pallas import tpu as pltpu
from jax.sharding import PartitionSpec as P

HEAT_RATE = 0.1
SHORTWAVE_RATE = 0.1
FRESH_RATE = 0.05
SIDE_RATE = 0.18
MIX_BASE = 0.03
MIX_WIND = 0.09
MIX_DECAY = 0.8

ROWS, COLS, LEVELS = 16, 512, 10
TILES = COLS // 128
F32, BF16 = jnp.float32, jnp.bfloat16
LIST_ROWS = 4 * 64
EDGE_ROWS = 24
VMEM = pl.BlockSpec(memory_space=pltpu.VMEM)
NN = (((1,), (0,)), ((), ()))
TN = (((0,), (0,)), ((), ()))
NT = (((1,), (1,)), ((), ()))


def iota(shape, axis):
    return lax.broadcasted_iota(jnp.int32, shape, axis)


def dot(x, y, dims=NN):
    return lax.dot_general(x, y, dims, preferred_element_type=F32)


def dot_split(ones, values):
    high = values.astype(BF16)
    low = (values - high.astype(F32)).astype(BF16)
    return dot(ones, high) + dot(ones, low)


def split_dot(values, ones):
    high = values.astype(BF16)
    low = (values - high.astype(F32)).astype(BF16)
    return dot(high, ones) + dot(low, ones)


def ocean_number(shape, axis):
    place = iota(shape, axis)
    return place % ROWS * TILES + place // ROWS


def atm_number(shape, axis):
    place = iota(shape, axis)
    return place % 8 * 8 + place // 8


def one_hot(number, names):
    return jnp.where(number == names, 1.0, 0.0).astype(BF16)


def group_mask():
    return iota((8, 128), 1) // 16 == iota((8, 128), 0)


def edge_columns(levels):
    lane = iota((ROWS, 128), 1)
    block = jnp.zeros((ROWS, 128), F32)
    for at, values in enumerate(levels):
        block = jnp.where(lane == at, values[:, 0:1], block)
        block = jnp.where(lane == 64 + at, values[:, COLS - 1 : COLS], block)
    return block


def outbound_kernel(air, table, panels, temp, salt, depth, own, to_gx, to_xe, to_xo, to_dg):
    odd_row = lax.axis_index("gy") % 2 == 1
    mask = group_mask()
    fold = (iota((128, 128), 0) % 16 == iota((128, 128), 1) % 16).astype(F32).astype(BF16)
    spread = []
    for c in range(8):
        for r in range(8):
            row = jnp.broadcast_to(air[c, r : r + 1, :].astype(F32), (8, 128))
            spread.append(jnp.where(mask, row, 0.0))
    tiled = dot(jnp.concatenate(spread, 0).astype(BF16), fold).astype(BF16)
    tiled = jnp.concatenate([tiled[c * 64 : (c + 1) * 64] for c in range(8)], 1)
    source = iota((64, 64), 0)
    target = ocean_number((64, 64), 0)
    for a in range(2):
        for b in range(2):
            picked = dot(one_hot(source, table[a, b, 0:1, :]), tiled, TN)
            planes = [[], [], [], []]
            for g in range(8):
                left = [
                    jnp.where(mask, picked[g * 8 : (g + 1) * 8, c * 128 : (c + 1) * 128], 0.0)
                    for c in range(8)
                ]
                piece = dot(
                    jnp.concatenate(left, 0).astype(BF16),
                    panels[2 * a + b, g * 128 : (g + 1) * 128, :],
                )
                f = [piece[c * 8 : (c + 1) * 8] for c in range(8)]
                planes[0].append(f[0] + f[1] + f[2])
                planes[1].append(f[3])
                planes[2].append(f[4] - f[5] + f[6])
                planes[3].append(f[7])
            pieces = jnp.concatenate([jnp.concatenate(p, 0) for p in planes], 1)
            summed = dot_split(one_hot(target, table[a, b, 1:2, :]), pieces)
            outs = {(1, 1): (own,), (1, 0): (to_gx,), (0, 1): (to_xe, to_xo), (0, 0): (to_dg,)}
            for out in outs[a, b]:
                for p in range(4):
                    out[p * 64 : (p + 1) * 64, :] = summed[:, p * 128 : (p + 1) * 128]
    deep = depth[...].astype(F32)
    levels = [temp[l] for l in range(LEVELS)] + [salt[l] for l in range(LEVELS)] + [deep]
    to_gx[LIST_ROWS : LIST_ROWS + ROWS, :] = edge_columns(levels)
    for out, first in ((to_xe, odd_row), (to_xo, jnp.logical_not(odd_row))):
        for base, rows in (
            (0, (temp[:, 0, :], temp[:, ROWS - 1, :])),
            (LEVELS, (salt[:, 0, :], salt[:, ROWS - 1, :])),
            (2 * LEVELS, (deep[0:1], deep[ROWS - 1 : ROWS])),
        ):
            edge = jnp.where(first, rows[0], rows[1])
            for s in range(TILES):
                at = LIST_ROWS + s * EDGE_ROWS + base
                out[at : at + edge.shape[0], :] = edge[:, s * 128 : (s + 1) * 128]


def beside(values, north, south, west, east):
    row, col = iota((ROWS, COLS), 0), iota((ROWS, COLS), 1)
    return (
        jnp.where(row == 0, north, pltpu.roll(values, 1, 0)),
        jnp.where(row == ROWS - 1, south, pltpu.roll(values, ROWS - 1, 0)),
        jnp.where(col == 0, west, pltpu.roll(values, 1, 1)),
        jnp.where(col == COLS - 1, east, pltpu.roll(values, COLS - 1, 1)),
    )


def advance(tracers, halos, depth, depths, planes, stores):
    heat, shortwave, fresh, gust = planes
    mixing = MIX_BASE + MIX_WIND * gust
    above = [None, None]
    for l in range(LEVELS):
        wet = depth > l
        wets = [d > l for d in depths]
        for t in range(2):
            centre = tracers[t][l]
            side = jnp.zeros_like(centre)
            for near, there in zip(beside(centre, *halos(t, l)), wets):
                side = side + jnp.where(there, near - centre, 0.0)
            change = SIDE_RATE * side
            if l < LEVELS - 1:
                across = mixing * (MIX_DECAY**l) * (tracers[t][l + 1] - centre)
                across = jnp.where(depth > l + 1, across, 0.0)
                change = change + across
            if l > 0:
                change = change - above[t]
            above[t] = across
            if t == 0:
                change = change + shortwave * (SHORTWAVE_RATE * 2.718281828459045 ** (-0.5 * l))
                if l == 0:
                    change = change + HEAT_RATE * heat
            elif l == 0:
                change = change - FRESH_RATE * fresh * centre
            stores(t, l, centre + jnp.where(wet, change, 0.0))


def first_kernel(
    own, core, zpair, xe, xo, dg, temp, salt, depth, new, cols, row_e, row_o, planes, depths
):
    odd_col = lax.axis_index("gx") % 2 == 1
    odd_row = lax.axis_index("gy") % 2 == 1

    def right(at, rows):
        return jnp.where(odd_col, zpair[at : at + rows, :], core[at : at + rows, :])

    def left(at, rows):
        return jnp.where(odd_col, core[at : at + rows, :], zpair[at : at + rows, :])

    def below(at, rows):
        return jnp.where(odd_row, xo[at : at + rows, :], xe[at : at + rows, :])

    def over(at, rows):
        return jnp.where(odd_row, xe[at : at + rows, :], xo[at : at + rows, :])

    forcing = []
    for p in range(4):
        parts = []
        for s in range(TILES):
            at = p * 64 + s * ROWS
            here = own[at : at + ROWS, :] + dg[at : at + ROWS, :]
            parts.append(here + right(at, ROWS) + below(at, ROWS))
        forcing.append(jnp.concatenate(parts, 1))
    squared = forcing[3] * forcing[3]
    forcing[3] = squared / (1.0 + squared)
    for p in range(4):
        planes[p] = forcing[p]
    west, east = left(LIST_ROWS, ROWS), right(LIST_ROWS, ROWS)
    norths = jnp.concatenate([over(LIST_ROWS + s * EDGE_ROWS, EDGE_ROWS) for s in range(TILES)], 1)
    souths = jnp.concatenate([below(LIST_ROWS + s * EDGE_ROWS, EDGE_ROWS) for s in range(TILES)], 1)

    def halos(t, l):
        at = t * LEVELS + l
        return (
            norths[at : at + 1],
            souths[at : at + 1],
            west[:, 64 + at : 65 + at],
            east[:, at : at + 1],
        )

    deep = depth[...].astype(F32)
    around = beside(deep, *halos(2, 0))
    for n in range(4):
        depths[n] = around[n]
    lane = iota((ROWS, 128), 1)
    block = [jnp.zeros((ROWS, 128), F32)]

    def store(t, l, value):
        new[t, l] = value
        at = t * LEVELS + l
        edge = jnp.where(lane == at, value[:, 0:1], block[0])
        block[0] = jnp.where(lane == 64 + at, value[:, COLS - 1 : COLS], edge)
        first, last = value[0:1], value[ROWS - 1 : ROWS]
        row_e[at : at + 1, :] = jnp.where(odd_row, first, last)
        row_o[at : at + 1, :] = jnp.where(odd_row, last, first)

    advance((temp, salt), halos, deep, around, forcing, store)
    cols[...] = block[0]


def second_kernel(
    old, core, zpair, xe, xo, planes, depths, depth, table, panels,
    new_temp, new_salt, own, to_gx, to_gy, to_dg,
):
    odd_col = lax.axis_index("gx") % 2 == 1
    odd_row = lax.axis_index("gy") % 2 == 1
    east = jnp.where(odd_col, zpair[...], core[...])
    west = jnp.where(odd_col, core[...], zpair[...])
    souths = jnp.where(odd_row, xo[...], xe[...])
    norths = jnp.where(odd_row, xe[...], xo[...])

    def halos(t, l):
        at = t * LEVELS + l
        return (
            norths[at : at + 1],
            souths[at : at + 1],
            west[:, 64 + at : 65 + at],
            east[:, at : at + 1],
        )

    deep = depth[...].astype(F32)
    around = [depths[n] for n in range(4)]
    top = {}

    def store(t, l, value):
        (new_temp, new_salt)[t][l] = value
        if l < 3:
            top[t, l] = value

    advance(
        (old.at[0], old.at[1]), halos, deep, around, [planes[p] for p in range(4)], store
    )
    wet_top = jnp.where(deep > 0, 1.0, 0.0)
    surface = (
        top[0, 0] * wet_top,
        top[1, 0] * wet_top,
        (top[0, 0] + top[0, 1] + top[0, 2]) / 3.0 * wet_top,
        wet_top,
    )
    blocks = jnp.concatenate(
        [
            jnp.concatenate([f[:, s * 128 : (s + 1) * 128] for s in range(TILES)], 0)
            for f in surface
        ],
        1,
    ).astype(BF16)
    mask = group_mask()
    place, lane = iota((512, 128), 0), iota((512, 128), 1)
    fold = jnp.where((place // 128 == lane // 16) & (place % 16 == lane % 16), 1.0, 0.0)
    fold = fold.astype(BF16)
    source = ocean_number((64, 64), 0)
    target = atm_number((64, 64), 0)
    outs = {(0, 0): own, (0, 1): to_gx, (1, 0): to_gy, (1, 1): to_dg}
    for a in range(2):
        for b in range(2):
            chosen = dot(one_hot(source, table[a, b, 0:1, :]), blocks, TN)
            kept = [[], [], [], []]
            for g in range(8):
                part = chosen[g * 8 : (g + 1) * 8]
                left = [part[:, c * 128 : (c + 1) * 128] for c in range(4)]
                piece = dot(
                    jnp.concatenate(left, 0).astype(BF16),
                    panels[2 * a + b, g * 128 : (g + 1) * 128, :],
                    NT,
                )
                for c in range(4):
                    kept[c].append(jnp.where(mask, piece[c * 8 : (c + 1) * 8], 0.0))
            kept = jnp.concatenate([jnp.concatenate(k, 0) for k in kept], 1)
            pieces = split_dot(kept, fold)
            outs[a, b][...] = dot_split(one_hot(target, table[a, b, 1:2, :]), pieces)


def final_kernel(own, gx, gy, dg, out):
    total = own[...] + gx[...] + gy[...] + dg[...]
    group = iota((8, 128), 1) // 16
    for c in range(4):
        field = jnp.zeros((8, 128), F32)
        for k in range(8):
            moved = pltpu.roll(total[k * 8 : (k + 1) * 8], (k - c) % 8 * 16, 1)
            field = jnp.where(group == k, moved, field)
        out[c] = field


def call(kernel, shapes, *args):
    return pl.pallas_call(
        kernel,
        out_shape=[jax.ShapeDtypeStruct(s, F32) for s in shapes],
        in_specs=[VMEM] * len(args),
        out_specs=[VMEM] * len(shapes),
        compiler_params=pltpu.CompilerParams(vmem_limit_bytes=24 * 1024 * 1024),
    )(*args)


def send(block, step):
    wide, high = lax.axis_size("gx"), lax.axis_size("gy")
    route = []
    for i in range(wide):
        for j in range(high):
            to = step(i, j)
            if 0 <= to[1] < high:
                route.append((i * high + j, to[0] % wide * high + to[1]))
    return lax.ppermute(block, ("gx", "gy"), route)


def pair(n):
    return n - 1 if n % 2 else n + 1


def other_pair(n):
    return n + 1 if n % 2 else n - 1


def per_device(air, out_tables, out_panels, depth, temp, salt, in_tables, in_panels):
    out_panels = out_panels.reshape(4, 1024, 128)
    in_panels = in_panels.reshape(4, 1024, 128)
    edged = LIST_ROWS + TILES * EDGE_ROWS
    own, to_gx, to_xe, to_xo, to_dg = call(
        outbound_kernel,
        [(LIST_ROWS, 128), (LIST_ROWS + ROWS, 128), (edged, 128), (edged, 128), (LIST_ROWS, 128)],
        air, out_tables[0, 0], out_panels, temp, salt, depth,
    )
    dg = send(to_dg, lambda i, j: (i - 1, j - 1))
    xo = send(to_xo, lambda i, j: (i, other_pair(j)))
    xe = send(to_xe, lambda i, j: (i, pair(j)))
    zpair = send(to_gx, lambda i, j: (other_pair(i), j))
    core = send(to_gx, lambda i, j: (pair(i), j))
    stepped, cols, row_e, row_o, planes, depths = call(
        first_kernel,
        [
            (2, LEVELS, ROWS, COLS), (ROWS, 128), (2 * LEVELS, COLS), (2 * LEVELS, COLS),
            (4, ROWS, COLS), (4, ROWS, COLS),
        ],
        own, core, zpair, xe, xo, dg, temp, salt, depth,
    )
    xo = send(row_o, lambda i, j: (i, other_pair(j)))
    xe = send(row_e, lambda i, j: (i, pair(j)))
    zpair = send(cols, lambda i, j: (other_pair(i), j))
    core = send(cols, lambda i, j: (pair(i), j))
    new_temp, new_salt, own, to_gx, to_gy, to_dg = call(
        second_kernel,
        [(LEVELS, ROWS, COLS)] * 2 + [(64, 128)] * 4,
        stepped, core, zpair, xe, xo, planes, depths, depth, in_tables[0, 0], in_panels,
    )
    dg = send(to_dg, lambda i, j: (i + 1, j + 1))
    gy = send(to_gy, lambda i, j: (i, j + 1))
    gx = send(to_gx, lambda i, j: (i + 1, j))
    (surface,) = call(final_kernel, [(4, 8, 128)], own, gx, gy, dg)
    return new_temp, new_salt, surface


def solution(mesh):
    in_specs = (
        P(None, "gy", "gx"),
        P("gy", "gx", None, None, None, None),
        P("gy", "gx", None, None, None, None, None),
        P("gy", "gx"),
        P(None, "gy", "gx"),
        P(None, "gy", "gx"),
        P("gy", "gx", None, None, None, None),
        P("gy", "gx", None, None, None, None, None),
    )
    out_specs = (P(None, "gy", "gx"), P(None, "gy", "gx"), P(None, "gy", "gx"))
    return jax.shard_map(
        per_device, mesh=mesh, in_specs=in_specs, out_specs=out_specs, check_vma=False
    )
```

time: 112 us -> 53.6 us (0.48)
  other arithmetic: 41.2 us -> 0 us
  waiting for transfers between devices: 25.2 us -> 11.2 us
  Pallas kernels: 0 us -> 7.94 us
  local copies, waits for them, and re-layouts: 10.7 us -> 6.01 us
  starting transfers between devices: 31.4 us -> 27.2 us
    scatter-add x2 -> x0, other arithmetic: 27.7 us -> none  [the longest x1 18.9 us: per_device(): jax.ops.segment_sum(arrived.reshape(-1, channels, block_dst), arrived_ids...]
    ppermute x16 -> x12, waiting for transfers between devices: 25.2 us -> 11.2 us  [send(): return lax.ppermute(block, ('gx', 'gy'), route)]
    pallas_call x0 -> x4, Pallas kernels: none -> 7.94 us  [call(): pl.pallas_call(kernel, out_shape=[jax.ShapeDtypeStruct(s, F32) for s in s...]
    unnamed x55 -> x20, local copies, waits for them, and re-layouts: 1.42 us -> 6.01 us
    ppermute x16 -> x12, starting transfers between devices: 31.4 us -> 27.2 us  [send(): return lax.ppermute(block, ('gx', 'gy'), route)]
    another operation x11 -> x0, other arithmetic: 3.25 us -> none  [the longest x1 2.12 us: route_forward(): arrived = jnp.stack([across, sectioned[:, 1]], 1)]
    slice x7 -> x0, local copies, waits for them, and re-layouts: 3.23 us -> none  [the longest x1 1.56 us: advance(): wet_mid = wet_pad[:, 1:-1, 1:-1]]
    mul x8 -> x0, other arithmetic: 2.76 us -> none  [the longest x3 0.99 us: advance(): mixing * wet_mid[:-1] * wet_mid[1:] * (centre[:, 1:] - centre[:, :-1])]
  transfers between devices with their start and end apart: 16 -> 12, of which waited for: 6 -> 4; matrix products, arithmetic and copies ran while one was open for 33% -> 0% of each run, Pallas kernels for 0% -> 0%
where the time goes in v1:
time: 53.6 us; the launch traced here: 53.1 us
  starting transfers between devices  27.2 us (51%)
  waiting for transfers between devices  11.2 us (21%)
  Pallas kernels  7.94 us (15%)
  local copies, waits for them, and re-layouts  6.01 us (11%)
  between operations  0.77 us (1%)
    ppermute x12, starting transfers between devices, send(): return lax.ppermute(block, ('gx', 'gy'), route)  27.2 us
    ppermute x12, waiting for transfers between devices, send(): return lax.ppermute(block, ('gx', 'gy'), route)  11.2 us
    pallas_call x4, Pallas kernels, call(): pl.pallas_call(kernel, out_shape=[jax.ShapeDtypeStruct(s, F32) for s in s...  7.94 us
    unnamed x20, local copies, waits for them, and re-layouts  6.01 us
  transfers between devices with their start and end apart: 12, of which 4 were waited for; matrix products, arithmetic and copies ran while one was open for 0% of the time, Pallas kernels for 0%

profile of v1, /device:TPU:8, one launch (start us, length us, event | category | flops | bytes accessed | tf_op | source)
XLA Modules:
  0.0 53.1 jit_solution(6194987248698531690)
XLA Ops:
  0.6 0.0 copy-start
  0.6 1.0 %copy-done = f32[10,16,512]{2,1,0:T(8,128)S(1)} copy-done((f32[10,16,512]{2,1,0:T(8,128)S(1)}, f32[10,16,512]{2,1,0:T(8,128)}, u32[]{:S(2)}) %copy-start) | copy-done | bytes 327704
  1.6 0.0 copy-start.2
  1.6 1.0 %copy-done.2 = f32[10,16,512]{2,1,0:T(8,128)S(1)} copy-done((f32[10,16,512]{2,1,0:T(8,128)S(1)}, f32[10,16,512]{2,1,0:T(8,128)}, u32[]{:S(2)}) %copy-start.2) | copy-done | bytes 327704
  2.6 0.0 copy-start.4
  2.6 1.2 %copy-done.4 = bf16[1,1,2,2,64,16,128]{6,5,4,3,2,1,0:T(8,128)(2,1)S(1)} copy-done((bf16[1,1,2,2,64,16,128]{6,5,4,3,2,1,0:T(8,128)(2,1)S(1)}, bf16[1,1,2,2,64,16,128]{6,5,4,3,2,1,0:T(8,128)(2,1)}, u32[]{:S(2)}) %copy-start.4) | copy-done | bytes 1048600
  3.8 0.0 copy-start.6
  3.8 0.8 %copy-done.6 = s32[16,512]{1,0:T(8,128)S(1)} copy-done((s32[16,512]{1,0:T(8,128)S(1)}, s32[16,512]{1,0:T(8,128)}, u32[]{:S(2)}) %copy-start.6) | copy-done | bytes 32792
  4.6 0.0 copy-start.7
  4.6 0.7 %copy-done.7 = bf16[8,8,128]{2,1,0:T(8,128)(2,1)S(1)} copy-done((bf16[8,8,128]{2,1,0:T(8,128)(2,1)S(1)}, bf16[8,8,128]{2,1,0:T(8,128)(2,1)}, u32[]{:S(2)}) %copy-start.7) | copy-done | bytes 16408
  5.3 0.0 copy-start.8
  5.3 0.7 %copy-done.8 = s32[1,1,2,2,2,64]{5,4,3,2,1,0:T(2,128)S(1)} copy-done((s32[1,1,2,2,2,64]{5,4,3,2,1,0:T(2,128)S(1)}, s32[1,1,2,2,2,64]{5,4,3,2,1,0:T(2,128)}, u32[]{:S(2)}) %copy-start.8) | copy-done | bytes 2072
  6.0 0.0 copy-start.1
  6.0 0.0 copy-start.3
  6.0 1.7 %shard_map.103 = (f32[256,128]{1,0:T(8,128)S(1)}, f32[272,128]{1,0:T(8,128)S(1)}, f32[352,128]{1,0:T(8,128)S(1)}, f32[352,128]{1,0:T(8,128)S(1)}, f32[256,128]{1,0:T(8,128)S(1)}) custom-call(bf16[8,8,128]{2,1,0:T(8,128)(2,1)S(1)} %copy-done.7, s32[2,2,2,64]{3,2,1,0:T(2,128)S(1)} %bitcast.6, bf16[4,1024,128]{2,1,0:T(8,128)(2,1)S(1)} %bitcast.4, ...), custom_call_target="tpu_custom_call" | custom-call | tf_op jit(solution)/shard_map/pallas_call | solution.py:312
  7.7 0.0 copy-start.5
  7.7 1.6 %collective-permute-start.2 = (f32[352,128]{1,0:T(8,128)S(1)}, f32[352,128]{1,0:T(8,128)S(1)}, u32[]{:S(2)}, u32[]{:S(2)}) collective-permute-start(f32[352,128]{1,0:T(8,128)S(1)} %get-tuple-element.22), channel_id=1, source_target_pairs={{0,1},{1,0},{2,3},{3,2},{4,5},{5,4},{6,7},{7,6},{8,9},{9,8},{10,11... | collective-permute-start | bytes 540680 | tf_op jit(solution)/shard_map/ppermute | solution.py:329
  9.3 3.9 %collective-permute-start.3 = (f32[352,128]{1,0:T(8,128)S(1)}, f32[352,128]{1,0:T(8,128)S(1)}, u32[]{:S(2)}, u32[]{:S(2)}) collective-permute-start(f32[352,128]{1,0:T(8,128)S(1)} %get-tuple-element.23), channel_id=1, source_target_pairs={{1,2},{2,1},{3,4},{4,3},{5,6},{6,5},{7,8},{8,7},{9,10},{10,9},{11,... | collective-permute-start | bytes 540680 | tf_op jit(solution)/shard_map/ppermute | solution.py:329
  13.2 3.0 %collective-permute-start.1 = (f32[272,128]{1,0:T(8,128)S(1)}, f32[272,128]{1,0:T(8,128)S(1)}, u32[]{:S(2)}, u32[]{:S(2)}) collective-permute-start(f32[272,128]{1,0:T(8,128)S(1)} %get-tuple-element.21), channel_id=1, source_target_pairs={{0,112},{1,113},{2,114},{3,115},{4,116},{5,117},{6,118},{7,119},{8... | collective-permute-start | bytes 417800 | tf_op jit(solution)/shard_map/ppermute | solution.py:329
  16.2 0.0 collective-permute-start
  16.2 4.8 %collective-permute-start.4 = (f32[256,128]{1,0:T(8,128)S(1)}, f32[256,128]{1,0:T(8,128)S(1)}, u32[]{:S(2)}, u32[]{:S(2)}) collective-permute-start(f32[256,128]{1,0:T(8,128)S(1)} %get-tuple-element.24), channel_id=1, source_target_pairs={{1,112},{2,113},{3,114},{4,115},{5,116},{6,117},{7,118},{8,119},{9... | collective-permute-start | bytes 393224 | tf_op jit(solution)/shard_map/ppermute | solution.py:329
  21.0 2.5 %collective-permute-done.4.dg = f32[256,128]{1,0:T(8,128)S(1)} collective-permute-done((f32[256,128]{1,0:T(8,128)S(1)}, f32[256,128]{1,0:T(8,128)S(1)}, u32[]{:S(2)}, u32[]{:S(2)}) %collective-permute-start.4) | collective-permute-done | bytes 131104 | tf_op jit(solution)/shard_map/ppermute | solution.py:329
  23.5 0.0 collective-permute-done.1.zpair
  23.5 0.0 collective-permute-done.core
  23.6 0.0 collective-permute-done.2.xe
  23.6 0.0 collective-permute-done.3.xo
  23.6 0.0 copy-done.1
  23.6 0.0 copy-done.3
  23.6 2.0 %shard_map.104 = (f32[2,10,16,512]{3,2,1,0:T(8,128)S(1)}, f32[16,128]{1,0:T(8,128)S(1)}, f32[20,512]{1,0:T(8,128)S(1)}, f32[20,512]{1,0:T(8,128)S(1)}, f32[4,16,...) custom-call(f32[256,128]{1,0:T(8,128)S(1)} %get-tuple-element.20.own, f32[272,128]{1,0:T(8,128)S(1)} %collective-permute-done.core, ...), custom_call_target="tpu_custom_call" | custom-call | tf_op jit(solution)/shard_map/pallas_call | solution.py:312
  25.6 0.1 collective-permute-start.7
  25.6 5.1 %collective-permute-start.8 = (f32[20,512]{1,0:T(8,128)S(1)}, f32[20,512]{1,0:T(8,128)S(1)}, u32[]{:S(2)}, u32[]{:S(2)}) collective-permute-start(f32[20,512]{1,0:T(8,128)S(1)} %get-tuple-element.28), channel_id=1, source_target_pairs={{1,2},{2,1},{3,4},{4,3},{5,6},{6,5},{7,8},{8,7},{9,10},{10,9},{11,... | collective-permute-start | bytes 122888 | tf_op jit(solution)/shard_map/ppermute | solution.py:329
  30.8 3.3 %collective-permute-start.6 = (f32[16,128]{1,0:T(8,128)S(1)}, f32[16,128]{1,0:T(8,128)S(1)}, u32[]{:S(2)}, u32[]{:S(2)}) collective-permute-start(f32[16,128]{1,0:T(8,128)S(1)} %get-tuple-element.26), channel_id=1, source_target_pairs={{0,112},{1,113},{2,114},{3,115},{4,116},{5,117},{6,118},{7,119},{8... | collective-permute-start | bytes 24584 | tf_op jit(solution)/shard_map/ppermute | solution.py:329
  34.1 0.0 collective-permute-start.5
  34.1 1.4 %collective-permute-done.6.zpair = f32[16,128]{1,0:T(8,128)S(1)} collective-permute-done((f32[16,128]{1,0:T(8,128)S(1)}, f32[16,128]{1,0:T(8,128)S(1)}, u32[]{:S(2)}, u32[]{:S(2)}) %collective-permute-start.6) | collective-permute-done | bytes 8224 | tf_op jit(solution)/shard_map/ppermute | solution.py:329
  35.4 0.0 collective-permute-done.5.core
  35.4 0.0 collective-permute-done.7.xe
  35.4 0.0 collective-permute-done.8.xo
  35.4 0.0 copy-start.9
  35.4 0.0 copy-done.5
  35.5 0.7 %copy-done.9 = s32[1,1,2,2,2,64]{5,4,3,2,1,0:T(2,128)S(1)} copy-done((s32[1,1,2,2,2,64]{5,4,3,2,1,0:T(2,128)S(1)}, s32[1,1,2,2,2,64]{5,4,3,2,1,0:T(2,128)}, u32[]{:S(2)}) %copy-start.9) | copy-done | bytes 2072
  36.1 3.5 %shard_map.105 = (f32[10,16,512]{2,1,0:T(8,128)}, f32[10,16,512]{2,1,0:T(8,128)}, f32[64,128]{1,0:T(8,128)S(1)}, f32[64,128]{1,0:T(8,128)S(1)}, f32[64,128]{1,0:T(8,128)S(1)}, /*index=5*/f32[64,128]{1,0:T(8,128)S(1)}) custom-call(f32[2,10,16,512]{3,2,1,0:T(8,128)S(1)} %get-tuple-element.25.old, f32[16,128]{1,0:T(8,128)S(1)} %collective-permute-done.5.core, ...), custom_call_target="tpu_custom_call" | custom-call | tf_op jit(solution)/shard_map/pallas_call | solution.py:312
  39.6 0.1 collective-permute-start.9
  39.7 3.2 %collective-permute-start.10 = (f32[64,128]{1,0:T(8,128)S(1)}, f32[64,128]{1,0:T(8,128)S(1)}, u32[]{:S(2)}, u32[]{:S(2)}) collective-permute-start(f32[64,128]{1,0:T(8,128)S(1)} %get-tuple-element.35), channel_id=1, source_target_pairs={{0,1},{1,2},{2,3},{3,4},{4,5},{5,6},{6,7},{7,8},{8,9},{9,10},{10,1... | collective-permute-start | bytes 98312 | tf_op jit(solution)/shard_map/ppermute | solution.py:329
  42.9 2.2 %collective-permute-start.11 = (f32[64,128]{1,0:T(8,128)S(1)}, f32[64,128]{1,0:T(8,128)S(1)}, u32[]{:S(2)}, u32[]{:S(2)}) collective-permute-start(f32[64,128]{1,0:T(8,128)S(1)} %get-tuple-element.36), channel_id=1, source_target_pairs={{0,17},{1,18},{2,19},{3,20},{4,21},{5,22},{6,23},{7,24},{8,25},{9,... | collective-permute-start | bytes 98312 | tf_op jit(solution)/shard_map/ppermute | solution.py:329
  45.1 0.0 collective-permute-done.9.gx
  45.1 2.5 %collective-permute-done.10.gy = f32[64,128]{1,0:T(8,128)S(1)} collective-permute-done((f32[64,128]{1,0:T(8,128)S(1)}, f32[64,128]{1,0:T(8,128)S(1)}, u32[]{:S(2)}, u32[]{:S(2)}) %collective-permute-start.10) | collective-permute-done | bytes 32800 | tf_op jit(solution)/shard_map/ppermute | solution.py:329
  47.6 4.7 %collective-permute-done.11.dg = f32[64,128]{1,0:T(8,128)S(1)} collective-permute-done((f32[64,128]{1,0:T(8,128)S(1)}, f32[64,128]{1,0:T(8,128)S(1)}, u32[]{:S(2)}, u32[]{:S(2)}) %collective-permute-start.11) | collective-permute-done | bytes 32800 | tf_op jit(solution)/shard_map/ppermute | solution.py:329
  52.4 0.7 %shard_map.106 = f32[4,8,128]{2,1,0:T(8,128)} custom-call(f32[64,128]{1,0:T(8,128)S(1)} %get-tuple-element.33.own, f32[64,128]{1,0:T(8,128)S(1)} %collective-permute-done.9.gx, f32[64,128]{1,0:T(8,128)S(1)} %collective-permute-done.10.gy, f32[64,128]{1,0:T(8,128)S(1)} %collective-permute-done.11.dg), custom_call_target="tpu_custom_call" | custom-call | tf_op jit(solution)/shard_map/pallas_call | solution.py:312
Async XLA Ops:
  0.6 1.0 %copy-start = (f32[10,16,512]{2,1,0:T(8,128)S(1)}, f32[10,16,512]{2,1,0:T(8,128)}, u32[]{:S(2)}) copy-start(f32[10,16,512]{2,1,0:T(8,128)} %temp.3) | copy-start | bytes 983044
  1.6 1.0 %copy-start.2 = (f32[10,16,512]{2,1,0:T(8,128)S(1)}, f32[10,16,512]{2,1,0:T(8,128)}, u32[]{:S(2)}) copy-start(f32[10,16,512]{2,1,0:T(8,128)} %salt.3) | copy-start | bytes 983044
  2.6 1.2 %copy-start.4 = (bf16[1,1,2,2,64,16,128]{6,5,4,3,2,1,0:T(8,128)(2,1)S(1)}, bf16[1,1,2,2,64,16,128]{6,5,4,3,2,1,0:T(8,128)(2,1)}, u32[]{:S(2)}) copy-start(bf16[1,1,2,2,64,16,128]{6,5,4,3,2,1,0:T(8,128)(2,1)} %param.10) | copy-start | bytes 3145732
  3.8 0.8 %copy-start.6 = (s32[16,512]{1,0:T(8,128)S(1)}, s32[16,512]{1,0:T(8,128)}, u32[]{:S(2)}) copy-start(s32[16,512]{1,0:T(8,128)} %depth.5) | copy-start | bytes 98308
  4.6 0.7 %copy-start.7 = (bf16[8,8,128]{2,1,0:T(8,128)(2,1)S(1)}, bf16[8,8,128]{2,1,0:T(8,128)(2,1)}, u32[]{:S(2)}) copy-start(bf16[8,8,128]{2,1,0:T(8,128)(2,1)} %air.1) | copy-start | bytes 49156
  5.3 0.7 %copy-start.8 = (s32[1,1,2,2,2,64]{5,4,3,2,1,0:T(2,128)S(1)}, s32[1,1,2,2,2,64]{5,4,3,2,1,0:T(2,128)}, u32[]{:S(2)}) copy-start(s32[1,1,2,2,2,64]{5,4,3,2,1,0:T(2,128)} %param.9) | copy-start | bytes 6148
  6.0 17.6 %copy-start.1 = (f32[10,16,512]{2,1,0:T(8,128)S(1)}, f32[10,16,512]{2,1,0:T(8,128)}, u32[]{:S(2)}) copy-start(f32[10,16,512]{2,1,0:T(8,128)} %temp.3) | copy-start | bytes 983044
  6.0 17.6 %copy-start.3 = (f32[10,16,512]{2,1,0:T(8,128)S(1)}, f32[10,16,512]{2,1,0:T(8,128)}, u32[]{:S(2)}) copy-start(f32[10,16,512]{2,1,0:T(8,128)} %salt.3) | copy-start | bytes 983044
  7.7 27.7 %copy-start.5 = (bf16[1,1,2,2,64,16,128]{6,5,4,3,2,1,0:T(8,128)(2,1)S(1)}, bf16[1,1,2,2,64,16,128]{6,5,4,3,2,1,0:T(8,128)(2,1)}, u32[]{:S(2)}) copy-start(bf16[1,1,2,2,64,16,128]{6,5,4,3,2,1,0:T(8,128)(2,1)} %param.15) | copy-start | bytes 3145732
  7.7 15.8 %collective-permute-start.2 = (f32[352,128]{1,0:T(8,128)S(1)}, f32[352,128]{1,0:T(8,128)S(1)}, u32[]{:S(2)}, u32[]{:S(2)}) collective-permute-start(f32[352,128]{1,0:T(8,128)S(1)} %get-tuple-element.22), channel_id=1, source_target_pairs={{0,1},{1,0},{2,3},{3,2},{4,5},{5,4},{6,7},{7,6},{8,9},{9,8},{10,11... | collective-permute-start | bytes 540680 | tf_op jit(solution)/shard_map/ppermute | solution.py:329
  9.3 14.3 %collective-permute-start.3 = (f32[352,128]{1,0:T(8,128)S(1)}, f32[352,128]{1,0:T(8,128)S(1)}, u32[]{:S(2)}, u32[]{:S(2)}) collective-permute-start(f32[352,128]{1,0:T(8,128)S(1)} %get-tuple-element.23), channel_id=1, source_target_pairs={{1,2},{2,1},{3,4},{4,3},{5,6},{6,5},{7,8},{8,7},{9,10},{10,9},{11,... | collective-permute-start | bytes 540680 | tf_op jit(solution)/shard_map/ppermute | solution.py:329
  13.2 10.4 %collective-permute-start.1 = (f32[272,128]{1,0:T(8,128)S(1)}, f32[272,128]{1,0:T(8,128)S(1)}, u32[]{:S(2)}, u32[]{:S(2)}) collective-permute-start(f32[272,128]{1,0:T(8,128)S(1)} %get-tuple-element.21), channel_id=1, source_target_pairs={{0,112},{1,113},{2,114},{3,115},{4,116},{5,117},{6,118},{7,119},{8... | collective-permute-start | bytes 417800 | tf_op jit(solution)/shard_map/ppermute | solution.py:329
  16.2 7.4 %collective-permute-start = (f32[272,128]{1,0:T(8,128)S(1)}, f32[272,128]{1,0:T(8,128)S(1)}, u32[]{:S(2)}, u32[]{:S(2)}) collective-permute-start(f32[272,128]{1,0:T(8,128)S(1)} %get-tuple-element.21), channel_id=1, source_target_pairs={{0,16},{1,17},{2,18},{3,19},{4,20},{5,21},{6,22},{7,23},{8,24},{9,... | collective-permute-start | bytes 417800 | tf_op jit(solution)/shard_map/ppermute | solution.py:329
  16.2 7.3 %collective-permute-start.4 = (f32[256,128]{1,0:T(8,128)S(1)}, f32[256,128]{1,0:T(8,128)S(1)}, u32[]{:S(2)}, u32[]{:S(2)}) collective-permute-start(f32[256,128]{1,0:T(8,128)S(1)} %get-tuple-element.24), channel_id=1, source_target_pairs={{1,112},{2,113},{3,114},{4,115},{5,116},{6,117},{7,118},{8,119},{9... | collective-permute-start | bytes 393224 | tf_op jit(solution)/shard_map/ppermute | solution.py:329
  25.6 9.9 %collective-permute-start.7 = (f32[20,512]{1,0:T(8,128)S(1)}, f32[20,512]{1,0:T(8,128)S(1)}, u32[]{:S(2)}, u32[]{:S(2)}) collective-permute-start(f32[20,512]{1,0:T(8,128)S(1)} %get-tuple-element.27), channel_id=1, source_target_pairs={{0,1},{1,0},{2,3},{3,2},{4,5},{5,4},{6,7},{7,6},{8,9},{9,8},{10,11... | collective-permute-start | bytes 122888 | tf_op jit(solution)/shard_map/ppermute | solution.py:329
  25.6 9.8 %collective-permute-start.8 = (f32[20,512]{1,0:T(8,128)S(1)}, f32[20,512]{1,0:T(8,128)S(1)}, u32[]{:S(2)}, u32[]{:S(2)}) collective-permute-start(f32[20,512]{1,0:T(8,128)S(1)} %get-tuple-element.28), channel_id=1, source_target_pairs={{1,2},{2,1},{3,4},{4,3},{5,6},{6,5},{7,8},{8,7},{9,10},{10,9},{11,... | collective-permute-start | bytes 122888 | tf_op jit(solution)/shard_map/ppermute | solution.py:329
  30.8 4.6 %collective-permute-start.6 = (f32[16,128]{1,0:T(8,128)S(1)}, f32[16,128]{1,0:T(8,128)S(1)}, u32[]{:S(2)}, u32[]{:S(2)}) collective-permute-start(f32[16,128]{1,0:T(8,128)S(1)} %get-tuple-element.26), channel_id=1, source_target_pairs={{0,112},{1,113},{2,114},{3,115},{4,116},{5,117},{6,118},{7,119},{8... | collective-permute-start | bytes 24584 | tf_op jit(solution)/shard_map/ppermute | solution.py:329
  34.1 1.4 %collective-permute-start.5 = (f32[16,128]{1,0:T(8,128)S(1)}, f32[16,128]{1,0:T(8,128)S(1)}, u32[]{:S(2)}, u32[]{:S(2)}) collective-permute-start(f32[16,128]{1,0:T(8,128)S(1)} %get-tuple-element.26), channel_id=1, source_target_pairs={{0,16},{1,17},{2,18},{3,19},{4,20},{5,21},{6,22},{7,23},{8,24},{9,... | collective-permute-start | bytes 24584 | tf_op jit(solution)/shard_map/ppermute | solution.py:329
  35.4 0.7 %copy-start.9 = (s32[1,1,2,2,2,64]{5,4,3,2,1,0:T(2,128)S(1)}, s32[1,1,2,2,2,64]{5,4,3,2,1,0:T(2,128)}, u32[]{:S(2)}) copy-start(s32[1,1,2,2,2,64]{5,4,3,2,1,0:T(2,128)} %param.14) | copy-start | bytes 6148
  39.6 5.5 %collective-permute-start.9 = (f32[64,128]{1,0:T(8,128)S(1)}, f32[64,128]{1,0:T(8,128)S(1)}, u32[]{:S(2)}, u32[]{:S(2)}) collective-permute-start(f32[64,128]{1,0:T(8,128)S(1)} %get-tuple-element.34), channel_id=1, source_target_pairs={{0,16},{1,17},{2,18},{3,19},{4,20},{5,21},{6,22},{7,23},{8,24},{9,... | collective-permute-start | bytes 98312 | tf_op jit(solution)/shard_map/ppermute | solution.py:329
  39.7 7.9 %collective-permute-start.10 = (f32[64,128]{1,0:T(8,128)S(1)}, f32[64,128]{1,0:T(8,128)S(1)}, u32[]{:S(2)}, u32[]{:S(2)}) collective-permute-start(f32[64,128]{1,0:T(8,128)S(1)} %get-tuple-element.35), channel_id=1, source_target_pairs={{0,1},{1,2},{2,3},{3,4},{4,5},{5,6},{6,7},{7,8},{8,9},{9,10},{10,1... | collective-permute-start | bytes 98312 | tf_op jit(solution)/shard_map/ppermute | solution.py:329
  42.9 9.5 %collective-permute-start.11 = (f32[64,128]{1,0:T(8,128)S(1)}, f32[64,128]{1,0:T(8,128)S(1)}, u32[]{:S(2)}, u32[]{:S(2)}) collective-permute-start(f32[64,128]{1,0:T(8,128)S(1)} %get-tuple-element.36), channel_id=1, source_target_pairs={{0,17},{1,18},{2,19},{3,20},{4,21},{5,22},{6,23},{7,24},{8,25},{9,... | collective-permute-start | bytes 98312 | tf_op jit(solution)/shard_map/ppermute | solution.py:329

commit v2 on v1

v2 whole, which is shorter than its diff:
```python
import jax
import jax.numpy as jnp
from jax import lax
from jax.experimental import pallas as pl
from jax.experimental.pallas import tpu as pltpu
from jax.sharding import PartitionSpec as P

HEAT_RATE = 0.1
SHORTWAVE_RATE = 0.1
FRESH_RATE = 0.05
SIDE_RATE = 0.18
MIX_BASE = 0.03
MIX_WIND = 0.09
MIX_DECAY = 0.8

ROWS, COLS, LEVELS = 16, 512, 10
TILES = COLS // 128
F32, BF16 = jnp.float32, jnp.bfloat16
LIST_ROWS = 4 * 64
EDGE_ROWS = 24
VMEM = pl.BlockSpec(memory_space=pltpu.VMEM)
HBM = pl.BlockSpec(memory_space=pltpu.HBM)
NN = (((1,), (0,)), ((), ()))
TN = (((0,), (0,)), ((), ()))
NT = (((1,), (1,)), ((), ()))


def iota(shape, axis):
    return lax.broadcasted_iota(jnp.int32, shape, axis)


def dot(x, y, dims=NN):
    return lax.dot_general(x, y, dims, preferred_element_type=F32)


def dot_split(ones, values):
    high = values.astype(BF16)
    low = (values - high.astype(F32)).astype(BF16)
    return dot(ones, high) + dot(ones, low)


def split_dot(values, ones):
    high = values.astype(BF16)
    low = (values - high.astype(F32)).astype(BF16)
    return dot(high, ones) + dot(low, ones)


def ocean_number(shape, axis):
    place = iota(shape, axis)
    return place % ROWS * TILES + place // ROWS


def atm_number(shape, axis):
    place = iota(shape, axis)
    return place % 8 * 8 + place // 8


def one_hot(number, names):
    return jnp.where(number == names, 1.0, 0.0).astype(BF16)


def group_mask():
    return iota((8, 128), 1) // 16 == iota((8, 128), 0)


def edge_columns(levels):
    lane = iota((ROWS, 128), 1)
    block = jnp.zeros((ROWS, 128), F32)
    for at, values in enumerate(levels):
        block = jnp.where(lane == at, values[:, 0:1], block)
        block = jnp.where(lane == 64 + at, values[:, COLS - 1 : COLS], block)
    return block


def spread_air(air, mask):
    fold = (iota((128, 128), 0) % 16 == iota((128, 128), 1) % 16).astype(F32).astype(BF16)
    spread = []
    for c in range(8):
        for r in range(8):
            row = jnp.broadcast_to(air[c, r : r + 1, :].astype(F32), (8, 128))
            spread.append(jnp.where(mask, row, 0.0))
    tiled = dot(jnp.concatenate(spread, 0).astype(BF16), fold).astype(BF16)
    return jnp.concatenate([tiled[c * 64 : (c + 1) * 64] for c in range(8)], 1)


def outbound_list(tiled, names, panel, mask, out):
    source = iota((64, 64), 0)
    target = ocean_number((64, 64), 0)
    picked = dot(one_hot(source, names[0:1, :]), tiled, TN)
    planes = [[], [], [], []]
    for g in range(8):
        left = [
            jnp.where(mask, picked[g * 8 : (g + 1) * 8, c * 128 : (c + 1) * 128], 0.0)
            for c in range(8)
        ]
        piece = dot(jnp.concatenate(left, 0).astype(BF16), panel[g * 128 : (g + 1) * 128, :])
        f = [piece[c * 8 : (c + 1) * 8] for c in range(8)]
        planes[0].append(f[0] + f[1] + f[2])
        planes[1].append(f[3])
        planes[2].append(f[4] - f[5] + f[6])
        planes[3].append(f[7])
    pieces = jnp.concatenate([jnp.concatenate(p, 0) for p in planes], 1)
    summed = dot_split(one_hot(target, names[1:2, :]), pieces)
    for p in range(4):
        out[p * 64 : (p + 1) * 64, :] = summed[:, p * 128 : (p + 1) * 128]


def fetch(sems, pairs):
    copies = [pltpu.make_async_copy(src, dst, sems.at[n]) for n, (src, dst) in enumerate(pairs)]
    for copy in copies:
        copy.start()
    return copies


def outbound_kernel(
    air_hbm, table_hbm, panels_hbm, temp_hbm, salt_hbm, depth_hbm, to_gx, to_gy, to_dg,
    air, table, panels, temp, salt, depth, sems,
):
    pairs = [(air_hbm, air), (table_hbm, table)]
    pairs += [(panels_hbm.at[n], panels.at[n]) for n in range(3)]
    pairs += [(temp_hbm, temp), (salt_hbm, salt), (depth_hbm, depth)]
    copies = fetch(sems, pairs)
    mask = group_mask()
    copies[0].wait()
    tiled = spread_air(air, mask)
    copies[1].wait()
    for n, out in ((0, to_dg), (1, to_gy), (2, to_gx)):
        copies[2 + n].wait()
        outbound_list(tiled, table[n // 2, n % 2], panels.at[n], mask, out)
    for copy in copies[5:]:
        copy.wait()
    deep = depth[...].astype(F32)
    levels = [temp[l] for l in range(LEVELS)] + [salt[l] for l in range(LEVELS)] + [deep]
    to_gx[LIST_ROWS : LIST_ROWS + ROWS, :] = edge_columns(levels)
    for base, edge in ((0, temp[:, 0, :]), (LEVELS, salt[:, 0, :]), (2 * LEVELS, deep[0:1])):
        for s in range(TILES):
            at = LIST_ROWS + s * EDGE_ROWS + base
            to_gy[at : at + edge.shape[0], :] = edge[:, s * 128 : (s + 1) * 128]


def beside(values, north, south, west, east):
    row, col = iota((ROWS, COLS), 0), iota((ROWS, COLS), 1)
    return (
        jnp.where(row == 0, north, pltpu.roll(values, 1, 0)),
        jnp.where(row == ROWS - 1, south, pltpu.roll(values, ROWS - 1, 0)),
        jnp.where(col == 0, west, pltpu.roll(values, 1, 1)),
        jnp.where(col == COLS - 1, east, pltpu.roll(values, COLS - 1, 1)),
    )


def side_sum(centre, nears, wets):
    side = jnp.zeros_like(centre)
    for near, there in zip(nears, wets):
        side = side + jnp.where(there, near - centre, 0.0)
    return SIDE_RATE * side


def inner_kernel(air, table, panels_hbm, temp, salt, depth, own, partial, panel, sem):
    copy = pltpu.make_async_copy(panels_hbm.at[3], panel, sem)
    copy.start()
    deep = depth[...].astype(F32)
    dry = jnp.zeros((1, 1), F32)
    around = beside(deep, dry, dry, dry, dry)
    for l in range(LEVELS):
        wet = deep > l
        wets = [d > l for d in around]
        for t, field in enumerate((temp, salt)):
            centre = field[l]
            side = side_sum(centre, beside(centre, dry, dry, dry, dry), wets)
            partial[t, l] = centre + jnp.where(wet, side, 0.0)
    mask = group_mask()
    tiled = spread_air(air, mask)
    copy.wait()
    outbound_list(tiled, table[1, 1], panel, mask, own)


def column_change(values, below, mixing, depth, l, across):
    change = 0.0 if l == 0 else -across
    if l < LEVELS - 1:
        across = mixing * (MIX_DECAY**l) * (below - values)
        across = jnp.where(depth > l + 1, across, 0.0)
        change = change + across
    return change, across


def source(t, l, planes, values):
    if t == 0:
        heating = planes[1] * (SHORTWAVE_RATE * 2.718281828459045 ** (-0.5 * l))
        return heating + HEAT_RATE * planes[0] if l == 0 else heating
    return -FRESH_RATE * planes[2] * values if l == 0 else 0.0


def first_kernel(
    own, core, zpair, gy, dg, partial, temp, salt, depth,
    new, cols, row_e, row_o, planes, depths, keep,
):
    odd_col = lax.axis_index("gx") % 2 == 1
    odd_row = lax.axis_index("gy") % 2 == 1

    def right(at, rows):
        return jnp.where(odd_col, zpair[at : at + rows, :], core[at : at + rows, :])

    def left(at, rows):
        return jnp.where(odd_col, core[at : at + rows, :], zpair[at : at + rows, :])

    forcing = []
    for p in range(4):
        parts = []
        for s in range(TILES):
            at = p * 64 + s * ROWS
            here = own[at : at + ROWS, :] + dg[at : at + ROWS, :]
            parts.append(here + right(at, ROWS) + gy[at : at + ROWS, :])
        forcing.append(jnp.concatenate(parts, 1))
    squared = forcing[3] * forcing[3]
    forcing[3] = squared / (1.0 + squared)
    for p in range(4):
        planes[p] = forcing[p]
    west, east = left(LIST_ROWS, ROWS), right(LIST_ROWS, ROWS)
    souths = [gy[LIST_ROWS + s * EDGE_ROWS : LIST_ROWS + (s + 1) * EDGE_ROWS, :] for s in range(TILES)]
    souths = jnp.concatenate(souths, 1)

    deep = depth[...].astype(F32)
    dry = jnp.zeros((1, 1), F32)
    last = 2 * LEVELS
    around = beside(deep, dry, souths[last : last + 1], west[:, 64 + last : 65 + last], east[:, last : last + 1])
    for n in range(4):
        depths[n] = around[n]
    lane = iota((ROWS, 128), 1)
    row = iota((8, COLS), 0)
    mixing = MIX_BASE + MIX_WIND * forcing[3]
    sides = ((0, west, 64, around[2], 0), (COLS - 128, east, 0, around[3], 127))
    block = jnp.zeros((ROWS, 128), F32)
    for t, field in enumerate((temp, salt)):
        across = None
        for l in range(LEVELS):
            at = t * LEVELS + l
            centre = field[l]
            change, across = column_change(
                centre, field[min(l + 1, LEVELS - 1)], mixing, deep, l, across
            )
            change = change + source(t, l, forcing, centre)
            new[t, l] = partial[t, l] + jnp.where(deep > l, change, 0.0)
            low = centre[8:16]
            here = (row == 7) & (around[1][8:16] > l) & (deep[8:16] > l)
            low = jnp.where(here, SIDE_RATE * (souths[at : at + 1] - low), 0.0)
            new[t, l, 8:16, :] += low
            for first, halo, offset, far, spot in sides:
                here = (lane == spot) & (far[:, first : first + 128] > l)
                here = here & (deep[:, first : first + 128] > l)
                near = halo[:, offset + at : offset + at + 1] - centre[:, first : first + 128]
                new[t, l, :, first : first + 128] += jnp.where(here, SIDE_RATE * near, 0.0)
            block = jnp.where(lane == at, new[t, l, :, 0:1], block)
            block = jnp.where(lane == 64 + at, new[t, l, :, COLS - 1 : COLS], block)
    cols[...] = block
    olds = (temp[:, 0, :], salt[:, 0, :])
    lows = (temp[:, ROWS - 1, :], salt[:, ROWS - 1, :])
    for t in range(2):
        span = slice(t * LEVELS, (t + 1) * LEVELS)
        first, final = new[t, :, 0, :], new[t, :, ROWS - 1, :]
        row_e[span, :] = jnp.where(odd_row, first, final)
        row_o[span, :] = jnp.where(odd_row, final, first)
        level = iota((LEVELS, COLS), 0)
        here = (souths[last : last + 1] > level) & (deep[ROWS - 1 : ROWS] > level)
        fix = jnp.where(here, SIDE_RATE * (lows[t] - souths[span]), 0.0)
        keep[span, :] = olds[t]
        keep[20 + t * LEVELS : 20 + (t + 1) * LEVELS, :] = fix
        for out in (row_e, row_o):
            out[20 + t * LEVELS : 20 + (t + 1) * LEVELS, :] = lows[t]
    keep[40:41, 0:128] = west[0:1]
    keep[41:42, 0:128] = east[0:1]
    for out in (row_e, row_o):
        out[40:41, :] = deep[ROWS - 1 : ROWS]
        out[41:42, 0:128] = west[ROWS - 1 : ROWS]
        out[42:43, 0:128] = east[ROWS - 1 : ROWS]


def inbound_list(blocks, names, panel, fold, mask, out):
    source_block = ocean_number((64, 64), 0)
    target = atm_number((64, 64), 0)
    chosen = dot(one_hot(source_block, names[0:1, :]), blocks, TN)
    kept = [[], [], [], []]
    for g in range(8):
        part = chosen[g * 8 : (g + 1) * 8]
        left = [part[:, c * 128 : (c + 1) * 128] for c in range(4)]
        piece = dot(
            jnp.concatenate(left, 0).astype(BF16), panel[g * 128 : (g + 1) * 128, :], NT
        )
        for c in range(4):
            kept[c].append(jnp.where(mask, piece[c * 8 : (c + 1) * 8], 0.0))
    kept = jnp.concatenate([jnp.concatenate(k, 0) for k in kept], 1)
    pieces = split_dot(kept, fold)
    out[...] = dot_split(one_hot(target, names[1:2, :]), pieces)


def inbound_fold():
    place, lane = iota((512, 128), 0), iota((512, 128), 1)
    fold = jnp.where((place // 128 == lane // 16) & (place % 16 == lane % 16), 1.0, 0.0)
    return fold.astype(BF16)


def second_kernel(
    old, core, zpair, xe, xo, planes, depths, keep, depth, table_hbm, panels,
    final, surface_blocks, to_gx, to_gy, to_dg, table, sem,
):
    copy = pltpu.make_async_copy(table_hbm, table, sem)
    copy.start()
    odd_col = lax.axis_index("gx") % 2 == 1
    odd_row = lax.axis_index("gy") % 2 == 1
    deep = depth[...].astype(F32)
    souths = jnp.where(odd_row, xo[...], xe[...])
    norths = jnp.where(odd_row, xe[...], xo[...])
    level = iota((2 * LEVELS, COLS), 0) % LEVELS
    here = (deep[0:1] > level) & (norths[40:41] > level)
    fix = jnp.where(here, SIDE_RATE * (norths[20:40] - keep[0:20, :]), 0.0)
    souths = souths[0:20] + keep[20:40, :]
    lane = iota((1, 128), 1)
    ends = []
    for halo, at, deepest in (
        (jnp.where(odd_col, core[...], zpair[...]), 0, 84),
        (jnp.where(odd_col, zpair[...], core[...]), 1, 20),
    ):
        mine, over = keep[40 + at : 41 + at, 0:128], norths[41 + at : 42 + at, 0:128]
        level = lane % 64 % LEVELS
        here = (mine[:, deepest : deepest + 1] > level) & (over[:, deepest : deepest + 1] > level)
        end_fix = jnp.where(here, SIDE_RATE * (over - mine), 0.0)
        ends.append(halo + jnp.where(iota((ROWS, 128), 0) == 0, end_fix, 0.0))
    west, east = ends
    row8, row = iota((8, COLS), 0), iota((ROWS, COLS), 0)
    around = [jnp.where(row == 0, norths[40:41], depths[0])] + [depths[n] for n in (1, 2, 3)]
    forcing = [planes[p] for p in range(4)]
    mixing = MIX_BASE + MIX_WIND * forcing[3]
    top = {}

    def whole(t, l):
        at = t * LEVELS + l
        high = old[t, l, 0:8, :] + jnp.where(row8 == 0, fix[at : at + 1], 0.0)
        return jnp.concatenate([high, old[t, l, 8:16, :]], 0)

    for t in range(2):
        across, centre = None, whole(t, 0)
        for l in range(LEVELS):
            at = t * LEVELS + l
            below = whole(t, l + 1) if l < LEVELS - 1 else None
            change, across = column_change(centre, below, mixing, deep, l, across)
            change = change + source(t, l, forcing, centre)
            nears = beside(
                centre,
                norths[at : at + 1],
                souths[at : at + 1],
                west[:, 64 + at : 65 + at],
                east[:, at : at + 1],
            )
            change = change + side_sum(centre, nears, [d > l for d in around])
            value = centre + jnp.where(deep > l, change, 0.0)
            final[t, l] = value
            if l < 3:
                top[t, l] = value
            centre = below
    wet_top = jnp.where(deep > 0, 1.0, 0.0)
    surface = (
        top[0, 0] * wet_top,
        top[1, 0] * wet_top,
        (top[0, 0] + top[0, 1] + top[0, 2]) / 3.0 * wet_top,
        wet_top,
    )
    parts = []
    for f in surface:
        parts.append(jnp.concatenate([f[:, s * 128 : (s + 1) * 128] for s in range(TILES)], 0))
    blocks = jnp.concatenate(parts, 1).astype(BF16)
    surface_blocks[...] = blocks
    mask, fold = group_mask(), inbound_fold()
    copy.wait()
    for n, out in ((3, to_dg), (2, to_gy), (1, to_gx)):
        inbound_list(blocks, table[n // 2, n % 2], panels.at[n], fold, mask, out)


def outer_kernel(final, blocks, table, panels, new_temp, new_salt, own, sems):
    copies = fetch(sems, [(final.at[0], new_temp), (final.at[1], new_salt)])
    inbound_list(blocks[...], table[0, 0], panels.at[0], inbound_fold(), group_mask(), own)
    for copy in copies:
        copy.wait()


def final_kernel(dg, gy, gx, own, out):
    total = own[...] + gx[...] + gy[...] + dg[...]
    group = iota((8, 128), 1) // 16
    for c in range(4):
        field = jnp.zeros((8, 128), F32)
        for k in range(8):
            moved = pltpu.roll(total[k * 8 : (k + 1) * 8], (k - c) % 8 * 16, 1)
            field = jnp.where(group == k, moved, field)
        out[c] = field


def call(kernel, shapes, args, scratch=(), hbm_in=(), hbm_out=(), mib=12):
    shapes = [s if isinstance(s, jax.ShapeDtypeStruct) else jax.ShapeDtypeStruct(s, F32) for s in shapes]
    return pl.pallas_call(
        kernel,
        out_shape=shapes,
        in_specs=[HBM if n in hbm_in else VMEM for n in range(len(args))],
        out_specs=[HBM if n in hbm_out else VMEM for n in range(len(shapes))],
        scratch_shapes=list(scratch),
        compiler_params=pltpu.CompilerParams(vmem_limit_bytes=mib * 1024 * 1024),
    )(*args)


def send(block, step):
    wide, high = lax.axis_size("gx"), lax.axis_size("gy")
    route = []
    for i in range(wide):
        for j in range(high):
            to = step(i, j)
            if 0 <= to[1] < high:
                route.append((i * high + j, to[0] % wide * high + to[1]))
    return lax.ppermute(block, ("gx", "gy"), route)


def pair(n):
    return n - 1 if n % 2 else n + 1


def other_pair(n):
    return n + 1 if n % 2 else n - 1


def per_device(air, out_tables, out_panels, depth, temp, salt, in_tables, in_panels):
    out_panels = out_panels.reshape(4, 1024, 128)
    in_panels = in_panels.reshape(4, 1024, 128)
    out_tables, in_tables = out_tables[0, 0], in_tables[0, 0]
    field = (2, LEVELS, ROWS, COLS)
    to_gx, to_gy, to_dg = call(
        outbound_kernel,
        [(LIST_ROWS + ROWS, 128), (LIST_ROWS + TILES * EDGE_ROWS, 128), (LIST_ROWS, 128)],
        [air, out_tables, out_panels, temp, salt, depth],
        [
            pltpu.VMEM(air.shape, BF16), pltpu.VMEM(out_tables.shape, jnp.int32),
            pltpu.VMEM((3, 1024, 128), BF16), pltpu.VMEM(temp.shape, F32),
            pltpu.VMEM(temp.shape, F32), pltpu.VMEM(depth.shape, jnp.int32),
            pltpu.SemaphoreType.DMA((8,)),
        ],
        hbm_in=range(6),
    )
    dg = send(to_dg, lambda i, j: (i - 1, j - 1))
    gy = send(to_gy, lambda i, j: (i, j - 1))
    zpair = send(to_gx, lambda i, j: (other_pair(i), j))
    core = send(to_gx, lambda i, j: (pair(i), j))
    own, partial = call(
        inner_kernel,
        [(LIST_ROWS, 128), field],
        [air, out_tables, out_panels, temp, salt, depth],
        [pltpu.VMEM((1024, 128), BF16), pltpu.SemaphoreType.DMA],
        hbm_in=(2,),
    )
    stepped, cols, row_e, row_o, planes, depths, keep = call(
        first_kernel,
        [field, (ROWS, 128), (48, COLS), (48, COLS), (4, ROWS, COLS), (4, ROWS, COLS), (48, COLS)],
        [own, core, zpair, gy, dg, partial, temp, salt, depth],
    )
    xo = send(row_o, lambda i, j: (i, other_pair(j)))
    xe = send(row_e, lambda i, j: (i, pair(j)))
    zpair = send(cols, lambda i, j: (other_pair(i), j))
    core = send(cols, lambda i, j: (pair(i), j))
    final, blocks, to_gx, to_gy, to_dg = call(
        second_kernel,
        [field, jax.ShapeDtypeStruct((64, COLS), BF16)] + [(64, 128)] * 3,
        [stepped, core, zpair, xe, xo, planes, depths, keep, depth, in_tables, in_panels],
        [pltpu.VMEM(in_tables.shape, jnp.int32), pltpu.SemaphoreType.DMA],
        hbm_in=(9,),
    )
    dg = send(to_dg, lambda i, j: (i + 1, j + 1))
    gy = send(to_gy, lambda i, j: (i, j + 1))
    gx = send(to_gx, lambda i, j: (i + 1, j))
    new_temp, new_salt, own = call(
        outer_kernel,
        [temp.shape, salt.shape, (64, 128)],
        [final, blocks, in_tables, in_panels],
        [pltpu.SemaphoreType.DMA((2,))],
        hbm_out=(0, 1),
    )
    (surface,) = call(final_kernel, [(4, 8, 128)], [dg, gy, gx, own])
    return new_temp, new_salt, surface


def solution(mesh):
    in_specs = (
        P(None, "gy", "gx"),
        P("gy", "gx", None, None, None, None),
        P("gy", "gx", None, None, None, None, None),
        P("gy", "gx"),
        P(None, "gy", "gx"),
        P(None, "gy", "gx"),
        P("gy", "gx", None, None, None, None),
        P("gy", "gx", None, None, None, None, None),
    )
    out_specs = (P(None, "gy", "gx"), P(None, "gy", "gx"), P(None, "gy", "gx"))
    return jax.shard_map(
        per_device, mesh=mesh, in_specs=in_specs, out_specs=out_specs, check_vma=False
    )
```

time: 53.6 us -> 49.7 us (0.927)
  the two profiles are of different devices: /device:TPU:8 before, /device:TPU:10 now
where the time goes in v2:
time: 49.7 us; the launch traced here: 49.2 us
  starting transfers between devices  26.3 us (53%)
  Pallas kernels  9.15 us (18%)
  waiting for transfers between devices  6.91 us (14%)
  local copies, waits for them, and re-layouts  6.01 us (12%)
  between operations  0.81 us (2%)
    ppermute x11, starting transfers between devices, send(): return lax.ppermute(block, ('gx', 'gy'), route)  26.3 us
    pallas_call x6, Pallas kernels, call(): pl.pallas_call(kernel, out_shape=shapes, in_specs=[HBM if n in hbm_in els...  9.15 us
    ppermute x11, waiting for transfers between devices, send(): return lax.ppermute(block, ('gx', 'gy'), route)  6.91 us
    unnamed x22, local copies, waits for them, and re-layouts  6.01 us
  transfers between devices with their start and end apart: 11, of which 4 were waited for; matrix products, arithmetic and copies ran while one was open for 0% of the time, Pallas kernels for 4%

profile of v2, /device:TPU:10, one launch (start us, length us, event | category | flops | bytes accessed | tf_op | source)
XLA Modules:
  0.0 49.2 jit_solution(17195172475862645736)
XLA Ops:
  0.6 0.0 copy-start.1
  0.6 1.2 %copy-done.1 = bf16[1,1,2,2,64,16,128]{6,5,4,3,2,1,0:T(8,128)(2,1)S(1)} copy-done((bf16[1,1,2,2,64,16,128]{6,5,4,3,2,1,0:T(8,128)(2,1)S(1)}, bf16[1,1,2,2,64,16,128]{6,5,4,3,2,1,0:T(8,128)(2,1)}, u32[]{:S(2)}) %copy-start.1) | copy-done | bytes 1048600
  1.9 0.0 copy-start.2
  1.9 1.0 %copy-done.2 = f32[10,16,512]{2,1,0:T(8,128)S(1)} copy-done((f32[10,16,512]{2,1,0:T(8,128)S(1)}, f32[10,16,512]{2,1,0:T(8,128)}, u32[]{:S(2)}) %copy-start.2) | copy-done | bytes 327704
  2.8 0.0 copy-start.4
  2.8 1.0 %copy-done.4 = f32[10,16,512]{2,1,0:T(8,128)S(1)} copy-done((f32[10,16,512]{2,1,0:T(8,128)S(1)}, f32[10,16,512]{2,1,0:T(8,128)}, u32[]{:S(2)}) %copy-start.4) | copy-done | bytes 327704
  3.8 0.0 copy-start.6
  3.8 0.8 %copy-done.6 = s32[16,512]{1,0:T(8,128)S(1)} copy-done((s32[16,512]{1,0:T(8,128)S(1)}, s32[16,512]{1,0:T(8,128)}, u32[]{:S(2)}) %copy-start.6) | copy-done | bytes 32792
  4.6 0.0 copy-start.8
  4.6 0.7 %copy-done.8 = bf16[8,8,128]{2,1,0:T(8,128)(2,1)S(1)} copy-done((bf16[8,8,128]{2,1,0:T(8,128)(2,1)S(1)}, bf16[8,8,128]{2,1,0:T(8,128)(2,1)}, u32[]{:S(2)}) %copy-start.8) | copy-done | bytes 16408
  5.3 0.0 copy-start.9
  5.3 0.7 %copy-done.9 = s32[1,1,2,2,2,64]{5,4,3,2,1,0:T(2,128)S(1)} copy-done((s32[1,1,2,2,2,64]{5,4,3,2,1,0:T(2,128)S(1)}, s32[1,1,2,2,2,64]{5,4,3,2,1,0:T(2,128)}, u32[]{:S(2)}) %copy-start.9) | copy-done | bytes 2072
  6.0 2.4 %shard_map.104 = (f32[272,128]{1,0:T(8,128)S(1)}, f32[352,128]{1,0:T(8,128)S(1)}, f32[256,128]{1,0:T(8,128)S(1)}) custom-call(bf16[8,8,128]{2,1,0:T(8,128)(2,1)S(1)} %copy-done.8, s32[2,2,2,64]{3,2,1,0:T(2,128)S(1)} %bitcast.8, bf16[4,1024,128]{2,1,0:T(8,128)(2,1)S(1)} %bitcast.6, f32[10,16,512]{2,1,0:T(8,128)S(1)} %copy-done.2, ...), custom_call_target="tpu_custom_call" | custom-call | tf_op jit(solution)/shard_map/pallas_call | solution.py:397
  8.4 2.4 %collective-permute-start.2 = (f32[352,128]{1,0:T(8,128)S(1)}, f32[352,128]{1,0:T(8,128)S(1)}, u32[]{:S(2)}, u32[]{:S(2)}) collective-permute-start(f32[352,128]{1,0:T(8,128)S(1)} %get-tuple-element.25), channel_id=1, source_target_pairs={{1,0},{2,1},{3,2},{4,3},{5,4},{6,5},{7,6},{8,7},{9,8},{10,9},{11,1... | collective-permute-start | bytes 540680 | tf_op jit(solution)/shard_map/ppermute | solution.py:415
  10.8 3.3 %collective-permute-start.1 = (f32[272,128]{1,0:T(8,128)S(1)}, f32[272,128]{1,0:T(8,128)S(1)}, u32[]{:S(2)}, u32[]{:S(2)}) collective-permute-start(f32[272,128]{1,0:T(8,128)S(1)} %get-tuple-element.24), channel_id=1, source_target_pairs={{0,112},{1,113},{2,114},{3,115},{4,116},{5,117},{6,118},{7,119},{8... | collective-permute-start | bytes 417800 | tf_op jit(solution)/shard_map/ppermute | solution.py:415
  14.1 0.0 collective-permute-start
  14.1 0.0 copy-start.3
  14.1 5.1 %collective-permute-start.3 = (f32[256,128]{1,0:T(8,128)S(1)}, f32[256,128]{1,0:T(8,128)S(1)}, u32[]{:S(2)}, u32[]{:S(2)}) collective-permute-start(f32[256,128]{1,0:T(8,128)S(1)} %get-tuple-element.26), channel_id=1, source_target_pairs={{1,112},{2,113},{3,114},{4,115},{5,116},{6,117},{7,118},{8,119},{9... | collective-permute-start | bytes 393224 | tf_op jit(solution)/shard_map/ppermute | solution.py:415
  19.3 1.3 %shard_map.103 = (f32[256,128]{1,0:T(8,128)S(1)}, f32[2,10,16,512]{3,2,1,0:T(8,128)S(1)}) custom-call(bf16[8,8,128]{2,1,0:T(8,128)(2,1)S(1)} %copy-done.8, s32[2,2,2,64]{3,2,1,0:T(2,128)S(1)} %bitcast.9, bf16[4,1024,128]{2,1,0:T(8,128)(2,1)S(1)} %bitcast.7, f32[10,16,512]{2,1,0:T(8,128)S(1)} %copy-done.2, f32[10,16,512]{2,1,0:T(8,128)S(1)} %copy-done.4, ...), custom_call_target="tpu_custom_call" | custom-call | tf_op jit(solution)/shard_map/pallas_call | solution.py:397
  20.6 0.0 copy-start
  20.6 1.5 %collective-permute-done.3.dg = f32[256,128]{1,0:T(8,128)S(1)} collective-permute-done((f32[256,128]{1,0:T(8,128)S(1)}, f32[256,128]{1,0:T(8,128)S(1)}, u32[]{:S(2)}, u32[]{:S(2)}) %collective-permute-start.3) | collective-permute-done | bytes 131104 | tf_op jit(solution)/shard_map/ppermute | solution.py:415
  22.1 0.0 collective-permute-done.1.zpair
  22.1 0.0 collective-permute-done.core
  22.1 0.0 collective-permute-done.2.gy
  22.1 0.0 copy-done.3
  22.1 0.0 copy-done.5
  22.2 0.0 copy-done.7
  22.2 1.1 %shard_map.105 = (f32[2,10,16,512]{3,2,1,0:T(8,128)S(1)}, f32[16,128]{1,0:T(8,128)S(1)}, f32[48,512]{1,0:T(8,128)S(1)}, f32[48,512]{1,0:T(8,128)S(1)}, f32[4,16,...) custom-call(f32[256,128]{1,0:T(8,128)S(1)} %get-tuple-element.23.own, ...), custom_call_target="tpu_custom_call" | custom-call | tf_op jit(solution)/shard_map/pallas_call | solution.py:397
  23.3 1.5 %collective-permute-start.6 = (f32[48,512]{1,0:T(8,128)S(1)}, f32[48,512]{1,0:T(8,128)S(1)}, u32[]{:S(2)}, u32[]{:S(2)}) collective-permute-start(f32[48,512]{1,0:T(8,128)S(1)} %get-tuple-element.30), channel_id=1, source_target_pairs={{0,1},{1,0},{2,3},{3,2},{4,5},{5,4},{6,7},{7,6},{8,9},{9,8},{10,11... | collective-permute-start | bytes 294920 | tf_op jit(solution)/shard_map/ppermute | solution.py:415
  24.8 4.3 %collective-permute-start.7 = (f32[48,512]{1,0:T(8,128)S(1)}, f32[48,512]{1,0:T(8,128)S(1)}, u32[]{:S(2)}, u32[]{:S(2)}) collective-permute-start(f32[48,512]{1,0:T(8,128)S(1)} %get-tuple-element.31), channel_id=1, source_target_pairs={{1,2},{2,1},{3,4},{4,3},{5,6},{6,5},{7,8},{8,7},{9,10},{10,9},{11,... | collective-permute-start | bytes 294920 | tf_op jit(solution)/shard_map/ppermute | solution.py:415
  29.1 2.7 %collective-permute-start.5 = (f32[16,128]{1,0:T(8,128)S(1)}, f32[16,128]{1,0:T(8,128)S(1)}, u32[]{:S(2)}, u32[]{:S(2)}) collective-permute-start(f32[16,128]{1,0:T(8,128)S(1)} %get-tuple-element.29), channel_id=1, source_target_pairs={{0,112},{1,113},{2,114},{3,115},{4,116},{5,117},{6,118},{7,119},{8... | collective-permute-start | bytes 24584 | tf_op jit(solution)/shard_map/ppermute | solution.py:415
  31.8 0.0 collective-permute-start.4
  31.8 1.7 %collective-permute-done.5.zpair = f32[16,128]{1,0:T(8,128)S(1)} collective-permute-done((f32[16,128]{1,0:T(8,128)S(1)}, f32[16,128]{1,0:T(8,128)S(1)}, u32[]{:S(2)}, u32[]{:S(2)}) %collective-permute-start.5) | collective-permute-done | bytes 8224 | tf_op jit(solution)/shard_map/ppermute | solution.py:415
  33.5 0.0 collective-permute-done.4.core
  33.5 0.0 collective-permute-done.6.xe
  33.5 0.0 collective-permute-done.7.xo
  33.5 0.0 copy-start.10
  33.5 0.0 copy-done
  33.5 0.7 %copy-done.10 = s32[1,1,2,2,2,64]{5,4,3,2,1,0:T(2,128)S(1)} copy-done((s32[1,1,2,2,2,64]{5,4,3,2,1,0:T(2,128)S(1)}, s32[1,1,2,2,2,64]{5,4,3,2,1,0:T(2,128)}, u32[]{:S(2)}) %copy-start.10) | copy-done | bytes 2072
  34.2 2.8 %shard_map.106 = (f32[2,10,16,512]{3,2,1,0:T(8,128)S(1)}, bf16[64,512]{1,0:T(8,128)(2,1)S(1)}, f32[64,128]{1,0:T(8,128)S(1)}, f32[64,128]{1,0:T(8,128)S(1)}, f32[64,128]{1,0:T(8,128)S(1)}) custom-call(f32[2,10,16,512]{3,2,1,0:T(8,128)S(1)} %get-tuple-element.28.old, f32[16,128]{1,0:T(8,128)S(1)} %collective-permute-done.4.core, ...), custom_call_target="tpu_custom_call" | custom-call | tf_op jit(solution)/shard_map/pallas_call | solution.py:397
  37.0 2.4 %collective-permute-start.8 = (f32[64,128]{1,0:T(8,128)S(1)}, f32[64,128]{1,0:T(8,128)S(1)}, u32[]{:S(2)}, u32[]{:S(2)}) collective-permute-start(f32[64,128]{1,0:T(8,128)S(1)} %get-tuple-element.39), channel_id=1, source_target_pairs={{0,17},{1,18},{2,19},{3,20},{4,21},{5,22},{6,23},{7,24},{8,25},{9,... | collective-permute-start | bytes 98312 | tf_op jit(solution)/shard_map/ppermute | solution.py:415
  39.5 4.4 %collective-permute-start.9 = (f32[64,128]{1,0:T(8,128)S(1)}, f32[64,128]{1,0:T(8,128)S(1)}, u32[]{:S(2)}, u32[]{:S(2)}) collective-permute-start(f32[64,128]{1,0:T(8,128)S(1)} %get-tuple-element.40), channel_id=1, source_target_pairs={{0,1},{1,2},{2,3},{3,4},{4,5},{5,6},{6,7},{7,8},{8,9},{9,10},{10,1... | collective-permute-start | bytes 98312 | tf_op jit(solution)/shard_map/ppermute | solution.py:415
  43.9 0.0 collective-permute-start.10
  43.9 0.9 %shard_map.107 = (f32[10,16,512]{2,1,0:T(8,128)}, f32[10,16,512]{2,1,0:T(8,128)}, f32[64,128]{1,0:T(8,128)S(1)}) custom-call(f32[2,10,16,512]{3,2,1,0:T(8,128)S(1)} %get-tuple-element.35.final, bf16[64,512]{1,0:T(8,128)(2,1)S(1)} %get-tuple-element.36.blocks, s32[2,2,2,64]{3,2,1,0:T(2,128)S(1)} %bitcast.11, bf16[4,1024,128]{2,1,0:T(8,128)(2,1)S(1)} %bitcast.5), custom_call_target="tpu_custom_call" | custom-call | tf_op jit(solution)/shard_map/pallas_call | solution.py:397
  44.8 0.0 collective-permute-done.8.dg
  44.8 0.7 %collective-permute-done.9.gy = f32[64,128]{1,0:T(8,128)S(1)} collective-permute-done((f32[64,128]{1,0:T(8,128)S(1)}, f32[64,128]{1,0:T(8,128)S(1)}, u32[]{:S(2)}, u32[]{:S(2)}) %collective-permute-start.9) | collective-permute-done | bytes 32800 | tf_op jit(solution)/shard_map/ppermute | solution.py:415
  45.5 3.0 %collective-permute-done.10.gx = f32[64,128]{1,0:T(8,128)S(1)} collective-permute-done((f32[64,128]{1,0:T(8,128)S(1)}, f32[64,128]{1,0:T(8,128)S(1)}, u32[]{:S(2)}, u32[]{:S(2)}) %collective-permute-start.10) | collective-permute-done | bytes 32800 | tf_op jit(solution)/shard_map/ppermute | solution.py:415
  48.5 0.7 %shard_map.108 = f32[4,8,128]{2,1,0:T(8,128)} custom-call(f32[64,128]{1,0:T(8,128)S(1)} %collective-permute-done.8.dg, f32[64,128]{1,0:T(8,128)S(1)} %collective-permute-done.9.gy, f32[64,128]{1,0:T(8,128)S(1)} %collective-permute-done.10.gx, f32[64,128]{1,0:T(8,128)S(1)} %get-tuple-element.42.own), custom_call_target="tpu_custom_call" | custom-call | tf_op jit(solution)/shard_map/pallas_call | solution.py:397
  (2 shorter events, 0.0 us)
Async XLA Ops:
  0.6 1.2 %copy-start.1 = (bf16[1,1,2,2,64,16,128]{6,5,4,3,2,1,0:T(8,128)(2,1)S(1)}, bf16[1,1,2,2,64,16,128]{6,5,4,3,2,1,0:T(8,128)(2,1)}, u32[]{:S(2)}) copy-start(bf16[1,1,2,2,64,16,128]{6,5,4,3,2,1,0:T(8,128)(2,1)} %param.10) | copy-start | bytes 3145732
  1.9 1.0 %copy-start.2 = (f32[10,16,512]{2,1,0:T(8,128)S(1)}, f32[10,16,512]{2,1,0:T(8,128)}, u32[]{:S(2)}) copy-start(f32[10,16,512]{2,1,0:T(8,128)} %temp.3) | copy-start | bytes 983044
  2.8 1.0 %copy-start.4 = (f32[10,16,512]{2,1,0:T(8,128)S(1)}, f32[10,16,512]{2,1,0:T(8,128)}, u32[]{:S(2)}) copy-start(f32[10,16,512]{2,1,0:T(8,128)} %salt.3) | copy-start | bytes 983044
  3.8 0.8 %copy-start.6 = (s32[16,512]{1,0:T(8,128)S(1)}, s32[16,512]{1,0:T(8,128)}, u32[]{:S(2)}) copy-start(s32[16,512]{1,0:T(8,128)} %depth.5) | copy-start | bytes 98308
  4.6 0.7 %copy-start.8 = (bf16[8,8,128]{2,1,0:T(8,128)(2,1)S(1)}, bf16[8,8,128]{2,1,0:T(8,128)(2,1)}, u32[]{:S(2)}) copy-start(bf16[8,8,128]{2,1,0:T(8,128)(2,1)} %air_hbm.1) | copy-start | bytes 49156
  5.3 0.7 %copy-start.9 = (s32[1,1,2,2,2,64]{5,4,3,2,1,0:T(2,128)S(1)}, s32[1,1,2,2,2,64]{5,4,3,2,1,0:T(2,128)}, u32[]{:S(2)}) copy-start(s32[1,1,2,2,2,64]{5,4,3,2,1,0:T(2,128)} %param.9) | copy-start | bytes 6148
  8.4 13.7 %collective-permute-start.2 = (f32[352,128]{1,0:T(8,128)S(1)}, f32[352,128]{1,0:T(8,128)S(1)}, u32[]{:S(2)}, u32[]{:S(2)}) collective-permute-start(f32[352,128]{1,0:T(8,128)S(1)} %get-tuple-element.25), channel_id=1, source_target_pairs={{1,0},{2,1},{3,2},{4,3},{5,4},{6,5},{7,6},{8,7},{9,8},{10,9},{11,1... | collective-permute-start | bytes 540680 | tf_op jit(solution)/shard_map/ppermute | solution.py:415
  10.8 11.3 %collective-permute-start.1 = (f32[272,128]{1,0:T(8,128)S(1)}, f32[272,128]{1,0:T(8,128)S(1)}, u32[]{:S(2)}, u32[]{:S(2)}) collective-permute-start(f32[272,128]{1,0:T(8,128)S(1)} %get-tuple-element.24), channel_id=1, source_target_pairs={{0,112},{1,113},{2,114},{3,115},{4,116},{5,117},{6,118},{7,119},{8... | collective-permute-start | bytes 417800 | tf_op jit(solution)/shard_map/ppermute | solution.py:415
  14.1 8.0 %collective-permute-start = (f32[272,128]{1,0:T(8,128)S(1)}, f32[272,128]{1,0:T(8,128)S(1)}, u32[]{:S(2)}, u32[]{:S(2)}) collective-permute-start(f32[272,128]{1,0:T(8,128)S(1)} %get-tuple-element.24), channel_id=1, source_target_pairs={{0,16},{1,17},{2,18},{3,19},{4,20},{5,21},{6,22},{7,23},{8,24},{9,... | collective-permute-start | bytes 417800 | tf_op jit(solution)/shard_map/ppermute | solution.py:415
  14.1 8.0 %copy-start.3 = (f32[10,16,512]{2,1,0:T(8,128)S(1)}, f32[10,16,512]{2,1,0:T(8,128)}, u32[]{:S(2)}) copy-start(f32[10,16,512]{2,1,0:T(8,128)} %temp.3) | copy-start | bytes 983044
  14.1 8.0 %copy-start.5 = (f32[10,16,512]{2,1,0:T(8,128)S(1)}, f32[10,16,512]{2,1,0:T(8,128)}, u32[]{:S(2)}) copy-start(f32[10,16,512]{2,1,0:T(8,128)} %salt.3) | copy-start | bytes 983044
  14.1 8.0 %copy-start.7 = (s32[16,512]{1,0:T(8,128)S(1)}, s32[16,512]{1,0:T(8,128)}, u32[]{:S(2)}) copy-start(s32[16,512]{1,0:T(8,128)} %depth.5) | copy-start | bytes 98308
  14.1 8.0 %collective-permute-start.3 = (f32[256,128]{1,0:T(8,128)S(1)}, f32[256,128]{1,0:T(8,128)S(1)}, u32[]{:S(2)}, u32[]{:S(2)}) collective-permute-start(f32[256,128]{1,0:T(8,128)S(1)} %get-tuple-element.26), channel_id=1, source_target_pairs={{1,112},{2,113},{3,114},{4,115},{5,116},{6,117},{7,118},{8,119},{9... | collective-permute-start | bytes 393224 | tf_op jit(solution)/shard_map/ppermute | solution.py:415
  20.6 12.9 %copy-start = (bf16[1,1,2,2,64,16,128]{6,5,4,3,2,1,0:T(8,128)(2,1)S(1)}, bf16[1,1,2,2,64,16,128]{6,5,4,3,2,1,0:T(8,128)(2,1)}, u32[]{:S(2)}) copy-start(bf16[1,1,2,2,64,16,128]{6,5,4,3,2,1,0:T(8,128)(2,1)} %param.15) | copy-start | bytes 3145732
  23.3 10.2 %collective-permute-start.6 = (f32[48,512]{1,0:T(8,128)S(1)}, f32[48,512]{1,0:T(8,128)S(1)}, u32[]{:S(2)}, u32[]{:S(2)}) collective-permute-start(f32[48,512]{1,0:T(8,128)S(1)} %get-tuple-element.30), channel_id=1, source_target_pairs={{0,1},{1,0},{2,3},{3,2},{4,5},{5,4},{6,7},{7,6},{8,9},{9,8},{10,11... | collective-permute-start | bytes 294920 | tf_op jit(solution)/shard_map/ppermute | solution.py:415
  24.8 8.7 %collective-permute-start.7 = (f32[48,512]{1,0:T(8,128)S(1)}, f32[48,512]{1,0:T(8,128)S(1)}, u32[]{:S(2)}, u32[]{:S(2)}) collective-permute-start(f32[48,512]{1,0:T(8,128)S(1)} %get-tuple-element.31), channel_id=1, source_target_pairs={{1,2},{2,1},{3,4},{4,3},{5,6},{6,5},{7,8},{8,7},{9,10},{10,9},{11,... | collective-permute-start | bytes 294920 | tf_op jit(solution)/shard_map/ppermute | solution.py:415
  29.1 4.4 %collective-permute-start.5 = (f32[16,128]{1,0:T(8,128)S(1)}, f32[16,128]{1,0:T(8,128)S(1)}, u32[]{:S(2)}, u32[]{:S(2)}) collective-permute-start(f32[16,128]{1,0:T(8,128)S(1)} %get-tuple-element.29), channel_id=1, source_target_pairs={{0,112},{1,113},{2,114},{3,115},{4,116},{5,117},{6,118},{7,119},{8... | collective-permute-start | bytes 24584 | tf_op jit(solution)/shard_map/ppermute | solution.py:415
  31.8 1.7 %collective-permute-start.4 = (f32[16,128]{1,0:T(8,128)S(1)}, f32[16,128]{1,0:T(8,128)S(1)}, u32[]{:S(2)}, u32[]{:S(2)}) collective-permute-start(f32[16,128]{1,0:T(8,128)S(1)} %get-tuple-element.29), channel_id=1, source_target_pairs={{0,16},{1,17},{2,18},{3,19},{4,20},{5,21},{6,22},{7,23},{8,24},{9,... | collective-permute-start | bytes 24584 | tf_op jit(solution)/shard_map/ppermute | solution.py:415
  33.5 0.7 %copy-start.10 = (s32[1,1,2,2,2,64]{5,4,3,2,1,0:T(2,128)S(1)}, s32[1,1,2,2,2,64]{5,4,3,2,1,0:T(2,128)}, u32[]{:S(2)}) copy-start(s32[1,1,2,2,2,64]{5,4,3,2,1,0:T(2,128)} %param.14) | copy-start | bytes 6148
  37.0 7.8 %collective-permute-start.8 = (f32[64,128]{1,0:T(8,128)S(1)}, f32[64,128]{1,0:T(8,128)S(1)}, u32[]{:S(2)}, u32[]{:S(2)}) collective-permute-start(f32[64,128]{1,0:T(8,128)S(1)} %get-tuple-element.39), channel_id=1, source_target_pairs={{0,17},{1,18},{2,19},{3,20},{4,21},{5,22},{6,23},{7,24},{8,25},{9,... | collective-permute-start | bytes 98312 | tf_op jit(solution)/shard_map/ppermute | solution.py:415
  39.5 6.0 %collective-permute-start.9 = (f32[64,128]{1,0:T(8,128)S(1)}, f32[64,128]{1,0:T(8,128)S(1)}, u32[]{:S(2)}, u32[]{:S(2)}) collective-permute-start(f32[64,128]{1,0:T(8,128)S(1)} %get-tuple-element.40), channel_id=1, source_target_pairs={{0,1},{1,2},{2,3},{3,4},{4,5},{5,6},{6,7},{7,8},{8,9},{9,10},{10,1... | collective-permute-start | bytes 98312 | tf_op jit(solution)/shard_map/ppermute | solution.py:415
  43.9 4.6 %collective-permute-start.10 = (f32[64,128]{1,0:T(8,128)S(1)}, f32[64,128]{1,0:T(8,128)S(1)}, u32[]{:S(2)}, u32[]{:S(2)}) collective-permute-start(f32[64,128]{1,0:T(8,128)S(1)} %get-tuple-element.41), channel_id=1, source_target_pairs={{0,16},{1,17},{2,18},{3,19},{4,20},{5,21},{6,22},{7,23},{8,24},{9,... | collective-permute-start | bytes 98312 | tf_op jit(solution)/shard_map/ppermute | solution.py:415

commit v3 on v2

--- a/solution.py
+++ b/solution.py
@@ -113,29 +113,26 @@
 
 
 def outbound_kernel(
-    air_hbm, table_hbm, panels_hbm, temp_hbm, salt_hbm, depth_hbm, to_gx, to_gy, to_dg,
+    air_hbm, table_hbm, panels_hbm, temp_hbm, salt_hbm, depth_hbm, to_gx,
     air, table, panels, temp, salt, depth, sems,
 ):
     pairs = [(air_hbm, air), (table_hbm, table)]
-    pairs += [(panels_hbm.at[n], panels.at[n]) for n in range(3)]
+    pairs += [(panels_hbm.at[2 * n], panels.at[n]) for n in range(2)]
     pairs += [(temp_hbm, temp), (salt_hbm, salt), (depth_hbm, depth)]
     copies = fetch(sems, pairs)
     mask = group_mask()
     copies[0].wait()
     tiled = spread_air(air, mask)
     copies[1].wait()
-    for n, out in ((0, to_dg), (1, to_gy), (2, to_gx)):
+    for n in range(2):
         copies[2 + n].wait()
-        outbound_list(tiled, table[n // 2, n % 2], panels.at[n], mask, out)
-    for copy in copies[5:]:
+        out = to_gx.at[n * LIST_ROWS : (n + 1) * LIST_ROWS]
+        outbound_list(tiled, table[n, 0], panels.at[n], mask, out)
+    for copy in copies[4:]:
         copy.wait()
     deep = depth[...].astype(F32)
     levels = [temp[l] for l in range(LEVELS)] + [salt[l] for l in range(LEVELS)] + [deep]
-    to_gx[LIST_ROWS : LIST_ROWS + ROWS, :] = edge_columns(levels)
-    for base, edge in ((0, temp[:, 0, :]), (LEVELS, salt[:, 0, :]), (2 * LEVELS, deep[0:1])):
-        for s in range(TILES):
-            at = LIST_ROWS + s * EDGE_ROWS + base
-            to_gy[at : at + edge.shape[0], :] = edge[:, s * 128 : (s + 1) * 128]
+    to_gx[2 * LIST_ROWS :, :] = edge_columns(levels)
 
 
 def beside(values, north, south, west, east):
@@ -155,9 +152,10 @@
     return SIDE_RATE * side
 
 
-def inner_kernel(air, table, panels_hbm, temp, salt, depth, own, partial, panel, sem):
-    copy = pltpu.make_async_copy(panels_hbm.at[3], panel, sem)
-    copy.start()
+def inner_kernel(
+    air, table, panels_hbm, temp, salt, depth, own, north, partial, panels, sems
+):
+    copies = fetch(sems, [(panels_hbm.at[2 * n + 1], panels.at[n]) for n in range(2)])
     deep = depth[...].astype(F32)
     dry = jnp.zeros((1, 1), F32)
     around = beside(deep, dry, dry, dry, dry)
@@ -168,10 +166,51 @@
             centre = field[l]
             side = side_sum(centre, beside(centre, dry, dry, dry, dry), wets)
             partial[t, l] = centre + jnp.where(wet, side, 0.0)
+    for base, edge in ((0, temp[:, 0, :]), (LEVELS, salt[:, 0, :]), (2 * LEVELS, deep[0:1])):
+        for s in range(TILES):
+            at = LIST_ROWS + s * EDGE_ROWS + base
+            north[at : at + edge.shape[0], :] = edge[:, s * 128 : (s + 1) * 128]
     mask = group_mask()
     tiled = spread_air(air, mask)
-    copy.wait()
-    outbound_list(tiled, table[1, 1], panel, mask, own)
+    for n, out in ((0, north), (1, own)):
+        copies[n].wait()
+        outbound_list(tiled, table[n, 1], panels.at[n], mask, out)
+
+
+def north_kernel(part, core, zpair, out):
+    odd_col = lax.axis_index("gx") % 2 == 1
+    out[0:LIST_ROWS, :] = part[0:LIST_ROWS, :] + jnp.where(
+        odd_col, zpair[0:LIST_ROWS, :], core[0:LIST_ROWS, :]
+    )
+    out[LIST_ROWS:, :] = part[LIST_ROWS:, :]
+
+
+def edge_kernel(own, core, zpair, partial, temp, salt, depth, base, west, east, depths, whole):
+    odd_col = lax.axis_index("gx") % 2 == 1
+    base[...] = own[...] + jnp.where(
+        odd_col, zpair[LIST_ROWS : 2 * LIST_ROWS, :], core[LIST_ROWS : 2 * LIST_ROWS, :]
+    )
+    left = jnp.where(odd_col, core[2 * LIST_ROWS :, :], zpair[2 * LIST_ROWS :, :])
+    right = jnp.where(odd_col, zpair[2 * LIST_ROWS :, :], core[2 * LIST_ROWS :, :])
+    west[...] = left
+    east[...] = right
+    deep = depth[...].astype(F32)
+    dry = jnp.zeros((1, 1), F32)
+    last = 2 * LEVELS
+    around = beside(deep, dry, dry, left[:, 64 + last : 65 + last], right[:, last : last + 1])
+    for n in range(4):
+        depths[n] = around[n]
+    lane = iota((ROWS, 128), 1)
+    sides = ((0, left, 64, around[2], 0), (COLS - 128, right, 0, around[3], 127))
+    for t, field in enumerate((temp, salt)):
+        for l in range(LEVELS):
+            at = t * LEVELS + l
+            whole[t, l] = partial[t, l]
+            for first, halo, offset, far, spot in sides:
+                here = (lane == spot) & (far[:, first : first + 128] > l)
+                here = here & (deep[:, first : first + 128] > l)
+                near = halo[:, offset + at : offset + at + 1] - field[l, :, first : first + 128]
+                whole[t, l, :, first : first + 128] += jnp.where(here, SIDE_RATE * near, 0.0)
 
 
 def column_change(values, below, mixing, depth, l, across):
@@ -191,44 +230,34 @@
 
 
 def first_kernel(
-    own, core, zpair, gy, dg, partial, temp, salt, depth,
+    gy, base, west, east, side_depths, partial, temp, salt, depth,
     new, cols, row_e, row_o, planes, depths, keep,
 ):
-    odd_col = lax.axis_index("gx") % 2 == 1
     odd_row = lax.axis_index("gy") % 2 == 1
-
-    def right(at, rows):
-        return jnp.where(odd_col, zpair[at : at + rows, :], core[at : at + rows, :])
-
-    def left(at, rows):
-        return jnp.where(odd_col, core[at : at + rows, :], zpair[at : at + rows, :])
-
     forcing = []
     for p in range(4):
         parts = []
         for s in range(TILES):
             at = p * 64 + s * ROWS
-            here = own[at : at + ROWS, :] + dg[at : at + ROWS, :]
-            parts.append(here + right(at, ROWS) + gy[at : at + ROWS, :])
+            parts.append(base[at : at + ROWS, :] + gy[at : at + ROWS, :])
         forcing.append(jnp.concatenate(parts, 1))
     squared = forcing[3] * forcing[3]
     forcing[3] = squared / (1.0 + squared)
     for p in range(4):
         planes[p] = forcing[p]
-    west, east = left(LIST_ROWS, ROWS), right(LIST_ROWS, ROWS)
     souths = [gy[LIST_ROWS + s * EDGE_ROWS : LIST_ROWS + (s + 1) * EDGE_ROWS, :] for s in range(TILES)]
     souths = jnp.concatenate(souths, 1)
-
     deep = depth[...].astype(F32)
-    dry = jnp.zeros((1, 1), F32)
     last = 2 * LEVELS
-    around = beside(deep, dry, souths[last : last + 1], west[:, 64 + last : 65 + last], east[:, last : last + 1])
-    for n in range(4):
-        depths[n] = around[n]
+    south = jnp.where(
+        iota((ROWS, COLS), 0) == ROWS - 1, souths[last : last + 1], side_depths[1]
+    )
+    for n in (0, 2, 3):
+        depths[n] = side_depths[n]
+    depths[1] = south
     lane = iota((ROWS, 128), 1)
     row = iota((8, COLS), 0)
     mixing = MIX_BASE + MIX_WIND * forcing[3]
-    sides = ((0, west, 64, around[2], 0), (COLS - 128, east, 0, around[3], 127))
     block = jnp.zeros((ROWS, 128), F32)
     for t, field in enumerate((temp, salt)):
         across = None
@@ -239,18 +268,14 @@
                 centre, field[min(l + 1, LEVELS - 1)], mixing, deep, l, across
             )
             change = change + source(t, l, forcing, centre)
-            new[t, l] = partial[t, l] + jnp.where(deep > l, change, 0.0)
             low = centre[8:16]
-            here = (row == 7) & (around[1][8:16] > l) & (deep[8:16] > l)
+            here = (row == 7) & (south[8:16] > l)
             low = jnp.where(here, SIDE_RATE * (souths[at : at + 1] - low), 0.0)
-            new[t, l, 8:16, :] += low
-            for first, halo, offset, far, spot in sides:
-                here = (lane == spot) & (far[:, first : first + 128] > l)
-                here = here & (deep[:, first : first + 128] > l)
-                near = halo[:, offset + at : offset + at + 1] - centre[:, first : first + 128]
-                new[t, l, :, first : first + 128] += jnp.where(here, SIDE_RATE * near, 0.0)
-            block = jnp.where(lane == at, new[t, l, :, 0:1], block)
-            block = jnp.where(lane == 64 + at, new[t, l, :, COLS - 1 : COLS], block)
+            change = jnp.concatenate([change[0:8], change[8:16] + low], 0)
+            value = partial[t, l] + jnp.where(deep > l, change, 0.0)
+            new[t, l] = value
+            block = jnp.where(lane == at, value[:, 0:1], block)
+            block = jnp.where(lane == 64 + at, value[:, COLS - 1 : COLS], block)
     cols[...] = block
     olds = (temp[:, 0, :], salt[:, 0, :])
     lows = (temp[:, ROWS - 1, :], salt[:, ROWS - 1, :])
@@ -266,12 +291,12 @@
         keep[20 + t * LEVELS : 20 + (t + 1) * LEVELS, :] = fix
         for out in (row_e, row_o):
             out[20 + t * LEVELS : 20 + (t + 1) * LEVELS, :] = lows[t]
-    keep[40:41, 0:128] = west[0:1]
-    keep[41:42, 0:128] = east[0:1]
+    keep[40:41, 0:128] = west[0:1, :]
+    keep[41:42, 0:128] = east[0:1, :]
     for out in (row_e, row_o):
         out[40:41, :] = deep[ROWS - 1 : ROWS]
-        out[41:42, 0:128] = west[ROWS - 1 : ROWS]
-        out[42:43, 0:128] = east[ROWS - 1 : ROWS]
+        out[41:42, 0:128] = west[ROWS - 1 : ROWS, :]
+        out[42:43, 0:128] = east[ROWS - 1 : ROWS, :]
 
 
 def inbound_list(blocks, names, panel, fold, mask, out):
@@ -300,7 +325,7 @@
 
 def second_kernel(
     old, core, zpair, xe, xo, planes, depths, keep, depth, table_hbm, panels,
-    final, surface_blocks, to_gx, to_gy, to_dg, table, sem,
+    final, surface_blocks, to_gx, table, sem,
 ):
     copy = pltpu.make_async_copy(table_hbm, table, sem)
     copy.start()
@@ -370,19 +395,26 @@
     surface_blocks[...] = blocks
     mask, fold = group_mask(), inbound_fold()
     copy.wait()
-    for n, out in ((3, to_dg), (2, to_gy), (1, to_gx)):
-        inbound_list(blocks, table[n // 2, n % 2], panels.at[n], fold, mask, out)
-
-
-def outer_kernel(final, blocks, table, panels, new_temp, new_salt, own, sems):
-    copies = fetch(sems, [(final.at[0], new_temp), (final.at[1], new_salt)])
-    inbound_list(blocks[...], table[0, 0], panels.at[0], inbound_fold(), group_mask(), own)
-    for copy in copies:
+    for a in range(2):
+        out = to_gx.at[a * 64 : (a + 1) * 64]
+        inbound_list(blocks, table[a, 1], panels.at[2 * a + 1], fold, mask, out)
+
+
+def outer_kernel(
+    final, blocks, table_hbm, panels, new_temp, new_salt, own, south, table, sems
+):
+    pairs = [(table_hbm, table), (final.at[0], new_temp), (final.at[1], new_salt)]
+    copies = fetch(sems, pairs)
+    copies[0].wait()
+    fold, mask = inbound_fold(), group_mask()
+    for a, out in ((1, south), (0, own)):
+        inbound_list(blocks[...], table[a, 0], panels.at[2 * a], fold, mask, out)
+    for copy in copies[1:]:
         copy.wait()
 
 
-def final_kernel(dg, gy, gx, own, out):
-    total = own[...] + gx[...] + gy[...] + dg[...]
+def final_kernel(gy, gx, own, out):
+    total = own[...] + gx[0:64, :] + gy[...]
     group = iota((8, 128), 1) // 16
     for c in range(4):
         field = jnp.zeros((8, 128), F32)
@@ -393,6 +425,10 @@
 
 
 def call(kernel, shapes, args, scratch=(), hbm_in=(), hbm_out=(), mib=12):
+    args = [
+        pltpu.with_memory_space_constraint(x, pltpu.HBM) if n in hbm_in else x
+        for n, x in enumerate(args)
+    ]
     shapes = [s if isinstance(s, jax.ShapeDtypeStruct) else jax.ShapeDtypeStruct(s, F32) for s in shapes]
     return pl.pallas_call(
         kernel,
@@ -428,56 +464,61 @@
     in_panels = in_panels.reshape(4, 1024, 128)
     out_tables, in_tables = out_tables[0, 0], in_tables[0, 0]
     field = (2, LEVELS, ROWS, COLS)
-    to_gx, to_gy, to_dg = call(
+    (to_gx,) = call(
         outbound_kernel,
-        [(LIST_ROWS + ROWS, 128), (LIST_ROWS + TILES * EDGE_ROWS, 128), (LIST_ROWS, 128)],
+        [(2 * LIST_ROWS + ROWS, 128)],
         [air, out_tables, out_panels, temp, salt, depth],
         [
             pltpu.VMEM(air.shape, BF16), pltpu.VMEM(out_tables.shape, jnp.int32),
-            pltpu.VMEM((3, 1024, 128), BF16), pltpu.VMEM(temp.shape, F32),
+            pltpu.VMEM((2, 1024, 128), BF16), pltpu.VMEM(temp.shape, F32),
             pltpu.VMEM(temp.shape, F32), pltpu.VMEM(depth.shape, jnp.int32),
-            pltpu.SemaphoreType.DMA((8,)),
+            pltpu.SemaphoreType.DMA((7,)),
         ],
         hbm_in=range(6),
     )
-    dg = send(to_dg, lambda i, j: (i - 1, j - 1))
-    gy = send(to_gy, lambda i, j: (i, j - 1))
     zpair = send(to_gx, lambda i, j: (other_pair(i), j))
     core = send(to_gx, lambda i, j: (pair(i), j))
-    own, partial = call(
+    own, north, partial = call(
         inner_kernel,
-        [(LIST_ROWS, 128), field],
+        [(LIST_ROWS, 128), (LIST_ROWS + TILES * EDGE_ROWS, 128), field],
         [air, out_tables, out_panels, temp, salt, depth],
-        [pltpu.VMEM((1024, 128), BF16), pltpu.SemaphoreType.DMA],
+        [pltpu.VMEM((2, 1024, 128), BF16), pltpu.SemaphoreType.DMA((2,))],
         hbm_in=(2,),
+    )
+    (to_gy,) = call(north_kernel, [north.shape], [north, core, zpair])
+    gy = send(to_gy, lambda i, j: (i, j - 1))
+    base, west, east, depths, partial = call(
+        edge_kernel,
+        [(LIST_ROWS, 128), (ROWS, 128), (ROWS, 128), (4, ROWS, COLS), field],
+        [own, core, zpair, partial, temp, salt, depth],
     )
     stepped, cols, row_e, row_o, planes, depths, keep = call(
         first_kernel,
         [field, (ROWS, 128), (48, COLS), (48, COLS), (4, ROWS, COLS), (4, ROWS, COLS), (48, COLS)],
-        [own, core, zpair, gy, dg, partial, temp, salt, depth],
+        [gy, base, west, east, depths, partial, temp, salt, depth],
     )
     xo = send(row_o, lambda i, j: (i, other_pair(j)))
     xe = send(row_e, lambda i, j: (i, pair(j)))
     zpair = send(cols, lambda i, j: (other_pair(i), j))
     core = send(cols, lambda i, j: (pair(i), j))
-    final, blocks, to_gx, to_gy, to_dg = call(
+    final, blocks, to_gx = call(
         second_kernel,
-        [field, jax.ShapeDtypeStruct((64, COLS), BF16)] + [(64, 128)] * 3,
+        [field, jax.ShapeDtypeStruct((64, COLS), BF16), (128, 128)],
         [stepped, core, zpair, xe, xo, planes, depths, keep, depth, in_tables, in_panels],
         [pltpu.VMEM(in_tables.shape, jnp.int32), pltpu.SemaphoreType.DMA],
         hbm_in=(9,),
     )
-    dg = send(to_dg, lambda i, j: (i + 1, j + 1))
-    gy = send(to_gy, lambda i, j: (i, j + 1))
     gx = send(to_gx, lambda i, j: (i + 1, j))
-    new_temp, new_salt, own = call(
+    new_temp, new_salt, own, south = call(
         outer_kernel,
-        [temp.shape, salt.shape, (64, 128)],
+        [temp.shape, salt.shape, (64, 128), (64, 128)],
         [final, blocks, in_tables, in_panels],
-        [pltpu.SemaphoreType.DMA((2,))],
+        [pltpu.VMEM(in_tables.shape, jnp.int32), pltpu.SemaphoreType.DMA((3,))],
+        hbm_in=(2,),
         hbm_out=(0, 1),
     )
-    (surface,) = call(final_kernel, [(4, 8, 128)], [dg, gy, gx, own])
+    gy = send(south + gx[64:128], lambda i, j: (i, j + 1))
+    (surface,) = call(final_kernel, [(4, 8, 128)], [gy, gx, own])
     return new_temp, new_salt, surface
 
 

time: 49.7 us -> 47 us (0.946)
  the two profiles are of different devices: /device:TPU:10 before, /device:TPU:8 now
where the time goes in v3:
time: 47 us; the launch traced here: 46.4 us
  starting transfers between devices  21.5 us (46%)
  waiting for transfers between devices  13.9 us (30%)
  Pallas kernels  10.2 us (22%)
  between operations  0.8 us (2%)
    ppermute x9, starting transfers between devices, send(): return lax.ppermute(block, ('gx', 'gy'), route)  21.5 us
    ppermute x9, waiting for transfers between devices, send(): return lax.ppermute(block, ('gx', 'gy'), route)  13.9 us
    pallas_call x8, Pallas kernels, call(): pl.pallas_call(kernel, out_shape=shapes, in_specs=[HBM if n in hbm_in els...  10.2 us
  transfers between devices with their start and end apart: 9, of which 5 were waited for; matrix products, arithmetic and copies ran while one was open for 0% of the time, Pallas kernels for 9%

profile of v3, /device:TPU:8, one launch (start us, length us, event | category | flops | bytes accessed | tf_op | source)
XLA Modules:
  0.0 46.4 jit_solution(11207330864885412263)
XLA Ops:
  0.6 0.0 copy-start
  0.6 0.0 copy-start.1
  0.7 0.0 copy-start.3
  0.7 0.0 copy-start.4
  0.7 0.0 copy-start.5
  0.7 2.4 %shard_map.104 = f32[528,128]{1,0:T(8,128)S(1)} custom-call(bf16[8,8,128]{2,1,0:T(8,128)(2,1)} %air_hbm.1, s32[2,2,2,64]{3,2,1,0:T(2,128)} %bitcast.6, bf16[4,1024,128]{2,1,0:T(8,128)(2,1)} %bitcast.8, f32[10,16,512]{2,1,0:T(8,128)} %temp.5, f32[10,16,512]{2,1,0:T(8,128)} %salt.5, s32[16,512]{1,0:T(8,128)} %depth.7), custom_call_target="tpu_custom_call" | custom-call | tf_op jit(solution)/shard_map/pallas_call | solution.py:433
  3.1 3.6 %collective-permute-start.1 = (f32[528,128]{1,0:T(8,128)S(1)}, f32[528,128]{1,0:T(8,128)S(1)}, u32[]{:S(2)}, u32[]{:S(2)}) collective-permute-start(f32[528,128]{1,0:T(8,128)S(1)} %shard_map.104), channel_id=1, source_target_pairs={{0,112},{1,113},{2,114},{3,115},{4,116},{5,117},{6,118},{7,119},{8... | collective-permute-start | bytes 811016 | tf_op jit(solution)/shard_map/ppermute | solution.py:451
  6.6 0.0 collective-permute-start
  6.6 0.0 copy-done
  6.7 0.0 copy-done.1
  6.7 0.0 copy-done.3
  6.7 0.0 copy-done.4
  6.7 0.0 copy-done.5
  6.7 2.1 %shard_map.103 = (f32[256,128]{1,0:T(8,128)S(1)}, f32[352,128]{1,0:T(8,128)S(1)}, f32[2,10,16,512]{3,2,1,0:T(8,128)S(1)}) custom-call(bf16[8,8,128]{2,1,0:T(8,128)(2,1)S(1)} %copy-done.4, s32[2,2,2,64]{3,2,1,0:T(2,128)S(1)} %bitcast.7, bf16[4,1024,128]{2,1,0:T(8,128)(2,1)} %bitcast.9, f32[10,16,512]{2,1,0:T(8,128)S(1)} %copy-done, ...), custom_call_target="tpu_custom_call" | custom-call | tf_op jit(solution)/shard_map/pallas_call | solution.py:433
  8.8 2.0 %collective-permute-done.1.zpair = f32[528,128]{1,0:T(8,128)S(1)} collective-permute-done((f32[528,128]{1,0:T(8,128)S(1)}, f32[528,128]{1,0:T(8,128)S(1)}, u32[]{:S(2)}, u32[]{:S(2)}) %collective-permute-start.1) | collective-permute-done | bytes 270368 | tf_op jit(solution)/shard_map/ppermute | solution.py:451
  10.8 0.0 collective-permute-done.core
  10.8 4.6 %collective-permute-start.2 = (f32[352,128]{1,0:T(8,128)S(1)}, f32[352,128]{1,0:T(8,128)S(1)}, u32[]{:S(2)}, u32[]{:S(2)}) collective-permute-start(f32[352,128]{1,0:T(8,128)S(1)} %shard_map.105), channel_id=1, source_target_pairs={{1,0},{2,1},{3,2},{4,3},{5,4},{6,5},{7,6},{8,7},{9,8},{10,9},{11,1... | collective-permute-start | bytes 540680 | tf_op jit(solution)/shard_map/ppermute | solution.py:451
  15.4 0.2 shard_map.106
  15.6 0.0 copy-start.2
  15.7 2.7 %collective-permute-done.2.gy = f32[352,128]{1,0:T(8,128)S(1)} collective-permute-done((f32[352,128]{1,0:T(8,128)S(1)}, f32[352,128]{1,0:T(8,128)S(1)}, u32[]{:S(2)}, u32[]{:S(2)}) %collective-permute-start.2) | collective-permute-done | bytes 180256 | tf_op jit(solution)/shard_map/ppermute | solution.py:451
  18.4 0.5 shard_map.107
  18.8 1.4 %collective-permute-start.5 = (f32[48,512]{1,0:T(8,128)S(1)}, f32[48,512]{1,0:T(8,128)S(1)}, u32[]{:S(2)}, u32[]{:S(2)}) collective-permute-start(f32[48,512]{1,0:T(8,128)S(1)} %get-tuple-element.35), channel_id=1, source_target_pairs={{0,1},{1,0},{2,3},{3,2},{4,5},{5,4},{6,7},{7,6},{8,9},{9,8},{10,11... | collective-permute-start | bytes 294920 | tf_op jit(solution)/shard_map/ppermute | solution.py:451
  20.2 5.2 %collective-permute-start.6 = (f32[48,512]{1,0:T(8,128)S(1)}, f32[48,512]{1,0:T(8,128)S(1)}, u32[]{:S(2)}, u32[]{:S(2)}) collective-permute-start(f32[48,512]{1,0:T(8,128)S(1)} %get-tuple-element.36), channel_id=1, source_target_pairs={{1,2},{2,1},{3,4},{4,3},{5,6},{6,5},{7,8},{8,7},{9,10},{10,9},{11,... | collective-permute-start | bytes 294920 | tf_op jit(solution)/shard_map/ppermute | solution.py:451
  25.4 3.7 %collective-permute-start.4 = (f32[16,128]{1,0:T(8,128)S(1)}, f32[16,128]{1,0:T(8,128)S(1)}, u32[]{:S(2)}, u32[]{:S(2)}) collective-permute-start(f32[16,128]{1,0:T(8,128)S(1)} %get-tuple-element.34), channel_id=1, source_target_pairs={{0,112},{1,113},{2,114},{3,115},{4,116},{5,117},{6,118},{7,119},{8... | collective-permute-start | bytes 24584 | tf_op jit(solution)/shard_map/ppermute | solution.py:451
  29.1 0.0 collective-permute-start.3
  29.1 1.4 %collective-permute-done.4.zpair = f32[16,128]{1,0:T(8,128)S(1)} collective-permute-done((f32[16,128]{1,0:T(8,128)S(1)}, f32[16,128]{1,0:T(8,128)S(1)}, u32[]{:S(2)}, u32[]{:S(2)}) %collective-permute-start.4) | collective-permute-done | bytes 8224 | tf_op jit(solution)/shard_map/ppermute | solution.py:451
  30.5 0.0 collective-permute-done.3.core
  30.5 0.0 collective-permute-done.5.xe
  30.5 0.0 collective-permute-done.6.xo
  30.5 0.0 copy-done.2
  30.5 2.4 %shard_map.108 = (f32[2,10,16,512]{3,2,1,0:T(8,128)S(1)}, bf16[64,512]{1,0:T(8,128)(2,1)S(1)}, f32[128,128]{1,0:T(8,128)S(1)}) custom-call(f32[2,10,16,512]{3,2,1,0:T(8,128)S(1)} %get-tuple-element.33.old, f32[16,128]{1,0:T(8,128)S(1)} %collective-permute-done.3.core, f32[16,128]{1,0:T(8,128)S(1)} %collective-permute-done.4.zpair, ...), custom_call_target="tpu_custom_call" | custom-call | tf_op jit(solution)/shard_map/pallas_call | solution.py:433
  32.9 0.0 collective-permute-start.7
  32.9 1.9 %shard_map.109 = (f32[10,16,512]{2,1,0:T(8,128)}, f32[10,16,512]{2,1,0:T(8,128)}, f32[64,128]{1,0:T(8,128)S(1)}, f32[64,128]{1,0:T(8,128)S(1)}) custom-call(f32[2,10,16,512]{3,2,1,0:T(8,128)S(1)} %get-tuple-element.40.final, bf16[64,512]{1,0:T(8,128)(2,1)S(1)} %get-tuple-element.41.blocks, s32[2,2,2,64]{3,2,1,0:T(2,128)} %bitcast.11, ...), custom_call_target="tpu_custom_call" | custom-call | tf_op jit(solution)/shard_map/pallas_call | solution.py:433
  34.9 3.0 %collective-permute-done.7.gx = f32[128,128]{1,0:T(8,128)S(1)} collective-permute-done((f32[128,128]{1,0:T(8,128)S(1)}, f32[128,128]{1,0:T(8,128)S(1)}, u32[]{:S(2)}, u32[]{:S(2)}) %collective-permute-start.7) | collective-permute-done | bytes 65568 | tf_op jit(solution)/shard_map/ppermute | solution.py:451
  37.8 3.1 %collective-permute-start.8 = (f32[64,128]{1,0:T(8,128)S(1)}, f32[64,128]{1,0:T(8,128)S(1)}, u32[]{:S(2)}, u32[]{:S(2)}) collective-permute-start(f32[64,128]{1,0:T(8,128)S(1)} %slice_add_fusion), channel_id=1, source_target_pairs={{0,1},{1,2},{2,3},{3,4},{4,5},{5,6},{6,7},{7,8},{8,9},{9,10},{10,1... | collective-permute-start | bytes 98312 | tf_op jit(solution)/shard_map/ppermute | solution.py:451
  41.0 4.8 %collective-permute-done.8.gy = f32[64,128]{1,0:T(8,128)S(1)} collective-permute-done((f32[64,128]{1,0:T(8,128)S(1)}, f32[64,128]{1,0:T(8,128)S(1)}, u32[]{:S(2)}, u32[]{:S(2)}) %collective-permute-start.8) | collective-permute-done | bytes 32800 | tf_op jit(solution)/shard_map/ppermute | solution.py:451
  45.7 0.7 %shard_map.110 = f32[4,8,128]{2,1,0:T(8,128)} custom-call(f32[64,128]{1,0:T(8,128)S(1)} %collective-permute-done.8.gy, f32[128,128]{1,0:T(8,128)S(1)} %collective-permute-done.7.gx, f32[64,128]{1,0:T(8,128)S(1)} %get-tuple-element.46.own), custom_call_target="tpu_custom_call" | custom-call | tf_op jit(solution)/shard_map/pallas_call | solution.py:433
  (2 shorter events, 0.0 us)
Async XLA Ops:
  0.6 6.0 %copy-start = (f32[10,16,512]{2,1,0:T(8,128)S(1)}, f32[10,16,512]{2,1,0:T(8,128)}, u32[]{:S(2)}) copy-start(f32[10,16,512]{2,1,0:T(8,128)} %temp.5) | copy-start | bytes 983044
  0.6 6.0 %copy-start.1 = (f32[10,16,512]{2,1,0:T(8,128)S(1)}, f32[10,16,512]{2,1,0:T(8,128)}, u32[]{:S(2)}) copy-start(f32[10,16,512]{2,1,0:T(8,128)} %salt.5) | copy-start | bytes 983044
  0.7 6.0 %copy-start.3 = (s32[16,512]{1,0:T(8,128)S(1)}, s32[16,512]{1,0:T(8,128)}, u32[]{:S(2)}) copy-start(s32[16,512]{1,0:T(8,128)} %depth.7) | copy-start | bytes 98308
  0.7 6.0 %copy-start.4 = (bf16[8,8,128]{2,1,0:T(8,128)(2,1)S(1)}, bf16[8,8,128]{2,1,0:T(8,128)(2,1)}, u32[]{:S(2)}) copy-start(bf16[8,8,128]{2,1,0:T(8,128)(2,1)} %air_hbm.1) | copy-start | bytes 49156
  0.7 6.0 %copy-start.5 = (s32[1,1,2,2,2,64]{5,4,3,2,1,0:T(2,128)S(1)}, s32[1,1,2,2,2,64]{5,4,3,2,1,0:T(2,128)}, u32[]{:S(2)}) copy-start(s32[1,1,2,2,2,64]{5,4,3,2,1,0:T(2,128)} %param.9) | copy-start | bytes 6148
  3.1 7.7 %collective-permute-start.1 = (f32[528,128]{1,0:T(8,128)S(1)}, f32[528,128]{1,0:T(8,128)S(1)}, u32[]{:S(2)}, u32[]{:S(2)}) collective-permute-start(f32[528,128]{1,0:T(8,128)S(1)} %shard_map.104), channel_id=1, source_target_pairs={{0,112},{1,113},{2,114},{3,115},{4,116},{5,117},{6,118},{7,119},{8... | collective-permute-start | bytes 811016 | tf_op jit(solution)/shard_map/ppermute | solution.py:451
  6.6 4.1 %collective-permute-start = (f32[528,128]{1,0:T(8,128)S(1)}, f32[528,128]{1,0:T(8,128)S(1)}, u32[]{:S(2)}, u32[]{:S(2)}) collective-permute-start(f32[528,128]{1,0:T(8,128)S(1)} %shard_map.104), channel_id=1, source_target_pairs={{0,16},{1,17},{2,18},{3,19},{4,20},{5,21},{6,22},{7,23},{8,24},{9,... | collective-permute-start | bytes 811016 | tf_op jit(solution)/shard_map/ppermute | solution.py:451
  10.8 7.6 %collective-permute-start.2 = (f32[352,128]{1,0:T(8,128)S(1)}, f32[352,128]{1,0:T(8,128)S(1)}, u32[]{:S(2)}, u32[]{:S(2)}) collective-permute-start(f32[352,128]{1,0:T(8,128)S(1)} %shard_map.105), channel_id=1, source_target_pairs={{1,0},{2,1},{3,2},{4,3},{5,4},{6,5},{7,6},{8,7},{9,8},{10,9},{11,1... | collective-permute-start | bytes 540680 | tf_op jit(solution)/shard_map/ppermute | solution.py:451
  15.6 14.9 %copy-start.2 = (bf16[1,1,2,2,64,16,128]{6,5,4,3,2,1,0:T(8,128)(2,1)S(1)}, bf16[1,1,2,2,64,16,128]{6,5,4,3,2,1,0:T(8,128)(2,1)}, u32[]{:S(2)}) copy-start(bf16[1,1,2,2,64,16,128]{6,5,4,3,2,1,0:T(8,128)(2,1)} %param.15) | copy-start | bytes 3145732
  18.8 11.6 %collective-permute-start.5 = (f32[48,512]{1,0:T(8,128)S(1)}, f32[48,512]{1,0:T(8,128)S(1)}, u32[]{:S(2)}, u32[]{:S(2)}) collective-permute-start(f32[48,512]{1,0:T(8,128)S(1)} %get-tuple-element.35), channel_id=1, source_target_pairs={{0,1},{1,0},{2,3},{3,2},{4,5},{5,4},{6,7},{7,6},{8,9},{9,8},{10,11... | collective-permute-start | bytes 294920 | tf_op jit(solution)/shard_map/ppermute | solution.py:451
  20.2 10.2 %collective-permute-start.6 = (f32[48,512]{1,0:T(8,128)S(1)}, f32[48,512]{1,0:T(8,128)S(1)}, u32[]{:S(2)}, u32[]{:S(2)}) collective-permute-start(f32[48,512]{1,0:T(8,128)S(1)} %get-tuple-element.36), channel_id=1, source_target_pairs={{1,2},{2,1},{3,4},{4,3},{5,6},{6,5},{7,8},{8,7},{9,10},{10,9},{11,... | collective-permute-start | bytes 294920 | tf_op jit(solution)/shard_map/ppermute | solution.py:451
  25.4 5.0 %collective-permute-start.4 = (f32[16,128]{1,0:T(8,128)S(1)}, f32[16,128]{1,0:T(8,128)S(1)}, u32[]{:S(2)}, u32[]{:S(2)}) collective-permute-start(f32[16,128]{1,0:T(8,128)S(1)} %get-tuple-element.34), channel_id=1, source_target_pairs={{0,112},{1,113},{2,114},{3,115},{4,116},{5,117},{6,118},{7,119},{8... | collective-permute-start | bytes 24584 | tf_op jit(solution)/shard_map/ppermute | solution.py:451
  29.1 1.4 %collective-permute-start.3 = (f32[16,128]{1,0:T(8,128)S(1)}, f32[16,128]{1,0:T(8,128)S(1)}, u32[]{:S(2)}, u32[]{:S(2)}) collective-permute-start(f32[16,128]{1,0:T(8,128)S(1)} %get-tuple-element.34), channel_id=1, source_target_pairs={{0,16},{1,17},{2,18},{3,19},{4,20},{5,21},{6,22},{7,23},{8,24},{9,... | collective-permute-start | bytes 24584 | tf_op jit(solution)/shard_map/ppermute | solution.py:451
  32.9 4.9 %collective-permute-start.7 = (f32[128,128]{1,0:T(8,128)S(1)}, f32[128,128]{1,0:T(8,128)S(1)}, u32[]{:S(2)}, u32[]{:S(2)}) collective-permute-start(f32[128,128]{1,0:T(8,128)S(1)} %get-tuple-element.45), channel_id=1, source_target_pairs={{0,16},{1,17},{2,18},{3,19},{4,20},{5,21},{6,22},{7,23},{8,24},{9,... | collective-permute-start | bytes 196616 | tf_op jit(solution)/shard_map/ppermute | solution.py:451
  37.8 7.9 %collective-permute-start.8 = (f32[64,128]{1,0:T(8,128)S(1)}, f32[64,128]{1,0:T(8,128)S(1)}, u32[]{:S(2)}, u32[]{:S(2)}) collective-permute-start(f32[64,128]{1,0:T(8,128)S(1)} %slice_add_fusion), channel_id=1, source_target_pairs={{0,1},{1,2},{2,3},{3,4},{4,5},{5,6},{6,7},{7,8},{8,9},{9,10},{10,1... | collective-permute-start | bytes 98312 | tf_op jit(solution)/shard_map/ppermute | solution.py:451

commit v4 on v3

--- a/solution.py
+++ b/solution.py
@@ -17,7 +17,6 @@
 TILES = COLS // 128
 F32, BF16 = jnp.float32, jnp.bfloat16
 LIST_ROWS = 4 * 64
-EDGE_ROWS = 24
 VMEM = pl.BlockSpec(memory_space=pltpu.VMEM)
 HBM = pl.BlockSpec(memory_space=pltpu.HBM)
 NN = (((1,), (0,)), ((), ()))
@@ -113,26 +112,29 @@
 
 
 def outbound_kernel(
-    air_hbm, table_hbm, panels_hbm, temp_hbm, salt_hbm, depth_hbm, to_gx,
-    air, table, panels, temp, salt, depth, sems,
+    air_hbm, table_hbm, panels_hbm, temp_hbm, salt_hbm, depth_hbm,
+    to_gx, tiled, table, panels, temp, salt, depth, air, panel, sems,
 ):
-    pairs = [(air_hbm, air), (table_hbm, table)]
-    pairs += [(panels_hbm.at[2 * n], panels.at[n]) for n in range(2)]
+    pairs = [(air_hbm, air), (table_hbm, table), (panels_hbm.at[0], panel)]
     pairs += [(temp_hbm, temp), (salt_hbm, salt), (depth_hbm, depth)]
-    copies = fetch(sems, pairs)
+    copies = fetch(sems, pairs + [(panels_hbm.at[1:4], panels)])
     mask = group_mask()
     copies[0].wait()
-    tiled = spread_air(air, mask)
+    tiled[...] = spread_air(air, mask)
     copies[1].wait()
-    for n in range(2):
-        copies[2 + n].wait()
-        out = to_gx.at[n * LIST_ROWS : (n + 1) * LIST_ROWS]
-        outbound_list(tiled, table[n, 0], panels.at[n], mask, out)
-    for copy in copies[4:]:
+    copies[2].wait()
+    outbound_list(tiled[...], table[0, 0], panel, mask, to_gx)
+    for copy in copies[3:]:
         copy.wait()
+
+
+def side_kernel(tiled, table, panels, temp, salt, depth, to_gx, north):
+    mask = group_mask()
     deep = depth[...].astype(F32)
     levels = [temp[l] for l in range(LEVELS)] + [salt[l] for l in range(LEVELS)] + [deep]
-    to_gx[2 * LIST_ROWS :, :] = edge_columns(levels)
+    to_gx[LIST_ROWS:, :] = edge_columns(levels)
+    outbound_list(tiled[...], table[1, 0], panels.at[1], mask, to_gx.at[0:LIST_ROWS])
+    outbound_list(tiled[...], table[0, 1], panels.at[0], mask, north)
 
 
 def beside(values, north, south, west, east):
@@ -152,10 +154,7 @@
     return SIDE_RATE * side
 
 
-def inner_kernel(
-    air, table, panels_hbm, temp, salt, depth, own, north, partial, panels, sems
-):
-    copies = fetch(sems, [(panels_hbm.at[2 * n + 1], panels.at[n]) for n in range(2)])
+def inner_kernel(tiled, table, panels, temp, salt, depth, own, partial):
     deep = depth[...].astype(F32)
     dry = jnp.zeros((1, 1), F32)
     around = beside(deep, dry, dry, dry, dry)
@@ -166,32 +165,21 @@
             centre = field[l]
             side = side_sum(centre, beside(centre, dry, dry, dry, dry), wets)
             partial[t, l] = centre + jnp.where(wet, side, 0.0)
-    for base, edge in ((0, temp[:, 0, :]), (LEVELS, salt[:, 0, :]), (2 * LEVELS, deep[0:1])):
-        for s in range(TILES):
-            at = LIST_ROWS + s * EDGE_ROWS + base
-            north[at : at + edge.shape[0], :] = edge[:, s * 128 : (s + 1) * 128]
-    mask = group_mask()
-    tiled = spread_air(air, mask)
-    for n, out in ((0, north), (1, own)):
-        copies[n].wait()
-        outbound_list(tiled, table[n, 1], panels.at[n], mask, out)
+    outbound_list(tiled[...], table[1, 1], panels.at[2], group_mask(), own)
 
 
 def north_kernel(part, core, zpair, out):
     odd_col = lax.axis_index("gx") % 2 == 1
-    out[0:LIST_ROWS, :] = part[0:LIST_ROWS, :] + jnp.where(
-        odd_col, zpair[0:LIST_ROWS, :], core[0:LIST_ROWS, :]
-    )
-    out[LIST_ROWS:, :] = part[LIST_ROWS:, :]
+    out[...] = part[...] + jnp.where(odd_col, zpair[...], core[...])
 
 
 def edge_kernel(own, core, zpair, partial, temp, salt, depth, base, west, east, depths, whole):
     odd_col = lax.axis_index("gx") % 2 == 1
     base[...] = own[...] + jnp.where(
-        odd_col, zpair[LIST_ROWS : 2 * LIST_ROWS, :], core[LIST_ROWS : 2 * LIST_ROWS, :]
-    )
-    left = jnp.where(odd_col, core[2 * LIST_ROWS :, :], zpair[2 * LIST_ROWS :, :])
-    right = jnp.where(odd_col, zpair[2 * LIST_ROWS :, :], core[2 * LIST_ROWS :, :])
+        odd_col, zpair[0:LIST_ROWS, :], core[0:LIST_ROWS, :]
+    )
+    left = jnp.where(odd_col, core[LIST_ROWS:, :], zpair[LIST_ROWS:, :])
+    right = jnp.where(odd_col, zpair[LIST_ROWS:, :], core[LIST_ROWS:, :])
     west[...] = left
     east[...] = right
     deep = depth[...].astype(F32)
@@ -230,8 +218,7 @@
 
 
 def first_kernel(
-    gy, base, west, east, side_depths, partial, temp, salt, depth,
-    new, cols, row_e, row_o, planes, depths, keep,
+    gy, base, west, east, partial, temp, salt, depth, new, cols, row_e, row_o, planes, keep
 ):
     odd_row = lax.axis_index("gy") % 2 == 1
     forcing = []
@@ -245,18 +232,8 @@
     forcing[3] = squared / (1.0 + squared)
     for p in range(4):
         planes[p] = forcing[p]
-    souths = [gy[LIST_ROWS + s * EDGE_ROWS : LIST_ROWS + (s + 1) * EDGE_ROWS, :] for s in range(TILES)]
-    souths = jnp.concatenate(souths, 1)
     deep = depth[...].astype(F32)
-    last = 2 * LEVELS
-    south = jnp.where(
-        iota((ROWS, COLS), 0) == ROWS - 1, souths[last : last + 1], side_depths[1]
-    )
-    for n in (0, 2, 3):
-        depths[n] = side_depths[n]
-    depths[1] = south
     lane = iota((ROWS, 128), 1)
-    row = iota((8, COLS), 0)
     mixing = MIX_BASE + MIX_WIND * forcing[3]
     block = jnp.zeros((ROWS, 128), F32)
     for t, field in enumerate((temp, salt)):
@@ -268,35 +245,25 @@
                 centre, field[min(l + 1, LEVELS - 1)], mixing, deep, l, across
             )
             change = change + source(t, l, forcing, centre)
-            low = centre[8:16]
-            here = (row == 7) & (south[8:16] > l)
-            low = jnp.where(here, SIDE_RATE * (souths[at : at + 1] - low), 0.0)
-            change = jnp.concatenate([change[0:8], change[8:16] + low], 0)
             value = partial[t, l] + jnp.where(deep > l, change, 0.0)
             new[t, l] = value
             block = jnp.where(lane == at, value[:, 0:1], block)
             block = jnp.where(lane == 64 + at, value[:, COLS - 1 : COLS], block)
     cols[...] = block
-    olds = (temp[:, 0, :], salt[:, 0, :])
-    lows = (temp[:, ROWS - 1, :], salt[:, ROWS - 1, :])
-    for t in range(2):
-        span = slice(t * LEVELS, (t + 1) * LEVELS)
-        first, final = new[t, :, 0, :], new[t, :, ROWS - 1, :]
-        row_e[span, :] = jnp.where(odd_row, first, final)
-        row_o[span, :] = jnp.where(odd_row, final, first)
-        level = iota((LEVELS, COLS), 0)
-        here = (souths[last : last + 1] > level) & (deep[ROWS - 1 : ROWS] > level)
-        fix = jnp.where(here, SIDE_RATE * (lows[t] - souths[span]), 0.0)
-        keep[span, :] = olds[t]
-        keep[20 + t * LEVELS : 20 + (t + 1) * LEVELS, :] = fix
-        for out in (row_e, row_o):
-            out[20 + t * LEVELS : 20 + (t + 1) * LEVELS, :] = lows[t]
-    keep[40:41, 0:128] = west[0:1, :]
-    keep[41:42, 0:128] = east[0:1, :]
-    for out in (row_e, row_o):
-        out[40:41, :] = deep[ROWS - 1 : ROWS]
-        out[41:42, 0:128] = west[ROWS - 1 : ROWS, :]
-        out[42:43, 0:128] = east[ROWS - 1 : ROWS, :]
+    edges = []
+    for r in (0, ROWS - 1):
+        rows = [new[0, :, r, :], new[1, :, r, :], temp[:, r, :], salt[:, r, :], deep[r : r + 1]]
+        edges.append(rows + [west[r : r + 1, :], east[r : r + 1, :]])
+    for out, first in ((row_e, odd_row), (row_o, jnp.logical_not(odd_row))):
+        at = 0
+        for a, b in zip(*edges):
+            out[at : at + a.shape[0], 0 : a.shape[1]] = jnp.where(first, a, b)
+            at += a.shape[0]
+    for n in range(2):
+        keep[20 * n : 20 * n + 10, :] = edges[n][2]
+        keep[20 * n + 10 : 20 * n + 20, :] = edges[n][3]
+        keep[40 + 2 * n : 41 + 2 * n, 0:128] = edges[n][5]
+        keep[41 + 2 * n : 42 + 2 * n, 0:128] = edges[n][6]
 
 
 def inbound_list(blocks, names, panel, fold, mask, out):
@@ -332,34 +299,45 @@
     odd_col = lax.axis_index("gx") % 2 == 1
     odd_row = lax.axis_index("gy") % 2 == 1
     deep = depth[...].astype(F32)
-    souths = jnp.where(odd_row, xo[...], xe[...])
-    norths = jnp.where(odd_row, xe[...], xo[...])
+    beyond = (jnp.where(odd_row, xe[...], xo[...]), jnp.where(odd_row, xo[...], xe[...]))
     level = iota((2 * LEVELS, COLS), 0) % LEVELS
-    here = (deep[0:1] > level) & (norths[40:41] > level)
-    fix = jnp.where(here, SIDE_RATE * (norths[20:40] - keep[0:20, :]), 0.0)
-    souths = souths[0:20] + keep[20:40, :]
-    lane = iota((1, 128), 1)
+    fixes, halo_rows = [], []
+    for n, other in enumerate(beyond):
+        r = n * (ROWS - 1)
+        here = (deep[r : r + 1] > level) & (other[40:41] > level)
+        fix = jnp.where(here, SIDE_RATE * (other[20:40] - keep[20 * n : 20 * n + 20, :]), 0.0)
+        fixes.append(fix)
+        halo_rows.append(other[0:20] - fix)
+    norths, souths = halo_rows
+    level = iota((1, 128), 1) % 64 % LEVELS
+    row = iota((ROWS, 128), 0)
     ends = []
     for halo, at, deepest in (
         (jnp.where(odd_col, core[...], zpair[...]), 0, 84),
         (jnp.where(odd_col, zpair[...], core[...]), 1, 20),
     ):
-        mine, over = keep[40 + at : 41 + at, 0:128], norths[41 + at : 42 + at, 0:128]
-        level = lane % 64 % LEVELS
-        here = (mine[:, deepest : deepest + 1] > level) & (over[:, deepest : deepest + 1] > level)
-        end_fix = jnp.where(here, SIDE_RATE * (over - mine), 0.0)
-        ends.append(halo + jnp.where(iota((ROWS, 128), 0) == 0, end_fix, 0.0))
+        for n, other in enumerate(beyond):
+            mine = keep[40 + 2 * n + at : 41 + 2 * n + at, 0:128]
+            far = other[41 + at : 42 + at, 0:128]
+            here = mine[:, deepest : deepest + 1] > level
+            here = here & (far[:, deepest : deepest + 1] > level)
+            fix = jnp.where(here, SIDE_RATE * (far - mine), 0.0)
+            halo = halo + jnp.where(row == n * (ROWS - 1), fix, 0.0)
+        ends.append(halo)
     west, east = ends
     row8, row = iota((8, COLS), 0), iota((ROWS, COLS), 0)
-    around = [jnp.where(row == 0, norths[40:41], depths[0])] + [depths[n] for n in (1, 2, 3)]
+    around = [depths[n] for n in range(4)]
+    around[0] = jnp.where(row == 0, beyond[0][40:41], around[0])
+    around[1] = jnp.where(row == ROWS - 1, beyond[1][40:41], around[1])
     forcing = [planes[p] for p in range(4)]
     mixing = MIX_BASE + MIX_WIND * forcing[3]
     top = {}
 
     def whole(t, l):
         at = t * LEVELS + l
-        high = old[t, l, 0:8, :] + jnp.where(row8 == 0, fix[at : at + 1], 0.0)
-        return jnp.concatenate([high, old[t, l, 8:16, :]], 0)
+        high = old[t, l, 0:8, :] + jnp.where(row8 == 0, fixes[0][at : at + 1], 0.0)
+        low = old[t, l, 8:16, :] + jnp.where(row8 == 7, fixes[1][at : at + 1], 0.0)
+        return jnp.concatenate([high, low], 0)
 
     for t in range(2):
         across, centre = None, whole(t, 0)
@@ -464,38 +442,50 @@
     in_panels = in_panels.reshape(4, 1024, 128)
     out_tables, in_tables = out_tables[0, 0], in_tables[0, 0]
     field = (2, LEVELS, ROWS, COLS)
-    (to_gx,) = call(
+    to_gx, tiled, out_tables, out_panels, temp, salt, depth = call(
         outbound_kernel,
-        [(2 * LIST_ROWS + ROWS, 128)],
+        [
+            (LIST_ROWS, 128),
+            jax.ShapeDtypeStruct((64, 1024), BF16),
+            jax.ShapeDtypeStruct(out_tables.shape, jnp.int32),
+            jax.ShapeDtypeStruct((3, 1024, 128), BF16),
+            temp.shape,
+            salt.shape,
+            jax.ShapeDtypeStruct(depth.shape, jnp.int32),
+        ],
         [air, out_tables, out_panels, temp, salt, depth],
         [
-            pltpu.VMEM(air.shape, BF16), pltpu.VMEM(out_tables.shape, jnp.int32),
-            pltpu.VMEM((2, 1024, 128), BF16), pltpu.VMEM(temp.shape, F32),
-            pltpu.VMEM(temp.shape, F32), pltpu.VMEM(depth.shape, jnp.int32),
+            pltpu.VMEM(air.shape, BF16),
+            pltpu.VMEM((1024, 128), BF16),
             pltpu.SemaphoreType.DMA((7,)),
         ],
         hbm_in=range(6),
     )
     zpair = send(to_gx, lambda i, j: (other_pair(i), j))
     core = send(to_gx, lambda i, j: (pair(i), j))
-    own, north, partial = call(
-        inner_kernel,
-        [(LIST_ROWS, 128), (LIST_ROWS + TILES * EDGE_ROWS, 128), field],
-        [air, out_tables, out_panels, temp, salt, depth],
-        [pltpu.VMEM((2, 1024, 128), BF16), pltpu.SemaphoreType.DMA((2,))],
-        hbm_in=(2,),
-    )
+    to_side, north = call(
+        side_kernel,
+        [(LIST_ROWS + ROWS, 128), (LIST_ROWS, 128)],
+        [tiled, out_tables, out_panels, temp, salt, depth],
+    )
+    side_z = send(to_side, lambda i, j: (other_pair(i), j))
+    side_core = send(to_side, lambda i, j: (pair(i), j))
     (to_gy,) = call(north_kernel, [north.shape], [north, core, zpair])
     gy = send(to_gy, lambda i, j: (i, j - 1))
+    own, partial = call(
+        inner_kernel,
+        [(LIST_ROWS, 128), field],
+        [tiled, out_tables, out_panels, temp, salt, depth],
+    )
     base, west, east, depths, partial = call(
         edge_kernel,
         [(LIST_ROWS, 128), (ROWS, 128), (ROWS, 128), (4, ROWS, COLS), field],
-        [own, core, zpair, partial, temp, salt, depth],
-    )
-    stepped, cols, row_e, row_o, planes, depths, keep = call(
+        [own, side_core, side_z, partial, temp, salt, depth],
+    )
+    stepped, cols, row_e, row_o, planes, keep = call(
         first_kernel,
-        [field, (ROWS, 128), (48, COLS), (48, COLS), (4, ROWS, COLS), (4, ROWS, COLS), (48, COLS)],
-        [gy, base, west, east, depths, partial, temp, salt, depth],
+        [field, (ROWS, 128), (43, COLS), (43, COLS), (4, ROWS, COLS), (44, COLS)],
+        [gy, base, west, east, partial, temp, salt, depth],
     )
     xo = send(row_o, lambda i, j: (i, other_pair(j)))
     xe = send(row_e, lambda i, j: (i, pair(j)))

time: 47 us -> 44 us (0.936)
  waiting for transfers between devices: 13.9 us -> 11.8 us
  Pallas kernels: 10.2 us -> 8.84 us
  starting transfers between devices: 21.5 us -> 22.1 us
    ppermute x9 -> x11, waiting for transfers between devices: 13.9 us -> 11.8 us  [send(): return lax.ppermute(block, ('gx', 'gy'), route)]
    pallas_call x8 -> x9, Pallas kernels: 10.2 us -> 8.84 us  [call(): pl.pallas_call(kernel, out_shape=shapes, in_specs=[HBM if n in hbm_in els...]
    ppermute x9 -> x11, starting transfers between devices: 21.5 us -> 22.1 us  [send(): return lax.ppermute(block, ('gx', 'gy'), route)]
  transfers between devices with their start and end apart: 9 -> 11, of which waited for: 5 -> 5; matrix products, arithmetic and copies ran while one was open for 0% -> 0% of each run, Pallas kernels for 9% -> 9%
where the time goes in v4:
time: 44 us; the launch traced here: 43.5 us
  starting transfers between devices  22.1 us (50%)
  waiting for transfers between devices  11.8 us (27%)
  Pallas kernels  8.84 us (20%)
  between operations  0.76 us (2%)
    ppermute x11, starting transfers between devices, send(): return lax.ppermute(block, ('gx', 'gy'), route)  22.1 us
    ppermute x11, waiting for transfers between devices, send(): return lax.ppermute(block, ('gx', 'gy'), route)  11.8 us
    pallas_call x9, Pallas kernels, call(): pl.pallas_call(kernel, out_shape=shapes, in_specs=[HBM if n in hbm_in els...  8.84 us
  transfers between devices with their start and end apart: 11, of which 5 were waited for; matrix products, arithmetic and copies ran while one was open for 0% of the time, Pallas kernels for 9%

profile of v4, /device:TPU:8, one launch (start us, length us, event | category | flops | bytes accessed | tf_op | source)
XLA Modules:
  0.0 43.5 jit_solution(17824837525871928040)
XLA Ops:
  0.6 1.6 %shard_map.103 = (f32[256,128]{1,0:T(8,128)S(1)}, bf16[64,1024]{1,0:T(8,128)(2,1)S(1)}, s32[2,2,2,64]{3,2,1,0:T(2,128)S(1)}, bf16[3,1024,128]{2,1,0:T(8,128)(2,1...) custom-call(bf16[8,8,128]{2,1,0:T(8,128)(2,1)} %air_hbm.1, ...), custom_call_target="tpu_custom_call" | custom-call | tf_op jit(solution)/shard_map/pallas_call | solution.py:411
  2.3 0.1 collective-permute-start
  2.4 4.1 %collective-permute-start.1 = (f32[256,128]{1,0:T(8,128)S(1)}, f32[256,128]{1,0:T(8,128)S(1)}, u32[]{:S(2)}, u32[]{:S(2)}) collective-permute-start(f32[256,128]{1,0:T(8,128)S(1)} %get-tuple-element.39), channel_id=1, source_target_pairs={{0,112},{1,113},{2,114},{3,115},{4,116},{5,117},{6,118},{7,119},{8... | collective-permute-start | bytes 393224 | tf_op jit(solution)/shard_map/ppermute | solution.py:429
  6.5 0.9 %shard_map.104 = (f32[272,128]{1,0:T(8,128)S(1)}, f32[256,128]{1,0:T(8,128)S(1)}) custom-call(bf16[64,1024]{1,0:T(8,128)(2,1)S(1)} %get-tuple-element.32.tiled, s32[2,2,2,64]{3,2,1,0:T(2,128)S(1)} %get-tuple-element.33.table, bf16[3,1024,128]{2,1,0:T(8,128)(2,1)S(1)} %get-tuple-element.34.panels, f32[10,16,512]{2,1,0:T(8,128)S(1)} %get-tuple-element.35.temp, ...), custom_call_target="tpu_custom_call" | custom-call | tf_op jit(solution)/shard_map/pallas_call | solution.py:411
  7.4 0.1 collective-permute-start.3
  7.5 0.5 %collective-permute-start.4 = (f32[272,128]{1,0:T(8,128)S(1)}, f32[272,128]{1,0:T(8,128)S(1)}, u32[]{:S(2)}, u32[]{:S(2)}) collective-permute-start(f32[272,128]{1,0:T(8,128)S(1)} %get-tuple-element.41), channel_id=1, source_target_pairs={{0,112},{1,113},{2,114},{3,115},{4,116},{5,117},{6,118},{7,119},{8... | collective-permute-start | bytes 417800 | tf_op jit(solution)/shard_map/ppermute | solution.py:429
  8.0 0.0 collective-permute-done.core
  8.0 1.1 %collective-permute-done.1.zpair = f32[256,128]{1,0:T(8,128)S(1)} collective-permute-done((f32[256,128]{1,0:T(8,128)S(1)}, f32[256,128]{1,0:T(8,128)S(1)}, u32[]{:S(2)}, u32[]{:S(2)}) %collective-permute-start.1) | collective-permute-done | bytes 131104 | tf_op jit(solution)/shard_map/ppermute | solution.py:429
  9.2 4.6 %collective-permute-start.2 = (f32[256,128]{1,0:T(8,128)S(1)}, f32[256,128]{1,0:T(8,128)S(1)}, u32[]{:S(2)}, u32[]{:S(2)}) collective-permute-start(f32[256,128]{1,0:T(8,128)S(1)} %shard_map.105), channel_id=1, source_target_pairs={{1,0},{2,1},{3,2},{4,3},{5,4},{6,5},{7,6},{8,7},{9,8},{10,9},{11,1... | collective-permute-start | bytes 393224 | tf_op jit(solution)/shard_map/ppermute | solution.py:429
  13.7 0.8 %shard_map.106 = (f32[256,128]{1,0:T(8,128)S(1)}, f32[2,10,16,512]{3,2,1,0:T(8,128)S(1)}) custom-call(bf16[64,1024]{1,0:T(8,128)(2,1)S(1)} %get-tuple-element.32.tiled, s32[2,2,2,64]{3,2,1,0:T(2,128)S(1)} %get-tuple-element.33.table, bf16[3,1024,128]{2,1,0:T(8,128)(2,1)S(1)} %get-tuple-element.34.panels, f32[10,16,512]{2,1,0:T(8,128)S(1)} %get-tuple-element.35.temp, ...), custom_call_target="tpu_custom_call" | custom-call | tf_op jit(solution)/shard_map/pallas_call | solution.py:411
  14.5 0.0 collective-permute-done.3.core
  14.5 0.0 collective-permute-done.4.zpair
  14.5 0.3 shard_map.107
  14.8 0.0 copy-start
  14.8 1.5 %collective-permute-done.2.gy = f32[256,128]{1,0:T(8,128)S(1)} collective-permute-done((f32[256,128]{1,0:T(8,128)S(1)}, f32[256,128]{1,0:T(8,128)S(1)}, u32[]{:S(2)}, u32[]{:S(2)}) %collective-permute-start.2) | collective-permute-done | bytes 131104 | tf_op jit(solution)/shard_map/ppermute | solution.py:429
  16.2 0.4 shard_map.108
  16.6 1.4 %collective-permute-start.7 = (f32[43,512]{1,0:T(8,128)S(1)}, f32[43,512]{1,0:T(8,128)S(1)}, u32[]{:S(2)}, u32[]{:S(2)}) collective-permute-start(f32[43,512]{1,0:T(8,128)S(1)} %get-tuple-element.49), channel_id=1, source_target_pairs={{0,1},{1,0},{2,3},{3,2},{4,5},{5,4},{6,7},{7,6},{8,9},{9,8},{10,11... | collective-permute-start | bytes 264200 | tf_op jit(solution)/shard_map/ppermute | solution.py:429
  18.0 5.2 %collective-permute-start.8 = (f32[43,512]{1,0:T(8,128)S(1)}, f32[43,512]{1,0:T(8,128)S(1)}, u32[]{:S(2)}, u32[]{:S(2)}) collective-permute-start(f32[43,512]{1,0:T(8,128)S(1)} %get-tuple-element.50), channel_id=1, source_target_pairs={{1,2},{2,1},{3,4},{4,3},{5,6},{6,5},{7,8},{8,7},{9,10},{10,9},{11,... | collective-permute-start | bytes 264200 | tf_op jit(solution)/shard_map/ppermute | solution.py:429
  23.2 0.1 collective-permute-start.5
  23.3 2.6 %collective-permute-start.6 = (f32[16,128]{1,0:T(8,128)S(1)}, f32[16,128]{1,0:T(8,128)S(1)}, u32[]{:S(2)}, u32[]{:S(2)}) collective-permute-start(f32[16,128]{1,0:T(8,128)S(1)} %get-tuple-element.48), channel_id=1, source_target_pairs={{0,112},{1,113},{2,114},{3,115},{4,116},{5,117},{6,118},{7,119},{8... | collective-permute-start | bytes 24584 | tf_op jit(solution)/shard_map/ppermute | solution.py:429
  25.9 0.0 collective-permute-done.5.core
  25.9 1.7 %collective-permute-done.6.zpair = f32[16,128]{1,0:T(8,128)S(1)} collective-permute-done((f32[16,128]{1,0:T(8,128)S(1)}, f32[16,128]{1,0:T(8,128)S(1)}, u32[]{:S(2)}, u32[]{:S(2)}) %collective-permute-start.6) | collective-permute-done | bytes 8224 | tf_op jit(solution)/shard_map/ppermute | solution.py:429
  27.7 0.0 collective-permute-done.7.xe
  27.7 0.0 collective-permute-done.8.xo
  27.7 0.0 copy-done
  27.7 2.3 %shard_map.109 = (f32[2,10,16,512]{3,2,1,0:T(8,128)S(1)}, bf16[64,512]{1,0:T(8,128)(2,1)S(1)}, f32[128,128]{1,0:T(8,128)S(1)}) custom-call(f32[2,10,16,512]{3,2,1,0:T(8,128)S(1)} %get-tuple-element.47.old, f32[16,128]{1,0:T(8,128)S(1)} %collective-permute-done.5.core, f32[16,128]{1,0:T(8,128)S(1)} %collective-permute-done.6.zpair, ...), custom_call_target="tpu_custom_call" | custom-call | tf_op jit(solution)/shard_map/pallas_call | solution.py:411
  29.9 0.0 collective-permute-start.9
  30.0 1.9 %shard_map.110 = (f32[10,16,512]{2,1,0:T(8,128)}, f32[10,16,512]{2,1,0:T(8,128)}, f32[64,128]{1,0:T(8,128)S(1)}, f32[64,128]{1,0:T(8,128)S(1)}) custom-call(f32[2,10,16,512]{3,2,1,0:T(8,128)S(1)} %get-tuple-element.54.final, bf16[64,512]{1,0:T(8,128)(2,1)S(1)} %get-tuple-element.55.blocks, s32[2,2,2,64]{3,2,1,0:T(2,128)} %bitcast.8, ...), custom_call_target="tpu_custom_call" | custom-call | tf_op jit(solution)/shard_map/pallas_call | solution.py:411
  31.9 3.0 %collective-permute-done.9.gx = f32[128,128]{1,0:T(8,128)S(1)} collective-permute-done((f32[128,128]{1,0:T(8,128)S(1)}, f32[128,128]{1,0:T(8,128)S(1)}, u32[]{:S(2)}, u32[]{:S(2)}) %collective-permute-start.9) | collective-permute-done | bytes 65568 | tf_op jit(solution)/shard_map/ppermute | solution.py:429
  34.9 3.4 %collective-permute-start.10 = (f32[64,128]{1,0:T(8,128)S(1)}, f32[64,128]{1,0:T(8,128)S(1)}, u32[]{:S(2)}, u32[]{:S(2)}) collective-permute-start(f32[64,128]{1,0:T(8,128)S(1)} %slice_add_fusion), channel_id=1, source_target_pairs={{0,1},{1,2},{2,3},{3,4},{4,5},{5,6},{6,7},{7,8},{8,9},{9,10},{10,1... | collective-permute-start | bytes 98312 | tf_op jit(solution)/shard_map/ppermute | solution.py:429
  38.3 4.5 %collective-permute-done.10.gy = f32[64,128]{1,0:T(8,128)S(1)} collective-permute-done((f32[64,128]{1,0:T(8,128)S(1)}, f32[64,128]{1,0:T(8,128)S(1)}, u32[]{:S(2)}, u32[]{:S(2)}) %collective-permute-start.10) | collective-permute-done | bytes 32800 | tf_op jit(solution)/shard_map/ppermute | solution.py:429
  42.8 0.7 %shard_map.111 = f32[4,8,128]{2,1,0:T(8,128)} custom-call(f32[64,128]{1,0:T(8,128)S(1)} %collective-permute-done.10.gy, f32[128,128]{1,0:T(8,128)S(1)} %collective-permute-done.9.gx, f32[64,128]{1,0:T(8,128)S(1)} %get-tuple-element.60.own), custom_call_target="tpu_custom_call" | custom-call | tf_op jit(solution)/shard_map/pallas_call | solution.py:411
  (2 shorter events, 0.0 us)
Async XLA Ops:
  2.3 5.7 %collective-permute-start = (f32[256,128]{1,0:T(8,128)S(1)}, f32[256,128]{1,0:T(8,128)S(1)}, u32[]{:S(2)}, u32[]{:S(2)}) collective-permute-start(f32[256,128]{1,0:T(8,128)S(1)} %get-tuple-element.39), channel_id=1, source_target_pairs={{0,16},{1,17},{2,18},{3,19},{4,20},{5,21},{6,22},{7,23},{8,24},{9,... | collective-permute-start | bytes 393224 | tf_op jit(solution)/shard_map/ppermute | solution.py:429
  2.4 6.8 %collective-permute-start.1 = (f32[256,128]{1,0:T(8,128)S(1)}, f32[256,128]{1,0:T(8,128)S(1)}, u32[]{:S(2)}, u32[]{:S(2)}) collective-permute-start(f32[256,128]{1,0:T(8,128)S(1)} %get-tuple-element.39), channel_id=1, source_target_pairs={{0,112},{1,113},{2,114},{3,115},{4,116},{5,117},{6,118},{7,119},{8... | collective-permute-start | bytes 393224 | tf_op jit(solution)/shard_map/ppermute | solution.py:429
  7.4 7.1 %collective-permute-start.3 = (f32[272,128]{1,0:T(8,128)S(1)}, f32[272,128]{1,0:T(8,128)S(1)}, u32[]{:S(2)}, u32[]{:S(2)}) collective-permute-start(f32[272,128]{1,0:T(8,128)S(1)} %get-tuple-element.41), channel_id=1, source_target_pairs={{0,16},{1,17},{2,18},{3,19},{4,20},{5,21},{6,22},{7,23},{8,24},{9,... | collective-permute-start | bytes 417800 | tf_op jit(solution)/shard_map/ppermute | solution.py:429
  7.5 7.0 %collective-permute-start.4 = (f32[272,128]{1,0:T(8,128)S(1)}, f32[272,128]{1,0:T(8,128)S(1)}, u32[]{:S(2)}, u32[]{:S(2)}) collective-permute-start(f32[272,128]{1,0:T(8,128)S(1)} %get-tuple-element.41), channel_id=1, source_target_pairs={{0,112},{1,113},{2,114},{3,115},{4,116},{5,117},{6,118},{7,119},{8... | collective-permute-start | bytes 417800 | tf_op jit(solution)/shard_map/ppermute | solution.py:429
  9.2 7.1 %collective-permute-start.2 = (f32[256,128]{1,0:T(8,128)S(1)}, f32[256,128]{1,0:T(8,128)S(1)}, u32[]{:S(2)}, u32[]{:S(2)}) collective-permute-start(f32[256,128]{1,0:T(8,128)S(1)} %shard_map.105), channel_id=1, source_target_pairs={{1,0},{2,1},{3,2},{4,3},{5,4},{6,5},{7,6},{8,7},{9,8},{10,9},{11,1... | collective-permute-start | bytes 393224 | tf_op jit(solution)/shard_map/ppermute | solution.py:429
  14.8 12.9 %copy-start = (bf16[1,1,2,2,64,16,128]{6,5,4,3,2,1,0:T(8,128)(2,1)S(1)}, bf16[1,1,2,2,64,16,128]{6,5,4,3,2,1,0:T(8,128)(2,1)}, u32[]{:S(2)}) copy-start(bf16[1,1,2,2,64,16,128]{6,5,4,3,2,1,0:T(8,128)(2,1)} %param.15) | copy-start | bytes 3145732
  16.6 11.0 %collective-permute-start.7 = (f32[43,512]{1,0:T(8,128)S(1)}, f32[43,512]{1,0:T(8,128)S(1)}, u32[]{:S(2)}, u32[]{:S(2)}) collective-permute-start(f32[43,512]{1,0:T(8,128)S(1)} %get-tuple-element.49), channel_id=1, source_target_pairs={{0,1},{1,0},{2,3},{3,2},{4,5},{5,4},{6,7},{7,6},{8,9},{9,8},{10,11... | collective-permute-start | bytes 264200 | tf_op jit(solution)/shard_map/ppermute | solution.py:429
  18.0 9.7 %collective-permute-start.8 = (f32[43,512]{1,0:T(8,128)S(1)}, f32[43,512]{1,0:T(8,128)S(1)}, u32[]{:S(2)}, u32[]{:S(2)}) collective-permute-start(f32[43,512]{1,0:T(8,128)S(1)} %get-tuple-element.50), channel_id=1, source_target_pairs={{1,2},{2,1},{3,4},{4,3},{5,6},{6,5},{7,8},{8,7},{9,10},{10,9},{11,... | collective-permute-start | bytes 264200 | tf_op jit(solution)/shard_map/ppermute | solution.py:429
  23.2 2.7 %collective-permute-start.5 = (f32[16,128]{1,0:T(8,128)S(1)}, f32[16,128]{1,0:T(8,128)S(1)}, u32[]{:S(2)}, u32[]{:S(2)}) collective-permute-start(f32[16,128]{1,0:T(8,128)S(1)} %get-tuple-element.48), channel_id=1, source_target_pairs={{0,16},{1,17},{2,18},{3,19},{4,20},{5,21},{6,22},{7,23},{8,24},{9,... | collective-permute-start | bytes 24584 | tf_op jit(solution)/shard_map/ppermute | solution.py:429
  23.3 4.4 %collective-permute-start.6 = (f32[16,128]{1,0:T(8,128)S(1)}, f32[16,128]{1,0:T(8,128)S(1)}, u32[]{:S(2)}, u32[]{:S(2)}) collective-permute-start(f32[16,128]{1,0:T(8,128)S(1)} %get-tuple-element.48), channel_id=1, source_target_pairs={{0,112},{1,113},{2,114},{3,115},{4,116},{5,117},{6,118},{7,119},{8... | collective-permute-start | bytes 24584 | tf_op jit(solution)/shard_map/ppermute | solution.py:429
  29.9 4.9 %collective-permute-start.9 = (f32[128,128]{1,0:T(8,128)S(1)}, f32[128,128]{1,0:T(8,128)S(1)}, u32[]{:S(2)}, u32[]{:S(2)}) collective-permute-start(f32[128,128]{1,0:T(8,128)S(1)} %get-tuple-element.59), channel_id=1, source_target_pairs={{0,16},{1,17},{2,18},{3,19},{4,20},{5,21},{6,22},{7,23},{8,24},{9,... | collective-permute-start | bytes 196616 | tf_op jit(solution)/shard_map/ppermute | solution.py:429
  34.9 7.9 %collective-permute-start.10 = (f32[64,128]{1,0:T(8,128)S(1)}, f32[64,128]{1,0:T(8,128)S(1)}, u32[]{:S(2)}, u32[]{:S(2)}) collective-permute-start(f32[64,128]{1,0:T(8,128)S(1)} %slice_add_fusion), channel_id=1, source_target_pairs={{0,1},{1,2},{2,3},{3,4},{4,5},{5,6},{6,7},{7,8},{8,9},{9,10},{10,1... | collective-permute-start | bytes 98312 | tf_op jit(solution)/shard_map/ppermute | solution.py:429

commit v5 on v4

--- a/solution.py
+++ b/solution.py
@@ -301,10 +301,12 @@
     deep = depth[...].astype(F32)
     beyond = (jnp.where(odd_row, xe[...], xo[...]), jnp.where(odd_row, xo[...], xe[...]))
     level = iota((2 * LEVELS, COLS), 0) % LEVELS
+    at_end = (lax.axis_index("gy") == 0, lax.axis_index("gy") == lax.axis_size("gy") - 1)
+    beyond_deep = [jnp.where(end, 0.0, other[40:41]) for end, other in zip(at_end, beyond)]
     fixes, halo_rows = [], []
     for n, other in enumerate(beyond):
         r = n * (ROWS - 1)
-        here = (deep[r : r + 1] > level) & (other[40:41] > level)
+        here = (deep[r : r + 1] > level) & (beyond_deep[n] > level)
         fix = jnp.where(here, SIDE_RATE * (other[20:40] - keep[20 * n : 20 * n + 20, :]), 0.0)
         fixes.append(fix)
         halo_rows.append(other[0:20] - fix)
@@ -320,15 +322,15 @@
             mine = keep[40 + 2 * n + at : 41 + 2 * n + at, 0:128]
             far = other[41 + at : 42 + at, 0:128]
             here = mine[:, deepest : deepest + 1] > level
-            here = here & (far[:, deepest : deepest + 1] > level)
+            here = here & (jnp.where(at_end[n], 0.0, far[:, deepest : deepest + 1]) > level)
             fix = jnp.where(here, SIDE_RATE * (far - mine), 0.0)
             halo = halo + jnp.where(row == n * (ROWS - 1), fix, 0.0)
         ends.append(halo)
     west, east = ends
     row8, row = iota((8, COLS), 0), iota((ROWS, COLS), 0)
     around = [depths[n] for n in range(4)]
-    around[0] = jnp.where(row == 0, beyond[0][40:41], around[0])
-    around[1] = jnp.where(row == ROWS - 1, beyond[1][40:41], around[1])
+    around[0] = jnp.where(row == 0, beyond_deep[0], around[0])
+    around[1] = jnp.where(row == ROWS - 1, beyond_deep[1], around[1])
     forcing = [planes[p] for p in range(4)]
     mixing = MIX_BASE + MIX_WIND * forcing[3]
     top = {}
@@ -424,8 +426,7 @@
     for i in range(wide):
         for j in range(high):
             to = step(i, j)
-            if 0 <= to[1] < high:
-                route.append((i * high + j, to[0] % wide * high + to[1]))
+            route.append((i * high + j, to[0] % wide * high + to[1] % high))
     return lax.ppermute(block, ("gx", "gy"), route)
 
 
@@ -435,6 +436,10 @@
 
 def other_pair(n):
     return n + 1 if n % 2 else n - 1
+
+
+def row_pair(i, j):
+    return (i, other_pair(j)) if 0 <= other_pair(j) < lax.axis_size("gy") else (pair(i), j)
 
 
 def per_device(air, out_tables, out_panels, depth, temp, salt, in_tables, in_panels):
@@ -487,7 +492,7 @@
         [field, (ROWS, 128), (43, COLS), (43, COLS), (4, ROWS, COLS), (44, COLS)],
         [gy, base, west, east, partial, temp, salt, depth],
     )
-    xo = send(row_o, lambda i, j: (i, other_pair(j)))
+    xo = send(row_o, row_pair)
     xe = send(row_e, lambda i, j: (i, pair(j)))
     zpair = send(cols, lambda i, j: (other_pair(i), j))
     core = send(cols, lambda i, j: (pair(i), j))

time: 44 us -> 38.3 us (0.87)
  starting transfers between devices: 22.1 us -> 16.3 us
    ppermute x11, starting transfers between devices: 22.1 us -> 16.3 us  [send(): return lax.ppermute(block, ('gx', 'gy'), route)]
  transfers between devices with their start and end apart: 11 -> 11, of which waited for: 5 -> 6; matrix products, arithmetic and copies ran while one was open for 0% -> 0% of each run, Pallas kernels for 9% -> 10%
where the time goes in v5:
time: 38.3 us; the launch traced here: 37.8 us
  starting transfers between devices  16.3 us (43%)
  waiting for transfers between devices  11.9 us (31%)
  Pallas kernels  8.85 us (23%)
  between operations  0.72 us (2%)
    ppermute x11, starting transfers between devices, send(): return lax.ppermute(block, ('gx', 'gy'), route)  16.3 us
    ppermute x11, waiting for transfers between devices, send(): return lax.ppermute(block, ('gx', 'gy'), route)  11.9 us
    pallas_call x9, Pallas kernels, call(): pl.pallas_call(kernel, out_shape=shapes, in_specs=[HBM if n in hbm_in els...  8.85 us
  transfers between devices with their start and end apart: 11, of which 6 were waited for; matrix products, arithmetic and copies ran while one was open for 0% of the time, Pallas kernels for 10%

profile of v5, /device:TPU:8, one launch (start us, length us, event | category | flops | bytes accessed | tf_op | source)
XLA Modules:
  0.0 37.8 jit_solution(9682132658290148666)
XLA Ops:
  0.6 1.6 %shard_map.103 = (f32[256,128]{1,0:T(8,128)S(1)}, bf16[64,1024]{1,0:T(8,128)(2,1)S(1)}, s32[2,2,2,64]{3,2,1,0:T(2,128)S(1)}, bf16[3,1024,128]{2,1,0:T(8,128)(2,1...) custom-call(bf16[8,8,128]{2,1,0:T(8,128)(2,1)} %air_hbm.1, ...), custom_call_target="tpu_custom_call" | custom-call | tf_op jit(solution)/shard_map/pallas_call | solution.py:413
  2.3 0.1 collective-permute-start
  2.4 4.1 %collective-permute-start.1 = (f32[256,128]{1,0:T(8,128)S(1)}, f32[256,128]{1,0:T(8,128)S(1)}, u32[]{:S(2)}, u32[]{:S(2)}) collective-permute-start(f32[256,128]{1,0:T(8,128)S(1)} %get-tuple-element.39), channel_id=1, source_target_pairs={{0,112},{1,113},{2,114},{3,115},{4,116},{5,117},{6,118},{7,119},{8... | collective-permute-start | bytes 393224 | tf_op jit(solution)/shard_map/ppermute | solution.py:430
  6.5 0.9 %shard_map.104 = (f32[272,128]{1,0:T(8,128)S(1)}, f32[256,128]{1,0:T(8,128)S(1)}) custom-call(bf16[64,1024]{1,0:T(8,128)(2,1)S(1)} %get-tuple-element.32.tiled, s32[2,2,2,64]{3,2,1,0:T(2,128)S(1)} %get-tuple-element.33.table, bf16[3,1024,128]{2,1,0:T(8,128)(2,1)S(1)} %get-tuple-element.34.panels, f32[10,16,512]{2,1,0:T(8,128)S(1)} %get-tuple-element.35.temp, ...), custom_call_target="tpu_custom_call" | custom-call | tf_op jit(solution)/shard_map/pallas_call | solution.py:413
  7.4 0.1 collective-permute-start.3
  7.5 0.5 %collective-permute-start.4 = (f32[272,128]{1,0:T(8,128)S(1)}, f32[272,128]{1,0:T(8,128)S(1)}, u32[]{:S(2)}, u32[]{:S(2)}) collective-permute-start(f32[272,128]{1,0:T(8,128)S(1)} %get-tuple-element.41), channel_id=1, source_target_pairs={{0,112},{1,113},{2,114},{3,115},{4,116},{5,117},{6,118},{7,119},{8... | collective-permute-start | bytes 417800 | tf_op jit(solution)/shard_map/ppermute | solution.py:430
  8.0 0.0 collective-permute-done.core
  8.0 1.1 %collective-permute-done.1.zpair = f32[256,128]{1,0:T(8,128)S(1)} collective-permute-done((f32[256,128]{1,0:T(8,128)S(1)}, f32[256,128]{1,0:T(8,128)S(1)}, u32[]{:S(2)}, u32[]{:S(2)}) %collective-permute-start.1) | collective-permute-done | bytes 131104 | tf_op jit(solution)/shard_map/ppermute | solution.py:430
  9.2 2.7 %collective-permute-start.2 = (f32[256,128]{1,0:T(8,128)S(1)}, f32[256,128]{1,0:T(8,128)S(1)}, u32[]{:S(2)}, u32[]{:S(2)}) collective-permute-start(f32[256,128]{1,0:T(8,128)S(1)} %shard_map.105), channel_id=1, source_target_pairs={{0,15},{1,0},{2,1},{3,2},{4,3},{5,4},{6,5},{7,6},{8,7},{9,8},{10,9... | collective-permute-start | bytes 393224 | tf_op jit(solution)/shard_map/ppermute | solution.py:430
  11.9 0.7 %shard_map.106 = (f32[256,128]{1,0:T(8,128)S(1)}, f32[2,10,16,512]{3,2,1,0:T(8,128)S(1)}) custom-call(bf16[64,1024]{1,0:T(8,128)(2,1)S(1)} %get-tuple-element.32.tiled, s32[2,2,2,64]{3,2,1,0:T(2,128)S(1)} %get-tuple-element.33.table, bf16[3,1024,128]{2,1,0:T(8,128)(2,1)S(1)} %get-tuple-element.34.panels, f32[10,16,512]{2,1,0:T(8,128)S(1)} %get-tuple-element.35.temp, ...), custom_call_target="tpu_custom_call" | custom-call | tf_op jit(solution)/shard_map/pallas_call | solution.py:413
  12.6 0.0 collective-permute-done.3.core
  12.7 0.6 %collective-permute-done.4.zpair = f32[272,128]{1,0:T(8,128)S(1)} collective-permute-done((f32[272,128]{1,0:T(8,128)S(1)}, f32[272,128]{1,0:T(8,128)S(1)}, u32[]{:S(2)}, u32[]{:S(2)}) %collective-permute-start.4) | collective-permute-done | bytes 139296 | tf_op jit(solution)/shard_map/ppermute | solution.py:430
  13.3 0.2 shard_map.107
  13.5 0.0 copy-start
  13.5 0.9 %collective-permute-done.2.gy = f32[256,128]{1,0:T(8,128)S(1)} collective-permute-done((f32[256,128]{1,0:T(8,128)S(1)}, f32[256,128]{1,0:T(8,128)S(1)}, u32[]{:S(2)}, u32[]{:S(2)}) %collective-permute-start.2) | collective-permute-done | bytes 131104 | tf_op jit(solution)/shard_map/ppermute | solution.py:430
  14.4 0.4 %shard_map.108 = (f32[2,10,16,512]{3,2,1,0:T(8,128)S(1)}, f32[16,128]{1,0:T(8,128)S(1)}, f32[43,512]{1,0:T(8,128)S(1)}, f32[43,512]{1,0:T(8,128)S(1)}, f32[4,16,512]{2,1,0:T(8,128)S(1)}, /*index=5*/f32[44,512]{1,0:T(8,128)S(1)}) custom-call(f32[256,128]{1,0:T(8,128)S(1)} %collective-permute-done.2.gy, f32[256,128]{1,0:T(8,128)S(1)} %get-tuple-element.43.base, ...), custom_call_target="tpu_custom_call" | custom-call | tf_op jit(solution)/shard_map/pallas_call | solution.py:413
  14.8 1.4 %collective-permute-start.7 = (f32[43,512]{1,0:T(8,128)S(1)}, f32[43,512]{1,0:T(8,128)S(1)}, u32[]{:S(2)}, u32[]{:S(2)}) collective-permute-start(f32[43,512]{1,0:T(8,128)S(1)} %get-tuple-element.49), channel_id=1, source_target_pairs={{0,1},{1,0},{2,3},{3,2},{4,5},{5,4},{6,7},{7,6},{8,9},{9,8},{10,11... | collective-permute-start | bytes 264200 | tf_op jit(solution)/shard_map/ppermute | solution.py:430
  16.2 3.4 %collective-permute-start.8 = (f32[43,512]{1,0:T(8,128)S(1)}, f32[43,512]{1,0:T(8,128)S(1)}, u32[]{:S(2)}, u32[]{:S(2)}) collective-permute-start(f32[43,512]{1,0:T(8,128)S(1)} %get-tuple-element.50), channel_id=1, source_target_pairs={{0,16},{1,2},{2,1},{3,4},{4,3},{5,6},{6,5},{7,8},{8,7},{9,10},{10,... | collective-permute-start | bytes 264200 | tf_op jit(solution)/shard_map/ppermute | solution.py:430
  19.5 0.0 collective-permute-start.5
  19.5 2.6 %collective-permute-start.6 = (f32[16,128]{1,0:T(8,128)S(1)}, f32[16,128]{1,0:T(8,128)S(1)}, u32[]{:S(2)}, u32[]{:S(2)}) collective-permute-start(f32[16,128]{1,0:T(8,128)S(1)} %get-tuple-element.48), channel_id=1, source_target_pairs={{0,112},{1,113},{2,114},{3,115},{4,116},{5,117},{6,118},{7,119},{8... | collective-permute-start | bytes 24584 | tf_op jit(solution)/shard_map/ppermute | solution.py:430
  22.2 0.0 collective-permute-done.5.core
  22.2 1.7 %collective-permute-done.6.zpair = f32[16,128]{1,0:T(8,128)S(1)} collective-permute-done((f32[16,128]{1,0:T(8,128)S(1)}, f32[16,128]{1,0:T(8,128)S(1)}, u32[]{:S(2)}, u32[]{:S(2)}) %collective-permute-start.6) | collective-permute-done | bytes 8224 | tf_op jit(solution)/shard_map/ppermute | solution.py:430
  23.8 0.0 collective-permute-done.7.xe
  23.8 0.0 collective-permute-done.8.xo
  23.8 0.0 copy-done
  23.8 2.3 %shard_map.109 = (f32[2,10,16,512]{3,2,1,0:T(8,128)S(1)}, bf16[64,512]{1,0:T(8,128)(2,1)S(1)}, f32[128,128]{1,0:T(8,128)S(1)}) custom-call(f32[2,10,16,512]{3,2,1,0:T(8,128)S(1)} %get-tuple-element.47.old, f32[16,128]{1,0:T(8,128)S(1)} %collective-permute-done.5.core, f32[16,128]{1,0:T(8,128)S(1)} %collective-permute-done.6.zpair, ...), custom_call_target="tpu_custom_call" | custom-call | tf_op jit(solution)/shard_map/pallas_call | solution.py:413
  26.1 0.0 collective-permute-start.9
  26.2 1.9 %shard_map.110 = (f32[10,16,512]{2,1,0:T(8,128)}, f32[10,16,512]{2,1,0:T(8,128)}, f32[64,128]{1,0:T(8,128)S(1)}, f32[64,128]{1,0:T(8,128)S(1)}) custom-call(f32[2,10,16,512]{3,2,1,0:T(8,128)S(1)} %get-tuple-element.54.final, bf16[64,512]{1,0:T(8,128)(2,1)S(1)} %get-tuple-element.55.blocks, s32[2,2,2,64]{3,2,1,0:T(2,128)} %bitcast.8, ...), custom_call_target="tpu_custom_call" | custom-call | tf_op jit(solution)/shard_map/pallas_call | solution.py:413
  28.1 3.0 %collective-permute-done.9.gx = f32[128,128]{1,0:T(8,128)S(1)} collective-permute-done((f32[128,128]{1,0:T(8,128)S(1)}, f32[128,128]{1,0:T(8,128)S(1)}, u32[]{:S(2)}, u32[]{:S(2)}) %collective-permute-start.9) | collective-permute-done | bytes 65568 | tf_op jit(solution)/shard_map/ppermute | solution.py:430
  31.1 1.4 %collective-permute-start.10 = (f32[64,128]{1,0:T(8,128)S(1)}, f32[64,128]{1,0:T(8,128)S(1)}, u32[]{:S(2)}, u32[]{:S(2)}) collective-permute-start(f32[64,128]{1,0:T(8,128)S(1)} %slice_add_fusion), channel_id=1, source_target_pairs={{0,1},{1,2},{2,3},{3,4},{4,5},{5,6},{6,7},{7,8},{8,9},{9,10},{10,1... | collective-permute-start | bytes 98312 | tf_op jit(solution)/shard_map/ppermute | solution.py:430
  32.5 4.6 %collective-permute-done.10.gy = f32[64,128]{1,0:T(8,128)S(1)} collective-permute-done((f32[64,128]{1,0:T(8,128)S(1)}, f32[64,128]{1,0:T(8,128)S(1)}, u32[]{:S(2)}, u32[]{:S(2)}) %collective-permute-start.10) | collective-permute-done | bytes 32800 | tf_op jit(solution)/shard_map/ppermute | solution.py:430
  37.1 0.7 %shard_map.111 = f32[4,8,128]{2,1,0:T(8,128)} custom-call(f32[64,128]{1,0:T(8,128)S(1)} %collective-permute-done.10.gy, f32[128,128]{1,0:T(8,128)S(1)} %collective-permute-done.9.gx, f32[64,128]{1,0:T(8,128)S(1)} %get-tuple-element.60.own), custom_call_target="tpu_custom_call" | custom-call | tf_op jit(solution)/shard_map/pallas_call | solution.py:413
  (2 shorter events, 0.0 us)
Async XLA Ops:
  2.3 5.7 %collective-permute-start = (f32[256,128]{1,0:T(8,128)S(1)}, f32[256,128]{1,0:T(8,128)S(1)}, u32[]{:S(2)}, u32[]{:S(2)}) collective-permute-start(f32[256,128]{1,0:T(8,128)S(1)} %get-tuple-element.39), channel_id=1, source_target_pairs={{0,16},{1,17},{2,18},{3,19},{4,20},{5,21},{6,22},{7,23},{8,24},{9,... | collective-permute-start | bytes 393224 | tf_op jit(solution)/shard_map/ppermute | solution.py:430
  2.4 6.8 %collective-permute-start.1 = (f32[256,128]{1,0:T(8,128)S(1)}, f32[256,128]{1,0:T(8,128)S(1)}, u32[]{:S(2)}, u32[]{:S(2)}) collective-permute-start(f32[256,128]{1,0:T(8,128)S(1)} %get-tuple-element.39), channel_id=1, source_target_pairs={{0,112},{1,113},{2,114},{3,115},{4,116},{5,117},{6,118},{7,119},{8... | collective-permute-start | bytes 393224 | tf_op jit(solution)/shard_map/ppermute | solution.py:430
  7.4 5.3 %collective-permute-start.3 = (f32[272,128]{1,0:T(8,128)S(1)}, f32[272,128]{1,0:T(8,128)S(1)}, u32[]{:S(2)}, u32[]{:S(2)}) collective-permute-start(f32[272,128]{1,0:T(8,128)S(1)} %get-tuple-element.41), channel_id=1, source_target_pairs={{0,16},{1,17},{2,18},{3,19},{4,20},{5,21},{6,22},{7,23},{8,24},{9,... | collective-permute-start | bytes 417800 | tf_op jit(solution)/shard_map/ppermute | solution.py:430
  7.5 5.8 %collective-permute-start.4 = (f32[272,128]{1,0:T(8,128)S(1)}, f32[272,128]{1,0:T(8,128)S(1)}, u32[]{:S(2)}, u32[]{:S(2)}) collective-permute-start(f32[272,128]{1,0:T(8,128)S(1)} %get-tuple-element.41), channel_id=1, source_target_pairs={{0,112},{1,113},{2,114},{3,115},{4,116},{5,117},{6,118},{7,119},{8... | collective-permute-start | bytes 417800 | tf_op jit(solution)/shard_map/ppermute | solution.py:430
  9.2 5.2 %collective-permute-start.2 = (f32[256,128]{1,0:T(8,128)S(1)}, f32[256,128]{1,0:T(8,128)S(1)}, u32[]{:S(2)}, u32[]{:S(2)}) collective-permute-start(f32[256,128]{1,0:T(8,128)S(1)} %shard_map.105), channel_id=1, source_target_pairs={{0,15},{1,0},{2,1},{3,2},{4,3},{5,4},{6,5},{7,6},{8,7},{9,8},{10,9... | collective-permute-start | bytes 393224 | tf_op jit(solution)/shard_map/ppermute | solution.py:430
  13.5 10.3 %copy-start = (bf16[1,1,2,2,64,16,128]{6,5,4,3,2,1,0:T(8,128)(2,1)S(1)}, bf16[1,1,2,2,64,16,128]{6,5,4,3,2,1,0:T(8,128)(2,1)}, u32[]{:S(2)}) copy-start(bf16[1,1,2,2,64,16,128]{6,5,4,3,2,1,0:T(8,128)(2,1)} %param.15) | copy-start | bytes 3145732
  14.8 9.0 %collective-permute-start.7 = (f32[43,512]{1,0:T(8,128)S(1)}, f32[43,512]{1,0:T(8,128)S(1)}, u32[]{:S(2)}, u32[]{:S(2)}) collective-permute-start(f32[43,512]{1,0:T(8,128)S(1)} %get-tuple-element.49), channel_id=1, source_target_pairs={{0,1},{1,0},{2,3},{3,2},{4,5},{5,4},{6,7},{7,6},{8,9},{9,8},{10,11... | collective-permute-start | bytes 264200 | tf_op jit(solution)/shard_map/ppermute | solution.py:430
  16.2 7.7 %collective-permute-start.8 = (f32[43,512]{1,0:T(8,128)S(1)}, f32[43,512]{1,0:T(8,128)S(1)}, u32[]{:S(2)}, u32[]{:S(2)}) collective-permute-start(f32[43,512]{1,0:T(8,128)S(1)} %get-tuple-element.50), channel_id=1, source_target_pairs={{0,16},{1,2},{2,1},{3,4},{4,3},{5,6},{6,5},{7,8},{8,7},{9,10},{10,... | collective-permute-start | bytes 264200 | tf_op jit(solution)/shard_map/ppermute | solution.py:430
  19.5 2.6 %collective-permute-start.5 = (f32[16,128]{1,0:T(8,128)S(1)}, f32[16,128]{1,0:T(8,128)S(1)}, u32[]{:S(2)}, u32[]{:S(2)}) collective-permute-start(f32[16,128]{1,0:T(8,128)S(1)} %get-tuple-element.48), channel_id=1, source_target_pairs={{0,16},{1,17},{2,18},{3,19},{4,20},{5,21},{6,22},{7,23},{8,24},{9,... | collective-permute-start | bytes 24584 | tf_op jit(solution)/shard_map/ppermute | solution.py:430
  19.5 4.3 %collective-permute-start.6 = (f32[16,128]{1,0:T(8,128)S(1)}, f32[16,128]{1,0:T(8,128)S(1)}, u32[]{:S(2)}, u32[]{:S(2)}) collective-permute-start(f32[16,128]{1,0:T(8,128)S(1)} %get-tuple-element.48), channel_id=1, source_target_pairs={{0,112},{1,113},{2,114},{3,115},{4,116},{5,117},{6,118},{7,119},{8... | collective-permute-start | bytes 24584 | tf_op jit(solution)/shard_map/ppermute | solution.py:430
  26.1 4.9 %collective-permute-start.9 = (f32[128,128]{1,0:T(8,128)S(1)}, f32[128,128]{1,0:T(8,128)S(1)}, u32[]{:S(2)}, u32[]{:S(2)}) collective-permute-start(f32[128,128]{1,0:T(8,128)S(1)} %get-tuple-element.59), channel_id=1, source_target_pairs={{0,16},{1,17},{2,18},{3,19},{4,20},{5,21},{6,22},{7,23},{8,24},{9,... | collective-permute-start | bytes 196616 | tf_op jit(solution)/shard_map/ppermute | solution.py:430
  31.1 6.0 %collective-permute-start.10 = (f32[64,128]{1,0:T(8,128)S(1)}, f32[64,128]{1,0:T(8,128)S(1)}, u32[]{:S(2)}, u32[]{:S(2)}) collective-permute-start(f32[64,128]{1,0:T(8,128)S(1)} %slice_add_fusion), channel_id=1, source_target_pairs={{0,1},{1,2},{2,3},{3,4},{4,5},{5,6},{6,7},{7,8},{8,9},{9,10},{10,1... | collective-permute-start | bytes 98312 | tf_op jit(solution)/shard_map/ppermute | solution.py:430

commit v6 on v5

--- a/solution.py
+++ b/solution.py
@@ -1,3 +1,5 @@
+import functools
+
 import jax
 import jax.numpy as jnp
 from jax import lax
@@ -259,6 +261,7 @@
         for a, b in zip(*edges):
             out[at : at + a.shape[0], 0 : a.shape[1]] = jnp.where(first, a, b)
             at += a.shape[0]
+    row_o[43:48, :] = jnp.zeros((5, COLS), F32)
     for n in range(2):
         keep[20 * n : 20 * n + 10, :] = edges[n][2]
         keep[20 * n + 10 : 20 * n + 20, :] = edges[n][3]
@@ -281,7 +284,7 @@
             kept[c].append(jnp.where(mask, piece[c * 8 : (c + 1) * 8], 0.0))
     kept = jnp.concatenate([jnp.concatenate(k, 0) for k in kept], 1)
     pieces = split_dot(kept, fold)
-    out[...] = dot_split(one_hot(target, names[1:2, :]), pieces)
+    out[0:64, :] = dot_split(one_hot(target, names[1:2, :]), pieces)
 
 
 def inbound_fold():
@@ -292,14 +295,15 @@
 
 def second_kernel(
     old, core, zpair, xe, xo, planes, depths, keep, depth, table_hbm, panels,
-    final, surface_blocks, to_gx, table, sem,
+    final, surface_blocks, to_dg, table, sem,
 ):
     copy = pltpu.make_async_copy(table_hbm, table, sem)
     copy.start()
     odd_col = lax.axis_index("gx") % 2 == 1
     odd_row = lax.axis_index("gy") % 2 == 1
     deep = depth[...].astype(F32)
-    beyond = (jnp.where(odd_row, xe[...], xo[...]), jnp.where(odd_row, xo[...], xe[...]))
+    row_e, row_o = xe[...], xo[0:43, :]
+    beyond = (jnp.where(odd_row, row_e, row_o), jnp.where(odd_row, row_o, row_e))
     level = iota((2 * LEVELS, COLS), 0) % LEVELS
     at_end = (lax.axis_index("gy") == 0, lax.axis_index("gy") == lax.axis_size("gy") - 1)
     beyond_deep = [jnp.where(end, 0.0, other[40:41]) for end, other in zip(at_end, beyond)]
@@ -373,28 +377,27 @@
         parts.append(jnp.concatenate([f[:, s * 128 : (s + 1) * 128] for s in range(TILES)], 0))
     blocks = jnp.concatenate(parts, 1).astype(BF16)
     surface_blocks[...] = blocks
-    mask, fold = group_mask(), inbound_fold()
     copy.wait()
-    for a in range(2):
-        out = to_gx.at[a * 64 : (a + 1) * 64]
-        inbound_list(blocks, table[a, 1], panels.at[2 * a + 1], fold, mask, out)
-
-
-def outer_kernel(
-    final, blocks, table_hbm, panels, new_temp, new_salt, own, south, table, sems
-):
-    pairs = [(table_hbm, table), (final.at[0], new_temp), (final.at[1], new_salt)]
-    copies = fetch(sems, pairs)
-    copies[0].wait()
+    inbound_list(blocks, table[1, 1], panels.at[3], inbound_fold(), group_mask(), to_dg)
+    to_dg[64:, :] = jnp.zeros((16, 128), F32)
+
+
+def inbound_kernel(a, b, blocks, table, panels, out):
     fold, mask = inbound_fold(), group_mask()
-    for a, out in ((1, south), (0, own)):
-        inbound_list(blocks[...], table[a, 0], panels.at[2 * a], fold, mask, out)
-    for copy in copies[1:]:
+    inbound_list(blocks[...], table[a, b], panels.at[2 * a + b], fold, mask, out)
+    if out.shape[0] > 64:
+        out[64:, :] = jnp.zeros((out.shape[0] - 64, 128), F32)
+
+
+def outer_kernel(final, blocks, table, panels, new_temp, new_salt, own, sems):
+    copies = fetch(sems, [(final.at[0], new_temp), (final.at[1], new_salt)])
+    inbound_kernel(0, 0, blocks, table, panels, own)
+    for copy in copies:
         copy.wait()
 
 
-def final_kernel(gy, gx, own, out):
-    total = own[...] + gx[0:64, :] + gy[...]
+def final_kernel(dg, gy, gx, own, out):
+    total = own[...] + gx[0:64, :] + gy[0:64, :] + dg[0:64, :]
     group = iota((8, 128), 1) // 16
     for c in range(4):
         field = jnp.zeros((8, 128), F32)
@@ -489,31 +492,42 @@
     )
     stepped, cols, row_e, row_o, planes, keep = call(
         first_kernel,
-        [field, (ROWS, 128), (43, COLS), (43, COLS), (4, ROWS, COLS), (44, COLS)],
+        [field, (ROWS, 128), (43, COLS), (48, COLS), (4, ROWS, COLS), (44, COLS)],
         [gy, base, west, east, partial, temp, salt, depth],
     )
     xo = send(row_o, row_pair)
     xe = send(row_e, lambda i, j: (i, pair(j)))
     zpair = send(cols, lambda i, j: (other_pair(i), j))
     core = send(cols, lambda i, j: (pair(i), j))
-    final, blocks, to_gx = call(
+    final, blocks, to_dg, in_tables = call(
         second_kernel,
-        [field, jax.ShapeDtypeStruct((64, COLS), BF16), (128, 128)],
+        [
+            field,
+            jax.ShapeDtypeStruct((64, COLS), BF16),
+            (80, 128),
+            jax.ShapeDtypeStruct(in_tables.shape, jnp.int32),
+        ],
         [stepped, core, zpair, xe, xo, planes, depths, keep, depth, in_tables, in_panels],
-        [pltpu.VMEM(in_tables.shape, jnp.int32), pltpu.SemaphoreType.DMA],
+        [pltpu.SemaphoreType.DMA],
         hbm_in=(9,),
     )
+    dg = send(to_dg, lambda i, j: (i + 1, j + 1) if j + 1 < lax.axis_size("gy") else (i, j + 1))
+    (to_gy,) = call(
+        functools.partial(inbound_kernel, 1, 0), [(72, 128)], [blocks, in_tables, in_panels]
+    )
+    gy = send(to_gy, lambda i, j: (i, j + 1))
+    (to_gx,) = call(
+        functools.partial(inbound_kernel, 0, 1), [(64, 128)], [blocks, in_tables, in_panels]
+    )
     gx = send(to_gx, lambda i, j: (i + 1, j))
-    new_temp, new_salt, own, south = call(
+    new_temp, new_salt, own = call(
         outer_kernel,
-        [temp.shape, salt.shape, (64, 128), (64, 128)],
+        [temp.shape, salt.shape, (64, 128)],
         [final, blocks, in_tables, in_panels],
-        [pltpu.VMEM(in_tables.shape, jnp.int32), pltpu.SemaphoreType.DMA((3,))],
-        hbm_in=(2,),
+        [pltpu.SemaphoreType.DMA((2,))],
         hbm_out=(0, 1),
     )
-    gy = send(south + gx[64:128], lambda i, j: (i, j + 1))
-    (surface,) = call(final_kernel, [(4, 8, 128)], [gy, gx, own])
+    (surface,) = call(final_kernel, [(4, 8, 128)], [dg, gy, gx, own])
     return new_temp, new_salt, surface
 
 

time: 38.3 us -> 35.1 us (0.916)
  waiting for transfers between devices: 11.9 us -> 8.6 us
  starting transfers between devices: 16.3 us -> 16.7 us
    ppermute x11 -> x12, waiting for transfers between devices: 11.9 us -> 8.6 us  [send(): return lax.ppermute(block, ('gx', 'gy'), route)]
    ppermute x11 -> x12, starting transfers between devices: 16.3 us -> 16.7 us  [send(): return lax.ppermute(block, ('gx', 'gy'), route)]
    pallas_call x9 -> x11, Pallas kernels: 8.85 us -> 8.53 us  [call(): pl.pallas_call(kernel, out_shape=shapes, in_specs=[HBM if n in hbm_in els...]
  transfers between devices with their start and end apart: 11 -> 12, of which waited for: 6 -> 6; matrix products, arithmetic and copies ran while one was open for 0% -> 0% of each run, Pallas kernels for 10% -> 12%
where the time goes in v6:
time: 35.1 us; the launch traced here: 34.6 us
  starting transfers between devices  16.7 us (48%)
  waiting for transfers between devices  8.6 us (25%)
  Pallas kernels  8.53 us (24%)
  between operations  0.73 us (2%)
    ppermute x12, starting transfers between devices, send(): return lax.ppermute(block, ('gx', 'gy'), route)  16.7 us
    ppermute x12, waiting for transfers between devices, send(): return lax.ppermute(block, ('gx', 'gy'), route)  8.6 us
    pallas_call x11, Pallas kernels, call(): pl.pallas_call(kernel, out_shape=shapes, in_specs=[HBM if n in hbm_in els...  8.53 us
  transfers between devices with their start and end apart: 12, of which 6 were waited for; matrix products, arithmetic and copies ran while one was open for 0% of the time, Pallas kernels for 12%

profile of v6, /device:TPU:8, one launch (start us, length us, event | category | flops | bytes accessed | tf_op | source)
XLA Modules:
  0.0 34.6 jit_solution(7559401131892117683)
XLA Ops:
  0.6 1.6 %shard_map.103 = (f32[256,128]{1,0:T(8,128)S(1)}, bf16[64,1024]{1,0:T(8,128)(2,1)S(1)}, s32[2,2,2,64]{3,2,1,0:T(2,128)S(1)}, bf16[3,1024,128]{2,1,0:T(8,128)(2,1...) custom-call(bf16[8,8,128]{2,1,0:T(8,128)(2,1)} %air_hbm.1, ...), custom_call_target="tpu_custom_call" | custom-call | tf_op jit(solution)/shard_map/pallas_call | solution.py:416
  2.3 0.1 collective-permute-start
  2.4 4.1 %collective-permute-start.1 = (f32[256,128]{1,0:T(8,128)S(1)}, f32[256,128]{1,0:T(8,128)S(1)}, u32[]{:S(2)}, u32[]{:S(2)}) collective-permute-start(f32[256,128]{1,0:T(8,128)S(1)} %get-tuple-element.39), channel_id=1, source_target_pairs={{0,112},{1,113},{2,114},{3,115},{4,116},{5,117},{6,118},{7,119},{8... | collective-permute-start | bytes 393224 | tf_op jit(solution)/shard_map/ppermute | solution.py:433
  6.5 0.9 %shard_map.104 = (f32[272,128]{1,0:T(8,128)S(1)}, f32[256,128]{1,0:T(8,128)S(1)}) custom-call(bf16[64,1024]{1,0:T(8,128)(2,1)S(1)} %get-tuple-element.32.tiled, s32[2,2,2,64]{3,2,1,0:T(2,128)S(1)} %get-tuple-element.33.table, bf16[3,1024,128]{2,1,0:T(8,128)(2,1)S(1)} %get-tuple-element.34.panels, f32[10,16,512]{2,1,0:T(8,128)S(1)} %get-tuple-element.35.temp, ...), custom_call_target="tpu_custom_call" | custom-call | tf_op jit(solution)/shard_map/pallas_call | solution.py:416
  7.4 0.1 collective-permute-start.3
  7.5 0.5 %collective-permute-start.4 = (f32[272,128]{1,0:T(8,128)S(1)}, f32[272,128]{1,0:T(8,128)S(1)}, u32[]{:S(2)}, u32[]{:S(2)}) collective-permute-start(f32[272,128]{1,0:T(8,128)S(1)} %get-tuple-element.41), channel_id=1, source_target_pairs={{0,112},{1,113},{2,114},{3,115},{4,116},{5,117},{6,118},{7,119},{8... | collective-permute-start | bytes 417800 | tf_op jit(solution)/shard_map/ppermute | solution.py:433
  8.0 0.0 collective-permute-done.core
  8.0 1.1 %collective-permute-done.1.zpair = f32[256,128]{1,0:T(8,128)S(1)} collective-permute-done((f32[256,128]{1,0:T(8,128)S(1)}, f32[256,128]{1,0:T(8,128)S(1)}, u32[]{:S(2)}, u32[]{:S(2)}) %collective-permute-start.1) | collective-permute-done | bytes 131104 | tf_op jit(solution)/shard_map/ppermute | solution.py:433
  9.2 2.7 %collective-permute-start.2 = (f32[256,128]{1,0:T(8,128)S(1)}, f32[256,128]{1,0:T(8,128)S(1)}, u32[]{:S(2)}, u32[]{:S(2)}) collective-permute-start(f32[256,128]{1,0:T(8,128)S(1)} %shard_map.105), channel_id=1, source_target_pairs={{0,15},{1,0},{2,1},{3,2},{4,3},{5,4},{6,5},{7,6},{8,7},{9,8},{10,9... | collective-permute-start | bytes 393224 | tf_op jit(solution)/shard_map/ppermute | solution.py:433
  11.9 0.7 %shard_map.106 = (f32[256,128]{1,0:T(8,128)S(1)}, f32[2,10,16,512]{3,2,1,0:T(8,128)S(1)}) custom-call(bf16[64,1024]{1,0:T(8,128)(2,1)S(1)} %get-tuple-element.32.tiled, s32[2,2,2,64]{3,2,1,0:T(2,128)S(1)} %get-tuple-element.33.table, bf16[3,1024,128]{2,1,0:T(8,128)(2,1)S(1)} %get-tuple-element.34.panels, f32[10,16,512]{2,1,0:T(8,128)S(1)} %get-tuple-element.35.temp, ...), custom_call_target="tpu_custom_call" | custom-call | tf_op jit(solution)/shard_map/pallas_call | solution.py:416
  12.6 0.0 collective-permute-done.3.core
  12.6 0.6 %collective-permute-done.4.zpair = f32[272,128]{1,0:T(8,128)S(1)} collective-permute-done((f32[272,128]{1,0:T(8,128)S(1)}, f32[272,128]{1,0:T(8,128)S(1)}, u32[]{:S(2)}, u32[]{:S(2)}) %collective-permute-start.4) | collective-permute-done | bytes 139296 | tf_op jit(solution)/shard_map/ppermute | solution.py:433
  13.3 0.3 shard_map.107
  13.5 0.0 copy-start
  13.5 0.9 %collective-permute-done.2.gy = f32[256,128]{1,0:T(8,128)S(1)} collective-permute-done((f32[256,128]{1,0:T(8,128)S(1)}, f32[256,128]{1,0:T(8,128)S(1)}, u32[]{:S(2)}, u32[]{:S(2)}) %collective-permute-start.2) | collective-permute-done | bytes 131104 | tf_op jit(solution)/shard_map/ppermute | solution.py:433
  14.4 0.4 %shard_map.108 = (f32[2,10,16,512]{3,2,1,0:T(8,128)S(1)}, f32[16,128]{1,0:T(8,128)S(1)}, f32[43,512]{1,0:T(8,128)S(1)}, f32[48,512]{1,0:T(8,128)S(1)}, f32[4,16,512]{2,1,0:T(8,128)S(1)}, /*index=5*/f32[44,512]{1,0:T(8,128)S(1)}) custom-call(f32[256,128]{1,0:T(8,128)S(1)} %collective-permute-done.2.gy, f32[256,128]{1,0:T(8,128)S(1)} %get-tuple-element.43.base, ...), custom_call_target="tpu_custom_call" | custom-call | tf_op jit(solution)/shard_map/pallas_call | solution.py:416
  14.8 4.6 %collective-permute-start.8 = (f32[48,512]{1,0:T(8,128)S(1)}, f32[48,512]{1,0:T(8,128)S(1)}, u32[]{:S(2)}, u32[]{:S(2)}) collective-permute-start(f32[48,512]{1,0:T(8,128)S(1)} %get-tuple-element.50), channel_id=1, source_target_pairs={{0,16},{1,2},{2,1},{3,4},{4,3},{5,6},{6,5},{7,8},{8,7},{9,10},{10,... | collective-permute-start | bytes 294920 | tf_op jit(solution)/shard_map/ppermute | solution.py:433
  19.4 0.0 collective-permute-start.7
  19.4 0.0 collective-permute-start.5
  19.4 2.6 %collective-permute-start.6 = (f32[16,128]{1,0:T(8,128)S(1)}, f32[16,128]{1,0:T(8,128)S(1)}, u32[]{:S(2)}, u32[]{:S(2)}) collective-permute-start(f32[16,128]{1,0:T(8,128)S(1)} %get-tuple-element.48), channel_id=1, source_target_pairs={{0,112},{1,113},{2,114},{3,115},{4,116},{5,117},{6,118},{7,119},{8... | collective-permute-start | bytes 24584 | tf_op jit(solution)/shard_map/ppermute | solution.py:433
  22.1 0.0 collective-permute-done.5.core
  22.1 1.7 %collective-permute-done.6.zpair = f32[16,128]{1,0:T(8,128)S(1)} collective-permute-done((f32[16,128]{1,0:T(8,128)S(1)}, f32[16,128]{1,0:T(8,128)S(1)}, u32[]{:S(2)}, u32[]{:S(2)}) %collective-permute-start.6) | collective-permute-done | bytes 8224 | tf_op jit(solution)/shard_map/ppermute | solution.py:433
  23.7 0.3 collective-permute-done.7.xe
  24.1 0.0 collective-permute-done.8.xo
  24.1 0.0 copy-done
  24.1 1.7 %shard_map.109 = (f32[2,10,16,512]{3,2,1,0:T(8,128)S(1)}, bf16[64,512]{1,0:T(8,128)(2,1)S(1)}, f32[80,128]{1,0:T(8,128)S(1)}, s32[2,2,2,64]{3,2,1,0:T(2,128)S(1)}) custom-call(f32[2,10,16,512]{3,2,1,0:T(8,128)S(1)} %get-tuple-element.47.old, f32[16,128]{1,0:T(8,128)S(1)} %collective-permute-done.5.core, f32[16,128]{1,0:T(8,128)S(1)} %collective-permute-done.6.zpair, ...), custom_call_target="tpu_custom_call" | custom-call | tf_op jit(solution)/shard_map/pallas_call | solution.py:416
  25.8 1.0 %collective-permute-start.9 = (f32[80,128]{1,0:T(8,128)S(1)}, f32[80,128]{1,0:T(8,128)S(1)}, u32[]{:S(2)}, u32[]{:S(2)}) collective-permute-start(f32[80,128]{1,0:T(8,128)S(1)} %get-tuple-element.59), channel_id=1, source_target_pairs={{0,17},{1,18},{2,19},{3,20},{4,21},{5,22},{6,23},{7,24},{8,25},{9,... | collective-permute-start | bytes 122888 | tf_op jit(solution)/shard_map/ppermute | solution.py:433
  26.8 0.7 %shard_map.111 = f32[72,128]{1,0:T(8,128)S(1)} custom-call(bf16[64,512]{1,0:T(8,128)(2,1)S(1)} %get-tuple-element.55.blocks, s32[2,2,2,64]{3,2,1,0:T(2,128)S(1)} %get-tuple-element.56.table, bf16[4,1024,128]{2,1,0:T(8,128)(2,1)S(1)} %bitcast.5), custom_call_target="tpu_custom_call" | custom-call | tf_op jit(solution)/shard_map/pallas_call | solution.py:416
  27.4 0.9 %collective-permute-start.10 = (f32[72,128]{1,0:T(8,128)S(1)}, f32[72,128]{1,0:T(8,128)S(1)}, u32[]{:S(2)}, u32[]{:S(2)}) collective-permute-start(f32[72,128]{1,0:T(8,128)S(1)} %shard_map.111), channel_id=1, source_target_pairs={{0,1},{1,2},{2,3},{3,4},{4,5},{5,6},{6,7},{7,8},{8,9},{9,10},{10,1... | collective-permute-start | bytes 110600 | tf_op jit(solution)/shard_map/ppermute | solution.py:433
  28.3 0.7 %shard_map.112 = f32[64,128]{1,0:T(8,128)S(1)} custom-call(bf16[64,512]{1,0:T(8,128)(2,1)S(1)} %get-tuple-element.55.blocks, s32[2,2,2,64]{3,2,1,0:T(2,128)S(1)} %get-tuple-element.56.table, bf16[4,1024,128]{2,1,0:T(8,128)(2,1)S(1)} %bitcast.6), custom_call_target="tpu_custom_call" | custom-call | tf_op jit(solution)/shard_map/pallas_call | solution.py:416
  29.0 0.0 collective-permute-start.11
  29.0 0.9 %shard_map.110 = (f32[10,16,512]{2,1,0:T(8,128)}, f32[10,16,512]{2,1,0:T(8,128)}, f32[64,128]{1,0:T(8,128)S(1)}) custom-call(f32[2,10,16,512]{3,2,1,0:T(8,128)S(1)} %get-tuple-element.54.final, bf16[64,512]{1,0:T(8,128)(2,1)S(1)} %get-tuple-element.55.blocks, s32[2,2,2,64]{3,2,1,0:T(2,128)S(1)} %get-tuple-element.56.table, bf16[4,1024,128]{2,1,0:T(8,128)(2,1)S(1)} %bitcast.7), custom_call_target="tpu_custom_call" | custom-call | tf_op jit(solution)/shard_map/pallas_call | solution.py:416
  29.9 4.0 %collective-permute-done.11.gx = f32[64,128]{1,0:T(8,128)S(1)} collective-permute-done((f32[64,128]{1,0:T(8,128)S(1)}, f32[64,128]{1,0:T(8,128)S(1)}, u32[]{:S(2)}, u32[]{:S(2)}) %collective-permute-start.11) | collective-permute-done | bytes 32800 | tf_op jit(solution)/shard_map/ppermute | solution.py:433
  33.8 0.0 collective-permute-done.10.gy
  33.8 0.0 collective-permute-done.9.dg
  33.9 0.7 %shard_map.113 = f32[4,8,128]{2,1,0:T(8,128)} custom-call(f32[80,128]{1,0:T(8,128)S(1)} %collective-permute-done.9.dg, f32[72,128]{1,0:T(8,128)S(1)} %collective-permute-done.10.gy, f32[64,128]{1,0:T(8,128)S(1)} %collective-permute-done.11.gx, f32[64,128]{1,0:T(8,128)S(1)} %get-tuple-element.60.own), custom_call_target="tpu_custom_call" | custom-call | tf_op jit(solution)/shard_map/pallas_call | solution.py:416
  (1 shorter events, 0.0 us)
Async XLA Ops:
  2.3 5.7 %collective-permute-start = (f32[256,128]{1,0:T(8,128)S(1)}, f32[256,128]{1,0:T(8,128)S(1)}, u32[]{:S(2)}, u32[]{:S(2)}) collective-permute-start(f32[256,128]{1,0:T(8,128)S(1)} %get-tuple-element.39), channel_id=1, source_target_pairs={{0,16},{1,17},{2,18},{3,19},{4,20},{5,21},{6,22},{7,23},{8,24},{9,... | collective-permute-start | bytes 393224 | tf_op jit(solution)/shard_map/ppermute | solution.py:433
  2.4 6.8 %collective-permute-start.1 = (f32[256,128]{1,0:T(8,128)S(1)}, f32[256,128]{1,0:T(8,128)S(1)}, u32[]{:S(2)}, u32[]{:S(2)}) collective-permute-start(f32[256,128]{1,0:T(8,128)S(1)} %get-tuple-element.39), channel_id=1, source_target_pairs={{0,112},{1,113},{2,114},{3,115},{4,116},{5,117},{6,118},{7,119},{8... | collective-permute-start | bytes 393224 | tf_op jit(solution)/shard_map/ppermute | solution.py:433
  7.4 5.2 %collective-permute-start.3 = (f32[272,128]{1,0:T(8,128)S(1)}, f32[272,128]{1,0:T(8,128)S(1)}, u32[]{:S(2)}, u32[]{:S(2)}) collective-permute-start(f32[272,128]{1,0:T(8,128)S(1)} %get-tuple-element.41), channel_id=1, source_target_pairs={{0,16},{1,17},{2,18},{3,19},{4,20},{5,21},{6,22},{7,23},{8,24},{9,... | collective-permute-start | bytes 417800 | tf_op jit(solution)/shard_map/ppermute | solution.py:433
  7.5 5.8 %collective-permute-start.4 = (f32[272,128]{1,0:T(8,128)S(1)}, f32[272,128]{1,0:T(8,128)S(1)}, u32[]{:S(2)}, u32[]{:S(2)}) collective-permute-start(f32[272,128]{1,0:T(8,128)S(1)} %get-tuple-element.41), channel_id=1, source_target_pairs={{0,112},{1,113},{2,114},{3,115},{4,116},{5,117},{6,118},{7,119},{8... | collective-permute-start | bytes 417800 | tf_op jit(solution)/shard_map/ppermute | solution.py:433
  9.2 5.2 %collective-permute-start.2 = (f32[256,128]{1,0:T(8,128)S(1)}, f32[256,128]{1,0:T(8,128)S(1)}, u32[]{:S(2)}, u32[]{:S(2)}) collective-permute-start(f32[256,128]{1,0:T(8,128)S(1)} %shard_map.105), channel_id=1, source_target_pairs={{0,15},{1,0},{2,1},{3,2},{4,3},{5,4},{6,5},{7,6},{8,7},{9,8},{10,9... | collective-permute-start | bytes 393224 | tf_op jit(solution)/shard_map/ppermute | solution.py:433
  13.5 10.6 %copy-start = (bf16[1,1,2,2,64,16,128]{6,5,4,3,2,1,0:T(8,128)(2,1)S(1)}, bf16[1,1,2,2,64,16,128]{6,5,4,3,2,1,0:T(8,128)(2,1)}, u32[]{:S(2)}) copy-start(bf16[1,1,2,2,64,16,128]{6,5,4,3,2,1,0:T(8,128)(2,1)} %param.15) | copy-start | bytes 3145732
  14.8 9.3 %collective-permute-start.8 = (f32[48,512]{1,0:T(8,128)S(1)}, f32[48,512]{1,0:T(8,128)S(1)}, u32[]{:S(2)}, u32[]{:S(2)}) collective-permute-start(f32[48,512]{1,0:T(8,128)S(1)} %get-tuple-element.50), channel_id=1, source_target_pairs={{0,16},{1,2},{2,1},{3,4},{4,3},{5,6},{6,5},{7,8},{8,7},{9,10},{10,... | collective-permute-start | bytes 294920 | tf_op jit(solution)/shard_map/ppermute | solution.py:433
  19.4 4.6 %collective-permute-start.7 = (f32[43,512]{1,0:T(8,128)S(1)}, f32[43,512]{1,0:T(8,128)S(1)}, u32[]{:S(2)}, u32[]{:S(2)}) collective-permute-start(f32[43,512]{1,0:T(8,128)S(1)} %get-tuple-element.49), channel_id=1, source_target_pairs={{0,1},{1,0},{2,3},{3,2},{4,5},{5,4},{6,7},{7,6},{8,9},{9,8},{10,11... | collective-permute-start | bytes 264200 | tf_op jit(solution)/shard_map/ppermute | solution.py:433
  19.4 2.6 %collective-permute-start.5 = (f32[16,128]{1,0:T(8,128)S(1)}, f32[16,128]{1,0:T(8,128)S(1)}, u32[]{:S(2)}, u32[]{:S(2)}) collective-permute-start(f32[16,128]{1,0:T(8,128)S(1)} %get-tuple-element.48), channel_id=1, source_target_pairs={{0,16},{1,17},{2,18},{3,19},{4,20},{5,21},{6,22},{7,23},{8,24},{9,... | collective-permute-start | bytes 24584 | tf_op jit(solution)/shard_map/ppermute | solution.py:433
  19.4 4.3 %collective-permute-start.6 = (f32[16,128]{1,0:T(8,128)S(1)}, f32[16,128]{1,0:T(8,128)S(1)}, u32[]{:S(2)}, u32[]{:S(2)}) collective-permute-start(f32[16,128]{1,0:T(8,128)S(1)} %get-tuple-element.48), channel_id=1, source_target_pairs={{0,112},{1,113},{2,114},{3,115},{4,116},{5,117},{6,118},{7,119},{8... | collective-permute-start | bytes 24584 | tf_op jit(solution)/shard_map/ppermute | solution.py:433
  25.8 8.1 %collective-permute-start.9 = (f32[80,128]{1,0:T(8,128)S(1)}, f32[80,128]{1,0:T(8,128)S(1)}, u32[]{:S(2)}, u32[]{:S(2)}) collective-permute-start(f32[80,128]{1,0:T(8,128)S(1)} %get-tuple-element.59), channel_id=1, source_target_pairs={{0,17},{1,18},{2,19},{3,20},{4,21},{5,22},{6,23},{7,24},{8,25},{9,... | collective-permute-start | bytes 122888 | tf_op jit(solution)/shard_map/ppermute | solution.py:433
  27.4 6.4 %collective-permute-start.10 = (f32[72,128]{1,0:T(8,128)S(1)}, f32[72,128]{1,0:T(8,128)S(1)}, u32[]{:S(2)}, u32[]{:S(2)}) collective-permute-start(f32[72,128]{1,0:T(8,128)S(1)} %shard_map.111), channel_id=1, source_target_pairs={{0,1},{1,2},{2,3},{3,4},{4,5},{5,6},{6,7},{7,8},{8,9},{9,10},{10,1... | collective-permute-start | bytes 110600 | tf_op jit(solution)/shard_map/ppermute | solution.py:433
  29.0 4.9 %collective-permute-start.11 = (f32[64,128]{1,0:T(8,128)S(1)}, f32[64,128]{1,0:T(8,128)S(1)}, u32[]{:S(2)}, u32[]{:S(2)}) collective-permute-start(f32[64,128]{1,0:T(8,128)S(1)} %shard_map.112), channel_id=1, source_target_pairs={{0,16},{1,17},{2,18},{3,19},{4,20},{5,21},{6,22},{7,23},{8,24},{9,... | collective-permute-start | bytes 98312 | tf_op jit(solution)/shard_map/ppermute | solution.py:433

commit v7 on v6

--- a/solution.py
+++ b/solution.py
@@ -19,6 +19,9 @@
 TILES = COLS // 128
 F32, BF16 = jnp.float32, jnp.bfloat16
 LIST_ROWS = 4 * 64
+FORCING_ORDER = ((0, 0), (1, 0), (0, 1))
+TOP_LEVELS = ((0, 3), (0, 1))
+SURFACE_ORDER = ((1, 1), (1, 0), (0, 1))
 VMEM = pl.BlockSpec(memory_space=pltpu.VMEM)
 HBM = pl.BlockSpec(memory_space=pltpu.HBM)
 NN = (((1,), (0,)), ((), ()))
@@ -37,7 +40,7 @@
 def dot_split(ones, values):
     high = values.astype(BF16)
     low = (values - high.astype(F32)).astype(BF16)
-    return dot(ones, high) + dot(ones, low)
+    return dot(jnp.concatenate([ones, ones], 1), jnp.concatenate([high, low], 0))
 
 
 def split_dot(values, ones):
@@ -84,7 +87,7 @@
     return jnp.concatenate([tiled[c * 64 : (c + 1) * 64] for c in range(8)], 1)
 
 
-def outbound_list(tiled, names, panel, mask, out):
+def outbound_list(tiled, names, panel, mask, outs):
     source = iota((64, 64), 0)
     target = ocean_number((64, 64), 0)
     picked = dot(one_hot(source, names[0:1, :]), tiled, TN)
@@ -102,8 +105,9 @@
         planes[3].append(f[7])
     pieces = jnp.concatenate([jnp.concatenate(p, 0) for p in planes], 1)
     summed = dot_split(one_hot(target, names[1:2, :]), pieces)
-    for p in range(4):
-        out[p * 64 : (p + 1) * 64, :] = summed[:, p * 128 : (p + 1) * 128]
+    for out in outs:
+        for p in range(4):
+            out[p * 64 : (p + 1) * 64, :] = summed[:, p * 128 : (p + 1) * 128]
 
 
 def fetch(sems, pairs):
@@ -113,30 +117,41 @@
     return copies
 
 
+def outbound_list_out(kind, tiled, table, panels, temp, salt, depth, outs):
+    a, b = kind
+    for out in outs:
+        if out.shape[0] > LIST_ROWS:
+            out[LIST_ROWS:, :] = jnp.zeros((out.shape[0] - LIST_ROWS, 128), F32)
+    if kind == (1, 0):
+        deep = depth[...].astype(F32)
+        levels = [temp[l] for l in range(LEVELS)] + [salt[l] for l in range(LEVELS)] + [deep]
+        block = edge_columns(levels)
+        for out in outs:
+            out[LIST_ROWS : LIST_ROWS + ROWS, :] = block
+    outbound_list(tiled, table[a, b], panels.at[2 * a + b], group_mask(), outs)
+
+
 def outbound_kernel(
-    air_hbm, table_hbm, panels_hbm, temp_hbm, salt_hbm, depth_hbm,
-    to_gx, tiled, table, panels, temp, salt, depth, air, panel, sems,
+    kind, air_hbm, table_hbm, panels_hbm, temp_hbm, salt_hbm, depth_hbm,
+    tiled, table, panels, temp, salt, depth, *rest,
 ):
-    pairs = [(air_hbm, air), (table_hbm, table), (panels_hbm.at[0], panel)]
+    outs, (air, sems) = rest[:-2], rest[-2:]
+    order = [2 * kind[0] + kind[1]]
+    order += [n for n in range(4) if n not in order]
+    pairs = [(air_hbm, air), (table_hbm, table), (panels_hbm.at[order[0]], panels.at[order[0]])]
     pairs += [(temp_hbm, temp), (salt_hbm, salt), (depth_hbm, depth)]
-    copies = fetch(sems, pairs + [(panels_hbm.at[1:4], panels)])
-    mask = group_mask()
+    copies = fetch(sems, pairs + [(panels_hbm.at[n], panels.at[n]) for n in order[1:]])
     copies[0].wait()
-    tiled[...] = spread_air(air, mask)
-    copies[1].wait()
-    copies[2].wait()
-    outbound_list(tiled[...], table[0, 0], panel, mask, to_gx)
-    for copy in copies[3:]:
+    tiled[...] = spread_air(air, group_mask())
+    for copy in copies[1:6]:
         copy.wait()
-
-
-def side_kernel(tiled, table, panels, temp, salt, depth, to_gx, north):
-    mask = group_mask()
-    deep = depth[...].astype(F32)
-    levels = [temp[l] for l in range(LEVELS)] + [salt[l] for l in range(LEVELS)] + [deep]
-    to_gx[LIST_ROWS:, :] = edge_columns(levels)
-    outbound_list(tiled[...], table[1, 0], panels.at[1], mask, to_gx.at[0:LIST_ROWS])
-    outbound_list(tiled[...], table[0, 1], panels.at[0], mask, north)
+    outbound_list_out(kind, tiled[...], table, panels, temp, salt, depth, outs)
+    for copy in copies[6:]:
+        copy.wait()
+
+
+def next_kernel(kind, tiled, table, panels, temp, salt, depth, *outs):
+    outbound_list_out(kind, tiled[...], table, panels, temp, salt, depth, outs)
 
 
 def beside(values, north, south, west, east):
@@ -156,7 +171,12 @@
     return SIDE_RATE * side
 
 
-def inner_kernel(tiled, table, panels, temp, salt, depth, own, partial):
+def inner_kernel(
+    tiled, table, panels, temp, salt, depth, in_table_hbm, own, partial, sources, targets, fold,
+    in_table, sem,
+):
+    copy = pltpu.make_async_copy(in_table_hbm, in_table, sem)
+    copy.start()
     deep = depth[...].astype(F32)
     dry = jnp.zeros((1, 1), F32)
     around = beside(deep, dry, dry, dry, dry)
@@ -167,12 +187,13 @@
             centre = field[l]
             side = side_sum(centre, beside(centre, dry, dry, dry, dry), wets)
             partial[t, l] = centre + jnp.where(wet, side, 0.0)
-    outbound_list(tiled[...], table[1, 1], panels.at[2], group_mask(), own)
-
-
-def north_kernel(part, core, zpair, out):
-    odd_col = lax.axis_index("gx") % 2 == 1
-    out[...] = part[...] + jnp.where(odd_col, zpair[...], core[...])
+    outbound_list(tiled[...], table[1, 1], panels.at[3], group_mask(), (own,))
+    copy.wait()
+    fold[...] = inbound_fold()
+    source_block, target = ocean_number((64, 64), 0), atm_number((64, 64), 0)
+    for n in range(4):
+        sources[n] = one_hot(source_block, in_table[n // 2, n % 2, 0:1, :])
+        targets[n] = one_hot(target, in_table[n // 2, n % 2, 1:2, :])
 
 
 def edge_kernel(own, core, zpair, partial, temp, salt, depth, base, west, east, depths, whole):
@@ -180,8 +201,9 @@
     base[...] = own[...] + jnp.where(
         odd_col, zpair[0:LIST_ROWS, :], core[0:LIST_ROWS, :]
     )
-    left = jnp.where(odd_col, core[LIST_ROWS:, :], zpair[LIST_ROWS:, :])
-    right = jnp.where(odd_col, zpair[LIST_ROWS:, :], core[LIST_ROWS:, :])
+    at = slice(LIST_ROWS, LIST_ROWS + ROWS)
+    left = jnp.where(odd_col, core[at, :], zpair[at, :])
+    right = jnp.where(odd_col, zpair[at, :], core[at, :])
     west[...] = left
     east[...] = right
     deep = depth[...].astype(F32)
@@ -220,15 +242,14 @@
 
 
 def first_kernel(
-    gy, base, west, east, partial, temp, salt, depth, new, cols, row_e, row_o, planes, keep
+    dg, gy, base, partial, temp, salt, depth, new, cols, planes
 ):
-    odd_row = lax.axis_index("gy") % 2 == 1
     forcing = []
     for p in range(4):
         parts = []
         for s in range(TILES):
             at = p * 64 + s * ROWS
-            parts.append(base[at : at + ROWS, :] + gy[at : at + ROWS, :])
+            parts.append(base[at : at + ROWS, :] + gy[at : at + ROWS, :] + dg[at : at + ROWS, :])
         forcing.append(jnp.concatenate(parts, 1))
     squared = forcing[3] * forcing[3]
     forcing[3] = squared / (1.0 + squared)
@@ -252,6 +273,11 @@
             block = jnp.where(lane == at, value[:, 0:1], block)
             block = jnp.where(lane == 64 + at, value[:, COLS - 1 : COLS], block)
     cols[...] = block
+
+
+def rows_kernel(new, temp, salt, depth, west, east, row_e, row_o, keep):
+    odd_row = lax.axis_index("gy") % 2 == 1
+    deep = depth[...].astype(F32)
     edges = []
     for r in (0, ROWS - 1):
         rows = [new[0, :, r, :], new[1, :, r, :], temp[:, r, :], salt[:, r, :], deep[r : r + 1]]
@@ -269,10 +295,9 @@
         keep[41 + 2 * n : 42 + 2 * n, 0:128] = edges[n][6]
 
 
-def inbound_list(blocks, names, panel, fold, mask, out):
-    source_block = ocean_number((64, 64), 0)
-    target = atm_number((64, 64), 0)
-    chosen = dot(one_hot(source_block, names[0:1, :]), blocks, TN)
+def inbound_list(blocks, source, target, panel, fold, out):
+    mask = group_mask()
+    chosen = dot(source, blocks, TN)
     kept = [[], [], [], []]
     for g in range(8):
         part = chosen[g * 8 : (g + 1) * 8]
@@ -284,7 +309,7 @@
             kept[c].append(jnp.where(mask, piece[c * 8 : (c + 1) * 8], 0.0))
     kept = jnp.concatenate([jnp.concatenate(k, 0) for k in kept], 1)
     pieces = split_dot(kept, fold)
-    out[0:64, :] = dot_split(one_hot(target, names[1:2, :]), pieces)
+    out[0:64, :] = dot_split(target, pieces)
 
 
 def inbound_fold():
@@ -293,12 +318,7 @@
     return fold.astype(BF16)
 
 
-def second_kernel(
-    old, core, zpair, xe, xo, planes, depths, keep, depth, table_hbm, panels,
-    final, surface_blocks, to_dg, table, sem,
-):
-    copy = pltpu.make_async_copy(table_hbm, table, sem)
-    copy.start()
+def second_step(levels, old, core, zpair, xe, xo, planes, depths, keep, depth, store):
     odd_col = lax.axis_index("gx") % 2 == 1
     odd_row = lax.axis_index("gy") % 2 == 1
     deep = depth[...].astype(F32)
@@ -337,17 +357,18 @@
     around[1] = jnp.where(row == ROWS - 1, beyond_deep[1], around[1])
     forcing = [planes[p] for p in range(4)]
     mixing = MIX_BASE + MIX_WIND * forcing[3]
-    top = {}
-
     def whole(t, l):
         at = t * LEVELS + l
         high = old[t, l, 0:8, :] + jnp.where(row8 == 0, fixes[0][at : at + 1], 0.0)
         low = old[t, l, 8:16, :] + jnp.where(row8 == 7, fixes[1][at : at + 1], 0.0)
         return jnp.concatenate([high, low], 0)
 
-    for t in range(2):
-        across, centre = None, whole(t, 0)
-        for l in range(LEVELS):
+    for t, (start, stop) in enumerate(levels):
+        across, centre = None, whole(t, start)
+        if start:
+            across = mixing * (MIX_DECAY ** (start - 1)) * (centre - whole(t, start - 1))
+            across = jnp.where(deep > start, across, 0.0)
+        for l in range(start, stop):
             at = t * LEVELS + l
             below = whole(t, l + 1) if l < LEVELS - 1 else None
             change, across = column_change(centre, below, mixing, deep, l, across)
@@ -360,11 +381,22 @@
                 east[:, at : at + 1],
             )
             change = change + side_sum(centre, nears, [d > l for d in around])
-            value = centre + jnp.where(deep > l, change, 0.0)
-            final[t, l] = value
-            if l < 3:
-                top[t, l] = value
+            store(t, l, centre + jnp.where(deep > l, change, 0.0))
             centre = below
+
+
+def second_kernel(
+    old, core, zpair, xe, xo, planes, depths, keep, depth, sources, targets, fold, panels,
+    top_temp, top_salt, surface_blocks, out,
+):
+    top = {}
+
+    def store(t, l, value):
+        (top_temp, top_salt)[t][l] = value
+        top[t, l] = value
+
+    second_step(TOP_LEVELS, old, core, zpair, xe, xo, planes, depths, keep, depth, store)
+    deep = depth[...].astype(F32)
     wet_top = jnp.where(deep > 0, 1.0, 0.0)
     surface = (
         top[0, 0] * wet_top,
@@ -377,21 +409,37 @@
         parts.append(jnp.concatenate([f[:, s * 128 : (s + 1) * 128] for s in range(TILES)], 0))
     blocks = jnp.concatenate(parts, 1).astype(BF16)
     surface_blocks[...] = blocks
-    copy.wait()
-    inbound_list(blocks, table[1, 1], panels.at[3], inbound_fold(), group_mask(), to_dg)
-    to_dg[64:, :] = jnp.zeros((16, 128), F32)
-
-
-def inbound_kernel(a, b, blocks, table, panels, out):
-    fold, mask = inbound_fold(), group_mask()
-    inbound_list(blocks[...], table[a, b], panels.at[2 * a + b], fold, mask, out)
+    inbound_kernel(*SURFACE_ORDER[0], surface_blocks, sources, targets, fold, panels, out)
+
+
+def inbound_kernel(a, b, blocks, sources, targets, fold, panels, out):
+    n = 2 * a + b
+    inbound_list(blocks[...], sources[n], targets[n], panels.at[n], fold[...], out)
     if out.shape[0] > 64:
         out[64:, :] = jnp.zeros((out.shape[0] - 64, 128), F32)
 
 
-def outer_kernel(final, blocks, table, panels, new_temp, new_salt, own, sems):
-    copies = fetch(sems, [(final.at[0], new_temp), (final.at[1], new_salt)])
-    inbound_kernel(0, 0, blocks, table, panels, own)
+def outer_kernel(
+    old, core, zpair, xe, xo, planes, depths, keep, depth, top_temp, top_salt,
+    blocks, sources, targets, fold, panels, new_temp, new_salt, own, rest, sems,
+):
+    pairs = []
+    for t, (top, new) in enumerate(((top_temp, new_temp), (top_salt, new_salt))):
+        count = TOP_LEVELS[t][1]
+        pairs.append((top, new.at[0:count]))
+    copies = fetch(sems.at[0:2], pairs)
+
+    def store(t, l, value):
+        rest[t, l] = value
+
+    levels = [(stop, LEVELS) for _, stop in TOP_LEVELS]
+    second_step(levels, old, core, zpair, xe, xo, planes, depths, keep, depth, store)
+    pairs = []
+    for t, new in enumerate((new_temp, new_salt)):
+        span = slice(TOP_LEVELS[t][1], LEVELS)
+        pairs.append((rest.at[t, span], new.at[span]))
+    copies += fetch(sems.at[2:4], pairs)
+    inbound_kernel(0, 0, blocks, sources, targets, fold, panels, own)
     for copy in copies:
         copy.wait()
 
@@ -445,86 +493,104 @@
     return (i, other_pair(j)) if 0 <= other_pair(j) < lax.axis_size("gy") else (pair(i), j)
 
 
+def outbound_shapes(n):
+    rows = LIST_ROWS + ROWS
+    shapes = [(rows + 8 * (3 - n), 128)]
+    return shapes + [(rows, 128)] if FORCING_ORDER[n] == (1, 0) else shapes
+
+
 def per_device(air, out_tables, out_panels, depth, temp, salt, in_tables, in_panels):
     out_panels = out_panels.reshape(4, 1024, 128)
     in_panels = in_panels.reshape(4, 1024, 128)
     out_tables, in_tables = out_tables[0, 0], in_tables[0, 0]
     field = (2, LEVELS, ROWS, COLS)
-    to_gx, tiled, out_tables, out_panels, temp, salt, depth = call(
-        outbound_kernel,
+    tiled, out_tables, out_panels, temp, salt, depth, *first = call(
+        functools.partial(outbound_kernel, FORCING_ORDER[0]),
         [
-            (LIST_ROWS, 128),
             jax.ShapeDtypeStruct((64, 1024), BF16),
             jax.ShapeDtypeStruct(out_tables.shape, jnp.int32),
-            jax.ShapeDtypeStruct((3, 1024, 128), BF16),
+            jax.ShapeDtypeStruct((4, 1024, 128), BF16),
             temp.shape,
             salt.shape,
             jax.ShapeDtypeStruct(depth.shape, jnp.int32),
-        ],
+        ] + outbound_shapes(0),
         [air, out_tables, out_panels, temp, salt, depth],
-        [
-            pltpu.VMEM(air.shape, BF16),
-            pltpu.VMEM((1024, 128), BF16),
-            pltpu.SemaphoreType.DMA((7,)),
-        ],
+        [pltpu.VMEM(air.shape, BF16), pltpu.SemaphoreType.DMA((9,))],
         hbm_in=range(6),
     )
-    zpair = send(to_gx, lambda i, j: (other_pair(i), j))
-    core = send(to_gx, lambda i, j: (pair(i), j))
-    to_side, north = call(
-        side_kernel,
-        [(LIST_ROWS + ROWS, 128), (LIST_ROWS, 128)],
-        [tiled, out_tables, out_panels, temp, salt, depth],
-    )
-    side_z = send(to_side, lambda i, j: (other_pair(i), j))
-    side_core = send(to_side, lambda i, j: (pair(i), j))
-    (to_gy,) = call(north_kernel, [north.shape], [north, core, zpair])
-    gy = send(to_gy, lambda i, j: (i, j - 1))
-    own, partial = call(
+    got = {}
+    for n, kind in enumerate(FORCING_ORDER):
+        blocks = first
+        if n:
+            blocks = call(
+                functools.partial(next_kernel, kind),
+                outbound_shapes(n),
+                [tiled, out_tables, out_panels, temp, salt, depth],
+            )
+        if kind == (0, 0):
+            got["dg"] = send(blocks[0], lambda i, j: (i - 1, j - 1) if j else (i, j - 1))
+        if kind == (0, 1):
+            got["gy"] = send(blocks[0], lambda i, j: (i, j - 1))
+        if kind == (1, 0):
+            got["z"] = send(blocks[0], lambda i, j: (other_pair(i), j))
+            got["core"] = send(blocks[1], lambda i, j: (pair(i), j))
+    dg, gy, zpair, core = got["dg"], got["gy"], got["z"], got["core"]
+    ones = jax.ShapeDtypeStruct((4, 64, 64), BF16)
+    own, partial, *maps = call(
         inner_kernel,
-        [(LIST_ROWS, 128), field],
-        [tiled, out_tables, out_panels, temp, salt, depth],
+        [(LIST_ROWS, 128), field, ones, ones, jax.ShapeDtypeStruct((512, 128), BF16)],
+        [tiled, out_tables, out_panels, temp, salt, depth, in_tables],
+        [pltpu.VMEM(in_tables.shape, jnp.int32), pltpu.SemaphoreType.DMA],
+        hbm_in=(6,),
     )
     base, west, east, depths, partial = call(
         edge_kernel,
         [(LIST_ROWS, 128), (ROWS, 128), (ROWS, 128), (4, ROWS, COLS), field],
-        [own, side_core, side_z, partial, temp, salt, depth],
-    )
-    stepped, cols, row_e, row_o, planes, keep = call(
+        [own, core, zpair, partial, temp, salt, depth],
+    )
+    stepped, cols, planes = call(
         first_kernel,
-        [field, (ROWS, 128), (43, COLS), (48, COLS), (4, ROWS, COLS), (44, COLS)],
-        [gy, base, west, east, partial, temp, salt, depth],
+        [field, (ROWS, 128), (4, ROWS, COLS)],
+        [dg, gy, base, partial, temp, salt, depth],
+    )
+    row_e, row_o, keep = call(
+        rows_kernel,
+        [(43, COLS), (48, COLS), (44, COLS)],
+        [stepped, temp, salt, depth, west, east],
     )
     xo = send(row_o, row_pair)
     xe = send(row_e, lambda i, j: (i, pair(j)))
     zpair = send(cols, lambda i, j: (other_pair(i), j))
     core = send(cols, lambda i, j: (pair(i), j))
-    final, blocks, to_dg, in_tables = call(
+    state = [stepped, core, zpair, xe, xo, planes, depths, keep, depth]
+    top_temp, top_salt, blocks, *first = call(
         second_kernel,
         [
-            field,
+            (TOP_LEVELS[0][1], ROWS, COLS),
+            (TOP_LEVELS[1][1], ROWS, COLS),
             jax.ShapeDtypeStruct((64, COLS), BF16),
             (80, 128),
-            jax.ShapeDtypeStruct(in_tables.shape, jnp.int32),
         ],
-        [stepped, core, zpair, xe, xo, planes, depths, keep, depth, in_tables, in_panels],
-        [pltpu.SemaphoreType.DMA],
-        hbm_in=(9,),
-    )
-    dg = send(to_dg, lambda i, j: (i + 1, j + 1) if j + 1 < lax.axis_size("gy") else (i, j + 1))
-    (to_gy,) = call(
-        functools.partial(inbound_kernel, 1, 0), [(72, 128)], [blocks, in_tables, in_panels]
-    )
-    gy = send(to_gy, lambda i, j: (i, j + 1))
-    (to_gx,) = call(
-        functools.partial(inbound_kernel, 0, 1), [(64, 128)], [blocks, in_tables, in_panels]
-    )
-    gx = send(to_gx, lambda i, j: (i + 1, j))
+        state + maps + [in_panels],
+    )
+    got = {}
+    for n, kind in enumerate(SURFACE_ORDER):
+        block = first
+        if n:
+            kernel = functools.partial(inbound_kernel, *kind)
+            block = call(kernel, [(80 - 8 * n, 128)], [blocks, *maps, in_panels])
+        steps = {
+            (1, 1): lambda i, j: (i + 1, j + 1) if j + 1 < lax.axis_size("gy") else (i, j + 1),
+            (1, 0): lambda i, j: (i, j + 1),
+            (0, 1): lambda i, j: (i + 1, j),
+        }
+        got[kind] = send(block[0], steps[kind])
+    dg, gy, gx = got[1, 1], got[1, 0], got[0, 1]
     new_temp, new_salt, own = call(
         outer_kernel,
         [temp.shape, salt.shape, (64, 128)],
-        [final, blocks, in_tables, in_panels],
-        [pltpu.SemaphoreType.DMA((2,))],
+        state + [top_temp, top_salt, blocks, *maps, in_panels],
+        [pltpu.VMEM(field, F32), pltpu.SemaphoreType.DMA((4,))],
         hbm_out=(0, 1),
     )
     (surface,) = call(final_kernel, [(4, 8, 128)], [dg, gy, gx, own])

time: 35.1 us -> 33.4 us (0.952)
  starting transfers between devices: 16.7 us -> 13.7 us
  Pallas kernels: 8.53 us -> 9.46 us
  waiting for transfers between devices: 8.6 us -> 9.06 us
    ppermute x12 -> x11, starting transfers between devices: 16.7 us -> 13.7 us  [send(): return lax.ppermute(block, ('gx', 'gy'), route)]
    pallas_call x11 -> x12, Pallas kernels: 8.53 us -> 9.46 us  [call(): pl.pallas_call(kernel, out_shape=shapes, in_specs=[HBM if n in hbm_in els...]
    ppermute x12 -> x11, waiting for transfers between devices: 8.6 us -> 9.06 us  [send(): return lax.ppermute(block, ('gx', 'gy'), route)]
  transfers between devices with their start and end apart: 12 -> 11, of which waited for: 6 -> 5; matrix products, arithmetic and copies ran while one was open for 0% -> 0% of each run, Pallas kernels for 12% -> 17%
where the time goes in v7:
time: 33.4 us; the launch traced here: 32.9 us
  starting transfers between devices  13.7 us (41%)
  Pallas kernels  9.46 us (28%)
  waiting for transfers between devices  9.06 us (27%)
  between operations  0.71 us (2%)
    ppermute x11, starting transfers between devices, send(): return lax.ppermute(block, ('gx', 'gy'), route)  13.7 us
    pallas_call x12, Pallas kernels, call(): pl.pallas_call(kernel, out_shape=shapes, in_specs=[HBM if n in hbm_in els...  9.46 us
    ppermute x11, waiting for transfers between devices, send(): return lax.ppermute(block, ('gx', 'gy'), route)  9.06 us
  transfers between devices with their start and end apart: 11, of which 5 were waited for; matrix products, arithmetic and copies ran while one was open for 0% of the time, Pallas kernels for 17%

profile of v7, /device:TPU:8, one launch (start us, length us, event | category | flops | bytes accessed | tf_op | source)
XLA Modules:
  0.0 32.9 jit_solution(6376134995665127102)
XLA Ops:
  0.6 1.8 %shard_map.103 = (bf16[64,1024]{1,0:T(8,128)(2,1)S(1)}, s32[2,2,2,64]{3,2,1,0:T(2,128)S(1)}, bf16[4,1024,128]{2,1,0:T(8,128)(2,1)S(1)}, f32[10,16,512]{2,1,0:T(8...) custom-call(bf16[8,8,128]{2,1,0:T(8,128)(2,1)} %air_hbm.1, ...), custom_call_target="tpu_custom_call" | custom-call | tf_op jit(solution)/shard_map/pallas_call | solution.py:464
  2.5 5.6 %collective-permute-start = (f32[296,128]{1,0:T(8,128)S(1)}, f32[296,128]{1,0:T(8,128)S(1)}, u32[]{:S(2)}, u32[]{:S(2)}) collective-permute-start(f32[296,128]{1,0:T(8,128)S(1)} %get-tuple-element.35), channel_id=1, source_target_pairs={{0,15},{1,112},{2,113},{3,114},{4,115},{5,116},{6,117},{7,118},{8,... | collective-permute-start | bytes 454664 | tf_op jit(solution)/shard_map/ppermute | solution.py:481
  8.1 0.5 %shard_map.106 = (f32[288,128]{1,0:T(8,128)S(1)}, f32[272,128]{1,0:T(8,128)S(1)}) custom-call(bf16[64,1024]{1,0:T(8,128)(2,1)S(1)} %get-tuple-element.36.tiled, s32[2,2,2,64]{3,2,1,0:T(2,128)S(1)} %get-tuple-element.37.table, bf16[4,1024,128]{2,1,0:T(8,128)(2,1)S(1)} %get-tuple-element.38.panels, f32[10,16,512]{2,1,0:T(8,128)S(1)} %get-tuple-element.39.temp, ...), custom_call_target="tpu_custom_call" | custom-call | tf_op jit(solution)/shard_map/pallas_call | solution.py:464
  8.6 0.9 %collective-permute-start.3 = (f32[288,128]{1,0:T(8,128)S(1)}, f32[288,128]{1,0:T(8,128)S(1)}, u32[]{:S(2)}, u32[]{:S(2)}) collective-permute-start(f32[288,128]{1,0:T(8,128)S(1)} %get-tuple-element.44), channel_id=1, source_target_pairs={{0,112},{1,113},{2,114},{3,115},{4,116},{5,117},{6,118},{7,119},{8... | collective-permute-start | bytes 442376 | tf_op jit(solution)/shard_map/ppermute | solution.py:481
  9.5 0.5 %shard_map.104 = f32[280,128]{1,0:T(8,128)S(1)} custom-call(bf16[64,1024]{1,0:T(8,128)(2,1)S(1)} %get-tuple-element.36.tiled, s32[2,2,2,64]{3,2,1,0:T(2,128)S(1)} %get-tuple-element.37.table, bf16[4,1024,128]{2,1,0:T(8,128)(2,1)S(1)} %get-tuple-element.38.panels, f32[10,16,512]{2,1,0:T(8,128)S(1)} %get-tuple-element.39.temp, ...), custom_call_target="tpu_custom_call" | custom-call | tf_op jit(solution)/shard_map/pallas_call | solution.py:464
  10.0 0.9 %collective-permute-start.1 = (f32[280,128]{1,0:T(8,128)S(1)}, f32[280,128]{1,0:T(8,128)S(1)}, u32[]{:S(2)}, u32[]{:S(2)}) collective-permute-start(f32[280,128]{1,0:T(8,128)S(1)} %shard_map.104), channel_id=1, source_target_pairs={{0,15},{1,0},{2,1},{3,2},{4,3},{5,4},{6,5},{7,6},{8,7},{9,8},{10,9... | collective-permute-start | bytes 430088 | tf_op jit(solution)/shard_map/ppermute | solution.py:481
  11.0 0.0 collective-permute-start.2
  11.0 1.3 %shard_map.105 = (f32[256,128]{1,0:T(8,128)S(1)}, f32[2,10,16,512]{3,2,1,0:T(8,128)S(1)}, bf16[4,64,64]{2,1,0:T(8,128)(2,1)S(1)}, bf16[4,64,64]{2,1,0:T(8,128)(2,1)S(1)}, bf16[512,128]{1,0:T(8,128)(2,1)S(1)}) custom-call(bf16[64,1024]{1,0:T(8,128)(2,1)S(1)} %get-tuple-element.36.tiled, s32[2,2,2,64]{3,2,1,0:T(2,128)S(1)} %get-tuple-element.37.table, ...), custom_call_target="tpu_custom_call" | custom-call | tf_op jit(solution)/shard_map/pallas_call | solution.py:464
  12.3 0.0 collective-permute-done.2.core
  12.3 2.2 %collective-permute-done.3.zpair = f32[288,128]{1,0:T(8,128)S(1)} collective-permute-done((f32[288,128]{1,0:T(8,128)S(1)}, f32[288,128]{1,0:T(8,128)S(1)}, u32[]{:S(2)}, u32[]{:S(2)}) %collective-permute-start.3) | collective-permute-done | bytes 147488 | tf_op jit(solution)/shard_map/ppermute | solution.py:481
  14.5 0.2 shard_map.107
  14.7 0.5 %collective-permute-done.1.gy = f32[280,128]{1,0:T(8,128)S(1)} collective-permute-done((f32[280,128]{1,0:T(8,128)S(1)}, f32[280,128]{1,0:T(8,128)S(1)}, u32[]{:S(2)}, u32[]{:S(2)}) %collective-permute-start.1) | collective-permute-done | bytes 143392 | tf_op jit(solution)/shard_map/ppermute | solution.py:481
  15.2 0.0 collective-permute-done.dg
  15.2 0.3 %shard_map.108 = (f32[2,10,16,512]{3,2,1,0:T(8,128)S(1)}, f32[16,128]{1,0:T(8,128)S(1)}, f32[4,16,512]{2,1,0:T(8,128)S(1)}) custom-call(f32[296,128]{1,0:T(8,128)S(1)} %collective-permute-done.dg, f32[280,128]{1,0:T(8,128)S(1)} %collective-permute-done.1.gy, f32[256,128]{1,0:T(8,128)S(1)} %get-tuple-element.46.base, ...), custom_call_target="tpu_custom_call" | custom-call | tf_op jit(solution)/shard_map/pallas_call | solution.py:464
  15.6 0.0 copy-start
  15.6 0.1 shard_map.109
  15.7 3.0 %collective-permute-start.7 = (f32[48,512]{1,0:T(8,128)S(1)}, f32[48,512]{1,0:T(8,128)S(1)}, u32[]{:S(2)}, u32[]{:S(2)}) collective-permute-start(f32[48,512]{1,0:T(8,128)S(1)} %get-tuple-element.53), channel_id=1, source_target_pairs={{0,16},{1,2},{2,1},{3,4},{4,3},{5,6},{6,5},{7,8},{8,7},{9,10},{10,... | collective-permute-start | bytes 294920 | tf_op jit(solution)/shard_map/ppermute | solution.py:481
  18.7 0.0 collective-permute-start.6
  18.7 1.5 %collective-permute-start.5 = (f32[16,128]{1,0:T(8,128)S(1)}, f32[16,128]{1,0:T(8,128)S(1)}, u32[]{:S(2)}, u32[]{:S(2)}) collective-permute-start(f32[16,128]{1,0:T(8,128)S(1)} %get-tuple-element.49), channel_id=1, source_target_pairs={{0,112},{1,113},{2,114},{3,115},{4,116},{5,117},{6,118},{7,119},{8... | collective-permute-start | bytes 24584 | tf_op jit(solution)/shard_map/ppermute | solution.py:481
  20.2 0.0 collective-permute-start.4
  20.2 2.8 %collective-permute-done.5.zpair = f32[16,128]{1,0:T(8,128)S(1)} collective-permute-done((f32[16,128]{1,0:T(8,128)S(1)}, f32[16,128]{1,0:T(8,128)S(1)}, u32[]{:S(2)}, u32[]{:S(2)}) %collective-permute-start.5) | collective-permute-done | bytes 8224 | tf_op jit(solution)/shard_map/ppermute | solution.py:481
  23.0 0.0 collective-permute-done.4.core
  23.0 0.3 collective-permute-done.6.xe
  23.3 0.0 collective-permute-done.7.xo
  23.3 0.0 copy-done
  23.3 0.9 %shard_map.110 = (f32[3,16,512]{2,1,0:T(8,128)S(1)}, f32[1,16,512]{2,1,0:T(8,128)S(1)}, bf16[64,512]{1,0:T(8,128)(2,1)S(1)}, f32[80,128]{1,0:T(8,128)S(1)}) custom-call(f32[2,10,16,512]{3,2,1,0:T(8,128)S(1)} %get-tuple-element.48.new.old, f32[16,128]{1,0:T(8,128)S(1)} %collective-permute-done.4.core, f32[16,128]{1,0:T(8,128)S(1)} %collective-permute-done.5.zpair, ...), custom_call_target="tpu_custom_call" | custom-call | tf_op jit(solution)/shard_map/pallas_call | solution.py:464
  24.2 0.0 collective-permute-start.8
  24.2 0.7 %shard_map.112 = f32[72,128]{1,0:T(8,128)S(1)} custom-call(bf16[64,512]{1,0:T(8,128)(2,1)S(1)} %get-tuple-element.62.blocks, bf16[4,64,64]{2,1,0:T(8,128)(2,1)S(1)} %get-tuple-element.57.sources, bf16[4,64,64]{2,1,0:T(8,128)(2,1)S(1)} %get-tuple-element.58.targets, bf16[512,128]{1,0:T(8,128)(2,1)S(1)} %get-tuple-element.59.fold, ...), custom_call_target="tpu_custom_call" | custom-call | tf_op jit(solution)/shard_map/pallas_call | solution.py:464
  24.9 1.7 %collective-permute-start.9 = (f32[72,128]{1,0:T(8,128)S(1)}, f32[72,128]{1,0:T(8,128)S(1)}, u32[]{:S(2)}, u32[]{:S(2)}) collective-permute-start(f32[72,128]{1,0:T(8,128)S(1)} %shard_map.112), channel_id=1, source_target_pairs={{0,1},{1,2},{2,3},{3,4},{4,5},{5,6},{6,7},{7,8},{8,9},{9,10},{10,1... | collective-permute-start | bytes 110600 | tf_op jit(solution)/shard_map/ppermute | solution.py:481
  26.6 0.7 %shard_map.113 = f32[64,128]{1,0:T(8,128)S(1)} custom-call(bf16[64,512]{1,0:T(8,128)(2,1)S(1)} %get-tuple-element.62.blocks, bf16[4,64,64]{2,1,0:T(8,128)(2,1)S(1)} %get-tuple-element.57.sources, bf16[4,64,64]{2,1,0:T(8,128)(2,1)S(1)} %get-tuple-element.58.targets, bf16[512,128]{1,0:T(8,128)(2,1)S(1)} %get-tuple-element.59.fold, ...), custom_call_target="tpu_custom_call" | custom-call | tf_op jit(solution)/shard_map/pallas_call | solution.py:464
  27.3 0.0 collective-permute-start.10
  27.3 1.7 %shard_map.111 = (f32[10,16,512]{2,1,0:T(8,128)}, f32[10,16,512]{2,1,0:T(8,128)}, f32[64,128]{1,0:T(8,128)S(1)}) custom-call(f32[2,10,16,512]{3,2,1,0:T(8,128)S(1)} %get-tuple-element.48.new.old, f32[16,128]{1,0:T(8,128)S(1)} %collective-permute-done.4.core, f32[16,128]{1,0:T(8,128)S(1)} %collective-permute-done.5.zpair, ...), custom_call_target="tpu_custom_call" | custom-call | tf_op jit(solution)/shard_map/pallas_call | solution.py:464
  29.0 3.2 %collective-permute-done.10.gx = f32[64,128]{1,0:T(8,128)S(1)} collective-permute-done((f32[64,128]{1,0:T(8,128)S(1)}, f32[64,128]{1,0:T(8,128)S(1)}, u32[]{:S(2)}, u32[]{:S(2)}) %collective-permute-start.10) | collective-permute-done | bytes 32800 | tf_op jit(solution)/shard_map/ppermute | solution.py:481
  32.2 0.0 collective-permute-done.9.gy
  32.2 0.0 collective-permute-done.8.dg
  32.2 0.7 %shard_map.114 = f32[4,8,128]{2,1,0:T(8,128)} custom-call(f32[80,128]{1,0:T(8,128)S(1)} %collective-permute-done.8.dg, f32[72,128]{1,0:T(8,128)S(1)} %collective-permute-done.9.gy, f32[64,128]{1,0:T(8,128)S(1)} %collective-permute-done.10.gx, f32[64,128]{1,0:T(8,128)S(1)} %get-tuple-element.66.own), custom_call_target="tpu_custom_call" | custom-call | tf_op jit(solution)/shard_map/pallas_call | solution.py:464
Async XLA Ops:
  2.5 12.8 %collective-permute-start = (f32[296,128]{1,0:T(8,128)S(1)}, f32[296,128]{1,0:T(8,128)S(1)}, u32[]{:S(2)}, u32[]{:S(2)}) collective-permute-start(f32[296,128]{1,0:T(8,128)S(1)} %get-tuple-element.35), channel_id=1, source_target_pairs={{0,15},{1,112},{2,113},{3,114},{4,115},{5,116},{6,117},{7,118},{8,... | collective-permute-start | bytes 454664 | tf_op jit(solution)/shard_map/ppermute | solution.py:481
  8.6 5.9 %collective-permute-start.3 = (f32[288,128]{1,0:T(8,128)S(1)}, f32[288,128]{1,0:T(8,128)S(1)}, u32[]{:S(2)}, u32[]{:S(2)}) collective-permute-start(f32[288,128]{1,0:T(8,128)S(1)} %get-tuple-element.44), channel_id=1, source_target_pairs={{0,112},{1,113},{2,114},{3,115},{4,116},{5,117},{6,118},{7,119},{8... | collective-permute-start | bytes 442376 | tf_op jit(solution)/shard_map/ppermute | solution.py:481
  10.0 5.2 %collective-permute-start.1 = (f32[280,128]{1,0:T(8,128)S(1)}, f32[280,128]{1,0:T(8,128)S(1)}, u32[]{:S(2)}, u32[]{:S(2)}) collective-permute-start(f32[280,128]{1,0:T(8,128)S(1)} %shard_map.104), channel_id=1, source_target_pairs={{0,15},{1,0},{2,1},{3,2},{4,3},{5,4},{6,5},{7,6},{8,7},{9,8},{10,9... | collective-permute-start | bytes 430088 | tf_op jit(solution)/shard_map/ppermute | solution.py:481
  11.0 1.4 %collective-permute-start.2 = (f32[272,128]{1,0:T(8,128)S(1)}, f32[272,128]{1,0:T(8,128)S(1)}, u32[]{:S(2)}, u32[]{:S(2)}) collective-permute-start(f32[272,128]{1,0:T(8,128)S(1)} %get-tuple-element.43), channel_id=1, source_target_pairs={{0,16},{1,17},{2,18},{3,19},{4,20},{5,21},{6,22},{7,23},{8,24},{9,... | collective-permute-start | bytes 417800 | tf_op jit(solution)/shard_map/ppermute | solution.py:481
  15.6 7.8 %copy-start = (bf16[1,1,2,2,64,16,128]{6,5,4,3,2,1,0:T(8,128)(2,1)S(1)}, bf16[1,1,2,2,64,16,128]{6,5,4,3,2,1,0:T(8,128)(2,1)}, u32[]{:S(2)}) copy-start(bf16[1,1,2,2,64,16,128]{6,5,4,3,2,1,0:T(8,128)(2,1)} %param.15) | copy-start | bytes 3145732
  15.7 7.6 %collective-permute-start.7 = (f32[48,512]{1,0:T(8,128)S(1)}, f32[48,512]{1,0:T(8,128)S(1)}, u32[]{:S(2)}, u32[]{:S(2)}) collective-permute-start(f32[48,512]{1,0:T(8,128)S(1)} %get-tuple-element.53), channel_id=1, source_target_pairs={{0,16},{1,2},{2,1},{3,4},{4,3},{5,6},{6,5},{7,8},{8,7},{9,10},{10,... | collective-permute-start | bytes 294920 | tf_op jit(solution)/shard_map/ppermute | solution.py:481
  18.7 4.6 %collective-permute-start.6 = (f32[43,512]{1,0:T(8,128)S(1)}, f32[43,512]{1,0:T(8,128)S(1)}, u32[]{:S(2)}, u32[]{:S(2)}) collective-permute-start(f32[43,512]{1,0:T(8,128)S(1)} %get-tuple-element.52), channel_id=1, source_target_pairs={{0,1},{1,0},{2,3},{3,2},{4,5},{5,4},{6,7},{7,6},{8,9},{9,8},{10,11... | collective-permute-start | bytes 264200 | tf_op jit(solution)/shard_map/ppermute | solution.py:481
  18.7 4.3 %collective-permute-start.5 = (f32[16,128]{1,0:T(8,128)S(1)}, f32[16,128]{1,0:T(8,128)S(1)}, u32[]{:S(2)}, u32[]{:S(2)}) collective-permute-start(f32[16,128]{1,0:T(8,128)S(1)} %get-tuple-element.49), channel_id=1, source_target_pairs={{0,112},{1,113},{2,114},{3,115},{4,116},{5,117},{6,118},{7,119},{8... | collective-permute-start | bytes 24584 | tf_op jit(solution)/shard_map/ppermute | solution.py:481
  20.2 2.8 %collective-permute-start.4 = (f32[16,128]{1,0:T(8,128)S(1)}, f32[16,128]{1,0:T(8,128)S(1)}, u32[]{:S(2)}, u32[]{:S(2)}) collective-permute-start(f32[16,128]{1,0:T(8,128)S(1)} %get-tuple-element.49), channel_id=1, source_target_pairs={{0,16},{1,17},{2,18},{3,19},{4,20},{5,21},{6,22},{7,23},{8,24},{9,... | collective-permute-start | bytes 24584 | tf_op jit(solution)/shard_map/ppermute | solution.py:481
  24.2 8.0 %collective-permute-start.8 = (f32[80,128]{1,0:T(8,128)S(1)}, f32[80,128]{1,0:T(8,128)S(1)}, u32[]{:S(2)}, u32[]{:S(2)}) collective-permute-start(f32[80,128]{1,0:T(8,128)S(1)} %get-tuple-element.65), channel_id=1, source_target_pairs={{0,17},{1,18},{2,19},{3,20},{4,21},{5,22},{6,23},{7,24},{8,25},{9,... | collective-permute-start | bytes 122888 | tf_op jit(solution)/shard_map/ppermute | solution.py:481
  24.9 7.3 %collective-permute-start.9 = (f32[72,128]{1,0:T(8,128)S(1)}, f32[72,128]{1,0:T(8,128)S(1)}, u32[]{:S(2)}, u32[]{:S(2)}) collective-permute-start(f32[72,128]{1,0:T(8,128)S(1)} %shard_map.112), channel_id=1, source_target_pairs={{0,1},{1,2},{2,3},{3,4},{4,5},{5,6},{6,7},{7,8},{8,9},{9,10},{10,1... | collective-permute-start | bytes 110600 | tf_op jit(solution)/shard_map/ppermute | solution.py:481
  27.3 4.9 %collective-permute-start.10 = (f32[64,128]{1,0:T(8,128)S(1)}, f32[64,128]{1,0:T(8,128)S(1)}, u32[]{:S(2)}, u32[]{:S(2)}) collective-permute-start(f32[64,128]{1,0:T(8,128)S(1)} %shard_map.113), channel_id=1, source_target_pairs={{0,16},{1,17},{2,18},{3,19},{4,20},{5,21},{6,22},{7,23},{8,24},{9,... | collective-permute-start | bytes 98312 | tf_op jit(solution)/shard_map/ppermute | solution.py:481

commit v8 on v7

--- a/solution.py
+++ b/solution.py
@@ -1,5 +1,3 @@
-import functools
-
 import jax
 import jax.numpy as jnp
 from jax import lax
@@ -19,9 +17,7 @@
 TILES = COLS // 128
 F32, BF16 = jnp.float32, jnp.bfloat16
 LIST_ROWS = 4 * 64
-FORCING_ORDER = ((0, 0), (1, 0), (0, 1))
 TOP_LEVELS = ((0, 3), (0, 1))
-SURFACE_ORDER = ((1, 1), (1, 0), (0, 1))
 VMEM = pl.BlockSpec(memory_space=pltpu.VMEM)
 HBM = pl.BlockSpec(memory_space=pltpu.HBM)
 NN = (((1,), (0,)), ((), ()))
@@ -87,27 +83,33 @@
     return jnp.concatenate([tiled[c * 64 : (c + 1) * 64] for c in range(8)], 1)
 
 
-def outbound_list(tiled, names, panel, mask, outs):
+def outbound_lists(kinds, tiled, table, panels, outs):
+    mask = group_mask()
     source = iota((64, 64), 0)
     target = ocean_number((64, 64), 0)
-    picked = dot(one_hot(source, names[0:1, :]), tiled, TN)
-    planes = [[], [], [], []]
-    for g in range(8):
-        left = [
-            jnp.where(mask, picked[g * 8 : (g + 1) * 8, c * 128 : (c + 1) * 128], 0.0)
-            for c in range(8)
-        ]
-        piece = dot(jnp.concatenate(left, 0).astype(BF16), panel[g * 128 : (g + 1) * 128, :])
-        f = [piece[c * 8 : (c + 1) * 8] for c in range(8)]
-        planes[0].append(f[0] + f[1] + f[2])
-        planes[1].append(f[3])
-        planes[2].append(f[4] - f[5] + f[6])
-        planes[3].append(f[7])
-    pieces = jnp.concatenate([jnp.concatenate(p, 0) for p in planes], 1)
-    summed = dot_split(one_hot(target, names[1:2, :]), pieces)
-    for out in outs:
-        for p in range(4):
-            out[p * 64 : (p + 1) * 64, :] = summed[:, p * 128 : (p + 1) * 128]
+    ones = jnp.concatenate([one_hot(source, table[a, b, 0:1, :]) for a, b in kinds], 1)
+    picked = dot(ones, tiled, TN)
+    pieces = []
+    for n, (a, b) in enumerate(kinds):
+        planes = [[], [], [], []]
+        for g in range(8):
+            part = picked[n * 64 + g * 8 : n * 64 + (g + 1) * 8]
+            left = [jnp.where(mask, part[:, c * 128 : (c + 1) * 128], 0.0) for c in range(8)]
+            piece = dot(
+                jnp.concatenate(left, 0).astype(BF16),
+                panels[2 * a + b, g * 128 : (g + 1) * 128, :],
+            )
+            f = [piece[c * 8 : (c + 1) * 8] for c in range(8)]
+            planes[0].append(f[0] + f[1] + f[2])
+            planes[1].append(f[3])
+            planes[2].append(f[4] - f[5] + f[6])
+            planes[3].append(f[7])
+        pieces.append(jnp.concatenate([jnp.concatenate(p, 0) for p in planes], 1))
+    for (a, b), values, places in zip(kinds, pieces, outs):
+        summed = dot_split(one_hot(target, table[a, b, 1:2, :]), values)
+        for out in places:
+            for p in range(4):
+                out[p * 64 : (p + 1) * 64, :] = summed[:, p * 128 : (p + 1) * 128]
 
 
 def fetch(sems, pairs):
@@ -117,41 +119,29 @@
     return copies
 
 
-def outbound_list_out(kind, tiled, table, panels, temp, salt, depth, outs):
-    a, b = kind
-    for out in outs:
-        if out.shape[0] > LIST_ROWS:
-            out[LIST_ROWS:, :] = jnp.zeros((out.shape[0] - LIST_ROWS, 128), F32)
-    if kind == (1, 0):
-        deep = depth[...].astype(F32)
-        levels = [temp[l] for l in range(LEVELS)] + [salt[l] for l in range(LEVELS)] + [deep]
-        block = edge_columns(levels)
-        for out in outs:
-            out[LIST_ROWS : LIST_ROWS + ROWS, :] = block
-    outbound_list(tiled, table[a, b], panels.at[2 * a + b], group_mask(), outs)
-
-
 def outbound_kernel(
-    kind, air_hbm, table_hbm, panels_hbm, temp_hbm, salt_hbm, depth_hbm,
-    tiled, table, panels, temp, salt, depth, *rest,
+    air_hbm, table_hbm, panels_hbm, temp_hbm, salt_hbm, depth_hbm,
+    tiled, table, panels, temp, salt, depth, to_dg, to_z, to_core, to_gy, air, sems,
 ):
-    outs, (air, sems) = rest[:-2], rest[-2:]
-    order = [2 * kind[0] + kind[1]]
-    order += [n for n in range(4) if n not in order]
-    pairs = [(air_hbm, air), (table_hbm, table), (panels_hbm.at[order[0]], panels.at[order[0]])]
+    pairs = [(air_hbm, air), (table_hbm, table)]
+    pairs += [(panels_hbm.at[n], panels.at[n]) for n in range(3)]
     pairs += [(temp_hbm, temp), (salt_hbm, salt), (depth_hbm, depth)]
-    copies = fetch(sems, pairs + [(panels_hbm.at[n], panels.at[n]) for n in order[1:]])
+    copies = fetch(sems, pairs + [(panels_hbm.at[3], panels.at[3])])
+    for out in (to_dg, to_z, to_gy):
+        out[LIST_ROWS:, :] = jnp.zeros((out.shape[0] - LIST_ROWS, 128), F32)
     copies[0].wait()
     tiled[...] = spread_air(air, group_mask())
-    for copy in copies[1:6]:
+    for copy in copies[1:8]:
         copy.wait()
-    outbound_list_out(kind, tiled[...], table, panels, temp, salt, depth, outs)
-    for copy in copies[6:]:
-        copy.wait()
-
-
-def next_kernel(kind, tiled, table, panels, temp, salt, depth, *outs):
-    outbound_list_out(kind, tiled[...], table, panels, temp, salt, depth, outs)
+    outbound_lists(
+        ((0, 0), (1, 0), (0, 1)), tiled[...], table, panels, ((to_dg,), (to_z, to_core), (to_gy,))
+    )
+    deep = depth[...].astype(F32)
+    levels = [temp[l] for l in range(LEVELS)] + [salt[l] for l in range(LEVELS)] + [deep]
+    block = edge_columns(levels)
+    for out in (to_z, to_core):
+        out[LIST_ROWS : LIST_ROWS + ROWS, :] = block
+    copies[8].wait()
 
 
 def beside(values, north, south, west, east):
@@ -187,12 +177,14 @@
             centre = field[l]
             side = side_sum(centre, beside(centre, dry, dry, dry, dry), wets)
             partial[t, l] = centre + jnp.where(wet, side, 0.0)
-    outbound_list(tiled[...], table[1, 1], panels.at[3], group_mask(), (own,))
+    outbound_lists(((1, 1),), tiled[...], table, panels, ((own,),))
     copy.wait()
     fold[...] = inbound_fold()
+    eye = one_hot(iota((64, 64), 0), iota((64, 64), 1))
     source_block, target = ocean_number((64, 64), 0), atm_number((64, 64), 0)
     for n in range(4):
-        sources[n] = one_hot(source_block, in_table[n // 2, n % 2, 0:1, :])
+        ones = one_hot(source_block, in_table[n // 2, n % 2, 0:1, :])
+        sources[n] = dot(ones, eye, TN).astype(BF16)
         targets[n] = one_hot(target, in_table[n // 2, n % 2, 1:2, :])
 
 
@@ -295,21 +287,27 @@
         keep[41 + 2 * n : 42 + 2 * n, 0:128] = edges[n][6]
 
 
-def inbound_list(blocks, source, target, panel, fold, out):
+def inbound_lists(kinds, blocks, sources, targets, fold, panels, outs):
     mask = group_mask()
-    chosen = dot(source, blocks, TN)
-    kept = [[], [], [], []]
-    for g in range(8):
-        part = chosen[g * 8 : (g + 1) * 8]
-        left = [part[:, c * 128 : (c + 1) * 128] for c in range(4)]
-        piece = dot(
-            jnp.concatenate(left, 0).astype(BF16), panel[g * 128 : (g + 1) * 128, :], NT
-        )
-        for c in range(4):
-            kept[c].append(jnp.where(mask, piece[c * 8 : (c + 1) * 8], 0.0))
-    kept = jnp.concatenate([jnp.concatenate(k, 0) for k in kept], 1)
-    pieces = split_dot(kept, fold)
-    out[0:64, :] = dot_split(target, pieces)
+    numbers = [2 * a + b for a, b in kinds]
+    chosen = dot(jnp.concatenate([sources[n] for n in numbers], 0), blocks)
+    lists = []
+    for m, n in enumerate(numbers):
+        kept = [[], [], [], []]
+        for g in range(8):
+            part = chosen[m * 64 + g * 8 : m * 64 + (g + 1) * 8]
+            left = [part[:, c * 128 : (c + 1) * 128] for c in range(4)]
+            piece = dot(
+                jnp.concatenate(left, 0).astype(BF16), panels[n, g * 128 : (g + 1) * 128, :], NT
+            )
+            for c in range(4):
+                kept[c].append(jnp.where(mask, piece[c * 8 : (c + 1) * 8], 0.0))
+        lists.append(jnp.concatenate([jnp.concatenate(k, 0) for k in kept], 1))
+    pieces = split_dot(jnp.concatenate(lists, 0), fold)
+    for m, (n, out) in enumerate(zip(numbers, outs)):
+        out[0:64, :] = dot_split(targets[n], pieces[m * 64 : (m + 1) * 64])
+        if out.shape[0] > 64:
+            out[64:, :] = jnp.zeros((out.shape[0] - 64, 128), F32)
 
 
 def inbound_fold():
@@ -387,7 +385,7 @@
 
 def second_kernel(
     old, core, zpair, xe, xo, planes, depths, keep, depth, sources, targets, fold, panels,
-    top_temp, top_salt, surface_blocks, out,
+    top_temp, top_salt, surface_blocks, to_dg, to_gy, to_gx,
 ):
     top = {}
 
@@ -409,14 +407,8 @@
         parts.append(jnp.concatenate([f[:, s * 128 : (s + 1) * 128] for s in range(TILES)], 0))
     blocks = jnp.concatenate(parts, 1).astype(BF16)
     surface_blocks[...] = blocks
-    inbound_kernel(*SURFACE_ORDER[0], surface_blocks, sources, targets, fold, panels, out)
-
-
-def inbound_kernel(a, b, blocks, sources, targets, fold, panels, out):
-    n = 2 * a + b
-    inbound_list(blocks[...], sources[n], targets[n], panels.at[n], fold[...], out)
-    if out.shape[0] > 64:
-        out[64:, :] = jnp.zeros((out.shape[0] - 64, 128), F32)
+    kinds, outs = ((1, 1), (1, 0), (0, 1)), (to_dg, to_gy, to_gx)
+    inbound_lists(kinds, blocks, sources, targets, fold[...], panels, outs)
 
 
 def outer_kernel(
@@ -439,7 +431,7 @@
         span = slice(TOP_LEVELS[t][1], LEVELS)
         pairs.append((rest.at[t, span], new.at[span]))
     copies += fetch(sems.at[2:4], pairs)
-    inbound_kernel(0, 0, blocks, sources, targets, fold, panels, own)
+    inbound_lists(((0, 0),), blocks[...], sources, targets, fold[...], panels, (own,))
     for copy in copies:
         copy.wait()
 
@@ -493,19 +485,14 @@
     return (i, other_pair(j)) if 0 <= other_pair(j) < lax.axis_size("gy") else (pair(i), j)
 
 
-def outbound_shapes(n):
-    rows = LIST_ROWS + ROWS
-    shapes = [(rows + 8 * (3 - n), 128)]
-    return shapes + [(rows, 128)] if FORCING_ORDER[n] == (1, 0) else shapes
-
-
 def per_device(air, out_tables, out_panels, depth, temp, salt, in_tables, in_panels):
     out_panels = out_panels.reshape(4, 1024, 128)
     in_panels = in_panels.reshape(4, 1024, 128)
     out_tables, in_tables = out_tables[0, 0], in_tables[0, 0]
     field = (2, LEVELS, ROWS, COLS)
-    tiled, out_tables, out_panels, temp, salt, depth, *first = call(
-        functools.partial(outbound_kernel, FORCING_ORDER[0]),
+    rows = LIST_ROWS + ROWS
+    tiled, out_tables, out_panels, temp, salt, depth, to_dg, to_z, to_core, to_gy = call(
+        outbound_kernel,
         [
             jax.ShapeDtypeStruct((64, 1024), BF16),
             jax.ShapeDtypeStruct(out_tables.shape, jnp.int32),
@@ -513,28 +500,19 @@
             temp.shape,
             salt.shape,
             jax.ShapeDtypeStruct(depth.shape, jnp.int32),
-        ] + outbound_shapes(0),
+            (rows + 24, 128),
+            (rows + 16, 128),
+            (rows, 128),
+            (rows + 8, 128),
+        ],
         [air, out_tables, out_panels, temp, salt, depth],
         [pltpu.VMEM(air.shape, BF16), pltpu.SemaphoreType.DMA((9,))],
         hbm_in=range(6),
     )
-    got = {}
-    for n, kind in enumerate(FORCING_ORDER):
-        blocks = first
-        if n:
-            blocks = call(
-                functools.partial(next_kernel, kind),
-                outbound_shapes(n),
-                [tiled, out_tables, out_panels, temp, salt, depth],
-            )
-        if kind == (0, 0):
-            got["dg"] = send(blocks[0], lambda i, j: (i - 1, j - 1) if j else (i, j - 1))
-        if kind == (0, 1):
-            got["gy"] = send(blocks[0], lambda i, j: (i, j - 1))
-        if kind == (1, 0):
-            got["z"] = send(blocks[0], lambda i, j: (other_pair(i), j))
-            got["core"] = send(blocks[1], lambda i, j: (pair(i), j))
-    dg, gy, zpair, core = got["dg"], got["gy"], got["z"], got["core"]
+    dg = send(to_dg, lambda i, j: (i - 1, j - 1) if j else (i, j - 1))
+    zpair = send(to_z, lambda i, j: (other_pair(i), j))
+    gy = send(to_gy, lambda i, j: (i, j - 1))
+    core = send(to_core, lambda i, j: (pair(i), j))
     ones = jax.ShapeDtypeStruct((4, 64, 64), BF16)
     own, partial, *maps = call(
         inner_kernel,
@@ -563,29 +541,21 @@
     zpair = send(cols, lambda i, j: (other_pair(i), j))
     core = send(cols, lambda i, j: (pair(i), j))
     state = [stepped, core, zpair, xe, xo, planes, depths, keep, depth]
-    top_temp, top_salt, blocks, *first = call(
+    top_temp, top_salt, blocks, to_dg, to_gy, to_gx = call(
         second_kernel,
         [
             (TOP_LEVELS[0][1], ROWS, COLS),
             (TOP_LEVELS[1][1], ROWS, COLS),
             jax.ShapeDtypeStruct((64, COLS), BF16),
             (80, 128),
+            (72, 128),
+            (64, 128),
         ],
         state + maps + [in_panels],
     )
-    got = {}
-    for n, kind in enumerate(SURFACE_ORDER):
-        block = first
-        if n:
-            kernel = functools.partial(inbound_kernel, *kind)
-            block = call(kernel, [(80 - 8 * n, 128)], [blocks, *maps, in_panels])
-        steps = {
-            (1, 1): lambda i, j: (i + 1, j + 1) if j + 1 < lax.axis_size("gy") else (i, j + 1),
-            (1, 0): lambda i, j: (i, j + 1),
-            (0, 1): lambda i, j: (i + 1, j),
-        }
-        got[kind] = send(block[0], steps[kind])
-    dg, gy, gx = got[1, 1], got[1, 0], got[0, 1]
+    dg = send(to_dg, lambda i, j: (i + 1, j + 1) if j + 1 < lax.axis_size("gy") else (i, j + 1))
+    gy = send(to_gy, lambda i, j: (i, j + 1))
+    gx = send(to_gx, lambda i, j: (i + 1, j))
     new_temp, new_salt, own = call(
         outer_kernel,
         [temp.shape, salt.shape, (64, 128)],

time: 33.4 us -> 32.8 us (0.982)
  Pallas kernels: 9.46 us -> 8.09 us
  starting transfers between devices: 13.7 us -> 14.9 us
  waiting for transfers between devices: 9.06 us -> 8.64 us
    pallas_call x12 -> x8, Pallas kernels: 9.46 us -> 8.09 us  [call(): pl.pallas_call(kernel, out_shape=shapes, in_specs=[HBM if n in hbm_in els...]
    ppermute x11, starting transfers between devices: 13.7 us -> 14.9 us  [send(): return lax.ppermute(block, ('gx', 'gy'), route)]
    ppermute x11, waiting for transfers between devices: 9.06 us -> 8.64 us  [send(): return lax.ppermute(block, ('gx', 'gy'), route)]
  transfers between devices with their start and end apart: 11 -> 11, of which waited for: 5 -> 6; matrix products, arithmetic and copies ran while one was open for 0% -> 0% of each run, Pallas kernels for 17% -> 11%
where the time goes in v8:
time: 32.8 us; the launch traced here: 32.3 us
  starting transfers between devices  14.9 us (45%)
  waiting for transfers between devices  8.64 us (26%)
  Pallas kernels  8.09 us (25%)
  between operations  0.72 us (2%)
    ppermute x11, starting transfers between devices, send(): return lax.ppermute(block, ('gx', 'gy'), route)  14.9 us
    ppermute x11, waiting for transfers between devices, send(): return lax.ppermute(block, ('gx', 'gy'), route)  8.64 us
    pallas_call x8, Pallas kernels, call(): pl.pallas_call(kernel, out_shape=shapes, in_specs=[HBM if n in hbm_in els...  8.09 us
  transfers between devices with their start and end apart: 11, of which 6 were waited for; matrix products, arithmetic and copies ran while one was open for 0% of the time, Pallas kernels for 11%

profile of v8, /device:TPU:8, one launch (start us, length us, event | category | flops | bytes accessed | tf_op | source)
XLA Modules:
  0.0 32.3 jit_solution(3532673860255014677)
XLA Ops:
  0.6 2.3 %shard_map.103 = (bf16[64,1024]{1,0:T(8,128)(2,1)S(1)}, s32[2,2,2,64]{3,2,1,0:T(2,128)S(1)}, bf16[4,1024,128]{2,1,0:T(8,128)(2,1)S(1)}, f32[10,16,512]{2,1,0:T(8...) custom-call(bf16[8,8,128]{2,1,0:T(8,128)(2,1)} %air_hbm.1, ...), custom_call_target="tpu_custom_call" | custom-call | tf_op jit(solution)/shard_map/pallas_call | solution.py:456
  2.9 5.6 %collective-permute-start = (f32[296,128]{1,0:T(8,128)S(1)}, f32[296,128]{1,0:T(8,128)S(1)}, u32[]{:S(2)}, u32[]{:S(2)}) collective-permute-start(f32[296,128]{1,0:T(8,128)S(1)} %get-tuple-element.38), channel_id=1, source_target_pairs={{0,15},{1,112},{2,113},{3,114},{4,115},{5,116},{6,117},{7,118},{8,... | collective-permute-start | bytes 454664 | tf_op jit(solution)/shard_map/ppermute | solution.py:473
  8.5 0.8 %collective-permute-start.3 = (f32[288,128]{1,0:T(8,128)S(1)}, f32[288,128]{1,0:T(8,128)S(1)}, u32[]{:S(2)}, u32[]{:S(2)}) collective-permute-start(f32[288,128]{1,0:T(8,128)S(1)} %get-tuple-element.48), channel_id=1, source_target_pairs={{0,112},{1,113},{2,114},{3,115},{4,116},{5,117},{6,118},{7,119},{8... | collective-permute-start | bytes 442376 | tf_op jit(solution)/shard_map/ppermute | solution.py:473
  9.4 0.8 %collective-permute-start.1 = (f32[280,128]{1,0:T(8,128)S(1)}, f32[280,128]{1,0:T(8,128)S(1)}, u32[]{:S(2)}, u32[]{:S(2)}) collective-permute-start(f32[280,128]{1,0:T(8,128)S(1)} %get-tuple-element.39), channel_id=1, source_target_pairs={{0,15},{1,0},{2,1},{3,2},{4,3},{5,4},{6,5},{7,6},{8,7},{9,8},{10,9... | collective-permute-start | bytes 430088 | tf_op jit(solution)/shard_map/ppermute | solution.py:473
  10.2 0.0 collective-permute-start.2
  10.2 1.5 %shard_map.104 = (f32[256,128]{1,0:T(8,128)S(1)}, f32[2,10,16,512]{3,2,1,0:T(8,128)S(1)}, bf16[4,64,64]{2,1,0:T(8,128)(2,1)S(1)}, bf16[4,64,64]{2,1,0:T(8,128)(2,1)S(1)}, bf16[512,128]{1,0:T(8,128)(2,1)S(1)}) custom-call(bf16[64,1024]{1,0:T(8,128)(2,1)S(1)} %get-tuple-element.40.tiled, s32[2,2,2,64]{3,2,1,0:T(2,128)S(1)} %get-tuple-element.41.table, ...), custom_call_target="tpu_custom_call" | custom-call | tf_op jit(solution)/shard_map/pallas_call | solution.py:456
  11.7 0.0 collective-permute-done.2.core
  11.7 2.6 %collective-permute-done.3.zpair = f32[288,128]{1,0:T(8,128)S(1)} collective-permute-done((f32[288,128]{1,0:T(8,128)S(1)}, f32[288,128]{1,0:T(8,128)S(1)}, u32[]{:S(2)}, u32[]{:S(2)}) %collective-permute-start.3) | collective-permute-done | bytes 147488 | tf_op jit(solution)/shard_map/ppermute | solution.py:473
  14.3 0.2 shard_map.105
  14.6 0.0 collective-permute-done.1.gy
  14.6 0.0 collective-permute-done.dg
  14.6 0.3 %shard_map.106 = (f32[2,10,16,512]{3,2,1,0:T(8,128)S(1)}, f32[16,128]{1,0:T(8,128)S(1)}, f32[4,16,512]{2,1,0:T(8,128)S(1)}) custom-call(f32[296,128]{1,0:T(8,128)S(1)} %collective-permute-done.dg, f32[280,128]{1,0:T(8,128)S(1)} %collective-permute-done.1.gy, f32[256,128]{1,0:T(8,128)S(1)} %get-tuple-element.50.base, ...), custom_call_target="tpu_custom_call" | custom-call | tf_op jit(solution)/shard_map/pallas_call | solution.py:456
  14.9 0.0 copy-start
  15.0 0.1 shard_map.107
  15.1 2.9 %collective-permute-start.7 = (f32[48,512]{1,0:T(8,128)S(1)}, f32[48,512]{1,0:T(8,128)S(1)}, u32[]{:S(2)}, u32[]{:S(2)}) collective-permute-start(f32[48,512]{1,0:T(8,128)S(1)} %get-tuple-element.57), channel_id=1, source_target_pairs={{0,16},{1,2},{2,1},{3,4},{4,3},{5,6},{6,5},{7,8},{8,7},{9,10},{10,... | collective-permute-start | bytes 294920 | tf_op jit(solution)/shard_map/ppermute | solution.py:473
  18.0 0.0 collective-permute-start.6
  18.0 2.8 %collective-permute-start.5 = (f32[16,128]{1,0:T(8,128)S(1)}, f32[16,128]{1,0:T(8,128)S(1)}, u32[]{:S(2)}, u32[]{:S(2)}) collective-permute-start(f32[16,128]{1,0:T(8,128)S(1)} %get-tuple-element.53), channel_id=1, source_target_pairs={{0,112},{1,113},{2,114},{3,115},{4,116},{5,117},{6,118},{7,119},{8... | collective-permute-start | bytes 24584 | tf_op jit(solution)/shard_map/ppermute | solution.py:473
  20.8 0.0 collective-permute-start.4
  20.8 1.5 %collective-permute-done.5.zpair = f32[16,128]{1,0:T(8,128)S(1)} collective-permute-done((f32[16,128]{1,0:T(8,128)S(1)}, f32[16,128]{1,0:T(8,128)S(1)}, u32[]{:S(2)}, u32[]{:S(2)}) %collective-permute-start.5) | collective-permute-done | bytes 8224 | tf_op jit(solution)/shard_map/ppermute | solution.py:473
  22.3 0.0 collective-permute-done.4.core
  22.3 0.3 collective-permute-done.6.xe
  22.6 0.0 collective-permute-done.7.xo
  22.6 0.0 copy-done
  22.6 1.2 %shard_map.108 = (f32[3,16,512]{2,1,0:T(8,128)S(1)}, f32[1,16,512]{2,1,0:T(8,128)S(1)}, bf16[64,512]{1,0:T(8,128)(2,1)S(1)}, f32[80,128]{1,0:T(8,128)S(1)}, f32[...) custom-call(f32[2,10,16,512]{3,2,1,0:T(8,128)S(1)} %get-tuple-element.52.new.old, f32[16,128]{1,0:T(8,128)S(1)} %collective-permute-done.4.core, ...), custom_call_target="tpu_custom_call" | custom-call | tf_op jit(solution)/shard_map/pallas_call | solution.py:456
  23.8 1.0 %collective-permute-start.8 = (f32[80,128]{1,0:T(8,128)S(1)}, f32[80,128]{1,0:T(8,128)S(1)}, u32[]{:S(2)}, u32[]{:S(2)}) collective-permute-start(f32[80,128]{1,0:T(8,128)S(1)} %get-tuple-element.69), channel_id=1, source_target_pairs={{0,17},{1,18},{2,19},{3,20},{4,21},{5,22},{6,23},{7,24},{8,25},{9,... | collective-permute-start | bytes 122888 | tf_op jit(solution)/shard_map/ppermute | solution.py:473
  24.8 0.9 %collective-permute-start.9 = (f32[72,128]{1,0:T(8,128)S(1)}, f32[72,128]{1,0:T(8,128)S(1)}, u32[]{:S(2)}, u32[]{:S(2)}) collective-permute-start(f32[72,128]{1,0:T(8,128)S(1)} %get-tuple-element.70), channel_id=1, source_target_pairs={{0,1},{1,2},{2,3},{3,4},{4,5},{5,6},{6,7},{7,8},{8,9},{9,10},{10,1... | collective-permute-start | bytes 110600 | tf_op jit(solution)/shard_map/ppermute | solution.py:473
  25.7 0.0 collective-permute-start.10
  25.7 1.7 %shard_map.109 = (f32[10,16,512]{2,1,0:T(8,128)}, f32[10,16,512]{2,1,0:T(8,128)}, f32[64,128]{1,0:T(8,128)S(1)}) custom-call(f32[2,10,16,512]{3,2,1,0:T(8,128)S(1)} %get-tuple-element.52.new.old, f32[16,128]{1,0:T(8,128)S(1)} %collective-permute-done.4.core, f32[16,128]{1,0:T(8,128)S(1)} %collective-permute-done.5.zpair, ...), custom_call_target="tpu_custom_call" | custom-call | tf_op jit(solution)/shard_map/pallas_call | solution.py:456
  27.4 2.8 %collective-permute-done.10.gx = f32[64,128]{1,0:T(8,128)S(1)} collective-permute-done((f32[64,128]{1,0:T(8,128)S(1)}, f32[64,128]{1,0:T(8,128)S(1)}, u32[]{:S(2)}, u32[]{:S(2)}) %collective-permute-start.10) | collective-permute-done | bytes 32800 | tf_op jit(solution)/shard_map/ppermute | solution.py:473
  30.2 0.6 %collective-permute-done.9.gy = f32[72,128]{1,0:T(8,128)S(1)} collective-permute-done((f32[72,128]{1,0:T(8,128)S(1)}, f32[72,128]{1,0:T(8,128)S(1)}, u32[]{:S(2)}, u32[]{:S(2)}) %collective-permute-start.9) | collective-permute-done | bytes 36896 | tf_op jit(solution)/shard_map/ppermute | solution.py:473
  30.8 0.8 %collective-permute-done.8.dg = f32[80,128]{1,0:T(8,128)S(1)} collective-permute-done((f32[80,128]{1,0:T(8,128)S(1)}, f32[80,128]{1,0:T(8,128)S(1)}, u32[]{:S(2)}, u32[]{:S(2)}) %collective-permute-start.8) | collective-permute-done | bytes 40992 | tf_op jit(solution)/shard_map/ppermute | solution.py:473
  31.6 0.7 %shard_map.110 = f32[4,8,128]{2,1,0:T(8,128)} custom-call(f32[80,128]{1,0:T(8,128)S(1)} %collective-permute-done.8.dg, f32[72,128]{1,0:T(8,128)S(1)} %collective-permute-done.9.gy, f32[64,128]{1,0:T(8,128)S(1)} %collective-permute-done.10.gx, f32[64,128]{1,0:T(8,128)S(1)} %get-tuple-element.72.own), custom_call_target="tpu_custom_call" | custom-call | tf_op jit(solution)/shard_map/pallas_call | solution.py:456
Async XLA Ops:
  2.9 11.7 %collective-permute-start = (f32[296,128]{1,0:T(8,128)S(1)}, f32[296,128]{1,0:T(8,128)S(1)}, u32[]{:S(2)}, u32[]{:S(2)}) collective-permute-start(f32[296,128]{1,0:T(8,128)S(1)} %get-tuple-element.38), channel_id=1, source_target_pairs={{0,15},{1,112},{2,113},{3,114},{4,115},{5,116},{6,117},{7,118},{8,... | collective-permute-start | bytes 454664 | tf_op jit(solution)/shard_map/ppermute | solution.py:473
  8.5 5.8 %collective-permute-start.3 = (f32[288,128]{1,0:T(8,128)S(1)}, f32[288,128]{1,0:T(8,128)S(1)}, u32[]{:S(2)}, u32[]{:S(2)}) collective-permute-start(f32[288,128]{1,0:T(8,128)S(1)} %get-tuple-element.48), channel_id=1, source_target_pairs={{0,112},{1,113},{2,114},{3,115},{4,116},{5,117},{6,118},{7,119},{8... | collective-permute-start | bytes 442376 | tf_op jit(solution)/shard_map/ppermute | solution.py:473
  9.4 5.2 %collective-permute-start.1 = (f32[280,128]{1,0:T(8,128)S(1)}, f32[280,128]{1,0:T(8,128)S(1)}, u32[]{:S(2)}, u32[]{:S(2)}) collective-permute-start(f32[280,128]{1,0:T(8,128)S(1)} %get-tuple-element.39), channel_id=1, source_target_pairs={{0,15},{1,0},{2,1},{3,2},{4,3},{5,4},{6,5},{7,6},{8,7},{9,8},{10,9... | collective-permute-start | bytes 430088 | tf_op jit(solution)/shard_map/ppermute | solution.py:473
  10.2 1.5 %collective-permute-start.2 = (f32[272,128]{1,0:T(8,128)S(1)}, f32[272,128]{1,0:T(8,128)S(1)}, u32[]{:S(2)}, u32[]{:S(2)}) collective-permute-start(f32[272,128]{1,0:T(8,128)S(1)} %get-tuple-element.47), channel_id=1, source_target_pairs={{0,16},{1,17},{2,18},{3,19},{4,20},{5,21},{6,22},{7,23},{8,24},{9,... | collective-permute-start | bytes 417800 | tf_op jit(solution)/shard_map/ppermute | solution.py:473
  14.9 7.6 %copy-start = (bf16[1,1,2,2,64,16,128]{6,5,4,3,2,1,0:T(8,128)(2,1)S(1)}, bf16[1,1,2,2,64,16,128]{6,5,4,3,2,1,0:T(8,128)(2,1)}, u32[]{:S(2)}) copy-start(bf16[1,1,2,2,64,16,128]{6,5,4,3,2,1,0:T(8,128)(2,1)} %param.15) | copy-start | bytes 3145732
  15.1 7.5 %collective-permute-start.7 = (f32[48,512]{1,0:T(8,128)S(1)}, f32[48,512]{1,0:T(8,128)S(1)}, u32[]{:S(2)}, u32[]{:S(2)}) collective-permute-start(f32[48,512]{1,0:T(8,128)S(1)} %get-tuple-element.57), channel_id=1, source_target_pairs={{0,16},{1,2},{2,1},{3,4},{4,3},{5,6},{6,5},{7,8},{8,7},{9,10},{10,... | collective-permute-start | bytes 294920 | tf_op jit(solution)/shard_map/ppermute | solution.py:473
  18.0 4.6 %collective-permute-start.6 = (f32[43,512]{1,0:T(8,128)S(1)}, f32[43,512]{1,0:T(8,128)S(1)}, u32[]{:S(2)}, u32[]{:S(2)}) collective-permute-start(f32[43,512]{1,0:T(8,128)S(1)} %get-tuple-element.56), channel_id=1, source_target_pairs={{0,1},{1,0},{2,3},{3,2},{4,5},{5,4},{6,7},{7,6},{8,9},{9,8},{10,11... | collective-permute-start | bytes 264200 | tf_op jit(solution)/shard_map/ppermute | solution.py:473
  18.0 4.3 %collective-permute-start.5 = (f32[16,128]{1,0:T(8,128)S(1)}, f32[16,128]{1,0:T(8,128)S(1)}, u32[]{:S(2)}, u32[]{:S(2)}) collective-permute-start(f32[16,128]{1,0:T(8,128)S(1)} %get-tuple-element.53), channel_id=1, source_target_pairs={{0,112},{1,113},{2,114},{3,115},{4,116},{5,117},{6,118},{7,119},{8... | collective-permute-start | bytes 24584 | tf_op jit(solution)/shard_map/ppermute | solution.py:473
  20.8 1.5 %collective-permute-start.4 = (f32[16,128]{1,0:T(8,128)S(1)}, f32[16,128]{1,0:T(8,128)S(1)}, u32[]{:S(2)}, u32[]{:S(2)}) collective-permute-start(f32[16,128]{1,0:T(8,128)S(1)} %get-tuple-element.53), channel_id=1, source_target_pairs={{0,16},{1,17},{2,18},{3,19},{4,20},{5,21},{6,22},{7,23},{8,24},{9,... | collective-permute-start | bytes 24584 | tf_op jit(solution)/shard_map/ppermute | solution.py:473
  23.8 7.8 %collective-permute-start.8 = (f32[80,128]{1,0:T(8,128)S(1)}, f32[80,128]{1,0:T(8,128)S(1)}, u32[]{:S(2)}, u32[]{:S(2)}) collective-permute-start(f32[80,128]{1,0:T(8,128)S(1)} %get-tuple-element.69), channel_id=1, source_target_pairs={{0,17},{1,18},{2,19},{3,20},{4,21},{5,22},{6,23},{7,24},{8,25},{9,... | collective-permute-start | bytes 122888 | tf_op jit(solution)/shard_map/ppermute | solution.py:473
  24.8 6.1 %collective-permute-start.9 = (f32[72,128]{1,0:T(8,128)S(1)}, f32[72,128]{1,0:T(8,128)S(1)}, u32[]{:S(2)}, u32[]{:S(2)}) collective-permute-start(f32[72,128]{1,0:T(8,128)S(1)} %get-tuple-element.70), channel_id=1, source_target_pairs={{0,1},{1,2},{2,3},{3,4},{4,5},{5,6},{6,7},{7,8},{8,9},{9,10},{10,1... | collective-permute-start | bytes 110600 | tf_op jit(solution)/shard_map/ppermute | solution.py:473
  25.7 4.6 %collective-permute-start.10 = (f32[64,128]{1,0:T(8,128)S(1)}, f32[64,128]{1,0:T(8,128)S(1)}, u32[]{:S(2)}, u32[]{:S(2)}) collective-permute-start(f32[64,128]{1,0:T(8,128)S(1)} %get-tuple-element.71), channel_id=1, source_target_pairs={{0,16},{1,17},{2,18},{3,19},{4,20},{5,21},{6,22},{7,23},{8,24},{9,... | collective-permute-start | bytes 98312 | tf_op jit(solution)/shard_map/ppermute | solution.py:473

commit v9 on v8

--- a/solution.py
+++ b/solution.py
@@ -83,12 +83,13 @@
     return jnp.concatenate([tiled[c * 64 : (c + 1) * 64] for c in range(8)], 1)
 
 
-def outbound_lists(kinds, tiled, table, panels, outs):
+def outbound_lists(kinds, tiled, table, panels, outs, wait=lambda: None):
     mask = group_mask()
     source = iota((64, 64), 0)
     target = ocean_number((64, 64), 0)
     ones = jnp.concatenate([one_hot(source, table[a, b, 0:1, :]) for a, b in kinds], 1)
     picked = dot(ones, tiled, TN)
+    wait()
     pieces = []
     for n, (a, b) in enumerate(kinds):
         planes = [[], [], [], []]
@@ -129,18 +130,22 @@
     copies = fetch(sems, pairs + [(panels_hbm.at[3], panels.at[3])])
     for out in (to_dg, to_z, to_gy):
         out[LIST_ROWS:, :] = jnp.zeros((out.shape[0] - LIST_ROWS, 128), F32)
+
+    def rest():
+        for copy in copies[2:8]:
+            copy.wait()
+        deep = depth[...].astype(F32)
+        levels = [temp[l] for l in range(LEVELS)] + [salt[l] for l in range(LEVELS)] + [deep]
+        block = edge_columns(levels)
+        for out in (to_z, to_core):
+            out[LIST_ROWS : LIST_ROWS + ROWS, :] = block
+
     copies[0].wait()
-    tiled[...] = spread_air(air, group_mask())
-    for copy in copies[1:8]:
-        copy.wait()
-    outbound_lists(
-        ((0, 0), (1, 0), (0, 1)), tiled[...], table, panels, ((to_dg,), (to_z, to_core), (to_gy,))
-    )
-    deep = depth[...].astype(F32)
-    levels = [temp[l] for l in range(LEVELS)] + [salt[l] for l in range(LEVELS)] + [deep]
-    block = edge_columns(levels)
-    for out in (to_z, to_core):
-        out[LIST_ROWS : LIST_ROWS + ROWS, :] = block
+    spread = spread_air(air, group_mask())
+    tiled[...] = spread
+    copies[1].wait()
+    kinds, outs = ((0, 0), (1, 0), (0, 1)), ((to_dg,), (to_z, to_core), (to_gy,))
+    outbound_lists(kinds, spread, table, panels, outs, rest)
     copies[8].wait()
 
 
@@ -279,7 +284,7 @@
         for a, b in zip(*edges):
             out[at : at + a.shape[0], 0 : a.shape[1]] = jnp.where(first, a, b)
             at += a.shape[0]
-    row_o[43:48, :] = jnp.zeros((5, COLS), F32)
+    row_e[43:48, :] = jnp.zeros((5, COLS), F32)
     for n in range(2):
         keep[20 * n : 20 * n + 10, :] = edges[n][2]
         keep[20 * n + 10 : 20 * n + 20, :] = edges[n][3]
@@ -320,7 +325,7 @@
     odd_col = lax.axis_index("gx") % 2 == 1
     odd_row = lax.axis_index("gy") % 2 == 1
     deep = depth[...].astype(F32)
-    row_e, row_o = xe[...], xo[0:43, :]
+    row_e, row_o = xe[0:43, :], xo[...]
     beyond = (jnp.where(odd_row, row_e, row_o), jnp.where(odd_row, row_o, row_e))
     level = iota((2 * LEVELS, COLS), 0) % LEVELS
     at_end = (lax.axis_index("gy") == 0, lax.axis_index("gy") == lax.axis_size("gy") - 1)
@@ -533,7 +538,7 @@
     )
     row_e, row_o, keep = call(
         rows_kernel,
-        [(43, COLS), (48, COLS), (44, COLS)],
+        [(48, COLS), (43, COLS), (44, COLS)],
         [stepped, temp, salt, depth, west, east],
     )
     xo = send(row_o, row_pair)

time: 32.8 us -> 32.2 us (0.982)
  waiting for transfers between devices: 8.64 us -> 8.22 us
    ppermute x11, waiting for transfers between devices: 8.64 us -> 8.22 us  [send(): return lax.ppermute(block, ('gx', 'gy'), route)]
  transfers between devices with their start and end apart: 11 -> 11, of which waited for: 6 -> 5; matrix products, arithmetic and copies ran while one was open for 0% -> 0% of each run, Pallas kernels for 11% -> 11%
where the time goes in v9:
time: 32.2 us; the launch traced here: 31.7 us
  starting transfers between devices  15 us (47%)
  waiting for transfers between devices  8.22 us (26%)
  Pallas kernels  7.78 us (24%)
  between operations  0.73 us (2%)
    ppermute x11, starting transfers between devices, send(): return lax.ppermute(block, ('gx', 'gy'), route)  15 us
    ppermute x11, waiting for transfers between devices, send(): return lax.ppermute(block, ('gx', 'gy'), route)  8.22 us
    pallas_call x8, Pallas kernels, call(): pl.pallas_call(kernel, out_shape=shapes, in_specs=[HBM if n in hbm_in els...  7.78 us
  transfers between devices with their start and end apart: 11, of which 5 were waited for; matrix products, arithmetic and copies ran while one was open for 0% of the time, Pallas kernels for 11%

profile of v9, /device:TPU:8, one launch (start us, length us, event | category | flops | bytes accessed | tf_op | source)
XLA Modules:
  0.0 31.7 jit_solution(10899369912889335751)
XLA Ops:
  0.6 2.0 %shard_map.103 = (bf16[64,1024]{1,0:T(8,128)(2,1)S(1)}, s32[2,2,2,64]{3,2,1,0:T(2,128)S(1)}, bf16[4,1024,128]{2,1,0:T(8,128)(2,1)S(1)}, f32[10,16,512]{2,1,0:T(8...) custom-call(bf16[8,8,128]{2,1,0:T(8,128)(2,1)} %air_hbm.1, ...), custom_call_target="tpu_custom_call" | custom-call | tf_op jit(solution)/shard_map/pallas_call | solution.py:461
  2.6 5.6 %collective-permute-start = (f32[296,128]{1,0:T(8,128)S(1)}, f32[296,128]{1,0:T(8,128)S(1)}, u32[]{:S(2)}, u32[]{:S(2)}) collective-permute-start(f32[296,128]{1,0:T(8,128)S(1)} %get-tuple-element.38), channel_id=1, source_target_pairs={{0,15},{1,112},{2,113},{3,114},{4,115},{5,116},{6,117},{7,118},{8,... | collective-permute-start | bytes 454664 | tf_op jit(solution)/shard_map/ppermute | solution.py:478
  8.2 0.8 %collective-permute-start.3 = (f32[288,128]{1,0:T(8,128)S(1)}, f32[288,128]{1,0:T(8,128)S(1)}, u32[]{:S(2)}, u32[]{:S(2)}) collective-permute-start(f32[288,128]{1,0:T(8,128)S(1)} %get-tuple-element.48), channel_id=1, source_target_pairs={{0,112},{1,113},{2,114},{3,115},{4,116},{5,117},{6,118},{7,119},{8... | collective-permute-start | bytes 442376 | tf_op jit(solution)/shard_map/ppermute | solution.py:478
  9.1 0.8 %collective-permute-start.1 = (f32[280,128]{1,0:T(8,128)S(1)}, f32[280,128]{1,0:T(8,128)S(1)}, u32[]{:S(2)}, u32[]{:S(2)}) collective-permute-start(f32[280,128]{1,0:T(8,128)S(1)} %get-tuple-element.39), channel_id=1, source_target_pairs={{0,15},{1,0},{2,1},{3,2},{4,3},{5,4},{6,5},{7,6},{8,7},{9,8},{10,9... | collective-permute-start | bytes 430088 | tf_op jit(solution)/shard_map/ppermute | solution.py:478
  9.9 0.0 collective-permute-start.2
  9.9 1.5 %shard_map.104 = (f32[256,128]{1,0:T(8,128)S(1)}, f32[2,10,16,512]{3,2,1,0:T(8,128)S(1)}, bf16[4,64,64]{2,1,0:T(8,128)(2,1)S(1)}, bf16[4,64,64]{2,1,0:T(8,128)(2,1)S(1)}, bf16[512,128]{1,0:T(8,128)(2,1)S(1)}) custom-call(bf16[64,1024]{1,0:T(8,128)(2,1)S(1)} %get-tuple-element.40.tiled, s32[2,2,2,64]{3,2,1,0:T(2,128)S(1)} %get-tuple-element.41.table, ...), custom_call_target="tpu_custom_call" | custom-call | tf_op jit(solution)/shard_map/pallas_call | solution.py:461
  11.4 0.0 collective-permute-done.2.core
  11.4 2.6 %collective-permute-done.3.zpair = f32[288,128]{1,0:T(8,128)S(1)} collective-permute-done((f32[288,128]{1,0:T(8,128)S(1)}, f32[288,128]{1,0:T(8,128)S(1)}, u32[]{:S(2)}, u32[]{:S(2)}) %collective-permute-start.3) | collective-permute-done | bytes 147488 | tf_op jit(solution)/shard_map/ppermute | solution.py:478
  14.0 0.2 shard_map.105
  14.3 0.0 collective-permute-done.1.gy
  14.3 0.0 collective-permute-done.dg
  14.3 0.3 %shard_map.106 = (f32[2,10,16,512]{3,2,1,0:T(8,128)S(1)}, f32[16,128]{1,0:T(8,128)S(1)}, f32[4,16,512]{2,1,0:T(8,128)S(1)}) custom-call(f32[296,128]{1,0:T(8,128)S(1)} %collective-permute-done.dg, f32[280,128]{1,0:T(8,128)S(1)} %collective-permute-done.1.gy, f32[256,128]{1,0:T(8,128)S(1)} %get-tuple-element.50.base, ...), custom_call_target="tpu_custom_call" | custom-call | tf_op jit(solution)/shard_map/pallas_call | solution.py:461
  14.6 0.0 copy-start
  14.6 0.1 shard_map.107
  14.7 0.1 collective-permute-start.6
  14.8 2.9 %collective-permute-start.7 = (f32[43,512]{1,0:T(8,128)S(1)}, f32[43,512]{1,0:T(8,128)S(1)}, u32[]{:S(2)}, u32[]{:S(2)}) collective-permute-start(f32[43,512]{1,0:T(8,128)S(1)} %get-tuple-element.57), channel_id=1, source_target_pairs={{0,16},{1,2},{2,1},{3,4},{4,3},{5,6},{6,5},{7,8},{8,7},{9,10},{10,... | collective-permute-start | bytes 264200 | tf_op jit(solution)/shard_map/ppermute | solution.py:478
  17.7 2.8 %collective-permute-start.5 = (f32[16,128]{1,0:T(8,128)S(1)}, f32[16,128]{1,0:T(8,128)S(1)}, u32[]{:S(2)}, u32[]{:S(2)}) collective-permute-start(f32[16,128]{1,0:T(8,128)S(1)} %get-tuple-element.53), channel_id=1, source_target_pairs={{0,112},{1,113},{2,114},{3,115},{4,116},{5,117},{6,118},{7,119},{8... | collective-permute-start | bytes 24584 | tf_op jit(solution)/shard_map/ppermute | solution.py:478
  20.5 0.0 collective-permute-start.4
  20.5 1.5 %collective-permute-done.5.zpair = f32[16,128]{1,0:T(8,128)S(1)} collective-permute-done((f32[16,128]{1,0:T(8,128)S(1)}, f32[16,128]{1,0:T(8,128)S(1)}, u32[]{:S(2)}, u32[]{:S(2)}) %collective-permute-start.5) | collective-permute-done | bytes 8224 | tf_op jit(solution)/shard_map/ppermute | solution.py:478
  22.0 0.0 collective-permute-done.4.core
  22.0 0.0 collective-permute-done.7.xo
  22.0 0.0 collective-permute-done.6.xe
  22.0 0.0 copy-done
  22.1 1.2 %shard_map.108 = (f32[3,16,512]{2,1,0:T(8,128)S(1)}, f32[1,16,512]{2,1,0:T(8,128)S(1)}, bf16[64,512]{1,0:T(8,128)(2,1)S(1)}, f32[80,128]{1,0:T(8,128)S(1)}, f32[...) custom-call(f32[2,10,16,512]{3,2,1,0:T(8,128)S(1)} %get-tuple-element.52.new.old, f32[16,128]{1,0:T(8,128)S(1)} %collective-permute-done.4.core, ...), custom_call_target="tpu_custom_call" | custom-call | tf_op jit(solution)/shard_map/pallas_call | solution.py:461
  23.3 0.7 %collective-permute-start.8 = (f32[80,128]{1,0:T(8,128)S(1)}, f32[80,128]{1,0:T(8,128)S(1)}, u32[]{:S(2)}, u32[]{:S(2)}) collective-permute-start(f32[80,128]{1,0:T(8,128)S(1)} %get-tuple-element.69), channel_id=1, source_target_pairs={{0,17},{1,18},{2,19},{3,20},{4,21},{5,22},{6,23},{7,24},{8,25},{9,... | collective-permute-start | bytes 122888 | tf_op jit(solution)/shard_map/ppermute | solution.py:478
  24.0 0.9 %collective-permute-start.9 = (f32[72,128]{1,0:T(8,128)S(1)}, f32[72,128]{1,0:T(8,128)S(1)}, u32[]{:S(2)}, u32[]{:S(2)}) collective-permute-start(f32[72,128]{1,0:T(8,128)S(1)} %get-tuple-element.70), channel_id=1, source_target_pairs={{0,1},{1,2},{2,3},{3,4},{4,5},{5,6},{6,7},{7,8},{8,9},{9,10},{10,1... | collective-permute-start | bytes 110600 | tf_op jit(solution)/shard_map/ppermute | solution.py:478
  24.9 0.2 collective-permute-start.10
  25.1 1.7 %shard_map.109 = (f32[10,16,512]{2,1,0:T(8,128)}, f32[10,16,512]{2,1,0:T(8,128)}, f32[64,128]{1,0:T(8,128)S(1)}) custom-call(f32[2,10,16,512]{3,2,1,0:T(8,128)S(1)} %get-tuple-element.52.new.old, f32[16,128]{1,0:T(8,128)S(1)} %collective-permute-done.4.core, f32[16,128]{1,0:T(8,128)S(1)} %collective-permute-done.5.zpair, ...), custom_call_target="tpu_custom_call" | custom-call | tf_op jit(solution)/shard_map/pallas_call | solution.py:461
  26.8 2.6 %collective-permute-done.10.gx = f32[64,128]{1,0:T(8,128)S(1)} collective-permute-done((f32[64,128]{1,0:T(8,128)S(1)}, f32[64,128]{1,0:T(8,128)S(1)}, u32[]{:S(2)}, u32[]{:S(2)}) %collective-permute-start.10) | collective-permute-done | bytes 32800 | tf_op jit(solution)/shard_map/ppermute | solution.py:478
  29.4 0.7 %collective-permute-done.9.gy = f32[72,128]{1,0:T(8,128)S(1)} collective-permute-done((f32[72,128]{1,0:T(8,128)S(1)}, f32[72,128]{1,0:T(8,128)S(1)}, u32[]{:S(2)}, u32[]{:S(2)}) %collective-permute-start.9) | collective-permute-done | bytes 36896 | tf_op jit(solution)/shard_map/ppermute | solution.py:478
  30.1 0.9 %collective-permute-done.8.dg = f32[80,128]{1,0:T(8,128)S(1)} collective-permute-done((f32[80,128]{1,0:T(8,128)S(1)}, f32[80,128]{1,0:T(8,128)S(1)}, u32[]{:S(2)}, u32[]{:S(2)}) %collective-permute-start.8) | collective-permute-done | bytes 40992 | tf_op jit(solution)/shard_map/ppermute | solution.py:478
  31.0 0.7 %shard_map.110 = f32[4,8,128]{2,1,0:T(8,128)} custom-call(f32[80,128]{1,0:T(8,128)S(1)} %collective-permute-done.8.dg, f32[72,128]{1,0:T(8,128)S(1)} %collective-permute-done.9.gy, f32[64,128]{1,0:T(8,128)S(1)} %collective-permute-done.10.gx, f32[64,128]{1,0:T(8,128)S(1)} %get-tuple-element.72.own), custom_call_target="tpu_custom_call" | custom-call | tf_op jit(solution)/shard_map/pallas_call | solution.py:461
Async XLA Ops:
  2.6 11.7 %collective-permute-start = (f32[296,128]{1,0:T(8,128)S(1)}, f32[296,128]{1,0:T(8,128)S(1)}, u32[]{:S(2)}, u32[]{:S(2)}) collective-permute-start(f32[296,128]{1,0:T(8,128)S(1)} %get-tuple-element.38), channel_id=1, source_target_pairs={{0,15},{1,112},{2,113},{3,114},{4,115},{5,116},{6,117},{7,118},{8,... | collective-permute-start | bytes 454664 | tf_op jit(solution)/shard_map/ppermute | solution.py:478
  8.2 5.8 %collective-permute-start.3 = (f32[288,128]{1,0:T(8,128)S(1)}, f32[288,128]{1,0:T(8,128)S(1)}, u32[]{:S(2)}, u32[]{:S(2)}) collective-permute-start(f32[288,128]{1,0:T(8,128)S(1)} %get-tuple-element.48), channel_id=1, source_target_pairs={{0,112},{1,113},{2,114},{3,115},{4,116},{5,117},{6,118},{7,119},{8... | collective-permute-start | bytes 442376 | tf_op jit(solution)/shard_map/ppermute | solution.py:478
  9.1 5.2 %collective-permute-start.1 = (f32[280,128]{1,0:T(8,128)S(1)}, f32[280,128]{1,0:T(8,128)S(1)}, u32[]{:S(2)}, u32[]{:S(2)}) collective-permute-start(f32[280,128]{1,0:T(8,128)S(1)} %get-tuple-element.39), channel_id=1, source_target_pairs={{0,15},{1,0},{2,1},{3,2},{4,3},{5,4},{6,5},{7,6},{8,7},{9,8},{10,9... | collective-permute-start | bytes 430088 | tf_op jit(solution)/shard_map/ppermute | solution.py:478
  9.9 1.5 %collective-permute-start.2 = (f32[272,128]{1,0:T(8,128)S(1)}, f32[272,128]{1,0:T(8,128)S(1)}, u32[]{:S(2)}, u32[]{:S(2)}) collective-permute-start(f32[272,128]{1,0:T(8,128)S(1)} %get-tuple-element.47), channel_id=1, source_target_pairs={{0,16},{1,17},{2,18},{3,19},{4,20},{5,21},{6,22},{7,23},{8,24},{9,... | collective-permute-start | bytes 417800 | tf_op jit(solution)/shard_map/ppermute | solution.py:478
  14.6 7.4 %copy-start = (bf16[1,1,2,2,64,16,128]{6,5,4,3,2,1,0:T(8,128)(2,1)S(1)}, bf16[1,1,2,2,64,16,128]{6,5,4,3,2,1,0:T(8,128)(2,1)}, u32[]{:S(2)}) copy-start(bf16[1,1,2,2,64,16,128]{6,5,4,3,2,1,0:T(8,128)(2,1)} %param.15) | copy-start | bytes 3145732
  14.7 7.3 %collective-permute-start.6 = (f32[48,512]{1,0:T(8,128)S(1)}, f32[48,512]{1,0:T(8,128)S(1)}, u32[]{:S(2)}, u32[]{:S(2)}) collective-permute-start(f32[48,512]{1,0:T(8,128)S(1)} %get-tuple-element.56), channel_id=1, source_target_pairs={{0,1},{1,0},{2,3},{3,2},{4,5},{5,4},{6,7},{7,6},{8,9},{9,8},{10,11... | collective-permute-start | bytes 294920 | tf_op jit(solution)/shard_map/ppermute | solution.py:478
  14.8 7.2 %collective-permute-start.7 = (f32[43,512]{1,0:T(8,128)S(1)}, f32[43,512]{1,0:T(8,128)S(1)}, u32[]{:S(2)}, u32[]{:S(2)}) collective-permute-start(f32[43,512]{1,0:T(8,128)S(1)} %get-tuple-element.57), channel_id=1, source_target_pairs={{0,16},{1,2},{2,1},{3,4},{4,3},{5,6},{6,5},{7,8},{8,7},{9,10},{10,... | collective-permute-start | bytes 264200 | tf_op jit(solution)/shard_map/ppermute | solution.py:478
  17.7 4.3 %collective-permute-start.5 = (f32[16,128]{1,0:T(8,128)S(1)}, f32[16,128]{1,0:T(8,128)S(1)}, u32[]{:S(2)}, u32[]{:S(2)}) collective-permute-start(f32[16,128]{1,0:T(8,128)S(1)} %get-tuple-element.53), channel_id=1, source_target_pairs={{0,112},{1,113},{2,114},{3,115},{4,116},{5,117},{6,118},{7,119},{8... | collective-permute-start | bytes 24584 | tf_op jit(solution)/shard_map/ppermute | solution.py:478
  20.5 1.5 %collective-permute-start.4 = (f32[16,128]{1,0:T(8,128)S(1)}, f32[16,128]{1,0:T(8,128)S(1)}, u32[]{:S(2)}, u32[]{:S(2)}) collective-permute-start(f32[16,128]{1,0:T(8,128)S(1)} %get-tuple-element.53), channel_id=1, source_target_pairs={{0,16},{1,17},{2,18},{3,19},{4,20},{5,21},{6,22},{7,23},{8,24},{9,... | collective-permute-start | bytes 24584 | tf_op jit(solution)/shard_map/ppermute | solution.py:478
  23.3 7.7 %collective-permute-start.8 = (f32[80,128]{1,0:T(8,128)S(1)}, f32[80,128]{1,0:T(8,128)S(1)}, u32[]{:S(2)}, u32[]{:S(2)}) collective-permute-start(f32[80,128]{1,0:T(8,128)S(1)} %get-tuple-element.69), channel_id=1, source_target_pairs={{0,17},{1,18},{2,19},{3,20},{4,21},{5,22},{6,23},{7,24},{8,25},{9,... | collective-permute-start | bytes 122888 | tf_op jit(solution)/shard_map/ppermute | solution.py:478
  24.0 6.2 %collective-permute-start.9 = (f32[72,128]{1,0:T(8,128)S(1)}, f32[72,128]{1,0:T(8,128)S(1)}, u32[]{:S(2)}, u32[]{:S(2)}) collective-permute-start(f32[72,128]{1,0:T(8,128)S(1)} %get-tuple-element.70), channel_id=1, source_target_pairs={{0,1},{1,2},{2,3},{3,4},{4,5},{5,6},{6,7},{7,8},{8,9},{9,10},{10,1... | collective-permute-start | bytes 110600 | tf_op jit(solution)/shard_map/ppermute | solution.py:478
  24.9 4.6 %collective-permute-start.10 = (f32[64,128]{1,0:T(8,128)S(1)}, f32[64,128]{1,0:T(8,128)S(1)}, u32[]{:S(2)}, u32[]{:S(2)}) collective-permute-start(f32[64,128]{1,0:T(8,128)S(1)} %get-tuple-element.71), channel_id=1, source_target_pairs={{0,16},{1,17},{2,18},{3,19},{4,20},{5,21},{6,22},{7,23},{8,24},{9,... | collective-permute-start | bytes 98312 | tf_op jit(solution)/shard_map/ppermute | solution.py:478

commit v10 on v9

--- a/solution.py
+++ b/solution.py
@@ -310,9 +310,10 @@
         lists.append(jnp.concatenate([jnp.concatenate(k, 0) for k in kept], 1))
     pieces = split_dot(jnp.concatenate(lists, 0), fold)
     for m, (n, out) in enumerate(zip(numbers, outs)):
-        out[0:64, :] = dot_split(targets[n], pieces[m * 64 : (m + 1) * 64])
-        if out.shape[0] > 64:
-            out[64:, :] = jnp.zeros((out.shape[0] - 64, 128), F32)
+        summed = dot_split(targets[n], pieces[m * 64 : (m + 1) * 64])
+        out[0:32, :] = summed[0:32] + pltpu.roll(summed[32:64], 64, 1)
+        if out.shape[0] > 32:
+            out[32:, :] = jnp.zeros((out.shape[0] - 32, 128), F32)
 
 
 def inbound_fold():
@@ -442,12 +443,13 @@
 
 
 def final_kernel(dg, gy, gx, own, out):
-    total = own[...] + gx[0:64, :] + gy[0:64, :] + dg[0:64, :]
+    total = own[...] + gx[0:32, :] + gy[0:32, :] + dg[0:32, :]
     group = iota((8, 128), 1) // 16
     for c in range(4):
         field = jnp.zeros((8, 128), F32)
         for k in range(8):
-            moved = pltpu.roll(total[k * 8 : (k + 1) * 8], (k - c) % 8 * 16, 1)
+            part = total[k % 4 * 8 : (k % 4 + 1) * 8]
+            moved = pltpu.roll(part, (k - c - k // 4 * 4) % 8 * 16, 1)
             field = jnp.where(group == k, moved, field)
         out[c] = field
 
@@ -552,9 +554,9 @@
             (TOP_LEVELS[0][1], ROWS, COLS),
             (TOP_LEVELS[1][1], ROWS, COLS),
             jax.ShapeDtypeStruct((64, COLS), BF16),
-            (80, 128),
-            (72, 128),
-            (64, 128),
+            (48, 128),
+            (40, 128),
+            (32, 128),
         ],
         state + maps + [in_panels],
     )
@@ -563,7 +565,7 @@
     gx = send(to_gx, lambda i, j: (i + 1, j))
     new_temp, new_salt, own = call(
         outer_kernel,
-        [temp.shape, salt.shape, (64, 128)],
+        [temp.shape, salt.shape, (32, 128)],
         state + [top_temp, top_salt, blocks, *maps, in_panels],
         [pltpu.VMEM(field, F32), pltpu.SemaphoreType.DMA((4,))],
         hbm_out=(0, 1),

time: 32.2 us -> 32.1 us (level)
  no operation moved by 1% of the time
where the time goes in v10:
time: 32.1 us; the launch traced here: 31.6 us
  starting transfers between devices  14.9 us (46%)
  waiting for transfers between devices  8.04 us (25%)
  Pallas kernels  7.84 us (24%)
  between operations  0.74 us (2%)
    ppermute x11, starting transfers between devices, send(): return lax.ppermute(block, ('gx', 'gy'), route)  14.9 us
    ppermute x11, waiting for transfers between devices, send(): return lax.ppermute(block, ('gx', 'gy'), route)  8.04 us
    pallas_call x8, Pallas kernels, call(): pl.pallas_call(kernel, out_shape=shapes, in_specs=[HBM if n in hbm_in els...  7.84 us
  transfers between devices with their start and end apart: 11, of which 5 were waited for; matrix products, arithmetic and copies ran while one was open for 0% of the time, Pallas kernels for 11%

profile of v10, /device:TPU:8, one launch (start us, length us, event | category | flops | bytes accessed | tf_op | source)
XLA Modules:
  0.0 31.6 jit_solution(12677852127417478822)
XLA Ops:
  0.6 2.0 %shard_map.103 = (bf16[64,1024]{1,0:T(8,128)(2,1)S(1)}, s32[2,2,2,64]{3,2,1,0:T(2,128)S(1)}, bf16[4,1024,128]{2,1,0:T(8,128)(2,1)S(1)}, f32[10,16,512]{2,1,0:T(8...) custom-call(bf16[8,8,128]{2,1,0:T(8,128)(2,1)} %air_hbm.1, ...), custom_call_target="tpu_custom_call" | custom-call | tf_op jit(solution)/shard_map/pallas_call | solution.py:463
  2.6 5.6 %collective-permute-start = (f32[296,128]{1,0:T(8,128)S(1)}, f32[296,128]{1,0:T(8,128)S(1)}, u32[]{:S(2)}, u32[]{:S(2)}) collective-permute-start(f32[296,128]{1,0:T(8,128)S(1)} %get-tuple-element.38), channel_id=1, source_target_pairs={{0,15},{1,112},{2,113},{3,114},{4,115},{5,116},{6,117},{7,118},{8,... | collective-permute-start | bytes 454664 | tf_op jit(solution)/shard_map/ppermute | solution.py:480
  8.2 0.8 %collective-permute-start.3 = (f32[288,128]{1,0:T(8,128)S(1)}, f32[288,128]{1,0:T(8,128)S(1)}, u32[]{:S(2)}, u32[]{:S(2)}) collective-permute-start(f32[288,128]{1,0:T(8,128)S(1)} %get-tuple-element.48), channel_id=1, source_target_pairs={{0,112},{1,113},{2,114},{3,115},{4,116},{5,117},{6,118},{7,119},{8... | collective-permute-start | bytes 442376 | tf_op jit(solution)/shard_map/ppermute | solution.py:480
  9.1 0.8 %collective-permute-start.1 = (f32[280,128]{1,0:T(8,128)S(1)}, f32[280,128]{1,0:T(8,128)S(1)}, u32[]{:S(2)}, u32[]{:S(2)}) collective-permute-start(f32[280,128]{1,0:T(8,128)S(1)} %get-tuple-element.39), channel_id=1, source_target_pairs={{0,15},{1,0},{2,1},{3,2},{4,3},{5,4},{6,5},{7,6},{8,7},{9,8},{10,9... | collective-permute-start | bytes 430088 | tf_op jit(solution)/shard_map/ppermute | solution.py:480
  9.9 0.0 collective-permute-start.2
  9.9 1.5 %shard_map.104 = (f32[256,128]{1,0:T(8,128)S(1)}, f32[2,10,16,512]{3,2,1,0:T(8,128)S(1)}, bf16[4,64,64]{2,1,0:T(8,128)(2,1)S(1)}, bf16[4,64,64]{2,1,0:T(8,128)(2,1)S(1)}, bf16[512,128]{1,0:T(8,128)(2,1)S(1)}) custom-call(bf16[64,1024]{1,0:T(8,128)(2,1)S(1)} %get-tuple-element.40.tiled, s32[2,2,2,64]{3,2,1,0:T(2,128)S(1)} %get-tuple-element.41.table, ...), custom_call_target="tpu_custom_call" | custom-call | tf_op jit(solution)/shard_map/pallas_call | solution.py:463
  11.4 0.0 collective-permute-done.2.core
  11.4 2.6 %collective-permute-done.3.zpair = f32[288,128]{1,0:T(8,128)S(1)} collective-permute-done((f32[288,128]{1,0:T(8,128)S(1)}, f32[288,128]{1,0:T(8,128)S(1)}, u32[]{:S(2)}, u32[]{:S(2)}) %collective-permute-start.3) | collective-permute-done | bytes 147488 | tf_op jit(solution)/shard_map/ppermute | solution.py:480
  14.0 0.2 shard_map.105
  14.3 0.0 collective-permute-done.1.gy
  14.3 0.0 collective-permute-done.dg
  14.3 0.3 %shard_map.106 = (f32[2,10,16,512]{3,2,1,0:T(8,128)S(1)}, f32[16,128]{1,0:T(8,128)S(1)}, f32[4,16,512]{2,1,0:T(8,128)S(1)}) custom-call(f32[296,128]{1,0:T(8,128)S(1)} %collective-permute-done.dg, f32[280,128]{1,0:T(8,128)S(1)} %collective-permute-done.1.gy, f32[256,128]{1,0:T(8,128)S(1)} %get-tuple-element.50.base, ...), custom_call_target="tpu_custom_call" | custom-call | tf_op jit(solution)/shard_map/pallas_call | solution.py:463
  14.6 0.0 copy-start
  14.6 0.1 shard_map.107
  14.7 0.1 collective-permute-start.6
  14.8 2.9 %collective-permute-start.7 = (f32[43,512]{1,0:T(8,128)S(1)}, f32[43,512]{1,0:T(8,128)S(1)}, u32[]{:S(2)}, u32[]{:S(2)}) collective-permute-start(f32[43,512]{1,0:T(8,128)S(1)} %get-tuple-element.57), channel_id=1, source_target_pairs={{0,16},{1,2},{2,1},{3,4},{4,3},{5,6},{6,5},{7,8},{8,7},{9,10},{10,... | collective-permute-start | bytes 264200 | tf_op jit(solution)/shard_map/ppermute | solution.py:480
  17.7 2.8 %collective-permute-start.5 = (f32[16,128]{1,0:T(8,128)S(1)}, f32[16,128]{1,0:T(8,128)S(1)}, u32[]{:S(2)}, u32[]{:S(2)}) collective-permute-start(f32[16,128]{1,0:T(8,128)S(1)} %get-tuple-element.53), channel_id=1, source_target_pairs={{0,112},{1,113},{2,114},{3,115},{4,116},{5,117},{6,118},{7,119},{8... | collective-permute-start | bytes 24584 | tf_op jit(solution)/shard_map/ppermute | solution.py:480
  20.5 0.0 collective-permute-start.4
  20.5 1.5 %collective-permute-done.5.zpair = f32[16,128]{1,0:T(8,128)S(1)} collective-permute-done((f32[16,128]{1,0:T(8,128)S(1)}, f32[16,128]{1,0:T(8,128)S(1)}, u32[]{:S(2)}, u32[]{:S(2)}) %collective-permute-start.5) | collective-permute-done | bytes 8224 | tf_op jit(solution)/shard_map/ppermute | solution.py:480
  22.0 0.0 collective-permute-done.4.core
  22.0 0.0 collective-permute-done.7.xo
  22.0 0.0 collective-permute-done.6.xe
  22.0 0.0 copy-done
  22.1 1.3 %shard_map.108 = (f32[3,16,512]{2,1,0:T(8,128)S(1)}, f32[1,16,512]{2,1,0:T(8,128)S(1)}, bf16[64,512]{1,0:T(8,128)(2,1)S(1)}, f32[48,128]{1,0:T(8,128)S(1)}, f32[...) custom-call(f32[2,10,16,512]{3,2,1,0:T(8,128)S(1)} %get-tuple-element.52.new.old, f32[16,128]{1,0:T(8,128)S(1)} %collective-permute-done.4.core, ...), custom_call_target="tpu_custom_call" | custom-call | tf_op jit(solution)/shard_map/pallas_call | solution.py:463
  23.3 0.7 %collective-permute-start.8 = (f32[48,128]{1,0:T(8,128)S(1)}, f32[48,128]{1,0:T(8,128)S(1)}, u32[]{:S(2)}, u32[]{:S(2)}) collective-permute-start(f32[48,128]{1,0:T(8,128)S(1)} %get-tuple-element.69), channel_id=1, source_target_pairs={{0,17},{1,18},{2,19},{3,20},{4,21},{5,22},{6,23},{7,24},{8,25},{9,... | collective-permute-start | bytes 73736 | tf_op jit(solution)/shard_map/ppermute | solution.py:480
  24.0 0.9 %collective-permute-start.9 = (f32[40,128]{1,0:T(8,128)S(1)}, f32[40,128]{1,0:T(8,128)S(1)}, u32[]{:S(2)}, u32[]{:S(2)}) collective-permute-start(f32[40,128]{1,0:T(8,128)S(1)} %get-tuple-element.70), channel_id=1, source_target_pairs={{0,1},{1,2},{2,3},{3,4},{4,5},{5,6},{6,7},{7,8},{8,9},{9,10},{10,1... | collective-permute-start | bytes 61448 | tf_op jit(solution)/shard_map/ppermute | solution.py:480
  24.9 0.2 collective-permute-start.10
  25.2 1.7 %shard_map.109 = (f32[10,16,512]{2,1,0:T(8,128)}, f32[10,16,512]{2,1,0:T(8,128)}, f32[32,128]{1,0:T(8,128)S(1)}) custom-call(f32[2,10,16,512]{3,2,1,0:T(8,128)S(1)} %get-tuple-element.52.new.old, f32[16,128]{1,0:T(8,128)S(1)} %collective-permute-done.4.core, f32[16,128]{1,0:T(8,128)S(1)} %collective-permute-done.5.zpair, ...), custom_call_target="tpu_custom_call" | custom-call | tf_op jit(solution)/shard_map/pallas_call | solution.py:463
  26.9 2.4 %collective-permute-done.10.gx = f32[32,128]{1,0:T(8,128)S(1)} collective-permute-done((f32[32,128]{1,0:T(8,128)S(1)}, f32[32,128]{1,0:T(8,128)S(1)}, u32[]{:S(2)}, u32[]{:S(2)}) %collective-permute-start.10) | collective-permute-done | bytes 16416 | tf_op jit(solution)/shard_map/ppermute | solution.py:480
  29.3 0.6 %collective-permute-done.9.gy = f32[40,128]{1,0:T(8,128)S(1)} collective-permute-done((f32[40,128]{1,0:T(8,128)S(1)}, f32[40,128]{1,0:T(8,128)S(1)}, u32[]{:S(2)}, u32[]{:S(2)}) %collective-permute-start.9) | collective-permute-done | bytes 20512 | tf_op jit(solution)/shard_map/ppermute | solution.py:480
  29.9 1.0 %collective-permute-done.8.dg = f32[48,128]{1,0:T(8,128)S(1)} collective-permute-done((f32[48,128]{1,0:T(8,128)S(1)}, f32[48,128]{1,0:T(8,128)S(1)}, u32[]{:S(2)}, u32[]{:S(2)}) %collective-permute-start.8) | collective-permute-done | bytes 24608 | tf_op jit(solution)/shard_map/ppermute | solution.py:480
  30.9 0.7 %shard_map.110 = f32[4,8,128]{2,1,0:T(8,128)} custom-call(f32[48,128]{1,0:T(8,128)S(1)} %collective-permute-done.8.dg, f32[40,128]{1,0:T(8,128)S(1)} %collective-permute-done.9.gy, f32[32,128]{1,0:T(8,128)S(1)} %collective-permute-done.10.gx, f32[32,128]{1,0:T(8,128)S(1)} %get-tuple-element.72.own), custom_call_target="tpu_custom_call" | custom-call | tf_op jit(solution)/shard_map/pallas_call | solution.py:463
Async XLA Ops:
  2.6 11.7 %collective-permute-start = (f32[296,128]{1,0:T(8,128)S(1)}, f32[296,128]{1,0:T(8,128)S(1)}, u32[]{:S(2)}, u32[]{:S(2)}) collective-permute-start(f32[296,128]{1,0:T(8,128)S(1)} %get-tuple-element.38), channel_id=1, source_target_pairs={{0,15},{1,112},{2,113},{3,114},{4,115},{5,116},{6,117},{7,118},{8,... | collective-permute-start | bytes 454664 | tf_op jit(solution)/shard_map/ppermute | solution.py:480
  8.2 5.8 %collective-permute-start.3 = (f32[288,128]{1,0:T(8,128)S(1)}, f32[288,128]{1,0:T(8,128)S(1)}, u32[]{:S(2)}, u32[]{:S(2)}) collective-permute-start(f32[288,128]{1,0:T(8,128)S(1)} %get-tuple-element.48), channel_id=1, source_target_pairs={{0,112},{1,113},{2,114},{3,115},{4,116},{5,117},{6,118},{7,119},{8... | collective-permute-start | bytes 442376 | tf_op jit(solution)/shard_map/ppermute | solution.py:480
  9.1 5.2 %collective-permute-start.1 = (f32[280,128]{1,0:T(8,128)S(1)}, f32[280,128]{1,0:T(8,128)S(1)}, u32[]{:S(2)}, u32[]{:S(2)}) collective-permute-start(f32[280,128]{1,0:T(8,128)S(1)} %get-tuple-element.39), channel_id=1, source_target_pairs={{0,15},{1,0},{2,1},{3,2},{4,3},{5,4},{6,5},{7,6},{8,7},{9,8},{10,9... | collective-permute-start | bytes 430088 | tf_op jit(solution)/shard_map/ppermute | solution.py:480
  9.9 1.5 %collective-permute-start.2 = (f32[272,128]{1,0:T(8,128)S(1)}, f32[272,128]{1,0:T(8,128)S(1)}, u32[]{:S(2)}, u32[]{:S(2)}) collective-permute-start(f32[272,128]{1,0:T(8,128)S(1)} %get-tuple-element.47), channel_id=1, source_target_pairs={{0,16},{1,17},{2,18},{3,19},{4,20},{5,21},{6,22},{7,23},{8,24},{9,... | collective-permute-start | bytes 417800 | tf_op jit(solution)/shard_map/ppermute | solution.py:480
  14.6 7.4 %copy-start = (bf16[1,1,2,2,64,16,128]{6,5,4,3,2,1,0:T(8,128)(2,1)S(1)}, bf16[1,1,2,2,64,16,128]{6,5,4,3,2,1,0:T(8,128)(2,1)}, u32[]{:S(2)}) copy-start(bf16[1,1,2,2,64,16,128]{6,5,4,3,2,1,0:T(8,128)(2,1)} %param.15) | copy-start | bytes 3145732
  14.7 7.3 %collective-permute-start.6 = (f32[48,512]{1,0:T(8,128)S(1)}, f32[48,512]{1,0:T(8,128)S(1)}, u32[]{:S(2)}, u32[]{:S(2)}) collective-permute-start(f32[48,512]{1,0:T(8,128)S(1)} %get-tuple-element.56), channel_id=1, source_target_pairs={{0,1},{1,0},{2,3},{3,2},{4,5},{5,4},{6,7},{7,6},{8,9},{9,8},{10,11... | collective-permute-start | bytes 294920 | tf_op jit(solution)/shard_map/ppermute | solution.py:480
  14.8 7.2 %collective-permute-start.7 = (f32[43,512]{1,0:T(8,128)S(1)}, f32[43,512]{1,0:T(8,128)S(1)}, u32[]{:S(2)}, u32[]{:S(2)}) collective-permute-start(f32[43,512]{1,0:T(8,128)S(1)} %get-tuple-element.57), channel_id=1, source_target_pairs={{0,16},{1,2},{2,1},{3,4},{4,3},{5,6},{6,5},{7,8},{8,7},{9,10},{10,... | collective-permute-start | bytes 264200 | tf_op jit(solution)/shard_map/ppermute | solution.py:480
  17.7 4.3 %collective-permute-start.5 = (f32[16,128]{1,0:T(8,128)S(1)}, f32[16,128]{1,0:T(8,128)S(1)}, u32[]{:S(2)}, u32[]{:S(2)}) collective-permute-start(f32[16,128]{1,0:T(8,128)S(1)} %get-tuple-element.53), channel_id=1, source_target_pairs={{0,112},{1,113},{2,114},{3,115},{4,116},{5,117},{6,118},{7,119},{8... | collective-permute-start | bytes 24584 | tf_op jit(solution)/shard_map/ppermute | solution.py:480
  20.5 1.5 %collective-permute-start.4 = (f32[16,128]{1,0:T(8,128)S(1)}, f32[16,128]{1,0:T(8,128)S(1)}, u32[]{:S(2)}, u32[]{:S(2)}) collective-permute-start(f32[16,128]{1,0:T(8,128)S(1)} %get-tuple-element.53), channel_id=1, source_target_pairs={{0,16},{1,17},{2,18},{3,19},{4,20},{5,21},{6,22},{7,23},{8,24},{9,... | collective-permute-start | bytes 24584 | tf_op jit(solution)/shard_map/ppermute | solution.py:480
  23.3 7.5 %collective-permute-start.8 = (f32[48,128]{1,0:T(8,128)S(1)}, f32[48,128]{1,0:T(8,128)S(1)}, u32[]{:S(2)}, u32[]{:S(2)}) collective-permute-start(f32[48,128]{1,0:T(8,128)S(1)} %get-tuple-element.69), channel_id=1, source_target_pairs={{0,17},{1,18},{2,19},{3,20},{4,21},{5,22},{6,23},{7,24},{8,25},{9,... | collective-permute-start | bytes 73736 | tf_op jit(solution)/shard_map/ppermute | solution.py:480
  24.0 5.9 %collective-permute-start.9 = (f32[40,128]{1,0:T(8,128)S(1)}, f32[40,128]{1,0:T(8,128)S(1)}, u32[]{:S(2)}, u32[]{:S(2)}) collective-permute-start(f32[40,128]{1,0:T(8,128)S(1)} %get-tuple-element.70), channel_id=1, source_target_pairs={{0,1},{1,2},{2,3},{3,4},{4,5},{5,6},{6,7},{7,8},{8,9},{9,10},{10,1... | collective-permute-start | bytes 61448 | tf_op jit(solution)/shard_map/ppermute | solution.py:480
  24.9 4.4 %collective-permute-start.10 = (f32[32,128]{1,0:T(8,128)S(1)}, f32[32,128]{1,0:T(8,128)S(1)}, u32[]{:S(2)}, u32[]{:S(2)}) collective-permute-start(f32[32,128]{1,0:T(8,128)S(1)} %get-tuple-element.71), channel_id=1, source_target_pairs={{0,16},{1,17},{2,18},{3,19},{4,20},{5,21},{6,22},{7,23},{8,24},{9,... | collective-permute-start | bytes 49160 | tf_op jit(solution)/shard_map/ppermute | solution.py:480

commit v11 on v10

--- a/solution.py
+++ b/solution.py
@@ -76,8 +76,9 @@
     fold = (iota((128, 128), 0) % 16 == iota((128, 128), 1) % 16).astype(F32).astype(BF16)
     spread = []
     for c in range(8):
+        field = air[c].astype(F32)
         for r in range(8):
-            row = jnp.broadcast_to(air[c, r : r + 1, :].astype(F32), (8, 128))
+            row = jnp.broadcast_to(field[r : r + 1], (8, 128))
             spread.append(jnp.where(mask, row, 0.0))
     tiled = dot(jnp.concatenate(spread, 0).astype(BF16), fold).astype(BF16)
     return jnp.concatenate([tiled[c * 64 : (c + 1) * 64] for c in range(8)], 1)

time: 32.1 us -> 32.1 us (level)
  no operation moved by 1% of the time
where the time goes in v11:
time: 32.1 us; the launch traced here: 31.6 us
  starting transfers between devices  14.9 us (46%)
  waiting for transfers between devices  8.05 us (25%)
  Pallas kernels  7.84 us (24%)
  between operations  0.74 us (2%)
    ppermute x11, starting transfers between devices, send(): return lax.ppermute(block, ('gx', 'gy'), route)  14.9 us
    ppermute x11, waiting for transfers between devices, send(): return lax.ppermute(block, ('gx', 'gy'), route)  8.05 us
    pallas_call x8, Pallas kernels, call(): pl.pallas_call(kernel, out_shape=shapes, in_specs=[HBM if n in hbm_in els...  7.84 us
  transfers between devices with their start and end apart: 11, of which 5 were waited for; matrix products, arithmetic and copies ran while one was open for 0% of the time, Pallas kernels for 11%

profile of v11, /device:TPU:8, one launch (start us, length us, event | category | flops | bytes accessed | tf_op | source)
XLA Modules:
  0.0 31.6 jit_solution(16539951451791286290)
XLA Ops:
  0.6 2.0 %shard_map.103 = (bf16[64,1024]{1,0:T(8,128)(2,1)S(1)}, s32[2,2,2,64]{3,2,1,0:T(2,128)S(1)}, bf16[4,1024,128]{2,1,0:T(8,128)(2,1)S(1)}, f32[10,16,512]{2,1,0:T(8...) custom-call(bf16[8,8,128]{2,1,0:T(8,128)(2,1)} %air_hbm.1, ...), custom_call_target="tpu_custom_call" | custom-call | tf_op jit(solution)/shard_map/pallas_call | solution.py:464
  2.6 5.6 %collective-permute-start = (f32[296,128]{1,0:T(8,128)S(1)}, f32[296,128]{1,0:T(8,128)S(1)}, u32[]{:S(2)}, u32[]{:S(2)}) collective-permute-start(f32[296,128]{1,0:T(8,128)S(1)} %get-tuple-element.38), channel_id=1, source_target_pairs={{0,15},{1,112},{2,113},{3,114},{4,115},{5,116},{6,117},{7,118},{8,... | collective-permute-start | bytes 454664 | tf_op jit(solution)/shard_map/ppermute | solution.py:481
  8.2 0.8 %collective-permute-start.3 = (f32[288,128]{1,0:T(8,128)S(1)}, f32[288,128]{1,0:T(8,128)S(1)}, u32[]{:S(2)}, u32[]{:S(2)}) collective-permute-start(f32[288,128]{1,0:T(8,128)S(1)} %get-tuple-element.48), channel_id=1, source_target_pairs={{0,112},{1,113},{2,114},{3,115},{4,116},{5,117},{6,118},{7,119},{8... | collective-permute-start | bytes 442376 | tf_op jit(solution)/shard_map/ppermute | solution.py:481
  9.1 0.8 %collective-permute-start.1 = (f32[280,128]{1,0:T(8,128)S(1)}, f32[280,128]{1,0:T(8,128)S(1)}, u32[]{:S(2)}, u32[]{:S(2)}) collective-permute-start(f32[280,128]{1,0:T(8,128)S(1)} %get-tuple-element.39), channel_id=1, source_target_pairs={{0,15},{1,0},{2,1},{3,2},{4,3},{5,4},{6,5},{7,6},{8,7},{9,8},{10,9... | collective-permute-start | bytes 430088 | tf_op jit(solution)/shard_map/ppermute | solution.py:481
  9.9 0.0 collective-permute-start.2
  9.9 1.5 %shard_map.104 = (f32[256,128]{1,0:T(8,128)S(1)}, f32[2,10,16,512]{3,2,1,0:T(8,128)S(1)}, bf16[4,64,64]{2,1,0:T(8,128)(2,1)S(1)}, bf16[4,64,64]{2,1,0:T(8,128)(2,1)S(1)}, bf16[512,128]{1,0:T(8,128)(2,1)S(1)}) custom-call(bf16[64,1024]{1,0:T(8,128)(2,1)S(1)} %get-tuple-element.40.tiled, s32[2,2,2,64]{3,2,1,0:T(2,128)S(1)} %get-tuple-element.41.table, ...), custom_call_target="tpu_custom_call" | custom-call | tf_op jit(solution)/shard_map/pallas_call | solution.py:464
  11.4 0.0 collective-permute-done.2.core
  11.4 2.6 %collective-permute-done.3.zpair = f32[288,128]{1,0:T(8,128)S(1)} collective-permute-done((f32[288,128]{1,0:T(8,128)S(1)}, f32[288,128]{1,0:T(8,128)S(1)}, u32[]{:S(2)}, u32[]{:S(2)}) %collective-permute-start.3) | collective-permute-done | bytes 147488 | tf_op jit(solution)/shard_map/ppermute | solution.py:481
  14.0 0.2 shard_map.105
  14.3 0.0 collective-permute-done.1.gy
  14.3 0.0 collective-permute-done.dg
  14.3 0.3 %shard_map.106 = (f32[2,10,16,512]{3,2,1,0:T(8,128)S(1)}, f32[16,128]{1,0:T(8,128)S(1)}, f32[4,16,512]{2,1,0:T(8,128)S(1)}) custom-call(f32[296,128]{1,0:T(8,128)S(1)} %collective-permute-done.dg, f32[280,128]{1,0:T(8,128)S(1)} %collective-permute-done.1.gy, f32[256,128]{1,0:T(8,128)S(1)} %get-tuple-element.50.base, ...), custom_call_target="tpu_custom_call" | custom-call | tf_op jit(solution)/shard_map/pallas_call | solution.py:464
  14.6 0.0 copy-start
  14.6 0.1 shard_map.107
  14.7 0.1 collective-permute-start.6
  14.8 2.9 %collective-permute-start.7 = (f32[43,512]{1,0:T(8,128)S(1)}, f32[43,512]{1,0:T(8,128)S(1)}, u32[]{:S(2)}, u32[]{:S(2)}) collective-permute-start(f32[43,512]{1,0:T(8,128)S(1)} %get-tuple-element.57), channel_id=1, source_target_pairs={{0,16},{1,2},{2,1},{3,4},{4,3},{5,6},{6,5},{7,8},{8,7},{9,10},{10,... | collective-permute-start | bytes 264200 | tf_op jit(solution)/shard_map/ppermute | solution.py:481
  17.7 2.8 %collective-permute-start.5 = (f32[16,128]{1,0:T(8,128)S(1)}, f32[16,128]{1,0:T(8,128)S(1)}, u32[]{:S(2)}, u32[]{:S(2)}) collective-permute-start(f32[16,128]{1,0:T(8,128)S(1)} %get-tuple-element.53), channel_id=1, source_target_pairs={{0,112},{1,113},{2,114},{3,115},{4,116},{5,117},{6,118},{7,119},{8... | collective-permute-start | bytes 24584 | tf_op jit(solution)/shard_map/ppermute | solution.py:481
  20.5 0.0 collective-permute-start.4
  20.5 1.5 %collective-permute-done.5.zpair = f32[16,128]{1,0:T(8,128)S(1)} collective-permute-done((f32[16,128]{1,0:T(8,128)S(1)}, f32[16,128]{1,0:T(8,128)S(1)}, u32[]{:S(2)}, u32[]{:S(2)}) %collective-permute-start.5) | collective-permute-done | bytes 8224 | tf_op jit(solution)/shard_map/ppermute | solution.py:481
  22.0 0.0 collective-permute-done.4.core
  22.0 0.0 collective-permute-done.7.xo
  22.0 0.0 collective-permute-done.6.xe
  22.0 0.0 copy-done
  22.1 1.3 %shard_map.108 = (f32[3,16,512]{2,1,0:T(8,128)S(1)}, f32[1,16,512]{2,1,0:T(8,128)S(1)}, bf16[64,512]{1,0:T(8,128)(2,1)S(1)}, f32[48,128]{1,0:T(8,128)S(1)}, f32[...) custom-call(f32[2,10,16,512]{3,2,1,0:T(8,128)S(1)} %get-tuple-element.52.new.old, f32[16,128]{1,0:T(8,128)S(1)} %collective-permute-done.4.core, ...), custom_call_target="tpu_custom_call" | custom-call | tf_op jit(solution)/shard_map/pallas_call | solution.py:464
  23.3 0.7 %collective-permute-start.8 = (f32[48,128]{1,0:T(8,128)S(1)}, f32[48,128]{1,0:T(8,128)S(1)}, u32[]{:S(2)}, u32[]{:S(2)}) collective-permute-start(f32[48,128]{1,0:T(8,128)S(1)} %get-tuple-element.69), channel_id=1, source_target_pairs={{0,17},{1,18},{2,19},{3,20},{4,21},{5,22},{6,23},{7,24},{8,25},{9,... | collective-permute-start | bytes 73736 | tf_op jit(solution)/shard_map/ppermute | solution.py:481
  24.0 0.9 %collective-permute-start.9 = (f32[40,128]{1,0:T(8,128)S(1)}, f32[40,128]{1,0:T(8,128)S(1)}, u32[]{:S(2)}, u32[]{:S(2)}) collective-permute-start(f32[40,128]{1,0:T(8,128)S(1)} %get-tuple-element.70), channel_id=1, source_target_pairs={{0,1},{1,2},{2,3},{3,4},{4,5},{5,6},{6,7},{7,8},{8,9},{9,10},{10,1... | collective-permute-start | bytes 61448 | tf_op jit(solution)/shard_map/ppermute | solution.py:481
  24.9 0.2 collective-permute-start.10
  25.2 1.7 %shard_map.109 = (f32[10,16,512]{2,1,0:T(8,128)}, f32[10,16,512]{2,1,0:T(8,128)}, f32[32,128]{1,0:T(8,128)S(1)}) custom-call(f32[2,10,16,512]{3,2,1,0:T(8,128)S(1)} %get-tuple-element.52.new.old, f32[16,128]{1,0:T(8,128)S(1)} %collective-permute-done.4.core, f32[16,128]{1,0:T(8,128)S(1)} %collective-permute-done.5.zpair, ...), custom_call_target="tpu_custom_call" | custom-call | tf_op jit(solution)/shard_map/pallas_call | solution.py:464
  26.9 2.4 %collective-permute-done.10.gx = f32[32,128]{1,0:T(8,128)S(1)} collective-permute-done((f32[32,128]{1,0:T(8,128)S(1)}, f32[32,128]{1,0:T(8,128)S(1)}, u32[]{:S(2)}, u32[]{:S(2)}) %collective-permute-start.10) | collective-permute-done | bytes 16416 | tf_op jit(solution)/shard_map/ppermute | solution.py:481
  29.3 0.6 %collective-permute-done.9.gy = f32[40,128]{1,0:T(8,128)S(1)} collective-permute-done((f32[40,128]{1,0:T(8,128)S(1)}, f32[40,128]{1,0:T(8,128)S(1)}, u32[]{:S(2)}, u32[]{:S(2)}) %collective-permute-start.9) | collective-permute-done | bytes 20512 | tf_op jit(solution)/shard_map/ppermute | solution.py:481
  29.9 1.0 %collective-permute-done.8.dg = f32[48,128]{1,0:T(8,128)S(1)} collective-permute-done((f32[48,128]{1,0:T(8,128)S(1)}, f32[48,128]{1,0:T(8,128)S(1)}, u32[]{:S(2)}, u32[]{:S(2)}) %collective-permute-start.8) | collective-permute-done | bytes 24608 | tf_op jit(solution)/shard_map/ppermute | solution.py:481
  30.9 0.7 %shard_map.110 = f32[4,8,128]{2,1,0:T(8,128)} custom-call(f32[48,128]{1,0:T(8,128)S(1)} %collective-permute-done.8.dg, f32[40,128]{1,0:T(8,128)S(1)} %collective-permute-done.9.gy, f32[32,128]{1,0:T(8,128)S(1)} %collective-permute-done.10.gx, f32[32,128]{1,0:T(8,128)S(1)} %get-tuple-element.72.own), custom_call_target="tpu_custom_call" | custom-call | tf_op jit(solution)/shard_map/pallas_call | solution.py:464
Async XLA Ops:
  2.6 11.7 %collective-permute-start = (f32[296,128]{1,0:T(8,128)S(1)}, f32[296,128]{1,0:T(8,128)S(1)}, u32[]{:S(2)}, u32[]{:S(2)}) collective-permute-start(f32[296,128]{1,0:T(8,128)S(1)} %get-tuple-element.38), channel_id=1, source_target_pairs={{0,15},{1,112},{2,113},{3,114},{4,115},{5,116},{6,117},{7,118},{8,... | collective-permute-start | bytes 454664 | tf_op jit(solution)/shard_map/ppermute | solution.py:481
  8.2 5.8 %collective-permute-start.3 = (f32[288,128]{1,0:T(8,128)S(1)}, f32[288,128]{1,0:T(8,128)S(1)}, u32[]{:S(2)}, u32[]{:S(2)}) collective-permute-start(f32[288,128]{1,0:T(8,128)S(1)} %get-tuple-element.48), channel_id=1, source_target_pairs={{0,112},{1,113},{2,114},{3,115},{4,116},{5,117},{6,118},{7,119},{8... | collective-permute-start | bytes 442376 | tf_op jit(solution)/shard_map/ppermute | solution.py:481
  9.1 5.2 %collective-permute-start.1 = (f32[280,128]{1,0:T(8,128)S(1)}, f32[280,128]{1,0:T(8,128)S(1)}, u32[]{:S(2)}, u32[]{:S(2)}) collective-permute-start(f32[280,128]{1,0:T(8,128)S(1)} %get-tuple-element.39), channel_id=1, source_target_pairs={{0,15},{1,0},{2,1},{3,2},{4,3},{5,4},{6,5},{7,6},{8,7},{9,8},{10,9... | collective-permute-start | bytes 430088 | tf_op jit(solution)/shard_map/ppermute | solution.py:481
  9.9 1.5 %collective-permute-start.2 = (f32[272,128]{1,0:T(8,128)S(1)}, f32[272,128]{1,0:T(8,128)S(1)}, u32[]{:S(2)}, u32[]{:S(2)}) collective-permute-start(f32[272,128]{1,0:T(8,128)S(1)} %get-tuple-element.47), channel_id=1, source_target_pairs={{0,16},{1,17},{2,18},{3,19},{4,20},{5,21},{6,22},{7,23},{8,24},{9,... | collective-permute-start | bytes 417800 | tf_op jit(solution)/shard_map/ppermute | solution.py:481
  14.6 7.4 %copy-start = (bf16[1,1,2,2,64,16,128]{6,5,4,3,2,1,0:T(8,128)(2,1)S(1)}, bf16[1,1,2,2,64,16,128]{6,5,4,3,2,1,0:T(8,128)(2,1)}, u32[]{:S(2)}) copy-start(bf16[1,1,2,2,64,16,128]{6,5,4,3,2,1,0:T(8,128)(2,1)} %param.15) | copy-start | bytes 3145732
  14.7 7.3 %collective-permute-start.6 = (f32[48,512]{1,0:T(8,128)S(1)}, f32[48,512]{1,0:T(8,128)S(1)}, u32[]{:S(2)}, u32[]{:S(2)}) collective-permute-start(f32[48,512]{1,0:T(8,128)S(1)} %get-tuple-element.56), channel_id=1, source_target_pairs={{0,1},{1,0},{2,3},{3,2},{4,5},{5,4},{6,7},{7,6},{8,9},{9,8},{10,11... | collective-permute-start | bytes 294920 | tf_op jit(solution)/shard_map/ppermute | solution.py:481
  14.8 7.2 %collective-permute-start.7 = (f32[43,512]{1,0:T(8,128)S(1)}, f32[43,512]{1,0:T(8,128)S(1)}, u32[]{:S(2)}, u32[]{:S(2)}) collective-permute-start(f32[43,512]{1,0:T(8,128)S(1)} %get-tuple-element.57), channel_id=1, source_target_pairs={{0,16},{1,2},{2,1},{3,4},{4,3},{5,6},{6,5},{7,8},{8,7},{9,10},{10,... | collective-permute-start | bytes 264200 | tf_op jit(solution)/shard_map/ppermute | solution.py:481
  17.7 4.3 %collective-permute-start.5 = (f32[16,128]{1,0:T(8,128)S(1)}, f32[16,128]{1,0:T(8,128)S(1)}, u32[]{:S(2)}, u32[]{:S(2)}) collective-permute-start(f32[16,128]{1,0:T(8,128)S(1)} %get-tuple-element.53), channel_id=1, source_target_pairs={{0,112},{1,113},{2,114},{3,115},{4,116},{5,117},{6,118},{7,119},{8... | collective-permute-start | bytes 24584 | tf_op jit(solution)/shard_map/ppermute | solution.py:481
  20.5 1.5 %collective-permute-start.4 = (f32[16,128]{1,0:T(8,128)S(1)}, f32[16,128]{1,0:T(8,128)S(1)}, u32[]{:S(2)}, u32[]{:S(2)}) collective-permute-start(f32[16,128]{1,0:T(8,128)S(1)} %get-tuple-element.53), channel_id=1, source_target_pairs={{0,16},{1,17},{2,18},{3,19},{4,20},{5,21},{6,22},{7,23},{8,24},{9,... | collective-permute-start | bytes 24584 | tf_op jit(solution)/shard_map/ppermute | solution.py:481
  23.3 7.5 %collective-permute-start.8 = (f32[48,128]{1,0:T(8,128)S(1)}, f32[48,128]{1,0:T(8,128)S(1)}, u32[]{:S(2)}, u32[]{:S(2)}) collective-permute-start(f32[48,128]{1,0:T(8,128)S(1)} %get-tuple-element.69), channel_id=1, source_target_pairs={{0,17},{1,18},{2,19},{3,20},{4,21},{5,22},{6,23},{7,24},{8,25},{9,... | collective-permute-start | bytes 73736 | tf_op jit(solution)/shard_map/ppermute | solution.py:481
  24.0 5.9 %collective-permute-start.9 = (f32[40,128]{1,0:T(8,128)S(1)}, f32[40,128]{1,0:T(8,128)S(1)}, u32[]{:S(2)}, u32[]{:S(2)}) collective-permute-start(f32[40,128]{1,0:T(8,128)S(1)} %get-tuple-element.70), channel_id=1, source_target_pairs={{0,1},{1,2},{2,3},{3,4},{4,5},{5,6},{6,7},{7,8},{8,9},{9,10},{10,1... | collective-permute-start | bytes 61448 | tf_op jit(solution)/shard_map/ppermute | solution.py:481
  24.9 4.4 %collective-permute-start.10 = (f32[32,128]{1,0:T(8,128)S(1)}, f32[32,128]{1,0:T(8,128)S(1)}, u32[]{:S(2)}, u32[]{:S(2)}) collective-permute-start(f32[32,128]{1,0:T(8,128)S(1)} %get-tuple-element.71), channel_id=1, source_target_pairs={{0,16},{1,17},{2,18},{3,19},{4,20},{5,21},{6,22},{7,23},{8,24},{9,... | collective-permute-start | bytes 49160 | tf_op jit(solution)/shard_map/ppermute | solution.py:481

commit v12 on v11

--- a/solution.py
+++ b/solution.py
@@ -555,8 +555,8 @@
             (TOP_LEVELS[0][1], ROWS, COLS),
             (TOP_LEVELS[1][1], ROWS, COLS),
             jax.ShapeDtypeStruct((64, COLS), BF16),
-            (48, 128),
-            (40, 128),
+            (32, 128),
+            (32, 128),
             (32, 128),
         ],
         state + maps + [in_panels],

time: 32.1 us -> 32 us (level)
  transfers between devices with their start and end apart: 11 -> 11, of which waited for: 5 -> 3; matrix products, arithmetic and copies ran while one was open for 0% -> 0% of each run, Pallas kernels for 11% -> 11%
where the time goes in v12:
time: 32 us; the launch traced here: 31.5 us
  starting transfers between devices  14.9 us (47%)
  waiting for transfers between devices  8 us (25%)
  Pallas kernels  7.78 us (24%)
  between operations  0.74 us (2%)
    ppermute x11, starting transfers between devices, send(): return lax.ppermute(block, ('gx', 'gy'), route)  14.9 us
    ppermute x11, waiting for transfers between devices, send(): return lax.ppermute(block, ('gx', 'gy'), route)  8 us
    pallas_call x8, Pallas kernels, call(): pl.pallas_call(kernel, out_shape=shapes, in_specs=[HBM if n in hbm_in els...  7.78 us
  transfers between devices with their start and end apart: 11, of which 3 were waited for; matrix products, arithmetic and copies ran while one was open for 0% of the time, Pallas kernels for 11%

profile of v12, /device:TPU:8, one launch (start us, length us, event | category | flops | bytes accessed | tf_op | source)
XLA Modules:
  0.0 31.5 jit_solution(11768002042260626861)
XLA Ops:
  0.6 1.9 %shard_map.103 = (bf16[64,1024]{1,0:T(8,128)(2,1)S(1)}, s32[2,2,2,64]{3,2,1,0:T(2,128)S(1)}, bf16[4,1024,128]{2,1,0:T(8,128)(2,1)S(1)}, f32[10,16,512]{2,1,0:T(8...) custom-call(bf16[8,8,128]{2,1,0:T(8,128)(2,1)} %air_hbm.1, ...), custom_call_target="tpu_custom_call" | custom-call | tf_op jit(solution)/shard_map/pallas_call | solution.py:464
  2.6 5.6 %collective-permute-start = (f32[296,128]{1,0:T(8,128)S(1)}, f32[296,128]{1,0:T(8,128)S(1)}, u32[]{:S(2)}, u32[]{:S(2)}) collective-permute-start(f32[296,128]{1,0:T(8,128)S(1)} %get-tuple-element.38), channel_id=1, source_target_pairs={{0,15},{1,112},{2,113},{3,114},{4,115},{5,116},{6,117},{7,118},{8,... | collective-permute-start | bytes 454664 | tf_op jit(solution)/shard_map/ppermute | solution.py:481
  8.2 0.8 %collective-permute-start.3 = (f32[288,128]{1,0:T(8,128)S(1)}, f32[288,128]{1,0:T(8,128)S(1)}, u32[]{:S(2)}, u32[]{:S(2)}) collective-permute-start(f32[288,128]{1,0:T(8,128)S(1)} %get-tuple-element.48), channel_id=1, source_target_pairs={{0,112},{1,113},{2,114},{3,115},{4,116},{5,117},{6,118},{7,119},{8... | collective-permute-start | bytes 442376 | tf_op jit(solution)/shard_map/ppermute | solution.py:481
  9.1 0.8 %collective-permute-start.1 = (f32[280,128]{1,0:T(8,128)S(1)}, f32[280,128]{1,0:T(8,128)S(1)}, u32[]{:S(2)}, u32[]{:S(2)}) collective-permute-start(f32[280,128]{1,0:T(8,128)S(1)} %get-tuple-element.39), channel_id=1, source_target_pairs={{0,15},{1,0},{2,1},{3,2},{4,3},{5,4},{6,5},{7,6},{8,7},{9,8},{10,9... | collective-permute-start | bytes 430088 | tf_op jit(solution)/shard_map/ppermute | solution.py:481
  9.9 0.0 collective-permute-start.2
  9.9 1.5 %shard_map.104 = (f32[256,128]{1,0:T(8,128)S(1)}, f32[2,10,16,512]{3,2,1,0:T(8,128)S(1)}, bf16[4,64,64]{2,1,0:T(8,128)(2,1)S(1)}, bf16[4,64,64]{2,1,0:T(8,128)(2,1)S(1)}, bf16[512,128]{1,0:T(8,128)(2,1)S(1)}) custom-call(bf16[64,1024]{1,0:T(8,128)(2,1)S(1)} %get-tuple-element.40.tiled, s32[2,2,2,64]{3,2,1,0:T(2,128)S(1)} %get-tuple-element.41.table, ...), custom_call_target="tpu_custom_call" | custom-call | tf_op jit(solution)/shard_map/pallas_call | solution.py:464
  11.4 0.0 collective-permute-done.2.core
  11.4 2.6 %collective-permute-done.3.zpair = f32[288,128]{1,0:T(8,128)S(1)} collective-permute-done((f32[288,128]{1,0:T(8,128)S(1)}, f32[288,128]{1,0:T(8,128)S(1)}, u32[]{:S(2)}, u32[]{:S(2)}) %collective-permute-start.3) | collective-permute-done | bytes 147488 | tf_op jit(solution)/shard_map/ppermute | solution.py:481
  14.0 0.2 shard_map.105
  14.2 0.0 collective-permute-done.1.gy
  14.3 0.0 collective-permute-done.dg
  14.3 0.3 %shard_map.106 = (f32[2,10,16,512]{3,2,1,0:T(8,128)S(1)}, f32[16,128]{1,0:T(8,128)S(1)}, f32[4,16,512]{2,1,0:T(8,128)S(1)}) custom-call(f32[296,128]{1,0:T(8,128)S(1)} %collective-permute-done.dg, f32[280,128]{1,0:T(8,128)S(1)} %collective-permute-done.1.gy, f32[256,128]{1,0:T(8,128)S(1)} %get-tuple-element.50.base, ...), custom_call_target="tpu_custom_call" | custom-call | tf_op jit(solution)/shard_map/pallas_call | solution.py:464
  14.6 0.0 copy-start
  14.6 0.1 shard_map.107
  14.7 0.1 collective-permute-start.6
  14.8 2.9 %collective-permute-start.7 = (f32[43,512]{1,0:T(8,128)S(1)}, f32[43,512]{1,0:T(8,128)S(1)}, u32[]{:S(2)}, u32[]{:S(2)}) collective-permute-start(f32[43,512]{1,0:T(8,128)S(1)} %get-tuple-element.57), channel_id=1, source_target_pairs={{0,16},{1,2},{2,1},{3,4},{4,3},{5,6},{6,5},{7,8},{8,7},{9,10},{10,... | collective-permute-start | bytes 264200 | tf_op jit(solution)/shard_map/ppermute | solution.py:481
  17.7 2.8 %collective-permute-start.5 = (f32[16,128]{1,0:T(8,128)S(1)}, f32[16,128]{1,0:T(8,128)S(1)}, u32[]{:S(2)}, u32[]{:S(2)}) collective-permute-start(f32[16,128]{1,0:T(8,128)S(1)} %get-tuple-element.53), channel_id=1, source_target_pairs={{0,112},{1,113},{2,114},{3,115},{4,116},{5,117},{6,118},{7,119},{8... | collective-permute-start | bytes 24584 | tf_op jit(solution)/shard_map/ppermute | solution.py:481
  20.5 0.0 collective-permute-start.4
  20.5 1.5 %collective-permute-done.5.zpair = f32[16,128]{1,0:T(8,128)S(1)} collective-permute-done((f32[16,128]{1,0:T(8,128)S(1)}, f32[16,128]{1,0:T(8,128)S(1)}, u32[]{:S(2)}, u32[]{:S(2)}) %collective-permute-start.5) | collective-permute-done | bytes 8224 | tf_op jit(solution)/shard_map/ppermute | solution.py:481
  22.0 0.0 collective-permute-done.4.core
  22.0 0.0 collective-permute-done.7.xo
  22.0 0.0 collective-permute-done.6.xe
  22.0 0.0 copy-done
  22.0 1.3 %shard_map.108 = (f32[3,16,512]{2,1,0:T(8,128)S(1)}, f32[1,16,512]{2,1,0:T(8,128)S(1)}, bf16[64,512]{1,0:T(8,128)(2,1)S(1)}, f32[32,128]{1,0:T(8,128)S(1)}, f32[...) custom-call(f32[2,10,16,512]{3,2,1,0:T(8,128)S(1)} %get-tuple-element.52.new.old, f32[16,128]{1,0:T(8,128)S(1)} %collective-permute-done.4.core, ...), custom_call_target="tpu_custom_call" | custom-call | tf_op jit(solution)/shard_map/pallas_call | solution.py:464
  23.3 0.7 %collective-permute-start.8 = (f32[32,128]{1,0:T(8,128)S(1)}, f32[32,128]{1,0:T(8,128)S(1)}, u32[]{:S(2)}, u32[]{:S(2)}) collective-permute-start(f32[32,128]{1,0:T(8,128)S(1)} %get-tuple-element.69), channel_id=1, source_target_pairs={{0,17},{1,18},{2,19},{3,20},{4,21},{5,22},{6,23},{7,24},{8,25},{9,... | collective-permute-start | bytes 49160 | tf_op jit(solution)/shard_map/ppermute | solution.py:481
  24.0 0.9 %collective-permute-start.9 = (f32[32,128]{1,0:T(8,128)S(1)}, f32[32,128]{1,0:T(8,128)S(1)}, u32[]{:S(2)}, u32[]{:S(2)}) collective-permute-start(f32[32,128]{1,0:T(8,128)S(1)} %get-tuple-element.70), channel_id=1, source_target_pairs={{0,1},{1,2},{2,3},{3,4},{4,5},{5,6},{6,7},{7,8},{8,9},{9,10},{10,1... | collective-permute-start | bytes 49160 | tf_op jit(solution)/shard_map/ppermute | solution.py:481
  24.9 0.2 collective-permute-start.10
  25.1 1.7 %shard_map.109 = (f32[10,16,512]{2,1,0:T(8,128)}, f32[10,16,512]{2,1,0:T(8,128)}, f32[32,128]{1,0:T(8,128)S(1)}) custom-call(f32[2,10,16,512]{3,2,1,0:T(8,128)S(1)} %get-tuple-element.52.new.old, f32[16,128]{1,0:T(8,128)S(1)} %collective-permute-done.4.core, f32[16,128]{1,0:T(8,128)S(1)} %collective-permute-done.5.zpair, ...), custom_call_target="tpu_custom_call" | custom-call | tf_op jit(solution)/shard_map/pallas_call | solution.py:464
  26.9 3.9 %collective-permute-done.8.dg = f32[32,128]{1,0:T(8,128)S(1)} collective-permute-done((f32[32,128]{1,0:T(8,128)S(1)}, f32[32,128]{1,0:T(8,128)S(1)}, u32[]{:S(2)}, u32[]{:S(2)}) %collective-permute-start.8) | collective-permute-done | bytes 16416 | tf_op jit(solution)/shard_map/ppermute | solution.py:481
  30.8 0.0 collective-permute-done.9.gy
  30.8 0.0 collective-permute-done.10.gx
  30.8 0.7 %shard_map.110 = f32[4,8,128]{2,1,0:T(8,128)} custom-call(f32[32,128]{1,0:T(8,128)S(1)} %collective-permute-done.8.dg, f32[32,128]{1,0:T(8,128)S(1)} %collective-permute-done.9.gy, f32[32,128]{1,0:T(8,128)S(1)} %collective-permute-done.10.gx, f32[32,128]{1,0:T(8,128)S(1)} %get-tuple-element.72.own), custom_call_target="tpu_custom_call" | custom-call | tf_op jit(solution)/shard_map/pallas_call | solution.py:464
Async XLA Ops:
  2.6 11.7 %collective-permute-start = (f32[296,128]{1,0:T(8,128)S(1)}, f32[296,128]{1,0:T(8,128)S(1)}, u32[]{:S(2)}, u32[]{:S(2)}) collective-permute-start(f32[296,128]{1,0:T(8,128)S(1)} %get-tuple-element.38), channel_id=1, source_target_pairs={{0,15},{1,112},{2,113},{3,114},{4,115},{5,116},{6,117},{7,118},{8,... | collective-permute-start | bytes 454664 | tf_op jit(solution)/shard_map/ppermute | solution.py:481
  8.2 5.8 %collective-permute-start.3 = (f32[288,128]{1,0:T(8,128)S(1)}, f32[288,128]{1,0:T(8,128)S(1)}, u32[]{:S(2)}, u32[]{:S(2)}) collective-permute-start(f32[288,128]{1,0:T(8,128)S(1)} %get-tuple-element.48), channel_id=1, source_target_pairs={{0,112},{1,113},{2,114},{3,115},{4,116},{5,117},{6,118},{7,119},{8... | collective-permute-start | bytes 442376 | tf_op jit(solution)/shard_map/ppermute | solution.py:481
  9.1 5.2 %collective-permute-start.1 = (f32[280,128]{1,0:T(8,128)S(1)}, f32[280,128]{1,0:T(8,128)S(1)}, u32[]{:S(2)}, u32[]{:S(2)}) collective-permute-start(f32[280,128]{1,0:T(8,128)S(1)} %get-tuple-element.39), channel_id=1, source_target_pairs={{0,15},{1,0},{2,1},{3,2},{4,3},{5,4},{6,5},{7,6},{8,7},{9,8},{10,9... | collective-permute-start | bytes 430088 | tf_op jit(solution)/shard_map/ppermute | solution.py:481
  9.9 1.5 %collective-permute-start.2 = (f32[272,128]{1,0:T(8,128)S(1)}, f32[272,128]{1,0:T(8,128)S(1)}, u32[]{:S(2)}, u32[]{:S(2)}) collective-permute-start(f32[272,128]{1,0:T(8,128)S(1)} %get-tuple-element.47), channel_id=1, source_target_pairs={{0,16},{1,17},{2,18},{3,19},{4,20},{5,21},{6,22},{7,23},{8,24},{9,... | collective-permute-start | bytes 417800 | tf_op jit(solution)/shard_map/ppermute | solution.py:481
  14.6 7.4 %copy-start = (bf16[1,1,2,2,64,16,128]{6,5,4,3,2,1,0:T(8,128)(2,1)S(1)}, bf16[1,1,2,2,64,16,128]{6,5,4,3,2,1,0:T(8,128)(2,1)}, u32[]{:S(2)}) copy-start(bf16[1,1,2,2,64,16,128]{6,5,4,3,2,1,0:T(8,128)(2,1)} %param.15) | copy-start | bytes 3145732
  14.7 7.3 %collective-permute-start.6 = (f32[48,512]{1,0:T(8,128)S(1)}, f32[48,512]{1,0:T(8,128)S(1)}, u32[]{:S(2)}, u32[]{:S(2)}) collective-permute-start(f32[48,512]{1,0:T(8,128)S(1)} %get-tuple-element.56), channel_id=1, source_target_pairs={{0,1},{1,0},{2,3},{3,2},{4,5},{5,4},{6,7},{7,6},{8,9},{9,8},{10,11... | collective-permute-start | bytes 294920 | tf_op jit(solution)/shard_map/ppermute | solution.py:481
  14.8 7.2 %collective-permute-start.7 = (f32[43,512]{1,0:T(8,128)S(1)}, f32[43,512]{1,0:T(8,128)S(1)}, u32[]{:S(2)}, u32[]{:S(2)}) collective-permute-start(f32[43,512]{1,0:T(8,128)S(1)} %get-tuple-element.57), channel_id=1, source_target_pairs={{0,16},{1,2},{2,1},{3,4},{4,3},{5,6},{6,5},{7,8},{8,7},{9,10},{10,... | collective-permute-start | bytes 264200 | tf_op jit(solution)/shard_map/ppermute | solution.py:481
  17.7 4.3 %collective-permute-start.5 = (f32[16,128]{1,0:T(8,128)S(1)}, f32[16,128]{1,0:T(8,128)S(1)}, u32[]{:S(2)}, u32[]{:S(2)}) collective-permute-start(f32[16,128]{1,0:T(8,128)S(1)} %get-tuple-element.53), channel_id=1, source_target_pairs={{0,112},{1,113},{2,114},{3,115},{4,116},{5,117},{6,118},{7,119},{8... | collective-permute-start | bytes 24584 | tf_op jit(solution)/shard_map/ppermute | solution.py:481
  20.5 1.5 %collective-permute-start.4 = (f32[16,128]{1,0:T(8,128)S(1)}, f32[16,128]{1,0:T(8,128)S(1)}, u32[]{:S(2)}, u32[]{:S(2)}) collective-permute-start(f32[16,128]{1,0:T(8,128)S(1)} %get-tuple-element.53), channel_id=1, source_target_pairs={{0,16},{1,17},{2,18},{3,19},{4,20},{5,21},{6,22},{7,23},{8,24},{9,... | collective-permute-start | bytes 24584 | tf_op jit(solution)/shard_map/ppermute | solution.py:481
  23.3 7.5 %collective-permute-start.8 = (f32[32,128]{1,0:T(8,128)S(1)}, f32[32,128]{1,0:T(8,128)S(1)}, u32[]{:S(2)}, u32[]{:S(2)}) collective-permute-start(f32[32,128]{1,0:T(8,128)S(1)} %get-tuple-element.69), channel_id=1, source_target_pairs={{0,17},{1,18},{2,19},{3,20},{4,21},{5,22},{6,23},{7,24},{8,25},{9,... | collective-permute-start | bytes 49160 | tf_op jit(solution)/shard_map/ppermute | solution.py:481
  24.0 6.8 %collective-permute-start.9 = (f32[32,128]{1,0:T(8,128)S(1)}, f32[32,128]{1,0:T(8,128)S(1)}, u32[]{:S(2)}, u32[]{:S(2)}) collective-permute-start(f32[32,128]{1,0:T(8,128)S(1)} %get-tuple-element.70), channel_id=1, source_target_pairs={{0,1},{1,2},{2,3},{3,4},{4,5},{5,6},{6,7},{7,8},{8,9},{9,10},{10,1... | collective-permute-start | bytes 49160 | tf_op jit(solution)/shard_map/ppermute | solution.py:481
  24.9 5.9 %collective-permute-start.10 = (f32[32,128]{1,0:T(8,128)S(1)}, f32[32,128]{1,0:T(8,128)S(1)}, u32[]{:S(2)}, u32[]{:S(2)}) collective-permute-start(f32[32,128]{1,0:T(8,128)S(1)} %get-tuple-element.71), channel_id=1, source_target_pairs={{0,16},{1,17},{2,18},{3,19},{4,20},{5,21},{6,22},{7,23},{8,24},{9,... | collective-permute-start | bytes 49160 | tf_op jit(solution)/shard_map/ppermute | solution.py:481
